TPU v7x, 32 devices: a whole 2x2x4 slice. The times are simulated.
32 devices in a mesh: gx: 8 (over y, x, core), gy: 4 (over z).
Axes of the slice: x: 2, y: 2, z: 4, core: 2. Of those that a mesh axis runs over, the one named last changes fastest.
Arguments:
- latent: bfloat16 [8, 4, 512, 128], P('gx', 'gy'), may hold values from -6 to 6
- neighbours: int32 [8, 4, 4, 512], P('gx', 'gy'), may hold values from 0 to 511
- top_rows: int32 [8, 4, 2, 256], P('gx', 'gy'), may hold values from 0 to 511
- bottom_rows: int32 [8, 4, 2, 256], P('gx', 'gy'), may hold values from 0 to 511
- edge_top: int32 [8, 4, 2, 1024], P('gx', 'gy'), may hold values from 0 to 255
- edge_bottom: int32 [8, 4, 2, 1024], P('gx', 'gy'), may hold values from 0 to 255
- live_count: int32 [2, 32], P(None, ('gx', 'gy')), may hold values from 1 to 1024, 20480 in all within a row
- edge_weights: bfloat16 [4, 4, 128, 128], replicated, may hold values from -0.5 to 0.5
- node_weights: bfloat16 [4, 3, 128, 128], replicated, may hold values from -0.25 to 0.25
- biases: float32 [4, 3, 128], replicated, may hold values from -3 to 3
Outputs:
- latent_out: bfloat16 [8, 4, 512, 128], P('gx', 'gy')
Inputs may be any that keep to these rules, and one draw needn't show every extreme that they name: `live_count`: live cross edges of each domain in each direction, at most 1024; in each direction some domain has exactly 1024.
All inputs are finite; a program needn't handle non-finite values. No bound on the sum of `live_count` on one device may be relied on, other than what follows from the above.
Results may differ from a plain program's by a relative error of at most 0.024.
Values may be sent and summed in bfloat16 or wider, within the bound.
No kernel may reach another device: no remote copies, remote signals or barrier semaphores. Data moves between devices by JAX's collectives and lax.ppermute only.
A program may use at most 64 MiB of HBM per device.

v0:
```python
import functools

import jax
import jax.numpy as jnp
from jax import lax
from jax.experimental import pallas as pl
from jax.experimental.pallas import tpu as pltpu
from jax.sharding import PartitionSpec as P

BF = jnp.bfloat16
F32 = jnp.float32
VMEM = pl.BlockSpec(memory_space=pltpu.VMEM)
SMEM = pl.BlockSpec(memory_space=pltpu.SMEM)


def shifted(block, axis, distance):
    devices = range(lax.axis_size(axis))
    route = [((i - distance) % len(devices), i) for i in devices]
    return lax.ppermute(block, axis, route)


def call(kernel, outs, *operands, in_specs=None, flops=1, name=None):
    moved = sum(o.size * o.dtype.itemsize for o in operands)
    return pl.pallas_call(
        kernel,
        out_shape=outs,
        in_specs=in_specs or [VMEM] * len(operands),
        out_specs=[VMEM] * len(outs),
        compiler_params=pltpu.CompilerParams(vmem_limit_bytes=40 << 20),
        cost_estimate=pl.CostEstimate(flops=flops, bytes_accessed=moved, transcendentals=0),
        name=name,
    )(*operands)


def dot(a, b):
    return jnp.dot(a, b, preferred_element_type=F32)


def half_silu(y):
    return y + y * jnp.tanh(y)


def column_one_hot(row, depth):
    return (lax.broadcasted_iota(jnp.int32, (depth, row.shape[1]), 0) == row).astype(BF)


def column_mask(bit, width):
    return jnp.broadcast_to(bit.astype(F32), (width, bit.shape[1])).T.astype(BF)


def cut(row, half):
    bit = (row >= half).astype(jnp.int32)
    return bit, row - bit * half


def halves(table):
    half = table.shape[0] // 2
    return jnp.concatenate([table[:half], table[half:]], axis=1)


def choose(both, mask):
    width = both.shape[1] // 2
    return jnp.where(mask > 0, both[:, width:], both[:, :width])


def by_half(values, mask):
    upper = values * mask
    return jnp.concatenate([values - upper, upper], axis=1)


def twice_diagonal(w):
    zero = jnp.zeros_like(w)
    return jnp.concatenate(
        [jnp.concatenate([w, zero], axis=1), jnp.concatenate([zero, w], axis=1)], axis=0
    )


def pick_faces(latent, pick_ref, pick_mask_ref, out_refs):
    table = halves(latent)
    for face, out in enumerate(out_refs):
        picked = choose(dot(pick_ref[face], table), pick_mask_ref[face]).astype(BF)
        out[0 : picked.shape[0], :] = picked


def first_kernel(
    latent_ref, tops_ref, bottoms_ref, etop_ref, ebot_ref, live_ref,
    top_x, top_y, bot_x, bot_y, pick_ref, pick_mask_ref,
):
    half = latent_ref.shape[0] // 2
    width = latent_ref.shape[1]
    for face in range(4):
        ref = (tops_ref, bottoms_ref)[face // 2]
        bit, low = cut(ref[face % 2 : face % 2 + 1, :], half)
        pick_ref[face] = column_one_hot(low, half).T
        pick_mask_ref[face] = column_mask(bit, width)
    pick_faces(latent_ref[...], pick_ref, pick_mask_ref, (top_x, top_y, bot_x, bot_y))
    faces = tops_ref.shape[1]
    slots = etop_ref.shape[1]
    lines = slots // width
    for d, out in enumerate((top_x, top_y)):
        live = lax.broadcasted_iota(jnp.int32, (1, slots), 1) < live_ref[d, 0]
        etop = etop_ref[d : d + 1, :].astype(F32)
        ebot = jnp.where(live, ebot_ref[d : d + 1, :], -1).astype(F32)
        rows = [v[:, i * width : (i + 1) * width] for v in (etop, ebot) for i in range(lines)]
        out[faces:, :] = jnp.concatenate(rows, axis=0).astype(BF)


def group(mine, theirs, face, live, sign, half, width):
    faces = face.shape[1]
    here = column_one_hot(mine, faces)
    gather = jnp.concatenate([here, column_one_hot(theirs, faces)], axis=0).T
    bit, low = cut(face, half)
    lines = jnp.concatenate([low, bit, jnp.zeros((6, faces), jnp.int32)], axis=0)
    ends = dot(lines.astype(F32).astype(BF), here).astype(jnp.int32)
    low, bit = ends[0:1, :], ends[1:2, :]
    ones = column_one_hot(jnp.where(live, low, -1), half)
    return gather, ones if sign > 0 else -ones, column_mask(bit, width)


def setup_kernel(
    nbr_ref, tops_ref, etop_ref, ebot_ref, live_ref,
    pick_ref, spread_ref, mask_ref, gather_ref, sum_ref, half_ref,
):
    half = spread_ref.shape[0]
    width = mask_ref.shape[1]
    rows = nbr_ref.shape[1]
    for k in range(nbr_ref.shape[0]):
        here = slice(k * rows, (k + 1) * rows)
        bit, low = cut(nbr_ref[k : k + 1, :], half)
        ones = column_one_hot(low, half)
        pick_ref[here, :] = ones.T
        spread_ref[:, here] = -ones
        mask_ref[here, :] = column_mask(bit, width)
    slots = etop_ref.shape[1]
    for d in range(2):
        live = lax.broadcasted_iota(jnp.int32, (1, slots), 1) < live_ref[d, 0]
        gather_ref[d], sum_ref[d], half_ref[d] = group(
            etop_ref[d : d + 1, :], ebot_ref[d : d + 1, :], tops_ref[d : d + 1, :],
            live, 1, half, width,
        )


def inner_kernel(
    step, latent_ref, tx_ref, ty_ref, bx_ref, by_ref, weights_ref, nodes_ref, biases_ref,
    pick_ref, spread_ref, mask_ref, total_ref, table_ref, fold_ref,
):
    rows, width = latent_ref.shape
    half = rows // 2
    faces = bx_ref.shape[0]
    w01 = jnp.concatenate([weights_ref[step, 0], weights_ref[step, 1]], axis=1) * BF(0.5)
    for face, ref in enumerate((tx_ref, ty_ref, bx_ref, by_ref)):
        end = face // 2
        table_ref[face] = dot(ref[0:faces, :], w01[:, end * width : (end + 1) * width]).astype(BF)
    fold_ref[...] = dot(weights_ref[step, 3], nodes_ref[step, 1]).astype(BF)
    both = dot(latent_ref[...], w01)
    source = both[:, :width] + biases_ref[step, 0:1, :] * 0.5
    table = halves(both[:, width:].astype(BF))
    w2 = twice_diagonal(weights_ref[step, 2] * BF(0.5))
    c1 = biases_ref[step, 1:2, :] * 0.5
    c1 = jnp.concatenate([c1, c1], axis=1)
    fanout = pick_ref.shape[0] // rows
    total = None
    ended = None
    for pair in range(0, fanout, 2):
        first = []
        for k in (pair, pair + 1):
            here = slice(k * rows, (k + 1) * rows)
            target = choose(dot(pick_ref[here, :], table), mask_ref[here, :])
            first.append(half_silu(target + source).astype(BF))
        second = half_silu(dot(jnp.concatenate(first, axis=1), w2) + c1)
        started = second[:, :width] + second[:, width:]
        total = started if total is None else total + started
        second = second.astype(BF)
        for i in range(2):
            k = pair + i
            here = slice(k * rows, (k + 1) * rows)
            values = by_half(second[:, i * width : (i + 1) * width], mask_ref[here, :])
            part = dot(spread_ref[:, here], values)
            ended = part if ended is None else ended + part
    total_ref[0:half, :] = total[0:half] + ended[:, :width]
    total_ref[half:, :] = total[half:] + ended[:, width:]


def cross(step, d, upper, lower, weights_ref, biases_ref, table_ref, groups):
    width = upper.shape[1]
    c0 = biases_ref[step, 0:1, :] * 0.5
    c1 = biases_ref[step, 1:2, :] * 0.5
    c1 = jnp.concatenate([c1, c1], axis=1)
    w2 = twice_diagonal(weights_ref[step, 2] * BF(0.5))
    far = (
        dot(upper, weights_ref[step, 1] * BF(0.5)).astype(BF),
        dot(lower, weights_ref[step, 0] * BF(0.5)).astype(BF),
    )
    first = []
    for i, (gather, _, _) in enumerate(groups):
        table = jnp.concatenate([table_ref[2 * i + d], far[i]], axis=0)
        first.append(half_silu(dot(gather, table) + c0).astype(BF))
    second = half_silu(dot(jnp.concatenate(first, axis=1), w2) + c1).astype(BF)
    total = None
    for i, (_, place, mask) in enumerate(groups):
        part = dot(place, by_half(second[:, i * width : (i + 1) * width], mask))
        total = part if total is None else total + part
    return total


def lower_group(payload_ref, bottoms_ref, d, half):
    faces = bottoms_ref.shape[1]
    width = payload_ref.shape[1]
    sent = payload_ref[faces:, :].astype(F32)
    lines = sent.shape[0] // 2

    def row(start):
        return jnp.concatenate([sent[start + i : start + i + 1, :] for i in range(lines)], axis=1)

    etop = row(0).astype(jnp.int32)
    ebot = row(lines).astype(jnp.int32)
    return group(ebot, etop, bottoms_ref[d : d + 1, :], ebot >= 0, -1, half, width)


def own_group(refs, d):
    return tuple(ref[d] for ref in refs)


def kept_group(refs):
    return tuple(ref[...] for ref in refs)


def x_kernel(step, *refs):
    (total_ref, upper_ref, lower_ref, weights_ref, biases_ref, table_ref) = refs[:6]
    own = refs[6:9]
    rows, width = total_ref.shape
    half = rows // 2
    faces = upper_ref.shape[0]
    if step == 0:
        bottoms_ref, out_ref = refs[9], refs[10]
        keep = refs[11:14]
        for ref, value in zip(keep, lower_group(lower_ref, bottoms_ref, 0, half)):
            ref[...] = value
    else:
        keep, out_ref = refs[9:12], refs[12]
    both = cross(
        step, 0, upper_ref[...], lower_ref[0:faces, :], weights_ref, biases_ref, table_ref,
        (own_group(own, 0), kept_group(keep)),
    )
    out_ref[0:half, :] = total_ref[0:half, :] + both[:, :width]
    out_ref[half:, :] = total_ref[half:, :] + both[:, width:]


def y_kernel(step, last, *refs):
    (total_ref, upper_ref, lower_ref, weights_ref, biases_ref, table_ref) = refs[:6]
    own = refs[6:9]
    latent_ref, nodes_ref, fold_ref = refs[9:12]
    rest = list(refs[12:])
    rows, width = total_ref.shape
    half = rows // 2
    faces = upper_ref.shape[0]
    if step == 0:
        bottoms_ref = rest.pop(0)
    else:
        keep, rest = rest[:3], rest[3:]
    if not last:
        pick_ref, pick_mask_ref, rest = rest[0], rest[1], rest[2:]
    out_ref = rest.pop(0)
    if not last:
        sends, rest = rest[:4], rest[4:]
    if step == 0:
        keep = rest
        for ref, value in zip(keep, lower_group(lower_ref, bottoms_ref, 1, half)):
            ref[...] = value
    both = cross(
        step, 1, upper_ref[...], lower_ref[0:faces, :], weights_ref, biases_ref, table_ref,
        (own_group(own, 1), kept_group(keep)),
    )
    arrived = total_ref[...] + jnp.concatenate([both[:, :width], both[:, width:]], axis=0)
    latent = latent_ref[...]
    matrix = jnp.concatenate([nodes_ref[step, 0], fold_ref[...]], axis=0) * BF(0.5)
    joined = jnp.concatenate([latent, arrived.astype(BF)], axis=1)
    update = half_silu(dot(joined, matrix) + biases_ref[step, 2:3, :] * 0.5).astype(BF)
    latent = (latent.astype(F32) + dot(update, nodes_ref[step, 2])).astype(BF)
    out_ref[...] = latent
    if not last:
        pick_faces(latent, pick_ref, pick_mask_ref, sends)


def local(
    latent,
    neighbours,
    top_rows,
    bottom_rows,
    edge_top,
    edge_bottom,
    live_count,
    edge_weights,
    node_weights,
    biases,
):
    latent_now = latent[0, 0]
    rows, width = latent_now.shape
    half = rows // 2
    nbr = neighbours[0, 0]
    tops = top_rows[0, 0]
    bottoms = bottom_rows[0, 0]
    etop = edge_top[0, 0]
    ebot = edge_bottom[0, 0]
    fanout = nbr.shape[0]
    faces = tops.shape[1]
    slots = etop.shape[1]
    steps = edge_weights.shape[0]
    like = jax.ShapeDtypeStruct
    face = like((faces, width), BF)
    packed = like((faces + 2 * (slots // width), width), BF)
    index_specs = [VMEM] * 4 + [SMEM]
    *sends, pick, pick_mask = call(
        first_kernel,
        [packed, packed, face, face, like((4, faces, half), BF), like((4, faces, width), BF)],
        latent_now, tops, bottoms, etop, ebot, live_count,
        in_specs=[VMEM] + index_specs,
        name="first",
    )
    group_like = [like((slots, 2 * faces), BF), like((half, slots), BF), like((slots, width), BF)]
    inner = call(
        setup_kernel,
        [like((fanout * rows, half), BF), like((half, fanout * rows), BF),
         like((fanout * rows, width), BF)]
        + [like((2,) + g.shape, BF) for g in group_like],
        nbr, tops, etop, ebot, live_count,
        in_specs=index_specs,
        name="setup",
    )
    inner, own = inner[:3], inner[3:]
    kept_x = kept_y = None
    for step in range(steps):
        last = step == steps - 1
        top_x, top_y, bot_x, bot_y = sends
        lower_y = shifted(top_y, "gy", 1)
        upper_y = shifted(bot_y, "gy", -1)
        lower_x = shifted(top_x, "gx", 1)
        upper_x = shifted(bot_x, "gx", -1)
        total, table, fold = call(
            functools.partial(inner_kernel, step),
            [like((rows, width), F32), like((4, faces, width), BF), like((width, width), BF)],
            latent_now, *sends, edge_weights, node_weights, biases, *inner,
            flops=1 << 30,
            name="inner",
        )
        first = step == 0
        total, *made = call(
            functools.partial(x_kernel, step),
            [like((rows, width), F32)] + (group_like if first else []),
            total, upper_x, lower_x, edge_weights, biases, table, *own,
            *([bottoms] if first else kept_x),
            flops=1 << 30,
            name="along_x",
        )
        kept_x = made if first else kept_x
        outs = [like((rows, width), BF)] + ([] if last else [face] * 4)
        latent_now, *made = call(
            functools.partial(y_kernel, step, last),
            outs + (group_like if first else []),
            total, upper_y, lower_y, edge_weights, biases, table, *own,
            latent_now, node_weights, fold,
            *([bottoms] if first else kept_y),
            *([] if last else [pick, pick_mask]),
            flops=1 << 30,
            name="along_y",
        )
        sends, made = made[:4], made[4:]
        kept_y = made if first else kept_y
    return latent_now[None, None]


def solution(mesh):
    return jax.shard_map(
        local,
        mesh=mesh,
        in_specs=(
            P("gx", "gy", None, None),
            P("gx", "gy", None, None),
            P("gx", "gy", None, None),
            P("gx", "gy", None, None),
            P("gx", "gy", None, None),
            P("gx", "gy", None, None),
            P(None, ("gx", "gy")),
            P(),
            P(),
            P(),
        ),
        out_specs=P("gx", "gy", None, None),
        check_vma=False,
    )
```

profile of v0, /device:TPU:0, one launch (start us, length us, event | category | flops | bytes accessed | tf_op | source)
XLA Modules:
  0.0 63.0 jit_solution(686866781947487251)
XLA Ops:
  0.0 0.7 %copy.11.live_ref = s32[2,1]{1,0:T(2,128)S(1)} copy(s32[2,1]{0,1:T(1,128)} %param.16) | data formatting | bytes 16 | tf_op args[6]
  0.7 0.9 %copy-done.4 = bf16[1,1,512,128]{3,2,1,0:T(8,128)(2,1)S(1)} copy-done((bf16[1,1,512,128]{3,2,1,0:T(8,128)(2,1)S(1)}, bf16[1,1,512,128]{3,2,1,0:T(8,128)(2,1)}, u32[]{:S(2)}) %copy-start.4) | copy-done | bytes 131096
  1.6 0.7 %copy-done.7 = s32[1,1,2,1024]{3,2,1,0:T(2,128)S(1)} copy-done((s32[1,1,2,1024]{3,2,1,0:T(2,128)S(1)}, s32[1,1,2,1024]{3,2,1,0:T(2,128)}, u32[]{:S(2)}) %copy-start.7) | copy-done | bytes 8216
  2.3 0.7 %copy-done.9 = s32[1,1,2,1024]{3,2,1,0:T(2,128)S(1)} copy-done((s32[1,1,2,1024]{3,2,1,0:T(2,128)S(1)}, s32[1,1,2,1024]{3,2,1,0:T(2,128)}, u32[]{:S(2)}) %copy-start.9) | copy-done | bytes 8216
  4.4 1.0 %first.1 = (bf16[272,128]{1,0:T(8,128)(2,1)S(1)}, bf16[272,128]{1,0:T(8,128)(2,1)S(1)}, bf16[256,128]{1,0:T(8,128)(2,1)S(1)}, bf16[256,128]{1,0:T(8,128)(2,1)S(1...) custom-call(bf16[512,128]{1,0:T(8,128)(2,1)S(1)} %bitcast.7, s32[2,256]{1,0:T(2,128)S(1)} %bitcast.17, ...), custom_call_target="tpu_custom_call" | custom-call | flops 1 | bytes 151560 | tf_op jit(solution)/shard_map/first/pallas_call | solution.py:24
  5.4 3.4 %collective-permute-start = (bf16[256,128]{1,0:T(8,128)(2,1)S(1)}, bf16[256,128]{1,0:T(8,128)(2,1)S(1)}, u32[]{:S(2)}, u32[]{:S(2)}) collective-permute-start(bf16[256,128]{1,0:T(8,128)(2,1)S(1)} %get-tuple-element.53.bx_ref), channel_id=1, source_target_pairs={{4,0},{8,4},{12,8},{16,12},{20,16},{24,20},{28,24},{0,28},{5,1},{9... | collective-permute-start | bytes 196616 | tf_op jit(solution)/shard_map/ppermute | solution.py:19
  8.8 3.6 %collective-permute-start.2 = (bf16[256,128]{1,0:T(8,128)(2,1)S(1)}, bf16[256,128]{1,0:T(8,128)(2,1)S(1)}, u32[]{:S(2)}, u32[]{:S(2)}) collective-permute-start(bf16[256,128]{1,0:T(8,128)(2,1)S(1)} %get-tuple-element.54.by_ref), channel_id=1, source_target_pairs={{1,0},{2,1},{3,2},{0,3},{5,4},{6,5},{7,6},{4,7},{9,8},{10,9},{11,1... | collective-permute-start | bytes 196616 | tf_op jit(solution)/shard_map/ppermute | solution.py:19
  12.4 0.7 %copy.13.biases_ref.refs_4_ = f32[4,3,128]{2,1,0:T(4,128)S(1)} copy(f32[4,3,128]{2,0,1:T(4,128)} %param.19) | data formatting | bytes 12288 | tf_op args[9]
  13.1 0.7 %copy-done.8 = s32[1,1,2,1024]{3,2,1,0:T(2,128)S(1)} copy-done((s32[1,1,2,1024]{3,2,1,0:T(2,128)S(1)}, s32[1,1,2,1024]{3,2,1,0:T(2,128)}, u32[]{:S(2)}) %copy-start.8) | copy-done | bytes 8216
  13.8 0.7 %copy-done.10 = s32[1,1,2,1024]{3,2,1,0:T(2,128)S(1)} copy-done((s32[1,1,2,1024]{3,2,1,0:T(2,128)S(1)}, s32[1,1,2,1024]{3,2,1,0:T(2,128)}, u32[]{:S(2)}) %copy-start.10) | copy-done | bytes 8216
  15.8 2.3 %setup.1 = (bf16[2048,256]{1,0:T(8,128)(2,1)S(1)}, bf16[256,2048]{1,0:T(8,128)(2,1)S(1)}, bf16[2048,128]{1,0:T(8,128)(2,1)S(1)}, bf16[2,1024,512]{2,1,0:T(8,128)...) custom-call(s32[4,512]{1,0:T(4,128)S(1)} %bitcast.19, s32[2,256]{1,0:T(2,128)S(1)} %bitcast.18, ...), custom_call_target="tpu_custom_call" | custom-call | flops 1 | bytes 26632 | tf_op jit(solution)/shard_map/setup/pallas_call | solution.py:24
  18.2 1.0 %copy-done = bf16[4,4,128,128]{3,2,1,0:T(8,128)(2,1)S(1)} copy-done((bf16[4,4,128,128]{3,2,1,0:T(8,128)(2,1)S(1)}, bf16[4,4,128,128]{3,2,1,0:T(8,128)(2,1)}, u32[]{:S(2)}) %copy-start) | copy-done | bytes 524312
  19.2 1.0 %copy-done.2 = bf16[4,3,128,128]{3,2,1,0:T(8,128)(2,1)S(1)} copy-done((bf16[4,3,128,128]{3,2,1,0:T(8,128)(2,1)S(1)}, bf16[4,3,128,128]{3,2,1,0:T(8,128)(2,1)}, u32[]{:S(2)}) %copy-start.2) | copy-done | bytes 393240
  20.2 0.9 %copy-done.5 = bf16[1,1,512,128]{3,2,1,0:T(8,128)(2,1)S(1)} copy-done((bf16[1,1,512,128]{3,2,1,0:T(8,128)(2,1)S(1)}, bf16[1,1,512,128]{3,2,1,0:T(8,128)(2,1)}, u32[]{:S(2)}) %copy-start.5) | copy-done | bytes 131096
  21.1 1.7 %inner.4 = (f32[512,128]{1,0:T(8,128)S(1)}, bf16[4,256,128]{2,1,0:T(8,128)(2,1)S(1)}, bf16[128,128]{1,0:T(8,128)(2,1)S(1)}) custom-call(bf16[512,128]{1,0:T(8,128)(2,1)S(1)} %bitcast.8, bf16[272,128]{1,0:T(8,128)(2,1)S(1)} %get-tuple-element.51.tx_ref, bf16[272,128]{1,0:T(8,128)(2,1)S(1)} %get-tuple-element.52.ty_ref, ...), custom_call_target="tpu_custom_call" | custom-call | flops 1073741824 | bytes 3946496 | tf_op jit(solution)/shard_map/inner/pallas_call | solution.py:24
  22.9 1.8 %along_x.4 = (f32[512,128]{1,0:T(8,128)S(1)}, bf16[1024,512]{1,0:T(8,128)(2,1)S(1)}, bf16[256,1024]{1,0:T(8,128)(2,1)S(1)}, bf16[1024,128]{1,0:T(8,128)(2,1)S(1)}) custom-call(f32[512,128]{1,0:T(8,128)S(1)} %get-tuple-element.58.refs_0_, bf16[256,128]{1,0:T(8,128)(2,1)S(1)} %collective-permute-done.refs_1_, ...), custom_call_target="tpu_custom_call" | custom-call | flops 1073741824 | bytes 4861952 | tf_op jit(solution)/shard_map/along_x/pallas_call | solution.py:24
  24.8 2.3 %along_y.4 = (bf16[512,128]{1,0:T(8,128)(2,1)S(1)}, bf16[256,128]{1,0:T(8,128)(2,1)S(1)}, bf16[256,128]{1,0:T(8,128)(2,1)S(1)}, bf16[256,128]{1,0:T(8,128)(2,1)S...) custom-call(f32[512,128]{1,0:T(8,128)S(1)} %get-tuple-element.63.ref, ...), custom_call_target="tpu_custom_call" | custom-call | flops 1073741824 | bytes 6205440 | tf_op jit(solution)/shard_map/along_y/pallas_call | solution.py:24
  27.2 2.7 %collective-permute-start.4 = (bf16[256,128]{1,0:T(8,128)(2,1)S(1)}, bf16[256,128]{1,0:T(8,128)(2,1)S(1)}, u32[]{:S(2)}, u32[]{:S(2)}) collective-permute-start(bf16[256,128]{1,0:T(8,128)(2,1)S(1)} %get-tuple-element.70.bx_ref), channel_id=1, source_target_pairs={{4,0},{8,4},{12,8},{16,12},{20,16},{24,20},{28,24},{0,28},{5,1},{9... | collective-permute-start | bytes 196616 | tf_op jit(solution)/shard_map/ppermute | solution.py:19
  29.9 3.7 %collective-permute-start.6 = (bf16[256,128]{1,0:T(8,128)(2,1)S(1)}, bf16[256,128]{1,0:T(8,128)(2,1)S(1)}, u32[]{:S(2)}, u32[]{:S(2)}) collective-permute-start(bf16[256,128]{1,0:T(8,128)(2,1)S(1)} %get-tuple-element.71.by_ref), channel_id=1, source_target_pairs={{1,0},{2,1},{3,2},{0,3},{5,4},{6,5},{7,6},{4,7},{9,8},{10,9},{11,1... | collective-permute-start | bytes 196616 | tf_op jit(solution)/shard_map/ppermute | solution.py:19
  33.6 1.7 %inner.5 = (f32[512,128]{1,0:T(8,128)S(1)}, bf16[4,256,128]{2,1,0:T(8,128)(2,1)S(1)}, bf16[128,128]{1,0:T(8,128)(2,1)S(1)}) custom-call(bf16[512,128]{1,0:T(8,128)(2,1)S(1)} %get-tuple-element.67.latent_ref.refs_9_, bf16[256,128]{1,0:T(8,128)(2,1)S(1)} %get-tuple-element.68.tx_ref, bf16[256,128]{1,0:T(8,128)(2,1)S(1)} %get-tuple-element.69.ty_ref, ...), custom_call_target="tpu_custom_call" | custom-call | flops 1073741824 | bytes 3938304 | tf_op jit(solution)/shard_map/inner/pallas_call | solution.py:24
  35.4 1.6 %along_x.5.refs_0_ = f32[512,128]{1,0:T(8,128)S(1)} custom-call(f32[512,128]{1,0:T(8,128)S(1)} %get-tuple-element.72.refs_0_, bf16[256,128]{1,0:T(8,128)(2,1)S(1)} %collective-permute-done.4.refs_1_, bf16[256,128]{1,0:T(8,128)(2,1)S(1)} %collective-permute-done.5.refs_2_, bf16[4,4,128,128]{3,2,1,0:T(8,128)(2,1)S(1)} %copy-done.1, ...), custom_call_target="tpu_custom_call" | custom-call | flops 1073741824 | bytes 6690816 | tf_op jit(solution)/shard_map/along_x/pallas_call | solution.py:24
  37.0 2.1 %along_y.5 = (bf16[512,128]{1,0:T(8,128)(2,1)S(1)}, bf16[256,128]{1,0:T(8,128)(2,1)S(1)}, bf16[256,128]{1,0:T(8,128)(2,1)S(1)}, bf16[256,128]{1,0:T(8,128)(2,1)S(1)}, bf16[256,128]{1,0:T(8,128)(2,1)S(1)}) custom-call(f32[512,128]{1,0:T(8,128)S(1)} %along_x.5.refs_0_, bf16[256,128]{1,0:T(8,128)(2,1)S(1)} %collective-permute-done.6.refs_1_, ...), custom_call_target="tpu_custom_call" | custom-call | flops 1073741824 | bytes 8034304 | tf_op jit(solution)/shard_map/along_y/pallas_call | solution.py:24
  39.2 2.6 %collective-permute-start.8 = (bf16[256,128]{1,0:T(8,128)(2,1)S(1)}, bf16[256,128]{1,0:T(8,128)(2,1)S(1)}, u32[]{:S(2)}, u32[]{:S(2)}) collective-permute-start(bf16[256,128]{1,0:T(8,128)(2,1)S(1)} %get-tuple-element.84.bx_ref), channel_id=1, source_target_pairs={{4,0},{8,4},{12,8},{16,12},{20,16},{24,20},{28,24},{0,28},{5,1},{9... | collective-permute-start | bytes 196616 | tf_op jit(solution)/shard_map/ppermute | solution.py:19
  41.8 3.5 %collective-permute-start.10 = (bf16[256,128]{1,0:T(8,128)(2,1)S(1)}, bf16[256,128]{1,0:T(8,128)(2,1)S(1)}, u32[]{:S(2)}, u32[]{:S(2)}) collective-permute-start(bf16[256,128]{1,0:T(8,128)(2,1)S(1)} %get-tuple-element.85.by_ref), channel_id=1, source_target_pairs={{1,0},{2,1},{3,2},{0,3},{5,4},{6,5},{7,6},{4,7},{9,8},{10,9},{11,1... | collective-permute-start | bytes 196616 | tf_op jit(solution)/shard_map/ppermute | solution.py:19
  45.3 1.7 %inner.6 = (f32[512,128]{1,0:T(8,128)S(1)}, bf16[4,256,128]{2,1,0:T(8,128)(2,1)S(1)}, bf16[128,128]{1,0:T(8,128)(2,1)S(1)}) custom-call(bf16[512,128]{1,0:T(8,128)(2,1)S(1)} %get-tuple-element.81.latent_ref.refs_9_, bf16[256,128]{1,0:T(8,128)(2,1)S(1)} %get-tuple-element.82.tx_ref, bf16[256,128]{1,0:T(8,128)(2,1)S(1)} %get-tuple-element.83.ty_ref, ...), custom_call_target="tpu_custom_call" | custom-call | flops 1073741824 | bytes 3938304 | tf_op jit(solution)/shard_map/inner/pallas_call | solution.py:24
  47.1 1.6 %along_x.6.refs_0_ = f32[512,128]{1,0:T(8,128)S(1)} custom-call(f32[512,128]{1,0:T(8,128)S(1)} %get-tuple-element.86.refs_0_, bf16[256,128]{1,0:T(8,128)(2,1)S(1)} %collective-permute-done.8.refs_1_, bf16[256,128]{1,0:T(8,128)(2,1)S(1)} %collective-permute-done.9.refs_2_, bf16[4,4,128,128]{3,2,1,0:T(8,128)(2,1)S(1)} %copy-done.1, ...), custom_call_target="tpu_custom_call" | custom-call | flops 1073741824 | bytes 6690816 | tf_op jit(solution)/shard_map/along_x/pallas_call | solution.py:24
  48.7 2.1 %along_y.6 = (bf16[512,128]{1,0:T(8,128)(2,1)S(1)}, bf16[256,128]{1,0:T(8,128)(2,1)S(1)}, bf16[256,128]{1,0:T(8,128)(2,1)S(1)}, bf16[256,128]{1,0:T(8,128)(2,1)S(1)}, bf16[256,128]{1,0:T(8,128)(2,1)S(1)}) custom-call(f32[512,128]{1,0:T(8,128)S(1)} %along_x.6.refs_0_, bf16[256,128]{1,0:T(8,128)(2,1)S(1)} %collective-permute-done.10.refs_1_, ...), custom_call_target="tpu_custom_call" | custom-call | flops 1073741824 | bytes 8034304 | tf_op jit(solution)/shard_map/along_y/pallas_call | solution.py:24
  51.0 2.6 %collective-permute-start.12 = (bf16[256,128]{1,0:T(8,128)(2,1)S(1)}, bf16[256,128]{1,0:T(8,128)(2,1)S(1)}, u32[]{:S(2)}, u32[]{:S(2)}) collective-permute-start(bf16[256,128]{1,0:T(8,128)(2,1)S(1)} %get-tuple-element.92.bx_ref), channel_id=1, source_target_pairs={{4,0},{8,4},{12,8},{16,12},{20,16},{24,20},{28,24},{0,28},{5,1},{9... | collective-permute-start | bytes 196616 | tf_op jit(solution)/shard_map/ppermute | solution.py:19
  53.5 3.5 %collective-permute-start.14 = (bf16[256,128]{1,0:T(8,128)(2,1)S(1)}, bf16[256,128]{1,0:T(8,128)(2,1)S(1)}, u32[]{:S(2)}, u32[]{:S(2)}) collective-permute-start(bf16[256,128]{1,0:T(8,128)(2,1)S(1)} %get-tuple-element.93.by_ref), channel_id=1, source_target_pairs={{1,0},{2,1},{3,2},{0,3},{5,4},{6,5},{7,6},{4,7},{9,8},{10,9},{11,1... | collective-permute-start | bytes 196616 | tf_op jit(solution)/shard_map/ppermute | solution.py:19
  57.1 1.7 %inner.7 = (f32[512,128]{1,0:T(8,128)S(1)}, bf16[4,256,128]{2,1,0:T(8,128)(2,1)S(1)}, bf16[128,128]{1,0:T(8,128)(2,1)S(1)}) custom-call(bf16[512,128]{1,0:T(8,128)(2,1)S(1)} %get-tuple-element.89.latent_ref.refs_9_, bf16[256,128]{1,0:T(8,128)(2,1)S(1)} %get-tuple-element.90.tx_ref, bf16[256,128]{1,0:T(8,128)(2,1)S(1)} %get-tuple-element.91.ty_ref, ...), custom_call_target="tpu_custom_call" | custom-call | flops 1073741824 | bytes 3938304 | tf_op jit(solution)/shard_map/inner/pallas_call | solution.py:24
  58.8 1.6 %along_x.7.refs_0_ = f32[512,128]{1,0:T(8,128)S(1)} custom-call(f32[512,128]{1,0:T(8,128)S(1)} %get-tuple-element.94.refs_0_, bf16[256,128]{1,0:T(8,128)(2,1)S(1)} %collective-permute-done.12.refs_1_, bf16[256,128]{1,0:T(8,128)(2,1)S(1)} %collective-permute-done.13.refs_2_, bf16[4,4,128,128]{3,2,1,0:T(8,128)(2,1)S(1)} %copy-done.1, ...), custom_call_target="tpu_custom_call" | custom-call | flops 1073741824 | bytes 6690816 | tf_op jit(solution)/shard_map/along_x/pallas_call | solution.py:24
  60.5 2.6 %along_y.7 = bf16[512,128]{1,0:T(8,128)(2,1)} custom-call(f32[512,128]{1,0:T(8,128)S(1)} %along_x.7.refs_0_, bf16[256,128]{1,0:T(8,128)(2,1)S(1)} %collective-permute-done.14.refs_1_, bf16[256,128]{1,0:T(8,128)(2,1)S(1)} %collective-permute-done.15.refs_2_, bf16[4,4,128,128]{3,2,1,0:T(8,128)(2,1)S(1)} %copy-done.1, ...), custom_call_target="tpu_custom_call" | custom-call | flops 1073741824 | bytes 7247872 | tf_op jit(solution)/shard_map/along_y/pallas_call | solution.py:24
  (48 shorter events, 3.2 us)
Async XLA Ops:
  0.7 0.9 %copy-start.4 = (bf16[1,1,512,128]{3,2,1,0:T(8,128)(2,1)S(1)}, bf16[1,1,512,128]{3,2,1,0:T(8,128)(2,1)}, u32[]{:S(2)}) copy-start(bf16[1,1,512,128]{3,2,1,0:T(8,128)(2,1)} %param.10) | copy-start | bytes 393220
  1.6 0.7 %copy-start.7 = (s32[1,1,2,1024]{3,2,1,0:T(2,128)S(1)}, s32[1,1,2,1024]{3,2,1,0:T(2,128)}, u32[]{:S(2)}) copy-start(s32[1,1,2,1024]{3,2,1,0:T(2,128)} %param.14) | copy-start | bytes 24580
  2.3 0.7 %copy-start.9 = (s32[1,1,2,1024]{3,2,1,0:T(2,128)S(1)}, s32[1,1,2,1024]{3,2,1,0:T(2,128)}, u32[]{:S(2)}) copy-start(s32[1,1,2,1024]{3,2,1,0:T(2,128)} %param.15) | copy-start | bytes 24580
  3.0 0.7 %copy-start.11 = (s32[1,1,2,256]{3,2,1,0:T(2,128)S(1)}, s32[1,1,2,256]{3,2,1,0:T(2,128)}, u32[]{:S(2)}) copy-start(s32[1,1,2,256]{3,2,1,0:T(2,128)} %param.13) | copy-start | bytes 6148
  3.7 0.7 %copy-start.13 = (s32[1,1,2,256]{3,2,1,0:T(2,128)S(1)}, s32[1,1,2,256]{3,2,1,0:T(2,128)}, u32[]{:S(2)}) copy-start(s32[1,1,2,256]{3,2,1,0:T(2,128)} %param.12) | copy-start | bytes 6148
  4.4 18.5 %copy-start.12 = (s32[1,1,2,256]{3,2,1,0:T(2,128)S(1)}, s32[1,1,2,256]{3,2,1,0:T(2,128)}, u32[]{:S(2)}) copy-start(s32[1,1,2,256]{3,2,1,0:T(2,128)} %param.13) | copy-start | bytes 6148
  5.4 17.5 %collective-permute-start = (bf16[256,128]{1,0:T(8,128)(2,1)S(1)}, bf16[256,128]{1,0:T(8,128)(2,1)S(1)}, u32[]{:S(2)}, u32[]{:S(2)}) collective-permute-start(bf16[256,128]{1,0:T(8,128)(2,1)S(1)} %get-tuple-element.53.bx_ref), channel_id=1, source_target_pairs={{4,0},{8,4},{12,8},{16,12},{20,16},{24,20},{28,24},{0,28},{5,1},{9... | collective-permute-start | bytes 196616 | tf_op jit(solution)/shard_map/ppermute | solution.py:19
  8.8 16.0 %collective-permute-start.2 = (bf16[256,128]{1,0:T(8,128)(2,1)S(1)}, bf16[256,128]{1,0:T(8,128)(2,1)S(1)}, u32[]{:S(2)}, u32[]{:S(2)}) collective-permute-start(bf16[256,128]{1,0:T(8,128)(2,1)S(1)} %get-tuple-element.54.by_ref), channel_id=1, source_target_pairs={{1,0},{2,1},{3,2},{0,3},{5,4},{6,5},{7,6},{4,7},{9,8},{10,9},{11,1... | collective-permute-start | bytes 196616 | tf_op jit(solution)/shard_map/ppermute | solution.py:19
  12.4 10.5 %collective-permute-start.1 = (bf16[272,128]{1,0:T(8,128)(2,1)S(1)}, bf16[272,128]{1,0:T(8,128)(2,1)S(1)}, u32[]{:S(2)}, u32[]{:S(2)}) collective-permute-start(bf16[272,128]{1,0:T(8,128)(2,1)S(1)} %get-tuple-element.51.tx_ref), channel_id=1, source_target_pairs={{28,0},{0,4},{4,8},{8,12},{12,16},{16,20},{20,24},{24,28},{29,1},{... | collective-permute-start | bytes 208904 | tf_op jit(solution)/shard_map/ppermute | solution.py:19
  12.4 12.4 %collective-permute-start.3 = (bf16[272,128]{1,0:T(8,128)(2,1)S(1)}, bf16[272,128]{1,0:T(8,128)(2,1)S(1)}, u32[]{:S(2)}, u32[]{:S(2)}) collective-permute-start(bf16[272,128]{1,0:T(8,128)(2,1)S(1)} %get-tuple-element.52.ty_ref), channel_id=1, source_target_pairs={{3,0},{0,1},{1,2},{2,3},{7,4},{4,5},{5,6},{6,7},{11,8},{8,9},{9,10... | collective-permute-start | bytes 208904 | tf_op jit(solution)/shard_map/ppermute | solution.py:19
  13.1 0.7 %copy-start.8 = (s32[1,1,2,1024]{3,2,1,0:T(2,128)S(1)}, s32[1,1,2,1024]{3,2,1,0:T(2,128)}, u32[]{:S(2)}) copy-start(s32[1,1,2,1024]{3,2,1,0:T(2,128)} %param.14) | copy-start | bytes 24580
  13.8 0.7 %copy-start.10 = (s32[1,1,2,1024]{3,2,1,0:T(2,128)S(1)}, s32[1,1,2,1024]{3,2,1,0:T(2,128)}, u32[]{:S(2)}) copy-start(s32[1,1,2,1024]{3,2,1,0:T(2,128)} %param.15) | copy-start | bytes 24580
  14.5 0.7 %copy-start.14 = (s32[1,1,2,256]{3,2,1,0:T(2,128)S(1)}, s32[1,1,2,256]{3,2,1,0:T(2,128)}, u32[]{:S(2)}) copy-start(s32[1,1,2,256]{3,2,1,0:T(2,128)} %param.12) | copy-start | bytes 6148
  15.1 0.7 %copy-start.15 = (s32[1,1,4,512]{3,2,1,0:T(4,128)S(1)}, s32[1,1,4,512]{3,2,1,0:T(4,128)}, u32[]{:S(2)}) copy-start(s32[1,1,4,512]{3,2,1,0:T(4,128)} %param.11) | copy-start | bytes 24580
  18.2 1.0 %copy-start = (bf16[4,4,128,128]{3,2,1,0:T(8,128)(2,1)S(1)}, bf16[4,4,128,128]{3,2,1,0:T(8,128)(2,1)}, u32[]{:S(2)}) copy-start(bf16[4,4,128,128]{3,2,1,0:T(8,128)(2,1)} %refs_3_.15) | copy-start | bytes 1572868
  19.2 1.0 %copy-start.2 = (bf16[4,3,128,128]{3,2,1,0:T(8,128)(2,1)S(1)}, bf16[4,3,128,128]{3,2,1,0:T(8,128)(2,1)}, u32[]{:S(2)}) copy-start(bf16[4,3,128,128]{3,2,1,0:T(8,128)(2,1)} %refs_10_.7) | copy-start | bytes 1179652
  20.2 0.9 %copy-start.5 = (bf16[1,1,512,128]{3,2,1,0:T(8,128)(2,1)S(1)}, bf16[1,1,512,128]{3,2,1,0:T(8,128)(2,1)}, u32[]{:S(2)}) copy-start(bf16[1,1,512,128]{3,2,1,0:T(8,128)(2,1)} %param.10) | copy-start | bytes 393220
  21.1 1.8 %copy-start.1 = (bf16[4,4,128,128]{3,2,1,0:T(8,128)(2,1)S(1)}, bf16[4,4,128,128]{3,2,1,0:T(8,128)(2,1)}, u32[]{:S(2)}) copy-start(bf16[4,4,128,128]{3,2,1,0:T(8,128)(2,1)} %refs_3_.15) | copy-start | bytes 1572868
  22.9 1.9 %copy-start.6 = (bf16[1,1,512,128]{3,2,1,0:T(8,128)(2,1)S(1)}, bf16[1,1,512,128]{3,2,1,0:T(8,128)(2,1)}, u32[]{:S(2)}) copy-start(bf16[1,1,512,128]{3,2,1,0:T(8,128)(2,1)} %param.10) | copy-start | bytes 393220
  24.8 8.8 %copy-start.3 = (bf16[4,3,128,128]{3,2,1,0:T(8,128)(2,1)S(1)}, bf16[4,3,128,128]{3,2,1,0:T(8,128)(2,1)}, u32[]{:S(2)}) copy-start(bf16[4,3,128,128]{3,2,1,0:T(8,128)(2,1)} %refs_10_.7) | copy-start | bytes 1179652
  27.1 8.3 %collective-permute-start.5 = (bf16[256,128]{1,0:T(8,128)(2,1)S(1)}, bf16[256,128]{1,0:T(8,128)(2,1)S(1)}, u32[]{:S(2)}, u32[]{:S(2)}) collective-permute-start(bf16[256,128]{1,0:T(8,128)(2,1)S(1)} %get-tuple-element.68.tx_ref), channel_id=1, source_target_pairs={{28,0},{0,4},{4,8},{8,12},{12,16},{16,20},{20,24},{24,28},{29,1},{... | collective-permute-start | bytes 196616 | tf_op jit(solution)/shard_map/ppermute | solution.py:19
  27.2 9.8 %collective-permute-start.7 = (bf16[256,128]{1,0:T(8,128)(2,1)S(1)}, bf16[256,128]{1,0:T(8,128)(2,1)S(1)}, u32[]{:S(2)}, u32[]{:S(2)}) collective-permute-start(bf16[256,128]{1,0:T(8,128)(2,1)S(1)} %get-tuple-element.69.ty_ref), channel_id=1, source_target_pairs={{3,0},{0,1},{1,2},{2,3},{7,4},{4,5},{5,6},{6,7},{11,8},{8,9},{9,10... | collective-permute-start | bytes 196616 | tf_op jit(solution)/shard_map/ppermute | solution.py:19
  27.2 8.1 %collective-permute-start.4 = (bf16[256,128]{1,0:T(8,128)(2,1)S(1)}, bf16[256,128]{1,0:T(8,128)(2,1)S(1)}, u32[]{:S(2)}, u32[]{:S(2)}) collective-permute-start(bf16[256,128]{1,0:T(8,128)(2,1)S(1)} %get-tuple-element.70.bx_ref), channel_id=1, source_target_pairs={{4,0},{8,4},{12,8},{16,12},{20,16},{24,20},{28,24},{0,28},{5,1},{9... | collective-permute-start | bytes 196616 | tf_op jit(solution)/shard_map/ppermute | solution.py:19
  29.9 7.1 %collective-permute-start.6 = (bf16[256,128]{1,0:T(8,128)(2,1)S(1)}, bf16[256,128]{1,0:T(8,128)(2,1)S(1)}, u32[]{:S(2)}, u32[]{:S(2)}) collective-permute-start(bf16[256,128]{1,0:T(8,128)(2,1)S(1)} %get-tuple-element.71.by_ref), channel_id=1, source_target_pairs={{1,0},{2,1},{3,2},{0,3},{5,4},{6,5},{7,6},{4,7},{9,8},{10,9},{11,1... | collective-permute-start | bytes 196616 | tf_op jit(solution)/shard_map/ppermute | solution.py:19
  39.1 8.0 %collective-permute-start.9 = (bf16[256,128]{1,0:T(8,128)(2,1)S(1)}, bf16[256,128]{1,0:T(8,128)(2,1)S(1)}, u32[]{:S(2)}, u32[]{:S(2)}) collective-permute-start(bf16[256,128]{1,0:T(8,128)(2,1)S(1)} %get-tuple-element.82.tx_ref), channel_id=1, source_target_pairs={{28,0},{0,4},{4,8},{8,12},{12,16},{16,20},{20,24},{24,28},{29,1},{... | collective-permute-start | bytes 196616 | tf_op jit(solution)/shard_map/ppermute | solution.py:19
  39.2 9.5 %collective-permute-start.11 = (bf16[256,128]{1,0:T(8,128)(2,1)S(1)}, bf16[256,128]{1,0:T(8,128)(2,1)S(1)}, u32[]{:S(2)}, u32[]{:S(2)}) collective-permute-start(bf16[256,128]{1,0:T(8,128)(2,1)S(1)} %get-tuple-element.83.ty_ref), channel_id=1, source_target_pairs={{3,0},{0,1},{1,2},{2,3},{7,4},{4,5},{5,6},{6,7},{11,8},{8,9},{9,10... | collective-permute-start | bytes 196616 | tf_op jit(solution)/shard_map/ppermute | solution.py:19
  39.2 7.9 %collective-permute-start.8 = (bf16[256,128]{1,0:T(8,128)(2,1)S(1)}, bf16[256,128]{1,0:T(8,128)(2,1)S(1)}, u32[]{:S(2)}, u32[]{:S(2)}) collective-permute-start(bf16[256,128]{1,0:T(8,128)(2,1)S(1)} %get-tuple-element.84.bx_ref), channel_id=1, source_target_pairs={{4,0},{8,4},{12,8},{16,12},{20,16},{24,20},{28,24},{0,28},{5,1},{9... | collective-permute-start | bytes 196616 | tf_op jit(solution)/shard_map/ppermute | solution.py:19
  41.8 6.9 %collective-permute-start.10 = (bf16[256,128]{1,0:T(8,128)(2,1)S(1)}, bf16[256,128]{1,0:T(8,128)(2,1)S(1)}, u32[]{:S(2)}, u32[]{:S(2)}) collective-permute-start(bf16[256,128]{1,0:T(8,128)(2,1)S(1)} %get-tuple-element.85.by_ref), channel_id=1, source_target_pairs={{1,0},{2,1},{3,2},{0,3},{5,4},{6,5},{7,6},{4,7},{9,8},{10,9},{11,1... | collective-permute-start | bytes 196616 | tf_op jit(solution)/shard_map/ppermute | solution.py:19
  50.8 8.0 %collective-permute-start.13 = (bf16[256,128]{1,0:T(8,128)(2,1)S(1)}, bf16[256,128]{1,0:T(8,128)(2,1)S(1)}, u32[]{:S(2)}, u32[]{:S(2)}) collective-permute-start(bf16[256,128]{1,0:T(8,128)(2,1)S(1)} %get-tuple-element.90.tx_ref), channel_id=1, source_target_pairs={{28,0},{0,4},{4,8},{8,12},{12,16},{16,20},{20,24},{24,28},{29,1},{... | collective-permute-start | bytes 196616 | tf_op jit(solution)/shard_map/ppermute | solution.py:19
  50.9 9.5 %collective-permute-start.15 = (bf16[256,128]{1,0:T(8,128)(2,1)S(1)}, bf16[256,128]{1,0:T(8,128)(2,1)S(1)}, u32[]{:S(2)}, u32[]{:S(2)}) collective-permute-start(bf16[256,128]{1,0:T(8,128)(2,1)S(1)} %get-tuple-element.91.ty_ref), channel_id=1, source_target_pairs={{3,0},{0,1},{1,2},{2,3},{7,4},{4,5},{5,6},{6,7},{11,8},{8,9},{9,10... | collective-permute-start | bytes 196616 | tf_op jit(solution)/shard_map/ppermute | solution.py:19
  51.0 7.9 %collective-permute-start.12 = (bf16[256,128]{1,0:T(8,128)(2,1)S(1)}, bf16[256,128]{1,0:T(8,128)(2,1)S(1)}, u32[]{:S(2)}, u32[]{:S(2)}) collective-permute-start(bf16[256,128]{1,0:T(8,128)(2,1)S(1)} %get-tuple-element.92.bx_ref), channel_id=1, source_target_pairs={{4,0},{8,4},{12,8},{16,12},{20,16},{24,20},{28,24},{0,28},{5,1},{9... | collective-permute-start | bytes 196616 | tf_op jit(solution)/shard_map/ppermute | solution.py:19
  53.5 6.9 %collective-permute-start.14 = (bf16[256,128]{1,0:T(8,128)(2,1)S(1)}, bf16[256,128]{1,0:T(8,128)(2,1)S(1)}, u32[]{:S(2)}, u32[]{:S(2)}) collective-permute-start(bf16[256,128]{1,0:T(8,128)(2,1)S(1)} %get-tuple-element.93.by_ref), channel_id=1, source_target_pairs={{1,0},{2,1},{3,2},{0,3},{5,4},{6,5},{7,6},{4,7},{9,8},{10,9},{11,1... | collective-permute-start | bytes 196616 | tf_op jit(solution)/shard_map/ppermute | solution.py:19
where the time goes:
time: 63.6 us; the launch traced here: 63 us
  starting transfers between devices  26 us (41%)
  Pallas kernels  25.9 us (41%)
  local copies, waits for them, and re-layouts  10.8 us (17%)
    ppermute x16, starting transfers between devices, shifted(): return lax.ppermute(block, axis, route)  26 us
    pallas_call x14, Pallas kernels, call(): pl.pallas_call(kernel, out_shape=outs, in_specs=in_specs or [VMEM] * len(...  25.9 us
    unnamed x34, local copies, waits for them, and re-layouts  10.8 us
  transfers between devices with their start and end apart: 16, of which 0 were waited for; matrix products, arithmetic and copies ran while one was open for 1% of the time, Pallas kernels for 25%

commit v1 on v0

v1 whole, which is shorter than its diff:
```python
import functools

import jax
import jax.numpy as jnp
from jax import lax
from jax.experimental import pallas as pl
from jax.experimental.pallas import tpu as pltpu
from jax.sharding import PartitionSpec as P

BF = jnp.bfloat16
F32 = jnp.float32
I32 = jnp.int32
VMEM = pl.BlockSpec(memory_space=pltpu.VMEM)
HBM = pl.BlockSpec(memory_space=pltpu.HBM)


def swapped(block, axis, odd):
    count = lax.axis_size(axis)
    route = []
    for i in range(odd, count, 2):
        j = (i + 1) % count
        route += [(i, j), (j, i)]
    return lax.ppermute(block, axis, route)


def call(kernel, outs, operands, in_specs=None, scratch=(), name=None):
    moved = sum(o.size * o.dtype.itemsize for o in operands)
    return pl.pallas_call(
        kernel,
        out_shape=outs,
        in_specs=in_specs or [VMEM] * len(operands),
        out_specs=[VMEM] * len(outs),
        scratch_shapes=list(scratch),
        compiler_params=pltpu.CompilerParams(vmem_limit_bytes=40 << 20),
        cost_estimate=pl.CostEstimate(flops=1 << 30, bytes_accessed=moved, transcendentals=0),
        name=name,
    )(*operands)


def dot(a, b):
    return jnp.dot(a, b, preferred_element_type=F32)


def half_silu(y):
    return y + y * jnp.tanh(y)


def column_one_hot(row, depth):
    return (lax.broadcasted_iota(I32, (depth, row.shape[1]), 0) == row).astype(BF)


def column_mask(bit, width):
    return jnp.broadcast_to(bit.astype(F32), (width, bit.shape[1])).T.astype(BF)


def cut(row, half):
    bit = (row >= half).astype(I32)
    return bit, row - bit * half


def halves(table):
    half = table.shape[0] // 2
    return jnp.concatenate([table[:half], table[half:]], axis=1)


def choose(both, mask):
    width = both.shape[1] // 2
    return jnp.where(mask > 0, both[:, width:], both[:, :width])


def by_half(values, mask):
    upper = values * mask
    return jnp.concatenate([values - upper, upper], axis=1)


def odd_place():
    return lax.axis_index("gx") % 2, lax.axis_index("gy") % 2


def in_order(odd, first, second):
    turned = odd == 1
    return jnp.where(turned, second, first), jnp.where(turned, first, second)


def pick_faces(latent, pick_ref, pick_mask_ref, out_refs):
    table = halves(latent)
    rows = [
        choose(dot(pick_ref[face], table), pick_mask_ref[face]).astype(BF) for face in range(4)
    ]
    for d, odd in enumerate(odd_place()):
        near, far = in_order(odd, rows[2 * d], rows[2 * d + 1])
        count = near.shape[0]
        out_refs[2 * d][0:count, :] = near
        out_refs[2 * d + 1][0:count, :] = far


def first_kernel(
    latent_hbm, tops_hbm, bottoms_hbm, etop_hbm, ebot_hbm, live_hbm,
    near_x, far_x, near_y, far_y, latent_ref, tops_ref, bottoms_ref, ends_ref,
    pick_ref, pick_mask_ref,
    etop_ref, ebot_ref, live_ref, sems,
):
    moves = [
        pltpu.make_async_copy(src, dst, sems.at[i])
        for i, (src, dst) in enumerate((
            (tops_hbm, tops_ref), (bottoms_hbm, bottoms_ref), (latent_hbm, latent_ref),
            (etop_hbm, etop_ref), (ebot_hbm, ebot_ref), (live_hbm, live_ref),
        ))
    ]
    for move in moves:
        move.start()
    half = latent_ref.shape[0] // 2
    width = latent_ref.shape[1]
    moves[0].wait()
    moves[1].wait()
    for face in range(4):
        d, ref = face // 2, (tops_ref, bottoms_ref)[face % 2]
        bit, low = cut(ref[d : d + 1, :], half)
        pick_ref[face] = column_one_hot(low, half).T
        pick_mask_ref[face] = column_mask(bit, width)
    for move in moves[2:]:
        move.wait()
    sends = (near_x, far_x, near_y, far_y)
    pick_faces(latent_ref[...], pick_ref, pick_mask_ref, sends)
    faces = tops_ref.shape[1]
    slots = etop_ref.shape[1]
    lines = slots // width
    for d in range(2):
        live = lax.broadcasted_iota(I32, (1, slots), 1) < live_ref[d, 0]
        etop = etop_ref[d : d + 1, :].astype(F32)
        ebot = jnp.where(live, ebot_ref[d : d + 1, :], -1).astype(F32)
        rows = [v[:, i * width : (i + 1) * width] for v in (etop, ebot) for i in range(lines)]
        ends = jnp.concatenate(rows, axis=0).astype(BF)
        ends_ref[d] = ends
        sends[2 * d][faces:, :] = ends
        sends[2 * d + 1][faces:, :] = ends


def unpacked(ends):
    ends = ends.astype(F32)
    lines = ends.shape[0] // 2

    def row(start):
        parts = [ends[start + i : start + i + 1, :] for i in range(lines)]
        return jnp.concatenate(parts, axis=1).astype(I32)

    return row(0), row(lines)


def group(mine, theirs, face, live, sign, half, width):
    faces = face.shape[1]
    here = column_one_hot(mine, faces)
    gather = jnp.concatenate([here, column_one_hot(theirs, faces)], axis=0).T
    bit, low = cut(face, half)
    lines = jnp.concatenate([low, bit, jnp.zeros((6, faces), I32)], axis=0)
    ends = dot(lines.astype(F32).astype(BF), here).astype(I32)
    low, bit = ends[0:1, :], ends[1:2, :]
    ones = column_one_hot(jnp.where(live, low, -1), half)
    return gather, ones if sign > 0 else -ones, column_mask(bit, width)


def setup_kernel(
    nbr_hbm, weights_hbm, nodes_hbm, biases_hbm, tops_ref, ends_ref,
    pick_ref, spread_ref, mask_ref, gather_ref, sum_ref, half_ref,
    ends_w_ref, hidden_ref, join_ref, out_w_ref, biases_ref,
    nbr_ref, weights_ref, nodes_ref, raw_biases_ref, sems,
):
    moves = [
        pltpu.make_async_copy(src, dst, sems.at[i])
        for i, (src, dst) in enumerate((
            (nbr_hbm, nbr_ref), (weights_hbm, weights_ref), (nodes_hbm, nodes_ref),
            (biases_hbm, raw_biases_ref),
        ))
    ]
    for move in moves:
        move.start()
    half = spread_ref.shape[0]
    width = mask_ref.shape[1]
    for d in range(2):
        etop, ebot = unpacked(ends_ref[d])
        gather_ref[d], sum_ref[d], half_ref[d] = group(
            etop, ebot, tops_ref[d : d + 1, :], ebot >= 0, 1, half, width
        )
    for move in moves:
        move.wait()
    rows = nbr_ref.shape[1]
    for k in range(nbr_ref.shape[0]):
        here = slice(k * rows, (k + 1) * rows)
        bit, low = cut(nbr_ref[k : k + 1, :], half)
        ones = column_one_hot(low, half)
        pick_ref[here, :] = ones.T
        spread_ref[:, here] = -ones
        mask_ref[here, :] = column_mask(bit, width)
    biases_ref[...] = raw_biases_ref[...] * 0.5
    zero = jnp.zeros((width, width), BF)
    for step in range(weights_ref.shape[0]):
        ends_w_ref[step, 0] = weights_ref[step, 0] * BF(0.5)
        ends_w_ref[step, 1] = weights_ref[step, 1] * BF(0.5)
        hidden = weights_ref[step, 2] * BF(0.5)
        hidden_ref[step] = jnp.concatenate(
            [jnp.concatenate([hidden, zero], axis=1), jnp.concatenate([zero, hidden], axis=1)],
            axis=0,
        )
        fold = dot(weights_ref[step, 3], nodes_ref[step, 1]).astype(BF)
        join_ref[step] = jnp.concatenate([nodes_ref[step, 0], fold], axis=0) * BF(0.5)
        out_w_ref[step] = nodes_ref[step, 2]


def inner_kernel(
    step, latent_ref, near_x, far_x, near_y, far_y, ends_w_ref, hidden_ref, biases_ref,
    pick_ref, spread_ref, mask_ref, total_ref, table_ref,
):
    rows, width = latent_ref.shape
    half = rows // 2
    faces = table_ref.shape[1]
    for d, odd in enumerate(odd_place()):
        near, far = (ref[0:faces, :] for ref in ((near_x, far_x), (near_y, far_y))[d])
        top, bottom = in_order(odd, near, far)
        table_ref[2 * d] = dot(top, ends_w_ref[step, 0]).astype(BF)
        table_ref[2 * d + 1] = dot(bottom, ends_w_ref[step, 1]).astype(BF)
    latent = latent_ref[...]
    source = dot(latent, ends_w_ref[step, 0]) + biases_ref[step, 0:1, :]
    table = halves(dot(latent, ends_w_ref[step, 1]).astype(BF))
    c1 = biases_ref[step, 1:2, :]
    c1 = jnp.concatenate([c1, c1], axis=1)
    fanout = pick_ref.shape[0] // rows
    total = None
    ended = None
    for pair in range(0, fanout, 2):
        first = []
        for k in (pair, pair + 1):
            here = slice(k * rows, (k + 1) * rows)
            target = choose(dot(pick_ref[here, :], table), mask_ref[here, :])
            first.append(half_silu(target + source).astype(BF))
        second = half_silu(dot(jnp.concatenate(first, axis=1), hidden_ref[step]) + c1)
        started = second[:, :width] + second[:, width:]
        total = started if total is None else total + started
        second = second.astype(BF)
        for i in range(2):
            k = pair + i
            here = slice(k * rows, (k + 1) * rows)
            values = by_half(second[:, i * width : (i + 1) * width], mask_ref[here, :])
            part = dot(spread_ref[:, here], values)
            ended = part if ended is None else ended + part
    total_ref[0:half, :] = total[0:half] + ended[:, :width]
    total_ref[half:, :] = total[half:] + ended[:, width:]


def cross(step, d, upper, lower, ends_w_ref, hidden_ref, biases_ref, table_ref, groups):
    width = upper.shape[1]
    c0 = biases_ref[step, 0:1, :]
    c1 = biases_ref[step, 1:2, :]
    c1 = jnp.concatenate([c1, c1], axis=1)
    far = (
        dot(upper, ends_w_ref[step, 1]).astype(BF),
        dot(lower, ends_w_ref[step, 0]).astype(BF),
    )
    first = []
    for i, (gather, _, _) in enumerate(groups):
        table = jnp.concatenate([table_ref[2 * d + i], far[i]], axis=0)
        first.append(half_silu(dot(gather, table) + c0).astype(BF))
    second = half_silu(dot(jnp.concatenate(first, axis=1), hidden_ref[step]) + c1).astype(BF)
    total = None
    for i, (_, place, mask) in enumerate(groups):
        part = dot(place, by_half(second[:, i * width : (i + 1) * width], mask))
        total = part if total is None else total + part
    return total


def lower_group(ends, bottoms_ref, d, half):
    etop, ebot = unpacked(ends)
    return group(ebot, etop, bottoms_ref[d : d + 1, :], ebot >= 0, -1, half, ends.shape[1])


def along(step, d, refs, rows):
    near_ref, far_ref, ends_w_ref, hidden_ref, biases_ref, table_ref = refs[:6]
    own = tuple(ref[d] for ref in refs[6:9])
    half = rows // 2
    faces = table_ref.shape[1]
    upper, lower = in_order(odd_place()[d], near_ref[...], far_ref[...])
    if step == 0:
        bottoms_ref, keep = refs[9], refs[-3:]
        for ref, value in zip(keep, lower_group(lower[faces:], bottoms_ref, d, half)):
            ref[...] = value
        used = 10
    else:
        keep = refs[9:12]
        used = 12
    both = cross(
        step, d, upper[:faces], lower[:faces], ends_w_ref, hidden_ref, biases_ref, table_ref,
        (own, tuple(ref[...] for ref in keep)),
    )
    return both, used


def x_kernel(step, total_ref, *refs):
    rows, width = total_ref.shape
    half = rows // 2
    both, used = along(step, 0, refs, rows)
    out_ref = refs[used]
    out_ref[0:half, :] = total_ref[0:half, :] + both[:, :width]
    out_ref[half:, :] = total_ref[half:, :] + both[:, width:]


def y_kernel(step, last, total_ref, *refs):
    rows, width = total_ref.shape
    both, used = along(step, 1, refs, rows)
    biases_ref = refs[4]
    latent_ref, join_ref, out_w_ref = refs[used : used + 3]
    rest = refs[used + 3 :]
    arrived = total_ref[...] + jnp.concatenate([both[:, :width], both[:, width:]], axis=0)
    latent = latent_ref[...]
    joined = jnp.concatenate([latent, arrived.astype(BF)], axis=1)
    update = half_silu(dot(joined, join_ref[step]) + biases_ref[step, 2:3, :]).astype(BF)
    latent = (latent.astype(F32) + dot(update, out_w_ref[step])).astype(BF)
    if last:
        rest[0][...] = latent
    else:
        pick_ref, pick_mask_ref, out_ref = rest[:3]
        out_ref[...] = latent
        pick_faces(latent, pick_ref, pick_mask_ref, rest[3:7])


def local(
    latent,
    neighbours,
    top_rows,
    bottom_rows,
    edge_top,
    edge_bottom,
    live_count,
    edge_weights,
    node_weights,
    biases,
):
    latent_now = latent[0, 0]
    rows, width = latent_now.shape
    half = rows // 2
    nbr = neighbours[0, 0]
    tops = top_rows[0, 0]
    bottoms = bottom_rows[0, 0]
    etop = edge_top[0, 0]
    ebot = edge_bottom[0, 0]
    fanout = nbr.shape[0]
    faces = tops.shape[1]
    slots = etop.shape[1]
    steps = edge_weights.shape[0]
    like = jax.ShapeDtypeStruct
    face = like((faces, width), BF)
    lines = 2 * (slots // width)
    packed = like((faces + lines, width), BF)
    *sends, latent_now, tops, bottoms, ends, pick, pick_mask = call(
        first_kernel,
        [packed] * 4 + [
            like((rows, width), BF), like(tops.shape, I32), like(tops.shape, I32),
            like((2, lines, width), BF), like((4, faces, half), BF), like((4, faces, width), BF),
        ],
        (latent_now, tops, bottoms, etop, ebot, live_count),
        in_specs=[HBM] * 6,
        scratch=[
            pltpu.VMEM(etop.shape, I32), pltpu.VMEM(etop.shape, I32),
            pltpu.SMEM(live_count.shape, I32), pltpu.SemaphoreType.DMA((6,)),
        ],
        name="first",
    )
    group_like = [
        like((slots, 2 * faces), BF), like((half, slots), BF), like((slots, width), BF)
    ]
    kept_x = kept_y = None
    for step in range(steps):
        first, last = step == 0, step == steps - 1
        near_x, far_x, near_y, far_y = sends
        got_far_y = swapped(far_y, "gy", 1)
        got_near_y = swapped(near_y, "gy", 0)
        got_far_x = swapped(far_x, "gx", 1)
        got_near_x = swapped(near_x, "gx", 0)
        if first:
            made = call(
                setup_kernel,
                [like((fanout * rows, half), BF), like((half, fanout * rows), BF),
                 like((fanout * rows, width), BF)]
                + [like((2,) + g.shape, BF) for g in group_like]
                + [like((steps, 2, width, width), BF), like((steps, 2 * width, 2 * width), BF),
                   like((steps, 2 * width, width), BF), like((steps, width, width), BF),
                   like(biases.shape, F32)],
                (nbr, edge_weights, node_weights, biases, tops, ends),
                in_specs=[HBM] * 4 + [VMEM] * 2,
                scratch=[
                    pltpu.VMEM(nbr.shape, I32), pltpu.VMEM(edge_weights.shape, BF),
                    pltpu.VMEM(node_weights.shape, BF), pltpu.VMEM(biases.shape, F32),
                    pltpu.SemaphoreType.DMA((4,)),
                ],
                name="setup",
            )
            inner, own = made[:3], made[3:6]
            ends_w, hidden, join, out_w, half_biases = made[6:]
            edge_net = (ends_w, hidden, half_biases)
        total, table = call(
            functools.partial(inner_kernel, step),
            [like((rows, width), F32), like((4, faces, width), BF)],
            (latent_now, *sends, *edge_net, *inner),
            name="inner",
        )
        total, *made = call(
            functools.partial(x_kernel, step),
            [like((rows, width), F32)] + (group_like if first else []),
            (total, got_near_x, got_far_x, *edge_net, table, *own,
             *([bottoms] if first else kept_x)),
            name="along_x",
        )
        kept_x = made if first else kept_x
        latent_now, *made = call(
            functools.partial(y_kernel, step, last),
            [like((rows, width), BF)] + ([] if last else [face] * 4)
            + (group_like if first else []),
            (total, got_near_y, got_far_y, *edge_net, table, *own,
             *([bottoms] if first else kept_y), latent_now, join, out_w,
             *([] if last else [pick, pick_mask])),
            name="along_y",
        )
        sends, made = made[:4], made[4:]
        kept_y = made if first else kept_y
    return latent_now[None, None]


def solution(mesh):
    return jax.shard_map(
        local,
        mesh=mesh,
        in_specs=(
            P("gx", "gy", None, None),
            P("gx", "gy", None, None),
            P("gx", "gy", None, None),
            P("gx", "gy", None, None),
            P("gx", "gy", None, None),
            P("gx", "gy", None, None),
            P(None, ("gx", "gy")),
            P(),
            P(),
            P(),
        ),
        out_specs=P("gx", "gy", None, None),
        check_vma=False,
    )
```

time: 63.6 us -> 53.1 us (0.83)
  starting transfers between devices: 26 us -> 17.4 us
  local copies, waits for them, and re-layouts: 10.8 us -> 4.5 us
  waiting for transfers between devices: 0.04 us -> 4.87 us
    ppermute x16, starting transfers between devices: 26 us -> 17.4 us  [swapped(): return lax.ppermute(block, axis, route)]
    unnamed x34 -> x20, local copies, waits for them, and re-layouts: 10.8 us -> 4.5 us
    ppermute x16, waiting for transfers between devices: 0.04 us -> 4.87 us  [swapped(): return lax.ppermute(block, axis, route)]
  transfers between devices with their start and end apart: 16 -> 16, of which waited for: 0 -> 5; matrix products, arithmetic and copies ran while one was open for 1% -> 0% of each run, Pallas kernels for 25% -> 30%
where the time goes in v1:
time: 53.1 us; the launch traced here: 52.8 us
  Pallas kernels  25.8 us (49%)
  starting transfers between devices  17.4 us (33%)
  waiting for transfers between devices  4.87 us (9%)
  local copies, waits for them, and re-layouts  4.5 us (8%)
    pallas_call x14, Pallas kernels, call(): pl.pallas_call(kernel, out_shape=outs, in_specs=in_specs or [VMEM] * len(...  25.8 us
    ppermute x16, starting transfers between devices, swapped(): return lax.ppermute(block, axis, route)  17.4 us
    ppermute x16, waiting for transfers between devices, swapped(): return lax.ppermute(block, axis, route)  4.87 us
    unnamed x20, local copies, waits for them, and re-layouts  4.5 us
  transfers between devices with their start and end apart: 16, of which 5 were waited for; matrix products, arithmetic and copies ran while one was open for 0% of the time, Pallas kernels for 30%

profile of v1, /device:TPU:0, one launch (start us, length us, event | category | flops | bytes accessed | tf_op | source)
XLA Modules:
  0.0 52.8 jit_solution(6467761313453194420)
XLA Ops:
  0.0 0.8 %copy.11.live_hbm = s32[2,1]{1,0:T(2,128)S(1)} copy(s32[2,1]{0,1:T(1,128)} %param.16) | data formatting | bytes 16 | tf_op args[6]
  0.8 0.9 %copy-done.2 = bf16[1,1,512,128]{3,2,1,0:T(8,128)(2,1)S(1)} copy-done((bf16[1,1,512,128]{3,2,1,0:T(8,128)(2,1)S(1)}, bf16[1,1,512,128]{3,2,1,0:T(8,128)(2,1)}, u32[]{:S(2)}) %copy-start.2) | copy-done | bytes 131096
  1.7 0.7 %copy-done.3 = s32[1,1,2,1024]{3,2,1,0:T(2,128)S(1)} copy-done((s32[1,1,2,1024]{3,2,1,0:T(2,128)S(1)}, s32[1,1,2,1024]{3,2,1,0:T(2,128)}, u32[]{:S(2)}) %copy-start.3) | copy-done | bytes 8216
  2.4 0.7 %copy-done.4 = s32[1,1,2,1024]{3,2,1,0:T(2,128)S(1)} copy-done((s32[1,1,2,1024]{3,2,1,0:T(2,128)S(1)}, s32[1,1,2,1024]{3,2,1,0:T(2,128)}, u32[]{:S(2)}) %copy-start.4) | copy-done | bytes 8216
  3.1 0.7 %copy-done.6 = s32[1,1,2,256]{3,2,1,0:T(2,128)S(1)} copy-done((s32[1,1,2,256]{3,2,1,0:T(2,128)S(1)}, s32[1,1,2,256]{3,2,1,0:T(2,128)}, u32[]{:S(2)}) %copy-start.6) | copy-done | bytes 2072
  4.5 1.1 %first.1 = (bf16[272,128]{1,0:T(8,128)(2,1)S(1)}, bf16[272,128]{1,0:T(8,128)(2,1)S(1)}, bf16[272,128]{1,0:T(8,128)(2,1)S(1)}, bf16[272,128]{1,0:T(8,128)(2,1)S(1...) custom-call(bf16[512,128]{1,0:T(8,128)(2,1)S(1)} %bitcast.7, ...), custom_call_target="tpu_custom_call" | custom-call | flops 1073741824 | bytes 151560 | tf_op jit(solution)/shard_map/first/pallas_call | solution.py:28
  6.1 3.6 %collective-permute-start.1 = (bf16[272,128]{1,0:T(8,128)(2,1)S(1)}, bf16[272,128]{1,0:T(8,128)(2,1)S(1)}, u32[]{:S(2)}, u32[]{:S(2)}) collective-permute-start(bf16[272,128]{1,0:T(8,128)(2,1)S(1)} %get-tuple-element.58.far_x), channel_id=1, source_target_pairs={{4,8},{8,4},{12,16},{16,12},{20,24},{24,20},{28,0},{0,28},{5,9},{9... | collective-permute-start | bytes 208904 | tf_op jit(solution)/shard_map/ppermute | solution.py:23
  9.7 1.6 %collective-permute-start.2 = (bf16[272,128]{1,0:T(8,128)(2,1)S(1)}, bf16[272,128]{1,0:T(8,128)(2,1)S(1)}, u32[]{:S(2)}, u32[]{:S(2)}) collective-permute-start(bf16[272,128]{1,0:T(8,128)(2,1)S(1)} %get-tuple-element.59.near_y), channel_id=1, source_target_pairs={{0,1},{1,0},{2,3},{3,2},{4,5},{5,4},{6,7},{7,6},{8,9},{9,8},{10,11... | collective-permute-start | bytes 208904 | tf_op jit(solution)/shard_map/ppermute | solution.py:23
  11.2 2.5 %collective-permute-start.3 = (bf16[272,128]{1,0:T(8,128)(2,1)S(1)}, bf16[272,128]{1,0:T(8,128)(2,1)S(1)}, u32[]{:S(2)}, u32[]{:S(2)}) collective-permute-start(bf16[272,128]{1,0:T(8,128)(2,1)S(1)} %get-tuple-element.60.far_y), channel_id=1, source_target_pairs={{1,2},{2,1},{3,0},{0,3},{5,6},{6,5},{7,4},{4,7},{9,10},{10,9},{11,... | collective-permute-start | bytes 208904 | tf_op jit(solution)/shard_map/ppermute | solution.py:23
  13.8 2.3 %setup.1 = (bf16[2048,256]{1,0:T(8,128)(2,1)S(1)}, bf16[256,2048]{1,0:T(8,128)(2,1)S(1)}, bf16[2048,128]{1,0:T(8,128)(2,1)S(1)}, bf16[2,1024,512]{2,1,0:T(8,128)...) custom-call(s32[4,512]{1,0:T(4,128)S(1)} %bitcast.10, ...), custom_call_target="tpu_custom_call" | custom-call | flops 1073741824 | bytes 942080 | tf_op jit(solution)/shard_map/setup/pallas_call | solution.py:28
  16.1 1.6 %inner.4 = (f32[512,128]{1,0:T(8,128)S(1)}, bf16[4,256,128]{2,1,0:T(8,128)(2,1)S(1)}) custom-call(bf16[512,128]{1,0:T(8,128)(2,1)S(1)} %get-tuple-element.56.latent_ref.refs_10_, bf16[272,128]{1,0:T(8,128)(2,1)S(1)} %get-tuple-element.57.near_x, bf16[272,128]{1,0:T(8,128)(2,1)S(1)} %get-tuple-element.58.far_x, ...), custom_call_target="tpu_custom_call" | custom-call | flops 1073741824 | bytes 3823616 | tf_op jit(solution)/shard_map/inner/pallas_call | solution.py:28
  17.7 1.9 %along_x.4 = (f32[512,128]{1,0:T(8,128)S(1)}, bf16[1024,512]{1,0:T(8,128)(2,1)S(1)}, bf16[256,1024]{1,0:T(8,128)(2,1)S(1)}, bf16[1024,128]{1,0:T(8,128)(2,1)S(1)}) custom-call(f32[512,128]{1,0:T(8,128)S(1)} %get-tuple-element.69.total_ref, bf16[272,128]{1,0:T(8,128)(2,1)S(1)} %collective-permute-done.refs_0_, ...), custom_call_target="tpu_custom_call" | custom-call | flops 1073741824 | bytes 5128192 | tf_op jit(solution)/shard_map/along_x/pallas_call | solution.py:28
  19.6 2.3 %along_y.4 = (bf16[512,128]{1,0:T(8,128)(2,1)S(1)}, bf16[256,128]{1,0:T(8,128)(2,1)S(1)}, bf16[256,128]{1,0:T(8,128)(2,1)S(1)}, bf16[256,128]{1,0:T(8,128)(2,1)S...) custom-call(f32[512,128]{1,0:T(8,128)S(1)} %get-tuple-element.75.tot, ...), custom_call_target="tpu_custom_call" | custom-call | flops 1073741824 | bytes 6438912 | tf_op jit(solution)/shard_map/along_y/pallas_call | solution.py:28
  23.4 0.9 %collective-permute-start.7 = (bf16[256,128]{1,0:T(8,128)(2,1)S(1)}, bf16[256,128]{1,0:T(8,128)(2,1)S(1)}, u32[]{:S(2)}, u32[]{:S(2)}) collective-permute-start(bf16[256,128]{1,0:T(8,128)(2,1)S(1)} %get-tuple-element.84.far_y), channel_id=1, source_target_pairs={{1,2},{2,1},{3,0},{0,3},{5,6},{6,5},{7,4},{4,7},{9,10},{10,9},{11,... | collective-permute-start | bytes 196616 | tf_op jit(solution)/shard_map/ppermute | solution.py:23
  24.3 1.6 %inner.5 = (f32[512,128]{1,0:T(8,128)S(1)}, bf16[4,256,128]{2,1,0:T(8,128)(2,1)S(1)}) custom-call(bf16[512,128]{1,0:T(8,128)(2,1)S(1)} %get-tuple-element.80.latent_ref.refs_12_, bf16[256,128]{1,0:T(8,128)(2,1)S(1)} %get-tuple-element.81.near_x, bf16[256,128]{1,0:T(8,128)(2,1)S(1)} %get-tuple-element.82.far_x, ...), custom_call_target="tpu_custom_call" | custom-call | flops 1073741824 | bytes 3807232 | tf_op jit(solution)/shard_map/inner/pallas_call | solution.py:28
  25.9 1.2 %collective-permute-done.5.refs_1_ = bf16[256,128]{1,0:T(8,128)(2,1)S(1)} collective-permute-done((bf16[256,128]{1,0:T(8,128)(2,1)S(1)}, bf16[256,128]{1,0:T(8,128)(2,1)S(1)}, u32[]{:S(2)}, u32[]{:S(2)}) %collective-permute-start.5) | collective-permute-done | bytes 65568 | tf_op jit(solution)/shard_map/ppermute | solution.py:23
  27.1 1.6 %along_x.5.total_ref = f32[512,128]{1,0:T(8,128)S(1)} custom-call(f32[512,128]{1,0:T(8,128)S(1)} %get-tuple-element.85.total_ref, bf16[256,128]{1,0:T(8,128)(2,1)S(1)} %collective-permute-done.4.refs_0_, bf16[256,128]{1,0:T(8,128)(2,1)S(1)} %collective-permute-done.5.refs_1_, bf16[4,2,128,128]{3,2,1,0:T(8,128)(2,1)S(1)} %get-tuple-element.63.ends_w_ref.refs_2_, ...), custom_call_target="tpu_custom_call" | custom-call | flops 1073741824 | bytes 6952960 | tf_op jit(solution)/shard_map/along_x/pallas_call | solution.py:28
  28.7 0.8 %collective-permute-done.7.refs_1_ = bf16[256,128]{1,0:T(8,128)(2,1)S(1)} collective-permute-done((bf16[256,128]{1,0:T(8,128)(2,1)S(1)}, bf16[256,128]{1,0:T(8,128)(2,1)S(1)}, u32[]{:S(2)}, u32[]{:S(2)}) %collective-permute-start.7) | collective-permute-done | bytes 65568 | tf_op jit(solution)/shard_map/ppermute | solution.py:23
  29.4 2.1 %along_y.5 = (bf16[512,128]{1,0:T(8,128)(2,1)S(1)}, bf16[256,128]{1,0:T(8,128)(2,1)S(1)}, bf16[256,128]{1,0:T(8,128)(2,1)S(1)}, bf16[256,128]{1,0:T(8,128)(2,1)S(1)}, bf16[256,128]{1,0:T(8,128)(2,1)S(1)}) custom-call(f32[512,128]{1,0:T(8,128)S(1)} %along_x.5.total_ref, bf16[256,128]{1,0:T(8,128)(2,1)S(1)} %collective-permute-done.6.refs_0_, ...), custom_call_target="tpu_custom_call" | custom-call | flops 1073741824 | bytes 8263680 | tf_op jit(solution)/shard_map/along_y/pallas_call | solution.py:28
  31.6 2.1 %collective-permute-start.9 = (bf16[256,128]{1,0:T(8,128)(2,1)S(1)}, bf16[256,128]{1,0:T(8,128)(2,1)S(1)}, u32[]{:S(2)}, u32[]{:S(2)}) collective-permute-start(bf16[256,128]{1,0:T(8,128)(2,1)S(1)} %get-tuple-element.95.far_x), channel_id=1, source_target_pairs={{4,8},{8,4},{12,16},{16,12},{20,24},{24,20},{28,0},{0,28},{5,9},{9... | collective-permute-start | bytes 196616 | tf_op jit(solution)/shard_map/ppermute | solution.py:23
  33.7 0.8 %collective-permute-start.10 = (bf16[256,128]{1,0:T(8,128)(2,1)S(1)}, bf16[256,128]{1,0:T(8,128)(2,1)S(1)}, u32[]{:S(2)}, u32[]{:S(2)}) collective-permute-start(bf16[256,128]{1,0:T(8,128)(2,1)S(1)} %get-tuple-element.96.near_y), channel_id=1, source_target_pairs={{0,1},{1,0},{2,3},{3,2},{4,5},{5,4},{6,7},{7,6},{8,9},{9,8},{10,11... | collective-permute-start | bytes 196616 | tf_op jit(solution)/shard_map/ppermute | solution.py:23
  34.6 1.4 %collective-permute-start.11 = (bf16[256,128]{1,0:T(8,128)(2,1)S(1)}, bf16[256,128]{1,0:T(8,128)(2,1)S(1)}, u32[]{:S(2)}, u32[]{:S(2)}) collective-permute-start(bf16[256,128]{1,0:T(8,128)(2,1)S(1)} %get-tuple-element.97.far_y), channel_id=1, source_target_pairs={{1,2},{2,1},{3,0},{0,3},{5,6},{6,5},{7,4},{4,7},{9,10},{10,9},{11,... | collective-permute-start | bytes 196616 | tf_op jit(solution)/shard_map/ppermute | solution.py:23
  35.9 1.8 %inner.6 = (f32[512,128]{1,0:T(8,128)S(1)}, bf16[4,256,128]{2,1,0:T(8,128)(2,1)S(1)}) custom-call(bf16[512,128]{1,0:T(8,128)(2,1)S(1)} %get-tuple-element.93.latent_ref.refs_12_, bf16[256,128]{1,0:T(8,128)(2,1)S(1)} %get-tuple-element.94.near_x, bf16[256,128]{1,0:T(8,128)(2,1)S(1)} %get-tuple-element.95.far_x, ...), custom_call_target="tpu_custom_call" | custom-call | flops 1073741824 | bytes 3807232 | tf_op jit(solution)/shard_map/inner/pallas_call | solution.py:28
  37.7 1.6 %along_x.6.total_ref = f32[512,128]{1,0:T(8,128)S(1)} custom-call(f32[512,128]{1,0:T(8,128)S(1)} %get-tuple-element.98.total_ref, bf16[256,128]{1,0:T(8,128)(2,1)S(1)} %collective-permute-done.8.refs_0_, bf16[256,128]{1,0:T(8,128)(2,1)S(1)} %collective-permute-done.9.refs_1_, bf16[4,2,128,128]{3,2,1,0:T(8,128)(2,1)S(1)} %get-tuple-element.63.ends_w_ref.refs_2_, ...), custom_call_target="tpu_custom_call" | custom-call | flops 1073741824 | bytes 6952960 | tf_op jit(solution)/shard_map/along_x/pallas_call | solution.py:28
  39.4 1.3 %collective-permute-done.11.refs_1_ = bf16[256,128]{1,0:T(8,128)(2,1)S(1)} collective-permute-done((bf16[256,128]{1,0:T(8,128)(2,1)S(1)}, bf16[256,128]{1,0:T(8,128)(2,1)S(1)}, u32[]{:S(2)}, u32[]{:S(2)}) %collective-permute-start.11) | collective-permute-done | bytes 65568 | tf_op jit(solution)/shard_map/ppermute | solution.py:23
  40.6 2.1 %along_y.6 = (bf16[512,128]{1,0:T(8,128)(2,1)S(1)}, bf16[256,128]{1,0:T(8,128)(2,1)S(1)}, bf16[256,128]{1,0:T(8,128)(2,1)S(1)}, bf16[256,128]{1,0:T(8,128)(2,1)S(1)}, bf16[256,128]{1,0:T(8,128)(2,1)S(1)}) custom-call(f32[512,128]{1,0:T(8,128)S(1)} %along_x.6.total_ref, bf16[256,128]{1,0:T(8,128)(2,1)S(1)} %collective-permute-done.10.refs_0_, ...), custom_call_target="tpu_custom_call" | custom-call | flops 1073741824 | bytes 8263680 | tf_op jit(solution)/shard_map/along_y/pallas_call | solution.py:28
  43.0 1.1 %collective-permute-start.14 = (bf16[256,128]{1,0:T(8,128)(2,1)S(1)}, bf16[256,128]{1,0:T(8,128)(2,1)S(1)}, u32[]{:S(2)}, u32[]{:S(2)}) collective-permute-start(bf16[256,128]{1,0:T(8,128)(2,1)S(1)} %get-tuple-element.103.near_y), channel_id=1, source_target_pairs={{0,1},{1,0},{2,3},{3,2},{4,5},{5,4},{6,7},{7,6},{8,9},{9,8},{10,11... | collective-permute-start | bytes 196616 | tf_op jit(solution)/shard_map/ppermute | solution.py:23
  44.2 1.2 %collective-permute-start.15 = (bf16[256,128]{1,0:T(8,128)(2,1)S(1)}, bf16[256,128]{1,0:T(8,128)(2,1)S(1)}, u32[]{:S(2)}, u32[]{:S(2)}) collective-permute-start(bf16[256,128]{1,0:T(8,128)(2,1)S(1)} %get-tuple-element.104.far_y), channel_id=1, source_target_pairs={{1,2},{2,1},{3,0},{0,3},{5,6},{6,5},{7,4},{4,7},{9,10},{10,9},{11,... | collective-permute-start | bytes 196616 | tf_op jit(solution)/shard_map/ppermute | solution.py:23
  45.3 1.6 %inner.7 = (f32[512,128]{1,0:T(8,128)S(1)}, bf16[4,256,128]{2,1,0:T(8,128)(2,1)S(1)}) custom-call(bf16[512,128]{1,0:T(8,128)(2,1)S(1)} %get-tuple-element.100.latent_ref.refs_12_, bf16[256,128]{1,0:T(8,128)(2,1)S(1)} %get-tuple-element.101.near_x, bf16[256,128]{1,0:T(8,128)(2,1)S(1)} %get-tuple-element.102.far_x, ...), custom_call_target="tpu_custom_call" | custom-call | flops 1073741824 | bytes 3807232 | tf_op jit(solution)/shard_map/inner/pallas_call | solution.py:28
  47.0 1.2 %collective-permute-done.13.refs_1_ = bf16[256,128]{1,0:T(8,128)(2,1)S(1)} collective-permute-done((bf16[256,128]{1,0:T(8,128)(2,1)S(1)}, bf16[256,128]{1,0:T(8,128)(2,1)S(1)}, u32[]{:S(2)}, u32[]{:S(2)}) %collective-permute-start.13) | collective-permute-done | bytes 65568 | tf_op jit(solution)/shard_map/ppermute | solution.py:23
  48.1 1.6 %along_x.7.total_ref = f32[512,128]{1,0:T(8,128)S(1)} custom-call(f32[512,128]{1,0:T(8,128)S(1)} %get-tuple-element.105.total_ref, bf16[256,128]{1,0:T(8,128)(2,1)S(1)} %collective-permute-done.12.refs_0_, bf16[256,128]{1,0:T(8,128)(2,1)S(1)} %collective-permute-done.13.refs_1_, bf16[4,2,128,128]{3,2,1,0:T(8,128)(2,1)S(1)} %get-tuple-element.63.ends_w_ref.refs_2_, ...), custom_call_target="tpu_custom_call" | custom-call | flops 1073741824 | bytes 6952960 | tf_op jit(solution)/shard_map/along_x/pallas_call | solution.py:28
  50.2 2.6 %along_y.7 = bf16[512,128]{1,0:T(8,128)(2,1)} custom-call(f32[512,128]{1,0:T(8,128)S(1)} %along_x.7.total_ref, bf16[256,128]{1,0:T(8,128)(2,1)S(1)} %collective-permute-done.14.refs_0_, bf16[256,128]{1,0:T(8,128)(2,1)S(1)} %collective-permute-done.15.refs_1_, bf16[4,2,128,128]{3,2,1,0:T(8,128)(2,1)S(1)} %get-tuple-element.63.ends_w_ref.refs_2_, ...), custom_call_target="tpu_custom_call" | custom-call | flops 1073741824 | bytes 7477248 | tf_op jit(solution)/shard_map/along_y/pallas_call | solution.py:28
  (34 shorter events, 3.4 us)
Async XLA Ops:
  0.0 13.7 %copy-start.1 = (bf16[4,3,128,128]{3,2,1,0:T(8,128)(2,1)S(1)}, bf16[4,3,128,128]{3,2,1,0:T(8,128)(2,1)}, u32[]{:S(2)}) copy-start(bf16[4,3,128,128]{3,2,1,0:T(8,128)(2,1)} %nodes_hbm.1) | copy-start | bytes 1179652
  0.0 13.7 %copy-start = (bf16[4,4,128,128]{3,2,1,0:T(8,128)(2,1)S(1)}, bf16[4,4,128,128]{3,2,1,0:T(8,128)(2,1)}, u32[]{:S(2)}) copy-start(bf16[4,4,128,128]{3,2,1,0:T(8,128)(2,1)} %weights_hbm.1) | copy-start | bytes 1572868
  0.8 0.9 %copy-start.2 = (bf16[1,1,512,128]{3,2,1,0:T(8,128)(2,1)S(1)}, bf16[1,1,512,128]{3,2,1,0:T(8,128)(2,1)}, u32[]{:S(2)}) copy-start(bf16[1,1,512,128]{3,2,1,0:T(8,128)(2,1)} %param.10) | copy-start | bytes 393220
  1.7 0.7 %copy-start.3 = (s32[1,1,2,1024]{3,2,1,0:T(2,128)S(1)}, s32[1,1,2,1024]{3,2,1,0:T(2,128)}, u32[]{:S(2)}) copy-start(s32[1,1,2,1024]{3,2,1,0:T(2,128)} %param.14) | copy-start | bytes 24580
  2.4 0.7 %copy-start.4 = (s32[1,1,2,1024]{3,2,1,0:T(2,128)S(1)}, s32[1,1,2,1024]{3,2,1,0:T(2,128)}, u32[]{:S(2)}) copy-start(s32[1,1,2,1024]{3,2,1,0:T(2,128)} %param.15) | copy-start | bytes 24580
  3.1 0.7 %copy-start.6 = (s32[1,1,2,256]{3,2,1,0:T(2,128)S(1)}, s32[1,1,2,256]{3,2,1,0:T(2,128)}, u32[]{:S(2)}) copy-start(s32[1,1,2,256]{3,2,1,0:T(2,128)} %param.12) | copy-start | bytes 6148
  3.8 0.7 %copy-start.7 = (s32[1,1,2,256]{3,2,1,0:T(2,128)S(1)}, s32[1,1,2,256]{3,2,1,0:T(2,128)}, u32[]{:S(2)}) copy-start(s32[1,1,2,256]{3,2,1,0:T(2,128)} %param.13) | copy-start | bytes 6148
  4.5 9.2 %copy-start.8 = (f32[4,3,128]{2,0,1:T(4,128)S(1)}, f32[4,3,128]{2,0,1:T(4,128)}, u32[]{:S(2)}) copy-start(f32[4,3,128]{2,0,1:T(4,128)} %param.19) | copy-start | bytes 18436
  4.5 9.3 %copy-start.5 = (s32[1,1,4,512]{3,2,1,0:T(4,128)S(1)}, s32[1,1,4,512]{3,2,1,0:T(4,128)}, u32[]{:S(2)}) copy-start(s32[1,1,4,512]{3,2,1,0:T(4,128)} %param.11) | copy-start | bytes 24580
  5.6 12.1 %collective-permute-start = (bf16[272,128]{1,0:T(8,128)(2,1)S(1)}, bf16[272,128]{1,0:T(8,128)(2,1)S(1)}, u32[]{:S(2)}, u32[]{:S(2)}) collective-permute-start(bf16[272,128]{1,0:T(8,128)(2,1)S(1)} %get-tuple-element.57.near_x), channel_id=1, source_target_pairs={{0,4},{4,0},{8,12},{12,8},{16,20},{20,16},{24,28},{28,24},{1,5},{5... | collective-permute-start | bytes 208904 | tf_op jit(solution)/shard_map/ppermute | solution.py:23
  6.1 11.6 %collective-permute-start.1 = (bf16[272,128]{1,0:T(8,128)(2,1)S(1)}, bf16[272,128]{1,0:T(8,128)(2,1)S(1)}, u32[]{:S(2)}, u32[]{:S(2)}) collective-permute-start(bf16[272,128]{1,0:T(8,128)(2,1)S(1)} %get-tuple-element.58.far_x), channel_id=1, source_target_pairs={{4,8},{8,4},{12,16},{16,12},{20,24},{24,20},{28,0},{0,28},{5,9},{9... | collective-permute-start | bytes 208904 | tf_op jit(solution)/shard_map/ppermute | solution.py:23
  9.7 9.9 %collective-permute-start.2 = (bf16[272,128]{1,0:T(8,128)(2,1)S(1)}, bf16[272,128]{1,0:T(8,128)(2,1)S(1)}, u32[]{:S(2)}, u32[]{:S(2)}) collective-permute-start(bf16[272,128]{1,0:T(8,128)(2,1)S(1)} %get-tuple-element.59.near_y), channel_id=1, source_target_pairs={{0,1},{1,0},{2,3},{3,2},{4,5},{5,4},{6,7},{7,6},{8,9},{9,8},{10,11... | collective-permute-start | bytes 208904 | tf_op jit(solution)/shard_map/ppermute | solution.py:23
  11.2 8.4 %collective-permute-start.3 = (bf16[272,128]{1,0:T(8,128)(2,1)S(1)}, bf16[272,128]{1,0:T(8,128)(2,1)S(1)}, u32[]{:S(2)}, u32[]{:S(2)}) collective-permute-start(bf16[272,128]{1,0:T(8,128)(2,1)S(1)} %get-tuple-element.60.far_y), channel_id=1, source_target_pairs={{1,2},{2,1},{3,0},{0,3},{5,6},{6,5},{7,4},{4,7},{9,10},{10,9},{11,... | collective-permute-start | bytes 208904 | tf_op jit(solution)/shard_map/ppermute | solution.py:23
  22.0 3.9 %collective-permute-start.4 = (bf16[256,128]{1,0:T(8,128)(2,1)S(1)}, bf16[256,128]{1,0:T(8,128)(2,1)S(1)}, u32[]{:S(2)}, u32[]{:S(2)}) collective-permute-start(bf16[256,128]{1,0:T(8,128)(2,1)S(1)} %get-tuple-element.81.near_x), channel_id=1, source_target_pairs={{0,4},{4,0},{8,12},{12,8},{16,20},{20,16},{24,28},{28,24},{1,5},{5... | collective-permute-start | bytes 196616 | tf_op jit(solution)/shard_map/ppermute | solution.py:23
  22.0 5.0 %collective-permute-start.5 = (bf16[256,128]{1,0:T(8,128)(2,1)S(1)}, bf16[256,128]{1,0:T(8,128)(2,1)S(1)}, u32[]{:S(2)}, u32[]{:S(2)}) collective-permute-start(bf16[256,128]{1,0:T(8,128)(2,1)S(1)} %get-tuple-element.82.far_x), channel_id=1, source_target_pairs={{4,8},{8,4},{12,16},{16,12},{20,24},{24,20},{28,0},{0,28},{5,9},{9... | collective-permute-start | bytes 196616 | tf_op jit(solution)/shard_map/ppermute | solution.py:23
  22.7 6.0 %collective-permute-start.6 = (bf16[256,128]{1,0:T(8,128)(2,1)S(1)}, bf16[256,128]{1,0:T(8,128)(2,1)S(1)}, u32[]{:S(2)}, u32[]{:S(2)}) collective-permute-start(bf16[256,128]{1,0:T(8,128)(2,1)S(1)} %get-tuple-element.83.near_y), channel_id=1, source_target_pairs={{0,1},{1,0},{2,3},{3,2},{4,5},{5,4},{6,7},{7,6},{8,9},{9,8},{10,11... | collective-permute-start | bytes 196616 | tf_op jit(solution)/shard_map/ppermute | solution.py:23
  23.4 6.1 %collective-permute-start.7 = (bf16[256,128]{1,0:T(8,128)(2,1)S(1)}, bf16[256,128]{1,0:T(8,128)(2,1)S(1)}, u32[]{:S(2)}, u32[]{:S(2)}) collective-permute-start(bf16[256,128]{1,0:T(8,128)(2,1)S(1)} %get-tuple-element.84.far_y), channel_id=1, source_target_pairs={{1,2},{2,1},{3,0},{0,3},{5,6},{6,5},{7,4},{4,7},{9,10},{10,9},{11,... | collective-permute-start | bytes 196616 | tf_op jit(solution)/shard_map/ppermute | solution.py:23
  31.5 6.2 %collective-permute-start.8 = (bf16[256,128]{1,0:T(8,128)(2,1)S(1)}, bf16[256,128]{1,0:T(8,128)(2,1)S(1)}, u32[]{:S(2)}, u32[]{:S(2)}) collective-permute-start(bf16[256,128]{1,0:T(8,128)(2,1)S(1)} %get-tuple-element.94.near_x), channel_id=1, source_target_pairs={{0,4},{4,0},{8,12},{12,8},{16,20},{20,16},{24,28},{28,24},{1,5},{5... | collective-permute-start | bytes 196616 | tf_op jit(solution)/shard_map/ppermute | solution.py:23
  31.6 6.1 %collective-permute-start.9 = (bf16[256,128]{1,0:T(8,128)(2,1)S(1)}, bf16[256,128]{1,0:T(8,128)(2,1)S(1)}, u32[]{:S(2)}, u32[]{:S(2)}) collective-permute-start(bf16[256,128]{1,0:T(8,128)(2,1)S(1)} %get-tuple-element.95.far_x), channel_id=1, source_target_pairs={{4,8},{8,4},{12,16},{16,12},{20,24},{24,20},{28,0},{0,28},{5,9},{9... | collective-permute-start | bytes 196616 | tf_op jit(solution)/shard_map/ppermute | solution.py:23
  33.7 5.6 %collective-permute-start.10 = (bf16[256,128]{1,0:T(8,128)(2,1)S(1)}, bf16[256,128]{1,0:T(8,128)(2,1)S(1)}, u32[]{:S(2)}, u32[]{:S(2)}) collective-permute-start(bf16[256,128]{1,0:T(8,128)(2,1)S(1)} %get-tuple-element.96.near_y), channel_id=1, source_target_pairs={{0,1},{1,0},{2,3},{3,2},{4,5},{5,4},{6,7},{7,6},{8,9},{9,8},{10,11... | collective-permute-start | bytes 196616 | tf_op jit(solution)/shard_map/ppermute | solution.py:23
  34.6 6.1 %collective-permute-start.11 = (bf16[256,128]{1,0:T(8,128)(2,1)S(1)}, bf16[256,128]{1,0:T(8,128)(2,1)S(1)}, u32[]{:S(2)}, u32[]{:S(2)}) collective-permute-start(bf16[256,128]{1,0:T(8,128)(2,1)S(1)} %get-tuple-element.97.far_y), channel_id=1, source_target_pairs={{1,2},{2,1},{3,0},{0,3},{5,6},{6,5},{7,4},{4,7},{9,10},{10,9},{11,... | collective-permute-start | bytes 196616 | tf_op jit(solution)/shard_map/ppermute | solution.py:23
  42.7 4.2 %collective-permute-start.12 = (bf16[256,128]{1,0:T(8,128)(2,1)S(1)}, bf16[256,128]{1,0:T(8,128)(2,1)S(1)}, u32[]{:S(2)}, u32[]{:S(2)}) collective-permute-start(bf16[256,128]{1,0:T(8,128)(2,1)S(1)} %get-tuple-element.101.near_x), channel_id=1, source_target_pairs={{0,4},{4,0},{8,12},{12,8},{16,20},{20,16},{24,28},{28,24},{1,5},{5... | collective-permute-start | bytes 196616 | tf_op jit(solution)/shard_map/ppermute | solution.py:23
  42.8 5.3 %collective-permute-start.13 = (bf16[256,128]{1,0:T(8,128)(2,1)S(1)}, bf16[256,128]{1,0:T(8,128)(2,1)S(1)}, u32[]{:S(2)}, u32[]{:S(2)}) collective-permute-start(bf16[256,128]{1,0:T(8,128)(2,1)S(1)} %get-tuple-element.102.far_x), channel_id=1, source_target_pairs={{4,8},{8,4},{12,16},{16,12},{20,24},{24,20},{28,0},{0,28},{5,9},{9... | collective-permute-start | bytes 196616 | tf_op jit(solution)/shard_map/ppermute | solution.py:23
  43.0 6.7 %collective-permute-start.14 = (bf16[256,128]{1,0:T(8,128)(2,1)S(1)}, bf16[256,128]{1,0:T(8,128)(2,1)S(1)}, u32[]{:S(2)}, u32[]{:S(2)}) collective-permute-start(bf16[256,128]{1,0:T(8,128)(2,1)S(1)} %get-tuple-element.103.near_y), channel_id=1, source_target_pairs={{0,1},{1,0},{2,3},{3,2},{4,5},{5,4},{6,7},{7,6},{8,9},{9,8},{10,11... | collective-permute-start | bytes 196616 | tf_op jit(solution)/shard_map/ppermute | solution.py:23
  44.2 6.1 %collective-permute-start.15 = (bf16[256,128]{1,0:T(8,128)(2,1)S(1)}, bf16[256,128]{1,0:T(8,128)(2,1)S(1)}, u32[]{:S(2)}, u32[]{:S(2)}) collective-permute-start(bf16[256,128]{1,0:T(8,128)(2,1)S(1)} %get-tuple-element.104.far_y), channel_id=1, source_target_pairs={{1,2},{2,1},{3,0},{0,3},{5,6},{6,5},{7,4},{4,7},{9,10},{10,9},{11,... | collective-permute-start | bytes 196616 | tf_op jit(solution)/shard_map/ppermute | solution.py:23

commit v2 on v1

--- a/solution.py
+++ b/solution.py
@@ -12,6 +12,10 @@
 I32 = jnp.int32
 VMEM = pl.BlockSpec(memory_space=pltpu.VMEM)
 HBM = pl.BlockSpec(memory_space=pltpu.HBM)
+
+NEAR_X, FAR_X, NEAR_Y, FAR_Y = range(4)
+ORDER = (FAR_Y, FAR_X, NEAR_Y, NEAR_X)
+PLACE = tuple(ORDER.index(link) for link in range(4))
 
 
 def swapped(block, axis, odd):
@@ -23,7 +27,7 @@
     return lax.ppermute(block, axis, route)
 
 
-def call(kernel, outs, operands, in_specs=None, scratch=(), name=None):
+def call(kernel, outs, operands, in_specs=None, scratch=(), name=None, grant=40 << 20):
     moved = sum(o.size * o.dtype.itemsize for o in operands)
     return pl.pallas_call(
         kernel,
@@ -31,7 +35,7 @@
         in_specs=in_specs or [VMEM] * len(operands),
         out_specs=[VMEM] * len(outs),
         scratch_shapes=list(scratch),
-        compiler_params=pltpu.CompilerParams(vmem_limit_bytes=40 << 20),
+        compiler_params=pltpu.CompilerParams(vmem_limit_bytes=grant),
         cost_estimate=pl.CostEstimate(flops=1 << 30, bytes_accessed=moved, transcendentals=0),
         name=name,
     )(*operands)
@@ -90,15 +94,14 @@
     for d, odd in enumerate(odd_place()):
         near, far = in_order(odd, rows[2 * d], rows[2 * d + 1])
         count = near.shape[0]
-        out_refs[2 * d][0:count, :] = near
-        out_refs[2 * d + 1][0:count, :] = far
+        out_refs[PLACE[2 * d]][0:count, :] = near
+        out_refs[PLACE[2 * d + 1]][0:count, :] = far
 
 
 def first_kernel(
     latent_hbm, tops_hbm, bottoms_hbm, etop_hbm, ebot_hbm, live_hbm,
-    near_x, far_x, near_y, far_y, latent_ref, tops_ref, bottoms_ref, ends_ref,
-    pick_ref, pick_mask_ref,
-    etop_ref, ebot_ref, live_ref, sems,
+    send_0, send_1, send_2, send_3, pick_ref, pick_mask_ref,
+    latent_ref, tops_ref, bottoms_ref, etop_ref, ebot_ref, live_ref, sems,
 ):
     moves = [
         pltpu.make_async_copy(src, dst, sems.at[i])
@@ -120,20 +123,19 @@
         pick_mask_ref[face] = column_mask(bit, width)
     for move in moves[2:]:
         move.wait()
-    sends = (near_x, far_x, near_y, far_y)
+    sends = (send_0, send_1, send_2, send_3)
     pick_faces(latent_ref[...], pick_ref, pick_mask_ref, sends)
     faces = tops_ref.shape[1]
     slots = etop_ref.shape[1]
     lines = slots // width
     for d in range(2):
-        live = lax.broadcasted_iota(I32, (1, slots), 1) < live_ref[d, 0]
+        live = lax.broadcasted_iota(I32, (1, slots), 1) < live_ref[0, d]
         etop = etop_ref[d : d + 1, :].astype(F32)
         ebot = jnp.where(live, ebot_ref[d : d + 1, :], -1).astype(F32)
         rows = [v[:, i * width : (i + 1) * width] for v in (etop, ebot) for i in range(lines)]
         ends = jnp.concatenate(rows, axis=0).astype(BF)
-        ends_ref[d] = ends
-        sends[2 * d][faces:, :] = ends
-        sends[2 * d + 1][faces:, :] = ends
+        sends[PLACE[2 * d]][faces:, :] = ends
+        sends[PLACE[2 * d + 1]][faces:, :] = ends
 
 
 def unpacked(ends):
@@ -160,14 +162,15 @@
 
 
 def setup_kernel(
-    nbr_hbm, weights_hbm, nodes_hbm, biases_hbm, tops_ref, ends_ref,
+    tops_hbm, etop_hbm, ebot_hbm, live_hbm, nbr_hbm, weights_hbm, nodes_hbm, biases_hbm,
     pick_ref, spread_ref, mask_ref, gather_ref, sum_ref, half_ref,
     ends_w_ref, hidden_ref, join_ref, out_w_ref, biases_ref,
-    nbr_ref, weights_ref, nodes_ref, raw_biases_ref, sems,
+    tops_ref, etop_ref, ebot_ref, live_ref, nbr_ref, weights_ref, nodes_ref, raw_biases_ref, sems,
 ):
     moves = [
         pltpu.make_async_copy(src, dst, sems.at[i])
         for i, (src, dst) in enumerate((
+            (tops_hbm, tops_ref), (etop_hbm, etop_ref), (ebot_hbm, ebot_ref), (live_hbm, live_ref),
             (nbr_hbm, nbr_ref), (weights_hbm, weights_ref), (nodes_hbm, nodes_ref),
             (biases_hbm, raw_biases_ref),
         ))
@@ -176,12 +179,16 @@
         move.start()
     half = spread_ref.shape[0]
     width = mask_ref.shape[1]
+    for move in moves[:4]:
+        move.wait()
+    slots = etop_ref.shape[1]
     for d in range(2):
-        etop, ebot = unpacked(ends_ref[d])
+        live = lax.broadcasted_iota(I32, (1, slots), 1) < live_ref[0, d]
         gather_ref[d], sum_ref[d], half_ref[d] = group(
-            etop, ebot, tops_ref[d : d + 1, :], ebot >= 0, 1, half, width
+            etop_ref[d : d + 1, :], ebot_ref[d : d + 1, :], tops_ref[d : d + 1, :],
+            live, 1, half, width,
         )
-    for move in moves:
+    for move in moves[4:]:
         move.wait()
     rows = nbr_ref.shape[1]
     for k in range(nbr_ref.shape[0]):
@@ -207,21 +214,22 @@
 
 
 def inner_kernel(
-    step, latent_ref, near_x, far_x, near_y, far_y, ends_w_ref, hidden_ref, biases_ref,
+    step, latent_ref, send_0, send_1, send_2, send_3, ends_w_ref, hidden_ref, biases_ref,
     pick_ref, spread_ref, mask_ref, total_ref, table_ref,
 ):
     rows, width = latent_ref.shape
     half = rows // 2
     faces = table_ref.shape[1]
+    sends = (send_0, send_1, send_2, send_3)
     for d, odd in enumerate(odd_place()):
-        near, far = (ref[0:faces, :] for ref in ((near_x, far_x), (near_y, far_y))[d])
+        near, far = (sends[PLACE[2 * d + i]][0:faces, :] for i in range(2))
         top, bottom = in_order(odd, near, far)
         table_ref[2 * d] = dot(top, ends_w_ref[step, 0]).astype(BF)
         table_ref[2 * d + 1] = dot(bottom, ends_w_ref[step, 1]).astype(BF)
     latent = latent_ref[...]
-    source = dot(latent, ends_w_ref[step, 0]) + biases_ref[step, 0:1, :]
+    source = dot(latent, ends_w_ref[step, 0]) + biases_ref[0, step : step + 1, :]
     table = halves(dot(latent, ends_w_ref[step, 1]).astype(BF))
-    c1 = biases_ref[step, 1:2, :]
+    c1 = biases_ref[1, step : step + 1, :]
     c1 = jnp.concatenate([c1, c1], axis=1)
     fanout = pick_ref.shape[0] // rows
     total = None
@@ -248,8 +256,8 @@
 
 def cross(step, d, upper, lower, ends_w_ref, hidden_ref, biases_ref, table_ref, groups):
     width = upper.shape[1]
-    c0 = biases_ref[step, 0:1, :]
-    c1 = biases_ref[step, 1:2, :]
+    c0 = biases_ref[0, step : step + 1, :]
+    c1 = biases_ref[1, step : step + 1, :]
     c1 = jnp.concatenate([c1, c1], axis=1)
     far = (
         dot(upper, ends_w_ref[step, 1]).astype(BF),
@@ -311,7 +319,7 @@
     arrived = total_ref[...] + jnp.concatenate([both[:, :width], both[:, width:]], axis=0)
     latent = latent_ref[...]
     joined = jnp.concatenate([latent, arrived.astype(BF)], axis=1)
-    update = half_silu(dot(joined, join_ref[step]) + biases_ref[step, 2:3, :]).astype(BF)
+    update = half_silu(dot(joined, join_ref[step]) + biases_ref[2, step : step + 1, :]).astype(BF)
     latent = (latent.astype(F32) + dot(update, out_w_ref[step])).astype(BF)
     if last:
         rest[0][...] = latent
@@ -341,6 +349,8 @@
     bottoms = bottom_rows[0, 0]
     etop = edge_top[0, 0]
     ebot = edge_bottom[0, 0]
+    live = live_count.T
+    bias_rows = jnp.swapaxes(biases, 0, 1)
     fanout = nbr.shape[0]
     faces = tops.shape[1]
     slots = etop.shape[1]
@@ -349,19 +359,18 @@
     face = like((faces, width), BF)
     lines = 2 * (slots // width)
     packed = like((faces + lines, width), BF)
-    *sends, latent_now, tops, bottoms, ends, pick, pick_mask = call(
+    *sends, pick, pick_mask = call(
         first_kernel,
-        [packed] * 4 + [
-            like((rows, width), BF), like(tops.shape, I32), like(tops.shape, I32),
-            like((2, lines, width), BF), like((4, faces, half), BF), like((4, faces, width), BF),
-        ],
-        (latent_now, tops, bottoms, etop, ebot, live_count),
+        [packed] * 4 + [like((4, faces, half), BF), like((4, faces, width), BF)],
+        (latent_now, tops, bottoms, etop, ebot, live),
         in_specs=[HBM] * 6,
         scratch=[
-            pltpu.VMEM(etop.shape, I32), pltpu.VMEM(etop.shape, I32),
-            pltpu.SMEM(live_count.shape, I32), pltpu.SemaphoreType.DMA((6,)),
+            pltpu.VMEM((rows, width), BF), pltpu.VMEM(tops.shape, I32),
+            pltpu.VMEM(tops.shape, I32), pltpu.VMEM(etop.shape, I32), pltpu.VMEM(etop.shape, I32),
+            pltpu.SMEM(live.shape, I32), pltpu.SemaphoreType.DMA((6,)),
         ],
         name="first",
+        grant=54 << 20,
     )
     group_like = [
         like((slots, 2 * faces), BF), like((half, slots), BF), like((slots, width), BF)
@@ -369,7 +378,7 @@
     kept_x = kept_y = None
     for step in range(steps):
         first, last = step == 0, step == steps - 1
-        near_x, far_x, near_y, far_y = sends
+        near_x, far_x, near_y, far_y = (sends[place] for place in PLACE)
         got_far_y = swapped(far_y, "gy", 1)
         got_near_y = swapped(near_y, "gy", 0)
         got_far_x = swapped(far_x, "gx", 1)
@@ -382,13 +391,15 @@
                 + [like((2,) + g.shape, BF) for g in group_like]
                 + [like((steps, 2, width, width), BF), like((steps, 2 * width, 2 * width), BF),
                    like((steps, 2 * width, width), BF), like((steps, width, width), BF),
-                   like(biases.shape, F32)],
-                (nbr, edge_weights, node_weights, biases, tops, ends),
-                in_specs=[HBM] * 4 + [VMEM] * 2,
+                   like(bias_rows.shape, F32)],
+                (tops, etop, ebot, live, nbr, edge_weights, node_weights, bias_rows),
+                in_specs=[HBM] * 8,
                 scratch=[
+                    pltpu.VMEM(tops.shape, I32), pltpu.VMEM(etop.shape, I32),
+                    pltpu.VMEM(etop.shape, I32), pltpu.SMEM(live.shape, I32),
                     pltpu.VMEM(nbr.shape, I32), pltpu.VMEM(edge_weights.shape, BF),
-                    pltpu.VMEM(node_weights.shape, BF), pltpu.VMEM(biases.shape, F32),
-                    pltpu.SemaphoreType.DMA((4,)),
+                    pltpu.VMEM(node_weights.shape, BF), pltpu.VMEM(bias_rows.shape, F32),
+                    pltpu.SemaphoreType.DMA((8,)),
                 ],
                 name="setup",
             )

time: 53.1 us -> 48.9 us (0.921)
  local copies, waits for them, and re-layouts: 4.5 us -> 0.07 us
  starting transfers between devices: 17.4 us -> 15.5 us
  Pallas kernels: 25.8 us -> 27.3 us
  waiting for transfers between devices: 4.87 us -> 5.54 us
    unnamed x20 -> x32, local copies, waits for them, and re-layouts: 4.5 us -> 0.07 us
    ppermute x16, starting transfers between devices: 17.4 us -> 15.5 us  [swapped(): return lax.ppermute(block, axis, route)]
    pallas_call x14, Pallas kernels: 25.8 us -> 27.3 us  [call(): pl.pallas_call(kernel, out_shape=outs, in_specs=in_specs or [VMEM] * len(...]
    ppermute x16, waiting for transfers between devices: 4.87 us -> 5.54 us  [swapped(): return lax.ppermute(block, axis, route)]
  transfers between devices with their start and end apart: 16 -> 16, of which waited for: 5 -> 4; matrix products, arithmetic and copies ran while one was open for 0% -> 0% of each run, Pallas kernels for 30% -> 32%
where the time goes in v2:
time: 48.9 us; the launch traced here: 48.8 us
  Pallas kernels  27.3 us (56%)
  starting transfers between devices  15.5 us (32%)
  waiting for transfers between devices  5.54 us (11%)
    pallas_call x14, Pallas kernels, call(): pl.pallas_call(kernel, out_shape=outs, in_specs=in_specs or [VMEM] * len(...  27.3 us
    ppermute x16, starting transfers between devices, swapped(): return lax.ppermute(block, axis, route)  15.5 us
    ppermute x16, waiting for transfers between devices, swapped(): return lax.ppermute(block, axis, route)  5.54 us
  transfers between devices with their start and end apart: 16, of which 4 were waited for; matrix products, arithmetic and copies ran while one was open for 0% of the time, Pallas kernels for 32%

profile of v2, /device:TPU:0, one launch (start us, length us, event | category | flops | bytes accessed | tf_op | source)
XLA Modules:
  0.0 48.8 jit_solution(2378048847638491140)
XLA Ops:
  0.0 2.3 %first.1 = (bf16[272,128]{1,0:T(8,128)(2,1)}, bf16[272,128]{1,0:T(8,128)(2,1)}, bf16[272,128]{1,0:T(8,128)(2,1)}, bf16[272,128]{1,0:T(8,128)(2,1)}, bf16[4,256,2...) custom-call(bf16[512,128]{1,0:T(8,128)(2,1)} %bitcast.9, s32[2,256]{1,0:T(2,128)} %bitcast.21, s32[2,256]{1,0:T(2,128)} %bitcast.12, ...), custom_call_target="tpu_custom_call" | custom-call | flops 1073741824 | bytes 151560 | tf_op jit(solution)/shard_map/first/pallas_call | solution.py:32
  2.3 0.0 copy-start.2
  2.4 0.0 copy-start.7
  2.4 5.1 %collective-permute-start.3 = (bf16[272,128]{1,0:T(8,128)(2,1)}, bf16[272,128]{1,0:T(8,128)(2,1)S(1)}, u32[]{:S(2)}, u32[]{:S(2)}) collective-permute-start(bf16[272,128]{1,0:T(8,128)(2,1)} %get-tuple-element.52.send_0), channel_id=1, source_target_pairs={{1,2},{2,1},{3,0},{0,3},{5,6},{6,5},{7,4},{4,7},{9,10},{10,9},{11,... | collective-permute-start | bytes 208904 | tf_op jit(solution)/shard_map/ppermute | solution.py:27
  7.5 1.6 %collective-permute-start.1 = (bf16[272,128]{1,0:T(8,128)(2,1)}, bf16[272,128]{1,0:T(8,128)(2,1)S(1)}, u32[]{:S(2)}, u32[]{:S(2)}) collective-permute-start(bf16[272,128]{1,0:T(8,128)(2,1)} %get-tuple-element.53.send_1), channel_id=1, source_target_pairs={{4,8},{8,4},{12,16},{16,12},{20,24},{24,20},{28,0},{0,28},{5,9},{9... | collective-permute-start | bytes 208904 | tf_op jit(solution)/shard_map/ppermute | solution.py:27
  9.2 2.7 %setup.1 = (bf16[2048,256]{1,0:T(8,128)(2,1)S(1)}, bf16[256,2048]{1,0:T(8,128)(2,1)S(1)}, bf16[2048,128]{1,0:T(8,128)(2,1)S(1)}, bf16[2,1024,512]{2,1,0:T(8,128)...) custom-call(s32[2,256]{1,0:T(2,128)S(1)} %bitcast.22, ...), custom_call_target="tpu_custom_call" | custom-call | flops 1073741824 | bytes 950280 | tf_op jit(solution)/shard_map/setup/pallas_call | solution.py:32
  11.9 0.0 copy-start.3
  12.0 1.6 %inner.4 = (f32[512,128]{1,0:T(8,128)S(1)}, bf16[4,256,128]{2,1,0:T(8,128)(2,1)S(1)}) custom-call(bf16[512,128]{1,0:T(8,128)(2,1)S(1)} %bitcast.10, bf16[272,128]{1,0:T(8,128)(2,1)S(1)} %copy-done.7, bf16[272,128]{1,0:T(8,128)(2,1)S(1)} %copy-done.9, bf16[272,128]{1,0:T(8,128)(2,1)S(1)} %copy-done.6, bf16[272,128]{1,0:T(8,128)(2,1)S(1)} %copy-done.8, ...), custom_call_target="tpu_custom_call" | custom-call | flops 1073741824 | bytes 3823616 | tf_op jit(solution)/shard_map/inner/pallas_call | solution.py:32
  13.7 1.9 %along_x.4 = (f32[512,128]{1,0:T(8,128)S(1)}, bf16[1024,512]{1,0:T(8,128)(2,1)S(1)}, bf16[256,1024]{1,0:T(8,128)(2,1)S(1)}, bf16[1024,128]{1,0:T(8,128)(2,1)S(1)}) custom-call(f32[512,128]{1,0:T(8,128)S(1)} %get-tuple-element.62.total_ref, bf16[272,128]{1,0:T(8,128)(2,1)S(1)} %collective-permute-done.refs_0_, ...), custom_call_target="tpu_custom_call" | custom-call | flops 1073741824 | bytes 5128192 | tf_op jit(solution)/shard_map/along_x/pallas_call | solution.py:32
  15.6 2.4 %along_y.4 = (bf16[512,128]{1,0:T(8,128)(2,1)S(1)}, bf16[256,128]{1,0:T(8,128)(2,1)S(1)}, bf16[256,128]{1,0:T(8,128)(2,1)S(1)}, bf16[256,128]{1,0:T(8,128)(2,1)S...) custom-call(f32[512,128]{1,0:T(8,128)S(1)} %get-tuple-element.67.tot, ...), custom_call_target="tpu_custom_call" | custom-call | flops 1073741824 | bytes 6438912 | tf_op jit(solution)/shard_map/along_y/pallas_call | solution.py:32
  18.0 1.0 %collective-permute-start.7 = (bf16[256,128]{1,0:T(8,128)(2,1)S(1)}, bf16[256,128]{1,0:T(8,128)(2,1)S(1)}, u32[]{:S(2)}, u32[]{:S(2)}) collective-permute-start(bf16[256,128]{1,0:T(8,128)(2,1)S(1)} %get-tuple-element.73.send_0), channel_id=1, source_target_pairs={{1,2},{2,1},{3,0},{0,3},{5,6},{6,5},{7,4},{4,7},{9,10},{10,9},{11,... | collective-permute-start | bytes 196616 | tf_op jit(solution)/shard_map/ppermute | solution.py:27
  18.9 0.7 %collective-permute-start.5 = (bf16[256,128]{1,0:T(8,128)(2,1)S(1)}, bf16[256,128]{1,0:T(8,128)(2,1)S(1)}, u32[]{:S(2)}, u32[]{:S(2)}) collective-permute-start(bf16[256,128]{1,0:T(8,128)(2,1)S(1)} %get-tuple-element.74.send_1), channel_id=1, source_target_pairs={{4,8},{8,4},{12,16},{16,12},{20,24},{24,20},{28,0},{0,28},{5,9},{9... | collective-permute-start | bytes 196616 | tf_op jit(solution)/shard_map/ppermute | solution.py:27
  19.6 1.5 %collective-permute-start.6 = (bf16[256,128]{1,0:T(8,128)(2,1)S(1)}, bf16[256,128]{1,0:T(8,128)(2,1)S(1)}, u32[]{:S(2)}, u32[]{:S(2)}) collective-permute-start(bf16[256,128]{1,0:T(8,128)(2,1)S(1)} %get-tuple-element.75.send_2), channel_id=1, source_target_pairs={{0,1},{1,0},{2,3},{3,2},{4,5},{5,4},{6,7},{7,6},{8,9},{9,8},{10,11... | collective-permute-start | bytes 196616 | tf_op jit(solution)/shard_map/ppermute | solution.py:27
  21.1 0.1 collective-permute-start.4
  21.1 1.6 %inner.5 = (f32[512,128]{1,0:T(8,128)S(1)}, bf16[4,256,128]{2,1,0:T(8,128)(2,1)S(1)}) custom-call(bf16[512,128]{1,0:T(8,128)(2,1)S(1)} %get-tuple-element.72.latent_ref.refs_12_, bf16[256,128]{1,0:T(8,128)(2,1)S(1)} %get-tuple-element.73.send_0, bf16[256,128]{1,0:T(8,128)(2,1)S(1)} %get-tuple-element.74.send_1, ...), custom_call_target="tpu_custom_call" | custom-call | flops 1073741824 | bytes 3807232 | tf_op jit(solution)/shard_map/inner/pallas_call | solution.py:32
  22.8 1.1 %collective-permute-done.5.refs_1_ = bf16[256,128]{1,0:T(8,128)(2,1)S(1)} collective-permute-done((bf16[256,128]{1,0:T(8,128)(2,1)S(1)}, bf16[256,128]{1,0:T(8,128)(2,1)S(1)}, u32[]{:S(2)}, u32[]{:S(2)}) %collective-permute-start.5) | collective-permute-done | bytes 65568 | tf_op jit(solution)/shard_map/ppermute | solution.py:27
  23.9 1.6 %along_x.5.total_ref = f32[512,128]{1,0:T(8,128)S(1)} custom-call(f32[512,128]{1,0:T(8,128)S(1)} %get-tuple-element.77.total_ref, bf16[256,128]{1,0:T(8,128)(2,1)S(1)} %collective-permute-done.4.refs_0_, bf16[256,128]{1,0:T(8,128)(2,1)S(1)} %collective-permute-done.5.refs_1_, bf16[4,2,128,128]{3,2,1,0:T(8,128)(2,1)S(1)} %get-tuple-element.56.ends_w_ref.refs_2_, ...), custom_call_target="tpu_custom_call" | custom-call | flops 1073741824 | bytes 6952960 | tf_op jit(solution)/shard_map/along_x/pallas_call | solution.py:32
  25.5 0.1 collective-permute-done.6.refs_0_
  25.6 2.1 %along_y.5 = (bf16[512,128]{1,0:T(8,128)(2,1)S(1)}, bf16[256,128]{1,0:T(8,128)(2,1)S(1)}, bf16[256,128]{1,0:T(8,128)(2,1)S(1)}, bf16[256,128]{1,0:T(8,128)(2,1)S(1)}, bf16[256,128]{1,0:T(8,128)(2,1)S(1)}) custom-call(f32[512,128]{1,0:T(8,128)S(1)} %along_x.5.total_ref, bf16[256,128]{1,0:T(8,128)(2,1)S(1)} %collective-permute-done.6.refs_0_, ...), custom_call_target="tpu_custom_call" | custom-call | flops 1073741824 | bytes 8263680 | tf_op jit(solution)/shard_map/along_y/pallas_call | solution.py:32
  27.7 3.2 %collective-permute-start.11 = (bf16[256,128]{1,0:T(8,128)(2,1)S(1)}, bf16[256,128]{1,0:T(8,128)(2,1)S(1)}, u32[]{:S(2)}, u32[]{:S(2)}) collective-permute-start(bf16[256,128]{1,0:T(8,128)(2,1)S(1)} %get-tuple-element.86.send_0), channel_id=1, source_target_pairs={{1,2},{2,1},{3,0},{0,3},{5,6},{6,5},{7,4},{4,7},{9,10},{10,9},{11,... | collective-permute-start | bytes 196616 | tf_op jit(solution)/shard_map/ppermute | solution.py:27
  30.9 0.4 collective-permute-start.9
  31.3 0.2 collective-permute-start.10
  31.5 1.6 %inner.6 = (f32[512,128]{1,0:T(8,128)S(1)}, bf16[4,256,128]{2,1,0:T(8,128)(2,1)S(1)}) custom-call(bf16[512,128]{1,0:T(8,128)(2,1)S(1)} %get-tuple-element.85.latent_ref.refs_12_, bf16[256,128]{1,0:T(8,128)(2,1)S(1)} %get-tuple-element.86.send_0, bf16[256,128]{1,0:T(8,128)(2,1)S(1)} %get-tuple-element.87.send_1, ...), custom_call_target="tpu_custom_call" | custom-call | flops 1073741824 | bytes 3807232 | tf_op jit(solution)/shard_map/inner/pallas_call | solution.py:32
  33.1 2.4 %collective-permute-done.9.refs_1_ = bf16[256,128]{1,0:T(8,128)(2,1)S(1)} collective-permute-done((bf16[256,128]{1,0:T(8,128)(2,1)S(1)}, bf16[256,128]{1,0:T(8,128)(2,1)S(1)}, u32[]{:S(2)}, u32[]{:S(2)}) %collective-permute-start.9) | collective-permute-done | bytes 65568 | tf_op jit(solution)/shard_map/ppermute | solution.py:27
  35.5 1.6 %along_x.6.total_ref = f32[512,128]{1,0:T(8,128)S(1)} custom-call(f32[512,128]{1,0:T(8,128)S(1)} %get-tuple-element.90.total_ref, bf16[256,128]{1,0:T(8,128)(2,1)S(1)} %collective-permute-done.8.refs_0_, bf16[256,128]{1,0:T(8,128)(2,1)S(1)} %collective-permute-done.9.refs_1_, bf16[4,2,128,128]{3,2,1,0:T(8,128)(2,1)S(1)} %get-tuple-element.56.ends_w_ref.refs_2_, ...), custom_call_target="tpu_custom_call" | custom-call | flops 1073741824 | bytes 6952960 | tf_op jit(solution)/shard_map/along_x/pallas_call | solution.py:32
  37.1 2.1 %along_y.6 = (bf16[512,128]{1,0:T(8,128)(2,1)S(1)}, bf16[256,128]{1,0:T(8,128)(2,1)S(1)}, bf16[256,128]{1,0:T(8,128)(2,1)S(1)}, bf16[256,128]{1,0:T(8,128)(2,1)S(1)}, bf16[256,128]{1,0:T(8,128)(2,1)S(1)}) custom-call(f32[512,128]{1,0:T(8,128)S(1)} %along_x.6.total_ref, bf16[256,128]{1,0:T(8,128)(2,1)S(1)} %collective-permute-done.10.refs_0_, ...), custom_call_target="tpu_custom_call" | custom-call | flops 1073741824 | bytes 8263680 | tf_op jit(solution)/shard_map/along_y/pallas_call | solution.py:32
  39.2 0.8 %collective-permute-start.15 = (bf16[256,128]{1,0:T(8,128)(2,1)S(1)}, bf16[256,128]{1,0:T(8,128)(2,1)S(1)}, u32[]{:S(2)}, u32[]{:S(2)}) collective-permute-start(bf16[256,128]{1,0:T(8,128)(2,1)S(1)} %get-tuple-element.93.send_0), channel_id=1, source_target_pairs={{1,2},{2,1},{3,0},{0,3},{5,6},{6,5},{7,4},{4,7},{9,10},{10,9},{11,... | collective-permute-start | bytes 196616 | tf_op jit(solution)/shard_map/ppermute | solution.py:27
  40.0 1.0 %collective-permute-start.13 = (bf16[256,128]{1,0:T(8,128)(2,1)S(1)}, bf16[256,128]{1,0:T(8,128)(2,1)S(1)}, u32[]{:S(2)}, u32[]{:S(2)}) collective-permute-start(bf16[256,128]{1,0:T(8,128)(2,1)S(1)} %get-tuple-element.94.send_1), channel_id=1, source_target_pairs={{4,8},{8,4},{12,16},{16,12},{20,24},{24,20},{28,0},{0,28},{5,9},{9... | collective-permute-start | bytes 196616 | tf_op jit(solution)/shard_map/ppermute | solution.py:27
  41.0 1.6 %inner.7 = (f32[512,128]{1,0:T(8,128)S(1)}, bf16[4,256,128]{2,1,0:T(8,128)(2,1)S(1)}) custom-call(bf16[512,128]{1,0:T(8,128)(2,1)S(1)} %get-tuple-element.92.latent_ref.refs_12_, bf16[256,128]{1,0:T(8,128)(2,1)S(1)} %get-tuple-element.93.send_0, bf16[256,128]{1,0:T(8,128)(2,1)S(1)} %get-tuple-element.94.send_1, ...), custom_call_target="tpu_custom_call" | custom-call | flops 1073741824 | bytes 3807232 | tf_op jit(solution)/shard_map/inner/pallas_call | solution.py:32
  42.7 1.9 %collective-permute-done.13.refs_1_ = bf16[256,128]{1,0:T(8,128)(2,1)S(1)} collective-permute-done((bf16[256,128]{1,0:T(8,128)(2,1)S(1)}, bf16[256,128]{1,0:T(8,128)(2,1)S(1)}, u32[]{:S(2)}, u32[]{:S(2)}) %collective-permute-start.13) | collective-permute-done | bytes 65568 | tf_op jit(solution)/shard_map/ppermute | solution.py:27
  44.6 1.6 %along_x.7.total_ref = f32[512,128]{1,0:T(8,128)S(1)} custom-call(f32[512,128]{1,0:T(8,128)S(1)} %get-tuple-element.97.total_ref, bf16[256,128]{1,0:T(8,128)(2,1)S(1)} %collective-permute-done.12.refs_0_, bf16[256,128]{1,0:T(8,128)(2,1)S(1)} %collective-permute-done.13.refs_1_, bf16[4,2,128,128]{3,2,1,0:T(8,128)(2,1)S(1)} %get-tuple-element.56.ends_w_ref.refs_2_, ...), custom_call_target="tpu_custom_call" | custom-call | flops 1073741824 | bytes 6952960 | tf_op jit(solution)/shard_map/along_x/pallas_call | solution.py:32
  46.2 2.6 %along_y.7 = bf16[512,128]{1,0:T(8,128)(2,1)} custom-call(f32[512,128]{1,0:T(8,128)S(1)} %along_x.7.total_ref, bf16[256,128]{1,0:T(8,128)(2,1)S(1)} %collective-permute-done.14.refs_0_, bf16[256,128]{1,0:T(8,128)(2,1)S(1)} %collective-permute-done.15.refs_1_, bf16[4,2,128,128]{3,2,1,0:T(8,128)(2,1)S(1)} %get-tuple-element.56.ends_w_ref.refs_2_, ...), custom_call_target="tpu_custom_call" | custom-call | flops 1073741824 | bytes 7477248 | tf_op jit(solution)/shard_map/along_y/pallas_call | solution.py:32
  (46 shorter events, 0.1 us)
Async XLA Ops:
  0.0 9.1 %copy-start.15 = (s32[2,1]{0,1:T(1,128)S(1)}, s32[2,1]{0,1:T(1,128)}, u32[]{:S(2)}) copy-start(s32[2,1]{0,1:T(1,128)} %param.16) | copy-start | bytes 28
  0.0 9.1 %copy-start.11 = (s32[1,1,2,1024]{3,2,1,0:T(2,128)S(1)}, s32[1,1,2,1024]{3,2,1,0:T(2,128)}, u32[]{:S(2)}) copy-start(s32[1,1,2,1024]{3,2,1,0:T(2,128)} %param.15) | copy-start | bytes 24580
  0.0 9.2 %copy-start.10 = (s32[1,1,2,1024]{3,2,1,0:T(2,128)S(1)}, s32[1,1,2,1024]{3,2,1,0:T(2,128)}, u32[]{:S(2)}) copy-start(s32[1,1,2,1024]{3,2,1,0:T(2,128)} %param.14) | copy-start | bytes 24580
  0.0 9.2 %copy-start.14 = (s32[1,1,2,256]{3,2,1,0:T(2,128)S(1)}, s32[1,1,2,256]{3,2,1,0:T(2,128)}, u32[]{:S(2)}) copy-start(s32[1,1,2,256]{3,2,1,0:T(2,128)} %param.12) | copy-start | bytes 6148
  0.0 9.2 %copy-start.13 = (f32[4,3,128]{2,0,1:T(4,128)S(1)}, f32[4,3,128]{2,0,1:T(4,128)}, u32[]{:S(2)}) copy-start(f32[4,3,128]{2,0,1:T(4,128)} %param.19) | copy-start | bytes 18436
  0.0 9.2 %copy-start.5 = (bf16[4,3,128,128]{3,2,1,0:T(8,128)(2,1)S(1)}, bf16[4,3,128,128]{3,2,1,0:T(8,128)(2,1)}, u32[]{:S(2)}) copy-start(bf16[4,3,128,128]{3,2,1,0:T(8,128)(2,1)} %nodes_hbm.1) | copy-start | bytes 1179652
  0.0 9.2 %copy-start.4 = (bf16[4,4,128,128]{3,2,1,0:T(8,128)(2,1)S(1)}, bf16[4,4,128,128]{3,2,1,0:T(8,128)(2,1)}, u32[]{:S(2)}) copy-start(bf16[4,4,128,128]{3,2,1,0:T(8,128)(2,1)} %weights_hbm.1) | copy-start | bytes 1572868
  0.0 9.2 %copy-start.12 = (s32[1,1,4,512]{3,2,1,0:T(4,128)S(1)}, s32[1,1,4,512]{3,2,1,0:T(4,128)}, u32[]{:S(2)}) copy-start(s32[1,1,4,512]{3,2,1,0:T(4,128)} %param.11) | copy-start | bytes 24580
  2.3 9.6 %copy-start.2 = (bf16[1,1,512,128]{3,2,1,0:T(8,128)(2,1)S(1)}, bf16[1,1,512,128]{3,2,1,0:T(8,128)(2,1)}, u32[]{:S(2)}) copy-start(bf16[1,1,512,128]{3,2,1,0:T(8,128)(2,1)} %param.10) | copy-start | bytes 393220
  2.4 9.6 %copy-start.6 = (bf16[272,128]{1,0:T(8,128)(2,1)S(1)}, bf16[272,128]{1,0:T(8,128)(2,1)}, u32[]{:S(2)}) copy-start(bf16[272,128]{1,0:T(8,128)(2,1)} %get-tuple-element.54.send_2) | copy-start | bytes 208900
  2.4 9.6 %copy-start.7 = (bf16[272,128]{1,0:T(8,128)(2,1)S(1)}, bf16[272,128]{1,0:T(8,128)(2,1)}, u32[]{:S(2)}) copy-start(bf16[272,128]{1,0:T(8,128)(2,1)} %get-tuple-element.52.send_0) | copy-start | bytes 208900
  2.4 9.6 %copy-start.8 = (bf16[272,128]{1,0:T(8,128)(2,1)S(1)}, bf16[272,128]{1,0:T(8,128)(2,1)}, u32[]{:S(2)}) copy-start(bf16[272,128]{1,0:T(8,128)(2,1)} %get-tuple-element.55.send_3) | copy-start | bytes 208900
  2.4 9.6 %copy-start.9 = (bf16[272,128]{1,0:T(8,128)(2,1)S(1)}, bf16[272,128]{1,0:T(8,128)(2,1)}, u32[]{:S(2)}) copy-start(bf16[272,128]{1,0:T(8,128)(2,1)} %get-tuple-element.53.send_1) | copy-start | bytes 208900
  2.4 13.2 %collective-permute-start.3 = (bf16[272,128]{1,0:T(8,128)(2,1)}, bf16[272,128]{1,0:T(8,128)(2,1)S(1)}, u32[]{:S(2)}, u32[]{:S(2)}) collective-permute-start(bf16[272,128]{1,0:T(8,128)(2,1)} %get-tuple-element.52.send_0), channel_id=1, source_target_pairs={{1,2},{2,1},{3,0},{0,3},{5,6},{6,5},{7,4},{4,7},{9,10},{10,9},{11,... | collective-permute-start | bytes 208904 | tf_op jit(solution)/shard_map/ppermute | solution.py:27
  7.5 6.1 %collective-permute-start.1 = (bf16[272,128]{1,0:T(8,128)(2,1)}, bf16[272,128]{1,0:T(8,128)(2,1)S(1)}, u32[]{:S(2)}, u32[]{:S(2)}) collective-permute-start(bf16[272,128]{1,0:T(8,128)(2,1)} %get-tuple-element.53.send_1), channel_id=1, source_target_pairs={{4,8},{8,4},{12,16},{16,12},{20,24},{24,20},{28,0},{0,28},{5,9},{9... | collective-permute-start | bytes 208904 | tf_op jit(solution)/shard_map/ppermute | solution.py:27
  9.1 6.4 %collective-permute-start.2 = (bf16[272,128]{1,0:T(8,128)(2,1)}, bf16[272,128]{1,0:T(8,128)(2,1)S(1)}, u32[]{:S(2)}, u32[]{:S(2)}) collective-permute-start(bf16[272,128]{1,0:T(8,128)(2,1)} %get-tuple-element.54.send_2), channel_id=1, source_target_pairs={{0,1},{1,0},{2,3},{3,2},{4,5},{5,4},{6,7},{7,6},{8,9},{9,8},{10,11... | collective-permute-start | bytes 208904 | tf_op jit(solution)/shard_map/ppermute | solution.py:27
  9.1 4.5 %collective-permute-start = (bf16[272,128]{1,0:T(8,128)(2,1)}, bf16[272,128]{1,0:T(8,128)(2,1)S(1)}, u32[]{:S(2)}, u32[]{:S(2)}) collective-permute-start(bf16[272,128]{1,0:T(8,128)(2,1)} %get-tuple-element.55.send_3), channel_id=1, source_target_pairs={{0,4},{4,0},{8,12},{12,8},{16,20},{20,16},{24,28},{28,24},{1,5},{5... | collective-permute-start | bytes 208904 | tf_op jit(solution)/shard_map/ppermute | solution.py:27
  11.9 1.7 %copy-start.3 = (s32[1,1,2,256]{3,2,1,0:T(2,128)S(1)}, s32[1,1,2,256]{3,2,1,0:T(2,128)}, u32[]{:S(2)}) copy-start(s32[1,1,2,256]{3,2,1,0:T(2,128)} %param.13) | copy-start | bytes 6148
  13.7 1.9 %copy-start = (bf16[4,256,256]{2,1,0:T(8,128)(2,1)S(1)}, bf16[4,256,256]{2,1,0:T(8,128)(2,1)}, u32[]{:S(2)}) copy-start(bf16[4,256,256]{2,1,0:T(8,128)(2,1)} %get-tuple-element.70.refs_13_.refs_15_) | copy-start | bytes 1572868
  13.7 1.9 %copy-start.1 = (bf16[4,256,128]{2,1,0:T(8,128)(2,1)S(1)}, bf16[4,256,128]{2,1,0:T(8,128)(2,1)}, u32[]{:S(2)}) copy-start(bf16[4,256,128]{2,1,0:T(8,128)(2,1)} %get-tuple-element.71.refs_14_.refs_16_) | copy-start | bytes 786436
  18.0 7.5 %collective-permute-start.7 = (bf16[256,128]{1,0:T(8,128)(2,1)S(1)}, bf16[256,128]{1,0:T(8,128)(2,1)S(1)}, u32[]{:S(2)}, u32[]{:S(2)}) collective-permute-start(bf16[256,128]{1,0:T(8,128)(2,1)S(1)} %get-tuple-element.73.send_0), channel_id=1, source_target_pairs={{1,2},{2,1},{3,0},{0,3},{5,6},{6,5},{7,4},{4,7},{9,10},{10,9},{11,... | collective-permute-start | bytes 196616 | tf_op jit(solution)/shard_map/ppermute | solution.py:27
  18.9 5.0 %collective-permute-start.5 = (bf16[256,128]{1,0:T(8,128)(2,1)S(1)}, bf16[256,128]{1,0:T(8,128)(2,1)S(1)}, u32[]{:S(2)}, u32[]{:S(2)}) collective-permute-start(bf16[256,128]{1,0:T(8,128)(2,1)S(1)} %get-tuple-element.74.send_1), channel_id=1, source_target_pairs={{4,8},{8,4},{12,16},{16,12},{20,24},{24,20},{28,0},{0,28},{5,9},{9... | collective-permute-start | bytes 196616 | tf_op jit(solution)/shard_map/ppermute | solution.py:27
  19.6 6.1 %collective-permute-start.6 = (bf16[256,128]{1,0:T(8,128)(2,1)S(1)}, bf16[256,128]{1,0:T(8,128)(2,1)S(1)}, u32[]{:S(2)}, u32[]{:S(2)}) collective-permute-start(bf16[256,128]{1,0:T(8,128)(2,1)S(1)} %get-tuple-element.75.send_2), channel_id=1, source_target_pairs={{0,1},{1,0},{2,3},{3,2},{4,5},{5,4},{6,7},{7,6},{8,9},{9,8},{10,11... | collective-permute-start | bytes 196616 | tf_op jit(solution)/shard_map/ppermute | solution.py:27
  21.1 2.8 %collective-permute-start.4 = (bf16[256,128]{1,0:T(8,128)(2,1)S(1)}, bf16[256,128]{1,0:T(8,128)(2,1)S(1)}, u32[]{:S(2)}, u32[]{:S(2)}) collective-permute-start(bf16[256,128]{1,0:T(8,128)(2,1)S(1)} %get-tuple-element.76.send_3), channel_id=1, source_target_pairs={{0,4},{4,0},{8,12},{12,8},{16,20},{20,16},{24,28},{28,24},{1,5},{5... | collective-permute-start | bytes 196616 | tf_op jit(solution)/shard_map/ppermute | solution.py:27
  27.7 9.4 %collective-permute-start.11 = (bf16[256,128]{1,0:T(8,128)(2,1)S(1)}, bf16[256,128]{1,0:T(8,128)(2,1)S(1)}, u32[]{:S(2)}, u32[]{:S(2)}) collective-permute-start(bf16[256,128]{1,0:T(8,128)(2,1)S(1)} %get-tuple-element.86.send_0), channel_id=1, source_target_pairs={{1,2},{2,1},{3,0},{0,3},{5,6},{6,5},{7,4},{4,7},{9,10},{10,9},{11,... | collective-permute-start | bytes 196616 | tf_op jit(solution)/shard_map/ppermute | solution.py:27
  30.9 4.6 %collective-permute-start.9 = (bf16[256,128]{1,0:T(8,128)(2,1)S(1)}, bf16[256,128]{1,0:T(8,128)(2,1)S(1)}, u32[]{:S(2)}, u32[]{:S(2)}) collective-permute-start(bf16[256,128]{1,0:T(8,128)(2,1)S(1)} %get-tuple-element.87.send_1), channel_id=1, source_target_pairs={{4,8},{8,4},{12,16},{16,12},{20,24},{24,20},{28,0},{0,28},{5,9},{9... | collective-permute-start | bytes 196616 | tf_op jit(solution)/shard_map/ppermute | solution.py:27
  31.3 5.8 %collective-permute-start.10 = (bf16[256,128]{1,0:T(8,128)(2,1)S(1)}, bf16[256,128]{1,0:T(8,128)(2,1)S(1)}, u32[]{:S(2)}, u32[]{:S(2)}) collective-permute-start(bf16[256,128]{1,0:T(8,128)(2,1)S(1)} %get-tuple-element.88.send_2), channel_id=1, source_target_pairs={{0,1},{1,0},{2,3},{3,2},{4,5},{5,4},{6,7},{7,6},{8,9},{9,8},{10,11... | collective-permute-start | bytes 196616 | tf_op jit(solution)/shard_map/ppermute | solution.py:27
  31.5 4.0 %collective-permute-start.8 = (bf16[256,128]{1,0:T(8,128)(2,1)S(1)}, bf16[256,128]{1,0:T(8,128)(2,1)S(1)}, u32[]{:S(2)}, u32[]{:S(2)}) collective-permute-start(bf16[256,128]{1,0:T(8,128)(2,1)S(1)} %get-tuple-element.89.send_3), channel_id=1, source_target_pairs={{0,4},{4,0},{8,12},{12,8},{16,20},{20,16},{24,28},{28,24},{1,5},{5... | collective-permute-start | bytes 196616 | tf_op jit(solution)/shard_map/ppermute | solution.py:27
  39.2 7.0 %collective-permute-start.15 = (bf16[256,128]{1,0:T(8,128)(2,1)S(1)}, bf16[256,128]{1,0:T(8,128)(2,1)S(1)}, u32[]{:S(2)}, u32[]{:S(2)}) collective-permute-start(bf16[256,128]{1,0:T(8,128)(2,1)S(1)} %get-tuple-element.93.send_0), channel_id=1, source_target_pairs={{1,2},{2,1},{3,0},{0,3},{5,6},{6,5},{7,4},{4,7},{9,10},{10,9},{11,... | collective-permute-start | bytes 196616 | tf_op jit(solution)/shard_map/ppermute | solution.py:27
  40.0 4.6 %collective-permute-start.13 = (bf16[256,128]{1,0:T(8,128)(2,1)S(1)}, bf16[256,128]{1,0:T(8,128)(2,1)S(1)}, u32[]{:S(2)}, u32[]{:S(2)}) collective-permute-start(bf16[256,128]{1,0:T(8,128)(2,1)S(1)} %get-tuple-element.94.send_1), channel_id=1, source_target_pairs={{4,8},{8,4},{12,16},{16,12},{20,24},{24,20},{28,0},{0,28},{5,9},{9... | collective-permute-start | bytes 196616 | tf_op jit(solution)/shard_map/ppermute | solution.py:27
  41.0 5.2 %collective-permute-start.14 = (bf16[256,128]{1,0:T(8,128)(2,1)S(1)}, bf16[256,128]{1,0:T(8,128)(2,1)S(1)}, u32[]{:S(2)}, u32[]{:S(2)}) collective-permute-start(bf16[256,128]{1,0:T(8,128)(2,1)S(1)} %get-tuple-element.95.send_2), channel_id=1, source_target_pairs={{0,1},{1,0},{2,3},{3,2},{4,5},{5,4},{6,7},{7,6},{8,9},{9,8},{10,11... | collective-permute-start | bytes 196616 | tf_op jit(solution)/shard_map/ppermute | solution.py:27
  41.0 3.6 %collective-permute-start.12 = (bf16[256,128]{1,0:T(8,128)(2,1)S(1)}, bf16[256,128]{1,0:T(8,128)(2,1)S(1)}, u32[]{:S(2)}, u32[]{:S(2)}) collective-permute-start(bf16[256,128]{1,0:T(8,128)(2,1)S(1)} %get-tuple-element.96.send_3), channel_id=1, source_target_pairs={{0,4},{4,0},{8,12},{12,8},{16,20},{20,16},{24,28},{28,24},{1,5},{5... | collective-permute-start | bytes 196616 | tf_op jit(solution)/shard_map/ppermute | solution.py:27

commit v3 on v2

--- a/solution.py
+++ b/solution.py
@@ -11,6 +11,7 @@
 F32 = jnp.float32
 I32 = jnp.int32
 VMEM = pl.BlockSpec(memory_space=pltpu.VMEM)
+SMEM = pl.BlockSpec(memory_space=pltpu.SMEM)
 HBM = pl.BlockSpec(memory_space=pltpu.HBM)
 
 NEAR_X, FAR_X, NEAR_Y, FAR_Y = range(4)
@@ -50,11 +51,12 @@
 
 
 def column_one_hot(row, depth):
-    return (lax.broadcasted_iota(I32, (depth, row.shape[1]), 0) == row).astype(BF)
+    depths = lax.broadcasted_iota(jnp.int16, (depth, row.shape[1]), 0)
+    return jnp.where(depths == row.astype(jnp.int16), BF(1), BF(0))
 
 
 def column_mask(bit, width):
-    return jnp.broadcast_to(bit.astype(F32), (width, bit.shape[1])).T.astype(BF)
+    return jnp.broadcast_to(bit.astype(F32).astype(BF), (width, bit.shape[1])).T
 
 
 def cut(row, half):
@@ -162,25 +164,12 @@
 
 
 def setup_kernel(
-    tops_hbm, etop_hbm, ebot_hbm, live_hbm, nbr_hbm, weights_hbm, nodes_hbm, biases_hbm,
+    tops_ref, etop_ref, ebot_ref, live_ref, nbr_ref, weights_ref, nodes_ref, raw_biases_ref,
     pick_ref, spread_ref, mask_ref, gather_ref, sum_ref, half_ref,
     ends_w_ref, hidden_ref, join_ref, out_w_ref, biases_ref,
-    tops_ref, etop_ref, ebot_ref, live_ref, nbr_ref, weights_ref, nodes_ref, raw_biases_ref, sems,
 ):
-    moves = [
-        pltpu.make_async_copy(src, dst, sems.at[i])
-        for i, (src, dst) in enumerate((
-            (tops_hbm, tops_ref), (etop_hbm, etop_ref), (ebot_hbm, ebot_ref), (live_hbm, live_ref),
-            (nbr_hbm, nbr_ref), (weights_hbm, weights_ref), (nodes_hbm, nodes_ref),
-            (biases_hbm, raw_biases_ref),
-        ))
-    ]
-    for move in moves:
-        move.start()
     half = spread_ref.shape[0]
     width = mask_ref.shape[1]
-    for move in moves[:4]:
-        move.wait()
     slots = etop_ref.shape[1]
     for d in range(2):
         live = lax.broadcasted_iota(I32, (1, slots), 1) < live_ref[0, d]
@@ -188,8 +177,6 @@
             etop_ref[d : d + 1, :], ebot_ref[d : d + 1, :], tops_ref[d : d + 1, :],
             live, 1, half, width,
         )
-    for move in moves[4:]:
-        move.wait()
     rows = nbr_ref.shape[1]
     for k in range(nbr_ref.shape[0]):
         here = slice(k * rows, (k + 1) * rows)
@@ -393,14 +380,7 @@
                    like((steps, 2 * width, width), BF), like((steps, width, width), BF),
                    like(bias_rows.shape, F32)],
                 (tops, etop, ebot, live, nbr, edge_weights, node_weights, bias_rows),
-                in_specs=[HBM] * 8,
-                scratch=[
-                    pltpu.VMEM(tops.shape, I32), pltpu.VMEM(etop.shape, I32),
-                    pltpu.VMEM(etop.shape, I32), pltpu.SMEM(live.shape, I32),
-                    pltpu.VMEM(nbr.shape, I32), pltpu.VMEM(edge_weights.shape, BF),
-                    pltpu.VMEM(node_weights.shape, BF), pltpu.VMEM(bias_rows.shape, F32),
-                    pltpu.SemaphoreType.DMA((8,)),
-                ],
+                in_specs=[VMEM] * 3 + [SMEM] + [VMEM] * 4,
                 name="setup",
             )
             inner, own = made[:3], made[3:6]

time: 48.9 us -> 47.7 us (0.975)
  Pallas kernels: 27.3 us -> 26.2 us
    pallas_call x14, Pallas kernels: 27.3 us -> 26.2 us  [call(): pl.pallas_call(kernel, out_shape=outs, in_specs=in_specs or [VMEM] * len(...]
  transfers between devices with their start and end apart: 16 -> 16, of which waited for: 4 -> 5; matrix products, arithmetic and copies ran while one was open for 0% -> 0% of each run, Pallas kernels for 32% -> 32%
where the time goes in v3:
time: 47.7 us; the launch traced here: 47.6 us
  Pallas kernels  26.2 us (55%)
  starting transfers between devices  15.6 us (33%)
  waiting for transfers between devices  5.3 us (11%)
    pallas_call x14, Pallas kernels, call(): pl.pallas_call(kernel, out_shape=outs, in_specs=in_specs or [VMEM] * len(...  26.2 us
    ppermute x16, starting transfers between devices, swapped(): return lax.ppermute(block, axis, route)  15.6 us
    ppermute x16, waiting for transfers between devices, swapped(): return lax.ppermute(block, axis, route)  5.3 us
  transfers between devices with their start and end apart: 16, of which 5 were waited for; matrix products, arithmetic and copies ran while one was open for 0% of the time, Pallas kernels for 32%

profile of v3, /device:TPU:0, one launch (start us, length us, event | category | flops | bytes accessed | tf_op | source)
XLA Modules:
  0.0 47.6 jit_solution(6453494105679988911)
XLA Ops:
  0.0 2.2 %first.1 = (bf16[272,128]{1,0:T(8,128)(2,1)}, bf16[272,128]{1,0:T(8,128)(2,1)}, bf16[272,128]{1,0:T(8,128)(2,1)}, bf16[272,128]{1,0:T(8,128)(2,1)}, bf16[4,256,2...) custom-call(bf16[512,128]{1,0:T(8,128)(2,1)} %bitcast.9, s32[2,256]{1,0:T(2,128)} %bitcast.21, s32[2,256]{1,0:T(2,128)} %bitcast.12, ...), custom_call_target="tpu_custom_call" | custom-call | flops 1073741824 | bytes 151560 | tf_op jit(solution)/shard_map/first/pallas_call | solution.py:33
  2.3 0.0 copy-start.2
  2.3 0.0 copy-start.7
  2.4 5.1 %collective-permute-start.3 = (bf16[272,128]{1,0:T(8,128)(2,1)}, bf16[272,128]{1,0:T(8,128)(2,1)S(1)}, u32[]{:S(2)}, u32[]{:S(2)}) collective-permute-start(bf16[272,128]{1,0:T(8,128)(2,1)} %get-tuple-element.52.send_0), channel_id=1, source_target_pairs={{1,2},{2,1},{3,0},{0,3},{5,6},{6,5},{7,4},{4,7},{9,10},{10,9},{11,... | collective-permute-start | bytes 208904 | tf_op jit(solution)/shard_map/ppermute | solution.py:28
  7.5 1.6 %collective-permute-start.1 = (bf16[272,128]{1,0:T(8,128)(2,1)}, bf16[272,128]{1,0:T(8,128)(2,1)S(1)}, u32[]{:S(2)}, u32[]{:S(2)}) collective-permute-start(bf16[272,128]{1,0:T(8,128)(2,1)} %get-tuple-element.53.send_1), channel_id=1, source_target_pairs={{4,8},{8,4},{12,16},{16,12},{20,24},{24,20},{28,0},{0,28},{5,9},{9... | collective-permute-start | bytes 208904 | tf_op jit(solution)/shard_map/ppermute | solution.py:28
  9.2 1.9 %setup.1 = (bf16[2048,256]{1,0:T(8,128)(2,1)S(1)}, bf16[256,2048]{1,0:T(8,128)(2,1)S(1)}, bf16[2048,128]{1,0:T(8,128)(2,1)S(1)}, bf16[2,1024,512]{2,1,0:T(8,128)...) custom-call(s32[2,256]{1,0:T(2,128)S(1)} %bitcast.22, ...), custom_call_target="tpu_custom_call" | custom-call | flops 1073741824 | bytes 950280 | tf_op jit(solution)/shard_map/setup/pallas_call | solution.py:33
  11.1 1.6 %inner.4 = (f32[512,128]{1,0:T(8,128)S(1)}, bf16[4,256,128]{2,1,0:T(8,128)(2,1)S(1)}) custom-call(bf16[512,128]{1,0:T(8,128)(2,1)S(1)} %bitcast.10, bf16[272,128]{1,0:T(8,128)(2,1)S(1)} %copy-done.7, bf16[272,128]{1,0:T(8,128)(2,1)S(1)} %copy-done.9, bf16[272,128]{1,0:T(8,128)(2,1)S(1)} %copy-done.6, bf16[272,128]{1,0:T(8,128)(2,1)S(1)} %copy-done.8, ...), custom_call_target="tpu_custom_call" | custom-call | flops 1073741824 | bytes 3823616 | tf_op jit(solution)/shard_map/inner/pallas_call | solution.py:33
  12.7 0.2 collective-permute-done.1.refs_1_
  13.0 1.7 %along_x.4 = (f32[512,128]{1,0:T(8,128)S(1)}, bf16[1024,512]{1,0:T(8,128)(2,1)S(1)}, bf16[256,1024]{1,0:T(8,128)(2,1)S(1)}, bf16[1024,128]{1,0:T(8,128)(2,1)S(1)}) custom-call(f32[512,128]{1,0:T(8,128)S(1)} %get-tuple-element.62.total_ref, bf16[272,128]{1,0:T(8,128)(2,1)S(1)} %collective-permute-done.refs_0_, ...), custom_call_target="tpu_custom_call" | custom-call | flops 1073741824 | bytes 5128192 | tf_op jit(solution)/shard_map/along_x/pallas_call | solution.py:33
  14.7 2.2 %along_y.4 = (bf16[512,128]{1,0:T(8,128)(2,1)S(1)}, bf16[256,128]{1,0:T(8,128)(2,1)S(1)}, bf16[256,128]{1,0:T(8,128)(2,1)S(1)}, bf16[256,128]{1,0:T(8,128)(2,1)S...) custom-call(f32[512,128]{1,0:T(8,128)S(1)} %get-tuple-element.67.tot, ...), custom_call_target="tpu_custom_call" | custom-call | flops 1073741824 | bytes 6438912 | tf_op jit(solution)/shard_map/along_y/pallas_call | solution.py:33
  16.9 0.8 %collective-permute-start.7 = (bf16[256,128]{1,0:T(8,128)(2,1)S(1)}, bf16[256,128]{1,0:T(8,128)(2,1)S(1)}, u32[]{:S(2)}, u32[]{:S(2)}) collective-permute-start(bf16[256,128]{1,0:T(8,128)(2,1)S(1)} %get-tuple-element.73.send_0), channel_id=1, source_target_pairs={{1,2},{2,1},{3,0},{0,3},{5,6},{6,5},{7,4},{4,7},{9,10},{10,9},{11,... | collective-permute-start | bytes 196616 | tf_op jit(solution)/shard_map/ppermute | solution.py:28
  17.7 0.7 %collective-permute-start.5 = (bf16[256,128]{1,0:T(8,128)(2,1)S(1)}, bf16[256,128]{1,0:T(8,128)(2,1)S(1)}, u32[]{:S(2)}, u32[]{:S(2)}) collective-permute-start(bf16[256,128]{1,0:T(8,128)(2,1)S(1)} %get-tuple-element.74.send_1), channel_id=1, source_target_pairs={{4,8},{8,4},{12,16},{16,12},{20,24},{24,20},{28,0},{0,28},{5,9},{9... | collective-permute-start | bytes 196616 | tf_op jit(solution)/shard_map/ppermute | solution.py:28
  18.3 1.5 %collective-permute-start.6 = (bf16[256,128]{1,0:T(8,128)(2,1)S(1)}, bf16[256,128]{1,0:T(8,128)(2,1)S(1)}, u32[]{:S(2)}, u32[]{:S(2)}) collective-permute-start(bf16[256,128]{1,0:T(8,128)(2,1)S(1)} %get-tuple-element.75.send_2), channel_id=1, source_target_pairs={{0,1},{1,0},{2,3},{3,2},{4,5},{5,4},{6,7},{7,6},{8,9},{9,8},{10,11... | collective-permute-start | bytes 196616 | tf_op jit(solution)/shard_map/ppermute | solution.py:28
  19.8 0.1 collective-permute-start.4
  19.9 1.6 %inner.5 = (f32[512,128]{1,0:T(8,128)S(1)}, bf16[4,256,128]{2,1,0:T(8,128)(2,1)S(1)}) custom-call(bf16[512,128]{1,0:T(8,128)(2,1)S(1)} %get-tuple-element.72.latent_ref.refs_12_, bf16[256,128]{1,0:T(8,128)(2,1)S(1)} %get-tuple-element.73.send_0, bf16[256,128]{1,0:T(8,128)(2,1)S(1)} %get-tuple-element.74.send_1, ...), custom_call_target="tpu_custom_call" | custom-call | flops 1073741824 | bytes 3807232 | tf_op jit(solution)/shard_map/inner/pallas_call | solution.py:33
  21.6 1.1 %collective-permute-done.5.refs_1_ = bf16[256,128]{1,0:T(8,128)(2,1)S(1)} collective-permute-done((bf16[256,128]{1,0:T(8,128)(2,1)S(1)}, bf16[256,128]{1,0:T(8,128)(2,1)S(1)}, u32[]{:S(2)}, u32[]{:S(2)}) %collective-permute-start.5) | collective-permute-done | bytes 65568 | tf_op jit(solution)/shard_map/ppermute | solution.py:28
  22.7 1.6 %along_x.5.total_ref = f32[512,128]{1,0:T(8,128)S(1)} custom-call(f32[512,128]{1,0:T(8,128)S(1)} %get-tuple-element.77.total_ref, bf16[256,128]{1,0:T(8,128)(2,1)S(1)} %collective-permute-done.4.refs_0_, bf16[256,128]{1,0:T(8,128)(2,1)S(1)} %collective-permute-done.5.refs_1_, bf16[4,2,128,128]{3,2,1,0:T(8,128)(2,1)S(1)} %get-tuple-element.56.ends_w_ref.refs_2_, ...), custom_call_target="tpu_custom_call" | custom-call | flops 1073741824 | bytes 6952960 | tf_op jit(solution)/shard_map/along_x/pallas_call | solution.py:33
  24.3 0.1 collective-permute-done.6.refs_0_
  24.4 2.1 %along_y.5 = (bf16[512,128]{1,0:T(8,128)(2,1)S(1)}, bf16[256,128]{1,0:T(8,128)(2,1)S(1)}, bf16[256,128]{1,0:T(8,128)(2,1)S(1)}, bf16[256,128]{1,0:T(8,128)(2,1)S(1)}, bf16[256,128]{1,0:T(8,128)(2,1)S(1)}) custom-call(f32[512,128]{1,0:T(8,128)S(1)} %along_x.5.total_ref, bf16[256,128]{1,0:T(8,128)(2,1)S(1)} %collective-permute-done.6.refs_0_, ...), custom_call_target="tpu_custom_call" | custom-call | flops 1073741824 | bytes 8263680 | tf_op jit(solution)/shard_map/along_y/pallas_call | solution.py:33
  26.5 3.2 %collective-permute-start.11 = (bf16[256,128]{1,0:T(8,128)(2,1)S(1)}, bf16[256,128]{1,0:T(8,128)(2,1)S(1)}, u32[]{:S(2)}, u32[]{:S(2)}) collective-permute-start(bf16[256,128]{1,0:T(8,128)(2,1)S(1)} %get-tuple-element.86.send_0), channel_id=1, source_target_pairs={{1,2},{2,1},{3,0},{0,3},{5,6},{6,5},{7,4},{4,7},{9,10},{10,9},{11,... | collective-permute-start | bytes 196616 | tf_op jit(solution)/shard_map/ppermute | solution.py:28
  29.7 0.7 %collective-permute-start.9 = (bf16[256,128]{1,0:T(8,128)(2,1)S(1)}, bf16[256,128]{1,0:T(8,128)(2,1)S(1)}, u32[]{:S(2)}, u32[]{:S(2)}) collective-permute-start(bf16[256,128]{1,0:T(8,128)(2,1)S(1)} %get-tuple-element.87.send_1), channel_id=1, source_target_pairs={{4,8},{8,4},{12,16},{16,12},{20,24},{24,20},{28,0},{0,28},{5,9},{9... | collective-permute-start | bytes 196616 | tf_op jit(solution)/shard_map/ppermute | solution.py:28
  30.3 0.0 collective-permute-start.8
  30.4 1.8 %inner.6 = (f32[512,128]{1,0:T(8,128)S(1)}, bf16[4,256,128]{2,1,0:T(8,128)(2,1)S(1)}) custom-call(bf16[512,128]{1,0:T(8,128)(2,1)S(1)} %get-tuple-element.85.latent_ref.refs_12_, bf16[256,128]{1,0:T(8,128)(2,1)S(1)} %get-tuple-element.86.send_0, bf16[256,128]{1,0:T(8,128)(2,1)S(1)} %get-tuple-element.87.send_1, ...), custom_call_target="tpu_custom_call" | custom-call | flops 1073741824 | bytes 3807232 | tf_op jit(solution)/shard_map/inner/pallas_call | solution.py:33
  32.2 2.1 %collective-permute-done.9.refs_1_ = bf16[256,128]{1,0:T(8,128)(2,1)S(1)} collective-permute-done((bf16[256,128]{1,0:T(8,128)(2,1)S(1)}, bf16[256,128]{1,0:T(8,128)(2,1)S(1)}, u32[]{:S(2)}, u32[]{:S(2)}) %collective-permute-start.9) | collective-permute-done | bytes 65568 | tf_op jit(solution)/shard_map/ppermute | solution.py:28
  34.3 1.6 %along_x.6.total_ref = f32[512,128]{1,0:T(8,128)S(1)} custom-call(f32[512,128]{1,0:T(8,128)S(1)} %get-tuple-element.90.total_ref, bf16[256,128]{1,0:T(8,128)(2,1)S(1)} %collective-permute-done.8.refs_0_, bf16[256,128]{1,0:T(8,128)(2,1)S(1)} %collective-permute-done.9.refs_1_, bf16[4,2,128,128]{3,2,1,0:T(8,128)(2,1)S(1)} %get-tuple-element.56.ends_w_ref.refs_2_, ...), custom_call_target="tpu_custom_call" | custom-call | flops 1073741824 | bytes 6952960 | tf_op jit(solution)/shard_map/along_x/pallas_call | solution.py:33
  35.9 2.1 %along_y.6 = (bf16[512,128]{1,0:T(8,128)(2,1)S(1)}, bf16[256,128]{1,0:T(8,128)(2,1)S(1)}, bf16[256,128]{1,0:T(8,128)(2,1)S(1)}, bf16[256,128]{1,0:T(8,128)(2,1)S(1)}, bf16[256,128]{1,0:T(8,128)(2,1)S(1)}) custom-call(f32[512,128]{1,0:T(8,128)S(1)} %along_x.6.total_ref, bf16[256,128]{1,0:T(8,128)(2,1)S(1)} %collective-permute-done.10.refs_0_, ...), custom_call_target="tpu_custom_call" | custom-call | flops 1073741824 | bytes 8263680 | tf_op jit(solution)/shard_map/along_y/pallas_call | solution.py:33
  38.0 0.8 %collective-permute-start.15 = (bf16[256,128]{1,0:T(8,128)(2,1)S(1)}, bf16[256,128]{1,0:T(8,128)(2,1)S(1)}, u32[]{:S(2)}, u32[]{:S(2)}) collective-permute-start(bf16[256,128]{1,0:T(8,128)(2,1)S(1)} %get-tuple-element.93.send_0), channel_id=1, source_target_pairs={{1,2},{2,1},{3,0},{0,3},{5,6},{6,5},{7,4},{4,7},{9,10},{10,9},{11,... | collective-permute-start | bytes 196616 | tf_op jit(solution)/shard_map/ppermute | solution.py:28
  38.8 1.2 %collective-permute-start.13 = (bf16[256,128]{1,0:T(8,128)(2,1)S(1)}, bf16[256,128]{1,0:T(8,128)(2,1)S(1)}, u32[]{:S(2)}, u32[]{:S(2)}) collective-permute-start(bf16[256,128]{1,0:T(8,128)(2,1)S(1)} %get-tuple-element.94.send_1), channel_id=1, source_target_pairs={{4,8},{8,4},{12,16},{16,12},{20,24},{24,20},{28,0},{0,28},{5,9},{9... | collective-permute-start | bytes 196616 | tf_op jit(solution)/shard_map/ppermute | solution.py:28
  40.0 1.6 %inner.7 = (f32[512,128]{1,0:T(8,128)S(1)}, bf16[4,256,128]{2,1,0:T(8,128)(2,1)S(1)}) custom-call(bf16[512,128]{1,0:T(8,128)(2,1)S(1)} %get-tuple-element.92.latent_ref.refs_12_, bf16[256,128]{1,0:T(8,128)(2,1)S(1)} %get-tuple-element.93.send_0, bf16[256,128]{1,0:T(8,128)(2,1)S(1)} %get-tuple-element.94.send_1, ...), custom_call_target="tpu_custom_call" | custom-call | flops 1073741824 | bytes 3807232 | tf_op jit(solution)/shard_map/inner/pallas_call | solution.py:33
  41.7 1.7 %collective-permute-done.13.refs_1_ = bf16[256,128]{1,0:T(8,128)(2,1)S(1)} collective-permute-done((bf16[256,128]{1,0:T(8,128)(2,1)S(1)}, bf16[256,128]{1,0:T(8,128)(2,1)S(1)}, u32[]{:S(2)}, u32[]{:S(2)}) %collective-permute-start.13) | collective-permute-done | bytes 65568 | tf_op jit(solution)/shard_map/ppermute | solution.py:28
  43.4 1.6 %along_x.7.total_ref = f32[512,128]{1,0:T(8,128)S(1)} custom-call(f32[512,128]{1,0:T(8,128)S(1)} %get-tuple-element.97.total_ref, bf16[256,128]{1,0:T(8,128)(2,1)S(1)} %collective-permute-done.12.refs_0_, bf16[256,128]{1,0:T(8,128)(2,1)S(1)} %collective-permute-done.13.refs_1_, bf16[4,2,128,128]{3,2,1,0:T(8,128)(2,1)S(1)} %get-tuple-element.56.ends_w_ref.refs_2_, ...), custom_call_target="tpu_custom_call" | custom-call | flops 1073741824 | bytes 6952960 | tf_op jit(solution)/shard_map/along_x/pallas_call | solution.py:33
  45.0 2.6 %along_y.7 = bf16[512,128]{1,0:T(8,128)(2,1)} custom-call(f32[512,128]{1,0:T(8,128)S(1)} %along_x.7.total_ref, bf16[256,128]{1,0:T(8,128)(2,1)S(1)} %collective-permute-done.14.refs_0_, bf16[256,128]{1,0:T(8,128)(2,1)S(1)} %collective-permute-done.15.refs_1_, bf16[4,2,128,128]{3,2,1,0:T(8,128)(2,1)S(1)} %get-tuple-element.56.ends_w_ref.refs_2_, ...), custom_call_target="tpu_custom_call" | custom-call | flops 1073741824 | bytes 7477248 | tf_op jit(solution)/shard_map/along_y/pallas_call | solution.py:33
  (46 shorter events, 0.1 us)
Async XLA Ops:
  0.0 9.1 %copy-start.15 = (s32[2,1]{0,1:T(1,128)S(1)}, s32[2,1]{0,1:T(1,128)}, u32[]{:S(2)}) copy-start(s32[2,1]{0,1:T(1,128)} %param.16) | copy-start | bytes 28
  0.0 9.1 %copy-start.11 = (s32[1,1,2,1024]{3,2,1,0:T(2,128)S(1)}, s32[1,1,2,1024]{3,2,1,0:T(2,128)}, u32[]{:S(2)}) copy-start(s32[1,1,2,1024]{3,2,1,0:T(2,128)} %param.15) | copy-start | bytes 24580
  0.0 9.1 %copy-start.10 = (s32[1,1,2,1024]{3,2,1,0:T(2,128)S(1)}, s32[1,1,2,1024]{3,2,1,0:T(2,128)}, u32[]{:S(2)}) copy-start(s32[1,1,2,1024]{3,2,1,0:T(2,128)} %param.14) | copy-start | bytes 24580
  0.0 9.1 %copy-start.14 = (s32[1,1,2,256]{3,2,1,0:T(2,128)S(1)}, s32[1,1,2,256]{3,2,1,0:T(2,128)}, u32[]{:S(2)}) copy-start(s32[1,1,2,256]{3,2,1,0:T(2,128)} %param.12) | copy-start | bytes 6148
  0.0 9.1 %copy-start.13 = (f32[4,3,128]{2,0,1:T(4,128)S(1)}, f32[4,3,128]{2,0,1:T(4,128)}, u32[]{:S(2)}) copy-start(f32[4,3,128]{2,0,1:T(4,128)} %param.19) | copy-start | bytes 18436
  0.0 9.1 %copy-start.5 = (bf16[4,3,128,128]{3,2,1,0:T(8,128)(2,1)S(1)}, bf16[4,3,128,128]{3,2,1,0:T(8,128)(2,1)}, u32[]{:S(2)}) copy-start(bf16[4,3,128,128]{3,2,1,0:T(8,128)(2,1)} %nodes_ref.1) | copy-start | bytes 1179652
  0.0 9.1 %copy-start.4 = (bf16[4,4,128,128]{3,2,1,0:T(8,128)(2,1)S(1)}, bf16[4,4,128,128]{3,2,1,0:T(8,128)(2,1)}, u32[]{:S(2)}) copy-start(bf16[4,4,128,128]{3,2,1,0:T(8,128)(2,1)} %weights_ref.1) | copy-start | bytes 1572868
  0.0 9.1 %copy-start.12 = (s32[1,1,4,512]{3,2,1,0:T(4,128)S(1)}, s32[1,1,4,512]{3,2,1,0:T(4,128)}, u32[]{:S(2)}) copy-start(s32[1,1,4,512]{3,2,1,0:T(4,128)} %param.11) | copy-start | bytes 24580
  2.3 8.7 %copy-start.2 = (bf16[1,1,512,128]{3,2,1,0:T(8,128)(2,1)S(1)}, bf16[1,1,512,128]{3,2,1,0:T(8,128)(2,1)}, u32[]{:S(2)}) copy-start(bf16[1,1,512,128]{3,2,1,0:T(8,128)(2,1)} %param.10) | copy-start | bytes 393220
  2.3 8.7 %copy-start.6 = (bf16[272,128]{1,0:T(8,128)(2,1)S(1)}, bf16[272,128]{1,0:T(8,128)(2,1)}, u32[]{:S(2)}) copy-start(bf16[272,128]{1,0:T(8,128)(2,1)} %get-tuple-element.54.send_2) | copy-start | bytes 208900
  2.3 8.7 %copy-start.7 = (bf16[272,128]{1,0:T(8,128)(2,1)S(1)}, bf16[272,128]{1,0:T(8,128)(2,1)}, u32[]{:S(2)}) copy-start(bf16[272,128]{1,0:T(8,128)(2,1)} %get-tuple-element.52.send_0) | copy-start | bytes 208900
  2.3 8.7 %copy-start.8 = (bf16[272,128]{1,0:T(8,128)(2,1)S(1)}, bf16[272,128]{1,0:T(8,128)(2,1)}, u32[]{:S(2)}) copy-start(bf16[272,128]{1,0:T(8,128)(2,1)} %get-tuple-element.55.send_3) | copy-start | bytes 208900
  2.3 8.7 %copy-start.9 = (bf16[272,128]{1,0:T(8,128)(2,1)S(1)}, bf16[272,128]{1,0:T(8,128)(2,1)}, u32[]{:S(2)}) copy-start(bf16[272,128]{1,0:T(8,128)(2,1)} %get-tuple-element.53.send_1) | copy-start | bytes 208900
  2.4 12.4 %collective-permute-start.3 = (bf16[272,128]{1,0:T(8,128)(2,1)}, bf16[272,128]{1,0:T(8,128)(2,1)S(1)}, u32[]{:S(2)}, u32[]{:S(2)}) collective-permute-start(bf16[272,128]{1,0:T(8,128)(2,1)} %get-tuple-element.52.send_0), channel_id=1, source_target_pairs={{1,2},{2,1},{3,0},{0,3},{5,6},{6,5},{7,4},{4,7},{9,10},{10,9},{11,... | collective-permute-start | bytes 208904 | tf_op jit(solution)/shard_map/ppermute | solution.py:28
  7.5 5.5 %collective-permute-start.1 = (bf16[272,128]{1,0:T(8,128)(2,1)}, bf16[272,128]{1,0:T(8,128)(2,1)S(1)}, u32[]{:S(2)}, u32[]{:S(2)}) collective-permute-start(bf16[272,128]{1,0:T(8,128)(2,1)} %get-tuple-element.53.send_1), channel_id=1, source_target_pairs={{4,8},{8,4},{12,16},{16,12},{20,24},{24,20},{28,0},{0,28},{5,9},{9... | collective-permute-start | bytes 208904 | tf_op jit(solution)/shard_map/ppermute | solution.py:28
  9.1 5.6 %collective-permute-start.2 = (bf16[272,128]{1,0:T(8,128)(2,1)}, bf16[272,128]{1,0:T(8,128)(2,1)S(1)}, u32[]{:S(2)}, u32[]{:S(2)}) collective-permute-start(bf16[272,128]{1,0:T(8,128)(2,1)} %get-tuple-element.54.send_2), channel_id=1, source_target_pairs={{0,1},{1,0},{2,3},{3,2},{4,5},{5,4},{6,7},{7,6},{8,9},{9,8},{10,11... | collective-permute-start | bytes 208904 | tf_op jit(solution)/shard_map/ppermute | solution.py:28
  9.1 3.9 %collective-permute-start = (bf16[272,128]{1,0:T(8,128)(2,1)}, bf16[272,128]{1,0:T(8,128)(2,1)S(1)}, u32[]{:S(2)}, u32[]{:S(2)}) collective-permute-start(bf16[272,128]{1,0:T(8,128)(2,1)} %get-tuple-element.55.send_3), channel_id=1, source_target_pairs={{0,4},{4,0},{8,12},{12,8},{16,20},{20,16},{24,28},{28,24},{1,5},{5... | collective-permute-start | bytes 208904 | tf_op jit(solution)/shard_map/ppermute | solution.py:28
  11.0 1.9 %copy-start.3 = (s32[1,1,2,256]{3,2,1,0:T(2,128)S(1)}, s32[1,1,2,256]{3,2,1,0:T(2,128)}, u32[]{:S(2)}) copy-start(s32[1,1,2,256]{3,2,1,0:T(2,128)} %param.13) | copy-start | bytes 6148
  13.0 1.8 %copy-start = (bf16[4,256,256]{2,1,0:T(8,128)(2,1)S(1)}, bf16[4,256,256]{2,1,0:T(8,128)(2,1)}, u32[]{:S(2)}) copy-start(bf16[4,256,256]{2,1,0:T(8,128)(2,1)} %get-tuple-element.70.refs_13_.refs_15_) | copy-start | bytes 1572868
  13.0 1.8 %copy-start.1 = (bf16[4,256,128]{2,1,0:T(8,128)(2,1)S(1)}, bf16[4,256,128]{2,1,0:T(8,128)(2,1)}, u32[]{:S(2)}) copy-start(bf16[4,256,128]{2,1,0:T(8,128)(2,1)} %get-tuple-element.71.refs_14_.refs_16_) | copy-start | bytes 786436
  16.9 7.3 %collective-permute-start.7 = (bf16[256,128]{1,0:T(8,128)(2,1)S(1)}, bf16[256,128]{1,0:T(8,128)(2,1)S(1)}, u32[]{:S(2)}, u32[]{:S(2)}) collective-permute-start(bf16[256,128]{1,0:T(8,128)(2,1)S(1)} %get-tuple-element.73.send_0), channel_id=1, source_target_pairs={{1,2},{2,1},{3,0},{0,3},{5,6},{6,5},{7,4},{4,7},{9,10},{10,9},{11,... | collective-permute-start | bytes 196616 | tf_op jit(solution)/shard_map/ppermute | solution.py:28
  17.7 5.0 %collective-permute-start.5 = (bf16[256,128]{1,0:T(8,128)(2,1)S(1)}, bf16[256,128]{1,0:T(8,128)(2,1)S(1)}, u32[]{:S(2)}, u32[]{:S(2)}) collective-permute-start(bf16[256,128]{1,0:T(8,128)(2,1)S(1)} %get-tuple-element.74.send_1), channel_id=1, source_target_pairs={{4,8},{8,4},{12,16},{16,12},{20,24},{24,20},{28,0},{0,28},{5,9},{9... | collective-permute-start | bytes 196616 | tf_op jit(solution)/shard_map/ppermute | solution.py:28
  18.3 6.1 %collective-permute-start.6 = (bf16[256,128]{1,0:T(8,128)(2,1)S(1)}, bf16[256,128]{1,0:T(8,128)(2,1)S(1)}, u32[]{:S(2)}, u32[]{:S(2)}) collective-permute-start(bf16[256,128]{1,0:T(8,128)(2,1)S(1)} %get-tuple-element.75.send_2), channel_id=1, source_target_pairs={{0,1},{1,0},{2,3},{3,2},{4,5},{5,4},{6,7},{7,6},{8,9},{9,8},{10,11... | collective-permute-start | bytes 196616 | tf_op jit(solution)/shard_map/ppermute | solution.py:28
  19.8 2.8 %collective-permute-start.4 = (bf16[256,128]{1,0:T(8,128)(2,1)S(1)}, bf16[256,128]{1,0:T(8,128)(2,1)S(1)}, u32[]{:S(2)}, u32[]{:S(2)}) collective-permute-start(bf16[256,128]{1,0:T(8,128)(2,1)S(1)} %get-tuple-element.76.send_3), channel_id=1, source_target_pairs={{0,4},{4,0},{8,12},{12,8},{16,20},{20,16},{24,28},{28,24},{1,5},{5... | collective-permute-start | bytes 196616 | tf_op jit(solution)/shard_map/ppermute | solution.py:28
  26.5 9.4 %collective-permute-start.11 = (bf16[256,128]{1,0:T(8,128)(2,1)S(1)}, bf16[256,128]{1,0:T(8,128)(2,1)S(1)}, u32[]{:S(2)}, u32[]{:S(2)}) collective-permute-start(bf16[256,128]{1,0:T(8,128)(2,1)S(1)} %get-tuple-element.86.send_0), channel_id=1, source_target_pairs={{1,2},{2,1},{3,0},{0,3},{5,6},{6,5},{7,4},{4,7},{9,10},{10,9},{11,... | collective-permute-start | bytes 196616 | tf_op jit(solution)/shard_map/ppermute | solution.py:28
  29.7 4.6 %collective-permute-start.9 = (bf16[256,128]{1,0:T(8,128)(2,1)S(1)}, bf16[256,128]{1,0:T(8,128)(2,1)S(1)}, u32[]{:S(2)}, u32[]{:S(2)}) collective-permute-start(bf16[256,128]{1,0:T(8,128)(2,1)S(1)} %get-tuple-element.87.send_1), channel_id=1, source_target_pairs={{4,8},{8,4},{12,16},{16,12},{20,24},{24,20},{28,0},{0,28},{5,9},{9... | collective-permute-start | bytes 196616 | tf_op jit(solution)/shard_map/ppermute | solution.py:28
  30.3 5.5 %collective-permute-start.10 = (bf16[256,128]{1,0:T(8,128)(2,1)S(1)}, bf16[256,128]{1,0:T(8,128)(2,1)S(1)}, u32[]{:S(2)}, u32[]{:S(2)}) collective-permute-start(bf16[256,128]{1,0:T(8,128)(2,1)S(1)} %get-tuple-element.88.send_2), channel_id=1, source_target_pairs={{0,1},{1,0},{2,3},{3,2},{4,5},{5,4},{6,7},{7,6},{8,9},{9,8},{10,11... | collective-permute-start | bytes 196616 | tf_op jit(solution)/shard_map/ppermute | solution.py:28
  30.3 3.9 %collective-permute-start.8 = (bf16[256,128]{1,0:T(8,128)(2,1)S(1)}, bf16[256,128]{1,0:T(8,128)(2,1)S(1)}, u32[]{:S(2)}, u32[]{:S(2)}) collective-permute-start(bf16[256,128]{1,0:T(8,128)(2,1)S(1)} %get-tuple-element.89.send_3), channel_id=1, source_target_pairs={{0,4},{4,0},{8,12},{12,8},{16,20},{20,16},{24,28},{28,24},{1,5},{5... | collective-permute-start | bytes 196616 | tf_op jit(solution)/shard_map/ppermute | solution.py:28
  38.0 7.0 %collective-permute-start.15 = (bf16[256,128]{1,0:T(8,128)(2,1)S(1)}, bf16[256,128]{1,0:T(8,128)(2,1)S(1)}, u32[]{:S(2)}, u32[]{:S(2)}) collective-permute-start(bf16[256,128]{1,0:T(8,128)(2,1)S(1)} %get-tuple-element.93.send_0), channel_id=1, source_target_pairs={{1,2},{2,1},{3,0},{0,3},{5,6},{6,5},{7,4},{4,7},{9,10},{10,9},{11,... | collective-permute-start | bytes 196616 | tf_op jit(solution)/shard_map/ppermute | solution.py:28
  38.8 4.6 %collective-permute-start.13 = (bf16[256,128]{1,0:T(8,128)(2,1)S(1)}, bf16[256,128]{1,0:T(8,128)(2,1)S(1)}, u32[]{:S(2)}, u32[]{:S(2)}) collective-permute-start(bf16[256,128]{1,0:T(8,128)(2,1)S(1)} %get-tuple-element.94.send_1), channel_id=1, source_target_pairs={{4,8},{8,4},{12,16},{16,12},{20,24},{24,20},{28,0},{0,28},{5,9},{9... | collective-permute-start | bytes 196616 | tf_op jit(solution)/shard_map/ppermute | solution.py:28
  40.0 5.0 %collective-permute-start.14 = (bf16[256,128]{1,0:T(8,128)(2,1)S(1)}, bf16[256,128]{1,0:T(8,128)(2,1)S(1)}, u32[]{:S(2)}, u32[]{:S(2)}) collective-permute-start(bf16[256,128]{1,0:T(8,128)(2,1)S(1)} %get-tuple-element.95.send_2), channel_id=1, source_target_pairs={{0,1},{1,0},{2,3},{3,2},{4,5},{5,4},{6,7},{7,6},{8,9},{9,8},{10,11... | collective-permute-start | bytes 196616 | tf_op jit(solution)/shard_map/ppermute | solution.py:28
  40.0 3.3 %collective-permute-start.12 = (bf16[256,128]{1,0:T(8,128)(2,1)S(1)}, bf16[256,128]{1,0:T(8,128)(2,1)S(1)}, u32[]{:S(2)}, u32[]{:S(2)}) collective-permute-start(bf16[256,128]{1,0:T(8,128)(2,1)S(1)} %get-tuple-element.96.send_3), channel_id=1, source_target_pairs={{0,4},{4,0},{8,12},{12,8},{16,20},{20,16},{24,28},{28,24},{1,5},{5... | collective-permute-start | bytes 196616 | tf_op jit(solution)/shard_map/ppermute | solution.py:28

commit v4 on v3

--- a/solution.py
+++ b/solution.py
@@ -13,6 +13,8 @@
 VMEM = pl.BlockSpec(memory_space=pltpu.VMEM)
 SMEM = pl.BlockSpec(memory_space=pltpu.SMEM)
 HBM = pl.BlockSpec(memory_space=pltpu.HBM)
+
+CUT = 128
 
 NEAR_X, FAR_X, NEAR_Y, FAR_Y = range(4)
 ORDER = (FAR_Y, FAR_X, NEAR_Y, NEAR_X)
@@ -222,21 +224,28 @@
     total = None
     ended = None
     for pair in range(0, fanout, 2):
-        first = []
-        for k in (pair, pair + 1):
-            here = slice(k * rows, (k + 1) * rows)
-            target = choose(dot(pick_ref[here, :], table), mask_ref[here, :])
-            first.append(half_silu(target + source).astype(BF))
-        second = half_silu(dot(jnp.concatenate(first, axis=1), hidden_ref[step]) + c1)
-        started = second[:, :width] + second[:, width:]
+        here = [slice(k * rows, (k + 1) * rows) for k in (pair, pair + 1)]
+        first = [
+            half_silu(choose(dot(pick_ref[k, :], table), mask_ref[k, :]) + source).astype(BF)
+            for k in here
+        ]
+        first = jnp.concatenate(first, axis=1)
+        second = [
+            half_silu(dot(first[a : a + CUT], hidden_ref[step]) + c1) for a in range(0, rows, CUT)
+        ]
+        started = jnp.concatenate([q[:, :width] + q[:, width:] for q in second], axis=0)
         total = started if total is None else total + started
-        second = second.astype(BF)
-        for i in range(2):
-            k = pair + i
-            here = slice(k * rows, (k + 1) * rows)
-            values = by_half(second[:, i * width : (i + 1) * width], mask_ref[here, :])
-            part = dot(spread_ref[:, here], values)
-            ended = part if ended is None else ended + part
+        second = jnp.concatenate([q.astype(BF) for q in second], axis=0)
+        values = [
+            by_half(second[:, i * width : (i + 1) * width], mask_ref[k, :])
+            for i, k in enumerate(here)
+        ]
+        part = jnp.concatenate(
+            [dot(spread_ref[a : a + CUT, here[0]], values[0])
+             + dot(spread_ref[a : a + CUT, here[1]], values[1]) for a in range(0, half, CUT)],
+            axis=0,
+        )
+        ended = part if ended is None else ended + part
     total_ref[0:half, :] = total[0:half] + ended[:, :width]
     total_ref[half:, :] = total[half:] + ended[:, width:]
 
@@ -254,11 +263,21 @@
     for i, (gather, _, _) in enumerate(groups):
         table = jnp.concatenate([table_ref[2 * d + i], far[i]], axis=0)
         first.append(half_silu(dot(gather, table) + c0).astype(BF))
-    second = half_silu(dot(jnp.concatenate(first, axis=1), hidden_ref[step]) + c1).astype(BF)
-    total = None
-    for i, (_, place, mask) in enumerate(groups):
-        part = dot(place, by_half(second[:, i * width : (i + 1) * width], mask))
-        total = part if total is None else total + part
+    first = jnp.concatenate(first, axis=1)
+    second = jnp.concatenate(
+        [half_silu(dot(first[a : a + CUT], hidden_ref[step]) + c1).astype(BF)
+         for a in range(0, first.shape[0], CUT)],
+        axis=0,
+    )
+    values = [
+        by_half(second[:, i * width : (i + 1) * width], mask)
+        for i, (_, _, mask) in enumerate(groups)
+    ]
+    total = jnp.concatenate(
+        [dot(groups[0][1][a : a + CUT], values[0]) + dot(groups[1][1][a : a + CUT], values[1])
+         for a in range(0, groups[0][1].shape[0], CUT)],
+        axis=0,
+    )
     return total
 
 

time: 47.7 us -> 46.4 us (0.973)
  Pallas kernels: 26.2 us -> 23.7 us
  waiting for transfers between devices: 5.3 us -> 6.79 us
    pallas_call x14, Pallas kernels: 26.2 us -> 23.7 us  [call(): pl.pallas_call(kernel, out_shape=outs, in_specs=in_specs or [VMEM] * len(...]
    ppermute x16, waiting for transfers between devices: 5.3 us -> 6.79 us  [swapped(): return lax.ppermute(block, axis, route)]
  transfers between devices with their start and end apart: 16 -> 16, of which waited for: 5 -> 5; matrix products, arithmetic and copies ran while one was open for 0% -> 0% of each run, Pallas kernels for 32% -> 29%
where the time goes in v4:
time: 46.4 us; the launch traced here: 46.3 us
  Pallas kernels  23.7 us (51%)
  starting transfers between devices  15.3 us (33%)
  waiting for transfers between devices  6.79 us (15%)
    pallas_call x14, Pallas kernels, call(): pl.pallas_call(kernel, out_shape=outs, in_specs=in_specs or [VMEM] * len(...  23.7 us
    ppermute x16, starting transfers between devices, swapped(): return lax.ppermute(block, axis, route)  15.3 us
    ppermute x16, waiting for transfers between devices, swapped(): return lax.ppermute(block, axis, route)  6.79 us
  transfers between devices with their start and end apart: 16, of which 5 were waited for; matrix products, arithmetic and copies ran while one was open for 0% of the time, Pallas kernels for 29%

profile of v4, /device:TPU:0, one launch (start us, length us, event | category | flops | bytes accessed | tf_op | source)
XLA Modules:
  0.0 46.3 jit_solution(3359199454330737120)
XLA Ops:
  0.0 2.2 %first.1 = (bf16[272,128]{1,0:T(8,128)(2,1)}, bf16[272,128]{1,0:T(8,128)(2,1)}, bf16[272,128]{1,0:T(8,128)(2,1)}, bf16[272,128]{1,0:T(8,128)(2,1)}, bf16[4,256,2...) custom-call(bf16[512,128]{1,0:T(8,128)(2,1)} %bitcast.9, s32[2,256]{1,0:T(2,128)} %bitcast.21, s32[2,256]{1,0:T(2,128)} %bitcast.12, ...), custom_call_target="tpu_custom_call" | custom-call | flops 1073741824 | bytes 151560 | tf_op jit(solution)/shard_map/first/pallas_call | solution.py:35
  2.3 0.0 copy-start.2
  2.3 0.0 copy-start.7
  2.4 5.1 %collective-permute-start.3 = (bf16[272,128]{1,0:T(8,128)(2,1)}, bf16[272,128]{1,0:T(8,128)(2,1)S(1)}, u32[]{:S(2)}, u32[]{:S(2)}) collective-permute-start(bf16[272,128]{1,0:T(8,128)(2,1)} %get-tuple-element.52.send_0), channel_id=1, source_target_pairs={{1,2},{2,1},{3,0},{0,3},{5,6},{6,5},{7,4},{4,7},{9,10},{10,9},{11,... | collective-permute-start | bytes 208904 | tf_op jit(solution)/shard_map/ppermute | solution.py:30
  7.5 1.6 %collective-permute-start.1 = (bf16[272,128]{1,0:T(8,128)(2,1)}, bf16[272,128]{1,0:T(8,128)(2,1)S(1)}, u32[]{:S(2)}, u32[]{:S(2)}) collective-permute-start(bf16[272,128]{1,0:T(8,128)(2,1)} %get-tuple-element.53.send_1), channel_id=1, source_target_pairs={{4,8},{8,4},{12,16},{16,12},{20,24},{24,20},{28,0},{0,28},{5,9},{9... | collective-permute-start | bytes 208904 | tf_op jit(solution)/shard_map/ppermute | solution.py:30
  9.2 1.9 %setup.1 = (bf16[2048,256]{1,0:T(8,128)(2,1)S(1)}, bf16[256,2048]{1,0:T(8,128)(2,1)S(1)}, bf16[2048,128]{1,0:T(8,128)(2,1)S(1)}, bf16[2,1024,512]{2,1,0:T(8,128)...) custom-call(s32[2,256]{1,0:T(2,128)S(1)} %bitcast.22, ...), custom_call_target="tpu_custom_call" | custom-call | flops 1073741824 | bytes 950280 | tf_op jit(solution)/shard_map/setup/pallas_call | solution.py:35
  11.0 0.0 copy-start.3
  11.1 1.6 %inner.4 = (f32[512,128]{1,0:T(8,128)S(1)}, bf16[4,256,128]{2,1,0:T(8,128)(2,1)S(1)}) custom-call(bf16[512,128]{1,0:T(8,128)(2,1)S(1)} %bitcast.10, bf16[272,128]{1,0:T(8,128)(2,1)S(1)} %copy-done.7, bf16[272,128]{1,0:T(8,128)(2,1)S(1)} %copy-done.9, bf16[272,128]{1,0:T(8,128)(2,1)S(1)} %copy-done.6, bf16[272,128]{1,0:T(8,128)(2,1)S(1)} %copy-done.8, ...), custom_call_target="tpu_custom_call" | custom-call | flops 1073741824 | bytes 3823616 | tf_op jit(solution)/shard_map/inner/pallas_call | solution.py:35
  12.7 0.3 collective-permute-done.1.refs_1_
  13.0 1.4 %along_x.4 = (f32[512,128]{1,0:T(8,128)S(1)}, bf16[1024,512]{1,0:T(8,128)(2,1)S(1)}, bf16[256,1024]{1,0:T(8,128)(2,1)S(1)}, bf16[1024,128]{1,0:T(8,128)(2,1)S(1)}) custom-call(f32[512,128]{1,0:T(8,128)S(1)} %get-tuple-element.62.total_ref, bf16[272,128]{1,0:T(8,128)(2,1)S(1)} %collective-permute-done.refs_0_, ...), custom_call_target="tpu_custom_call" | custom-call | flops 1073741824 | bytes 5128192 | tf_op jit(solution)/shard_map/along_x/pallas_call | solution.py:35
  14.4 2.0 %along_y.4 = (bf16[512,128]{1,0:T(8,128)(2,1)S(1)}, bf16[256,128]{1,0:T(8,128)(2,1)S(1)}, bf16[256,128]{1,0:T(8,128)(2,1)S(1)}, bf16[256,128]{1,0:T(8,128)(2,1)S...) custom-call(f32[512,128]{1,0:T(8,128)S(1)} %get-tuple-element.67.tot, ...), custom_call_target="tpu_custom_call" | custom-call | flops 1073741824 | bytes 6438912 | tf_op jit(solution)/shard_map/along_y/pallas_call | solution.py:35
  16.4 0.7 %collective-permute-start.7 = (bf16[256,128]{1,0:T(8,128)(2,1)S(1)}, bf16[256,128]{1,0:T(8,128)(2,1)S(1)}, u32[]{:S(2)}, u32[]{:S(2)}) collective-permute-start(bf16[256,128]{1,0:T(8,128)(2,1)S(1)} %get-tuple-element.73.send_0), channel_id=1, source_target_pairs={{1,2},{2,1},{3,0},{0,3},{5,6},{6,5},{7,4},{4,7},{9,10},{10,9},{11,... | collective-permute-start | bytes 196616 | tf_op jit(solution)/shard_map/ppermute | solution.py:30
  17.1 0.7 %collective-permute-start.5 = (bf16[256,128]{1,0:T(8,128)(2,1)S(1)}, bf16[256,128]{1,0:T(8,128)(2,1)S(1)}, u32[]{:S(2)}, u32[]{:S(2)}) collective-permute-start(bf16[256,128]{1,0:T(8,128)(2,1)S(1)} %get-tuple-element.74.send_1), channel_id=1, source_target_pairs={{4,8},{8,4},{12,16},{16,12},{20,24},{24,20},{28,0},{0,28},{5,9},{9... | collective-permute-start | bytes 196616 | tf_op jit(solution)/shard_map/ppermute | solution.py:30
  17.7 1.5 %collective-permute-start.6 = (bf16[256,128]{1,0:T(8,128)(2,1)S(1)}, bf16[256,128]{1,0:T(8,128)(2,1)S(1)}, u32[]{:S(2)}, u32[]{:S(2)}) collective-permute-start(bf16[256,128]{1,0:T(8,128)(2,1)S(1)} %get-tuple-element.75.send_2), channel_id=1, source_target_pairs={{0,1},{1,0},{2,3},{3,2},{4,5},{5,4},{6,7},{7,6},{8,9},{9,8},{10,11... | collective-permute-start | bytes 196616 | tf_op jit(solution)/shard_map/ppermute | solution.py:30
  19.2 0.1 collective-permute-start.4
  19.3 1.5 %inner.5 = (f32[512,128]{1,0:T(8,128)S(1)}, bf16[4,256,128]{2,1,0:T(8,128)(2,1)S(1)}) custom-call(bf16[512,128]{1,0:T(8,128)(2,1)S(1)} %get-tuple-element.72.latent_ref.refs_12_, bf16[256,128]{1,0:T(8,128)(2,1)S(1)} %get-tuple-element.73.send_0, bf16[256,128]{1,0:T(8,128)(2,1)S(1)} %get-tuple-element.74.send_1, ...), custom_call_target="tpu_custom_call" | custom-call | flops 1073741824 | bytes 3807232 | tf_op jit(solution)/shard_map/inner/pallas_call | solution.py:35
  20.9 1.4 %collective-permute-done.5.refs_1_ = bf16[256,128]{1,0:T(8,128)(2,1)S(1)} collective-permute-done((bf16[256,128]{1,0:T(8,128)(2,1)S(1)}, bf16[256,128]{1,0:T(8,128)(2,1)S(1)}, u32[]{:S(2)}, u32[]{:S(2)}) %collective-permute-start.5) | collective-permute-done | bytes 65568 | tf_op jit(solution)/shard_map/ppermute | solution.py:30
  22.3 1.3 %along_x.5.total_ref = f32[512,128]{1,0:T(8,128)S(1)} custom-call(f32[512,128]{1,0:T(8,128)S(1)} %get-tuple-element.77.total_ref, bf16[256,128]{1,0:T(8,128)(2,1)S(1)} %collective-permute-done.4.refs_0_, bf16[256,128]{1,0:T(8,128)(2,1)S(1)} %collective-permute-done.5.refs_1_, bf16[4,2,128,128]{3,2,1,0:T(8,128)(2,1)S(1)} %get-tuple-element.56.ends_w_ref.refs_2_, ...), custom_call_target="tpu_custom_call" | custom-call | flops 1073741824 | bytes 6952960 | tf_op jit(solution)/shard_map/along_x/pallas_call | solution.py:35
  23.6 0.2 collective-permute-done.6.refs_0_
  23.8 1.9 %along_y.5 = (bf16[512,128]{1,0:T(8,128)(2,1)S(1)}, bf16[256,128]{1,0:T(8,128)(2,1)S(1)}, bf16[256,128]{1,0:T(8,128)(2,1)S(1)}, bf16[256,128]{1,0:T(8,128)(2,1)S(1)}, bf16[256,128]{1,0:T(8,128)(2,1)S(1)}) custom-call(f32[512,128]{1,0:T(8,128)S(1)} %along_x.5.total_ref, bf16[256,128]{1,0:T(8,128)(2,1)S(1)} %collective-permute-done.6.refs_0_, ...), custom_call_target="tpu_custom_call" | custom-call | flops 1073741824 | bytes 8263680 | tf_op jit(solution)/shard_map/along_y/pallas_call | solution.py:35
  25.7 2.8 %collective-permute-start.11 = (bf16[256,128]{1,0:T(8,128)(2,1)S(1)}, bf16[256,128]{1,0:T(8,128)(2,1)S(1)}, u32[]{:S(2)}, u32[]{:S(2)}) collective-permute-start(bf16[256,128]{1,0:T(8,128)(2,1)S(1)} %get-tuple-element.86.send_0), channel_id=1, source_target_pairs={{1,2},{2,1},{3,0},{0,3},{5,6},{6,5},{7,4},{4,7},{9,10},{10,9},{11,... | collective-permute-start | bytes 196616 | tf_op jit(solution)/shard_map/ppermute | solution.py:30
  28.5 0.7 %collective-permute-start.9 = (bf16[256,128]{1,0:T(8,128)(2,1)S(1)}, bf16[256,128]{1,0:T(8,128)(2,1)S(1)}, u32[]{:S(2)}, u32[]{:S(2)}) collective-permute-start(bf16[256,128]{1,0:T(8,128)(2,1)S(1)} %get-tuple-element.87.send_1), channel_id=1, source_target_pairs={{4,8},{8,4},{12,16},{16,12},{20,24},{24,20},{28,0},{0,28},{5,9},{9... | collective-permute-start | bytes 196616 | tf_op jit(solution)/shard_map/ppermute | solution.py:30
  29.2 1.5 %inner.6 = (f32[512,128]{1,0:T(8,128)S(1)}, bf16[4,256,128]{2,1,0:T(8,128)(2,1)S(1)}) custom-call(bf16[512,128]{1,0:T(8,128)(2,1)S(1)} %get-tuple-element.85.latent_ref.refs_12_, bf16[256,128]{1,0:T(8,128)(2,1)S(1)} %get-tuple-element.86.send_0, bf16[256,128]{1,0:T(8,128)(2,1)S(1)} %get-tuple-element.87.send_1, ...), custom_call_target="tpu_custom_call" | custom-call | flops 1073741824 | bytes 3807232 | tf_op jit(solution)/shard_map/inner/pallas_call | solution.py:35
  30.8 2.4 %collective-permute-done.9.refs_1_ = bf16[256,128]{1,0:T(8,128)(2,1)S(1)} collective-permute-done((bf16[256,128]{1,0:T(8,128)(2,1)S(1)}, bf16[256,128]{1,0:T(8,128)(2,1)S(1)}, u32[]{:S(2)}, u32[]{:S(2)}) %collective-permute-start.9) | collective-permute-done | bytes 65568 | tf_op jit(solution)/shard_map/ppermute | solution.py:30
  33.1 1.5 %along_x.6.total_ref = f32[512,128]{1,0:T(8,128)S(1)} custom-call(f32[512,128]{1,0:T(8,128)S(1)} %get-tuple-element.90.total_ref, bf16[256,128]{1,0:T(8,128)(2,1)S(1)} %collective-permute-done.8.refs_0_, bf16[256,128]{1,0:T(8,128)(2,1)S(1)} %collective-permute-done.9.refs_1_, bf16[4,2,128,128]{3,2,1,0:T(8,128)(2,1)S(1)} %get-tuple-element.56.ends_w_ref.refs_2_, ...), custom_call_target="tpu_custom_call" | custom-call | flops 1073741824 | bytes 6952960 | tf_op jit(solution)/shard_map/along_x/pallas_call | solution.py:35
  34.6 1.9 %along_y.6 = (bf16[512,128]{1,0:T(8,128)(2,1)S(1)}, bf16[256,128]{1,0:T(8,128)(2,1)S(1)}, bf16[256,128]{1,0:T(8,128)(2,1)S(1)}, bf16[256,128]{1,0:T(8,128)(2,1)S(1)}, bf16[256,128]{1,0:T(8,128)(2,1)S(1)}) custom-call(f32[512,128]{1,0:T(8,128)S(1)} %along_x.6.total_ref, bf16[256,128]{1,0:T(8,128)(2,1)S(1)} %collective-permute-done.10.refs_0_, ...), custom_call_target="tpu_custom_call" | custom-call | flops 1073741824 | bytes 8263680 | tf_op jit(solution)/shard_map/along_y/pallas_call | solution.py:35
  36.6 1.5 %collective-permute-start.15 = (bf16[256,128]{1,0:T(8,128)(2,1)S(1)}, bf16[256,128]{1,0:T(8,128)(2,1)S(1)}, u32[]{:S(2)}, u32[]{:S(2)}) collective-permute-start(bf16[256,128]{1,0:T(8,128)(2,1)S(1)} %get-tuple-element.93.send_0), channel_id=1, source_target_pairs={{1,2},{2,1},{3,0},{0,3},{5,6},{6,5},{7,4},{4,7},{9,10},{10,9},{11,... | collective-permute-start | bytes 196616 | tf_op jit(solution)/shard_map/ppermute | solution.py:30
  38.1 0.6 %collective-permute-start.13 = (bf16[256,128]{1,0:T(8,128)(2,1)S(1)}, bf16[256,128]{1,0:T(8,128)(2,1)S(1)}, u32[]{:S(2)}, u32[]{:S(2)}) collective-permute-start(bf16[256,128]{1,0:T(8,128)(2,1)S(1)} %get-tuple-element.94.send_1), channel_id=1, source_target_pairs={{4,8},{8,4},{12,16},{16,12},{20,24},{24,20},{28,0},{0,28},{5,9},{9... | collective-permute-start | bytes 196616 | tf_op jit(solution)/shard_map/ppermute | solution.py:30
  38.7 1.5 %inner.7 = (f32[512,128]{1,0:T(8,128)S(1)}, bf16[4,256,128]{2,1,0:T(8,128)(2,1)S(1)}) custom-call(bf16[512,128]{1,0:T(8,128)(2,1)S(1)} %get-tuple-element.92.latent_ref.refs_12_, bf16[256,128]{1,0:T(8,128)(2,1)S(1)} %get-tuple-element.93.send_0, bf16[256,128]{1,0:T(8,128)(2,1)S(1)} %get-tuple-element.94.send_1, ...), custom_call_target="tpu_custom_call" | custom-call | flops 1073741824 | bytes 3807232 | tf_op jit(solution)/shard_map/inner/pallas_call | solution.py:35
  40.2 2.4 %collective-permute-done.13.refs_1_ = bf16[256,128]{1,0:T(8,128)(2,1)S(1)} collective-permute-done((bf16[256,128]{1,0:T(8,128)(2,1)S(1)}, bf16[256,128]{1,0:T(8,128)(2,1)S(1)}, u32[]{:S(2)}, u32[]{:S(2)}) %collective-permute-start.13) | collective-permute-done | bytes 65568 | tf_op jit(solution)/shard_map/ppermute | solution.py:30
  42.7 1.3 %along_x.7.total_ref = f32[512,128]{1,0:T(8,128)S(1)} custom-call(f32[512,128]{1,0:T(8,128)S(1)} %get-tuple-element.97.total_ref, bf16[256,128]{1,0:T(8,128)(2,1)S(1)} %collective-permute-done.12.refs_0_, bf16[256,128]{1,0:T(8,128)(2,1)S(1)} %collective-permute-done.13.refs_1_, bf16[4,2,128,128]{3,2,1,0:T(8,128)(2,1)S(1)} %get-tuple-element.56.ends_w_ref.refs_2_, ...), custom_call_target="tpu_custom_call" | custom-call | flops 1073741824 | bytes 6952960 | tf_op jit(solution)/shard_map/along_x/pallas_call | solution.py:35
  44.0 2.3 %along_y.7 = bf16[512,128]{1,0:T(8,128)(2,1)} custom-call(f32[512,128]{1,0:T(8,128)S(1)} %along_x.7.total_ref, bf16[256,128]{1,0:T(8,128)(2,1)S(1)} %collective-permute-done.14.refs_0_, bf16[256,128]{1,0:T(8,128)(2,1)S(1)} %collective-permute-done.15.refs_1_, bf16[4,2,128,128]{3,2,1,0:T(8,128)(2,1)S(1)} %get-tuple-element.56.ends_w_ref.refs_2_, ...), custom_call_target="tpu_custom_call" | custom-call | flops 1073741824 | bytes 7477248 | tf_op jit(solution)/shard_map/along_y/pallas_call | solution.py:35
  (46 shorter events, 0.1 us)
Async XLA Ops:
  0.0 9.1 %copy-start.15 = (s32[2,1]{0,1:T(1,128)S(1)}, s32[2,1]{0,1:T(1,128)}, u32[]{:S(2)}) copy-start(s32[2,1]{0,1:T(1,128)} %param.16) | copy-start | bytes 28
  0.0 9.1 %copy-start.11 = (s32[1,1,2,1024]{3,2,1,0:T(2,128)S(1)}, s32[1,1,2,1024]{3,2,1,0:T(2,128)}, u32[]{:S(2)}) copy-start(s32[1,1,2,1024]{3,2,1,0:T(2,128)} %param.15) | copy-start | bytes 24580
  0.0 9.1 %copy-start.10 = (s32[1,1,2,1024]{3,2,1,0:T(2,128)S(1)}, s32[1,1,2,1024]{3,2,1,0:T(2,128)}, u32[]{:S(2)}) copy-start(s32[1,1,2,1024]{3,2,1,0:T(2,128)} %param.14) | copy-start | bytes 24580
  0.0 9.1 %copy-start.14 = (s32[1,1,2,256]{3,2,1,0:T(2,128)S(1)}, s32[1,1,2,256]{3,2,1,0:T(2,128)}, u32[]{:S(2)}) copy-start(s32[1,1,2,256]{3,2,1,0:T(2,128)} %param.12) | copy-start | bytes 6148
  0.0 9.1 %copy-start.13 = (f32[4,3,128]{2,0,1:T(4,128)S(1)}, f32[4,3,128]{2,0,1:T(4,128)}, u32[]{:S(2)}) copy-start(f32[4,3,128]{2,0,1:T(4,128)} %param.19) | copy-start | bytes 18436
  0.0 9.1 %copy-start.5 = (bf16[4,3,128,128]{3,2,1,0:T(8,128)(2,1)S(1)}, bf16[4,3,128,128]{3,2,1,0:T(8,128)(2,1)}, u32[]{:S(2)}) copy-start(bf16[4,3,128,128]{3,2,1,0:T(8,128)(2,1)} %nodes_ref.1) | copy-start | bytes 1179652
  0.0 9.1 %copy-start.4 = (bf16[4,4,128,128]{3,2,1,0:T(8,128)(2,1)S(1)}, bf16[4,4,128,128]{3,2,1,0:T(8,128)(2,1)}, u32[]{:S(2)}) copy-start(bf16[4,4,128,128]{3,2,1,0:T(8,128)(2,1)} %weights_ref.1) | copy-start | bytes 1572868
  0.0 9.1 %copy-start.12 = (s32[1,1,4,512]{3,2,1,0:T(4,128)S(1)}, s32[1,1,4,512]{3,2,1,0:T(4,128)}, u32[]{:S(2)}) copy-start(s32[1,1,4,512]{3,2,1,0:T(4,128)} %param.11) | copy-start | bytes 24580
  2.3 8.7 %copy-start.2 = (bf16[1,1,512,128]{3,2,1,0:T(8,128)(2,1)S(1)}, bf16[1,1,512,128]{3,2,1,0:T(8,128)(2,1)}, u32[]{:S(2)}) copy-start(bf16[1,1,512,128]{3,2,1,0:T(8,128)(2,1)} %param.10) | copy-start | bytes 393220
  2.3 8.7 %copy-start.6 = (bf16[272,128]{1,0:T(8,128)(2,1)S(1)}, bf16[272,128]{1,0:T(8,128)(2,1)}, u32[]{:S(2)}) copy-start(bf16[272,128]{1,0:T(8,128)(2,1)} %get-tuple-element.54.send_2) | copy-start | bytes 208900
  2.3 8.7 %copy-start.7 = (bf16[272,128]{1,0:T(8,128)(2,1)S(1)}, bf16[272,128]{1,0:T(8,128)(2,1)}, u32[]{:S(2)}) copy-start(bf16[272,128]{1,0:T(8,128)(2,1)} %get-tuple-element.52.send_0) | copy-start | bytes 208900
  2.3 8.7 %copy-start.8 = (bf16[272,128]{1,0:T(8,128)(2,1)S(1)}, bf16[272,128]{1,0:T(8,128)(2,1)}, u32[]{:S(2)}) copy-start(bf16[272,128]{1,0:T(8,128)(2,1)} %get-tuple-element.55.send_3) | copy-start | bytes 208900
  2.3 8.7 %copy-start.9 = (bf16[272,128]{1,0:T(8,128)(2,1)S(1)}, bf16[272,128]{1,0:T(8,128)(2,1)}, u32[]{:S(2)}) copy-start(bf16[272,128]{1,0:T(8,128)(2,1)} %get-tuple-element.53.send_1) | copy-start | bytes 208900
  2.4 12.0 %collective-permute-start.3 = (bf16[272,128]{1,0:T(8,128)(2,1)}, bf16[272,128]{1,0:T(8,128)(2,1)S(1)}, u32[]{:S(2)}, u32[]{:S(2)}) collective-permute-start(bf16[272,128]{1,0:T(8,128)(2,1)} %get-tuple-element.52.send_0), channel_id=1, source_target_pairs={{1,2},{2,1},{3,0},{0,3},{5,6},{6,5},{7,4},{4,7},{9,10},{10,9},{11,... | collective-permute-start | bytes 208904 | tf_op jit(solution)/shard_map/ppermute | solution.py:30
  7.5 5.5 %collective-permute-start.1 = (bf16[272,128]{1,0:T(8,128)(2,1)}, bf16[272,128]{1,0:T(8,128)(2,1)S(1)}, u32[]{:S(2)}, u32[]{:S(2)}) collective-permute-start(bf16[272,128]{1,0:T(8,128)(2,1)} %get-tuple-element.53.send_1), channel_id=1, source_target_pairs={{4,8},{8,4},{12,16},{16,12},{20,24},{24,20},{28,0},{0,28},{5,9},{9... | collective-permute-start | bytes 208904 | tf_op jit(solution)/shard_map/ppermute | solution.py:30
  9.1 5.3 %collective-permute-start.2 = (bf16[272,128]{1,0:T(8,128)(2,1)}, bf16[272,128]{1,0:T(8,128)(2,1)S(1)}, u32[]{:S(2)}, u32[]{:S(2)}) collective-permute-start(bf16[272,128]{1,0:T(8,128)(2,1)} %get-tuple-element.54.send_2), channel_id=1, source_target_pairs={{0,1},{1,0},{2,3},{3,2},{4,5},{5,4},{6,7},{7,6},{8,9},{9,8},{10,11... | collective-permute-start | bytes 208904 | tf_op jit(solution)/shard_map/ppermute | solution.py:30
  9.1 3.9 %collective-permute-start = (bf16[272,128]{1,0:T(8,128)(2,1)}, bf16[272,128]{1,0:T(8,128)(2,1)S(1)}, u32[]{:S(2)}, u32[]{:S(2)}) collective-permute-start(bf16[272,128]{1,0:T(8,128)(2,1)} %get-tuple-element.55.send_3), channel_id=1, source_target_pairs={{0,4},{4,0},{8,12},{12,8},{16,20},{20,16},{24,28},{28,24},{1,5},{5... | collective-permute-start | bytes 208904 | tf_op jit(solution)/shard_map/ppermute | solution.py:30
  11.0 1.9 %copy-start.3 = (s32[1,1,2,256]{3,2,1,0:T(2,128)S(1)}, s32[1,1,2,256]{3,2,1,0:T(2,128)}, u32[]{:S(2)}) copy-start(s32[1,1,2,256]{3,2,1,0:T(2,128)} %param.13) | copy-start | bytes 6148
  13.0 1.4 %copy-start = (bf16[4,256,256]{2,1,0:T(8,128)(2,1)S(1)}, bf16[4,256,256]{2,1,0:T(8,128)(2,1)}, u32[]{:S(2)}) copy-start(bf16[4,256,256]{2,1,0:T(8,128)(2,1)} %get-tuple-element.70.refs_13_.refs_15_) | copy-start | bytes 1572868
  13.0 1.4 %copy-start.1 = (bf16[4,256,128]{2,1,0:T(8,128)(2,1)S(1)}, bf16[4,256,128]{2,1,0:T(8,128)(2,1)}, u32[]{:S(2)}) copy-start(bf16[4,256,128]{2,1,0:T(8,128)(2,1)} %get-tuple-element.71.refs_14_.refs_16_) | copy-start | bytes 786436
  16.4 7.2 %collective-permute-start.7 = (bf16[256,128]{1,0:T(8,128)(2,1)S(1)}, bf16[256,128]{1,0:T(8,128)(2,1)S(1)}, u32[]{:S(2)}, u32[]{:S(2)}) collective-permute-start(bf16[256,128]{1,0:T(8,128)(2,1)S(1)} %get-tuple-element.73.send_0), channel_id=1, source_target_pairs={{1,2},{2,1},{3,0},{0,3},{5,6},{6,5},{7,4},{4,7},{9,10},{10,9},{11,... | collective-permute-start | bytes 196616 | tf_op jit(solution)/shard_map/ppermute | solution.py:30
  17.1 5.2 %collective-permute-start.5 = (bf16[256,128]{1,0:T(8,128)(2,1)S(1)}, bf16[256,128]{1,0:T(8,128)(2,1)S(1)}, u32[]{:S(2)}, u32[]{:S(2)}) collective-permute-start(bf16[256,128]{1,0:T(8,128)(2,1)S(1)} %get-tuple-element.74.send_1), channel_id=1, source_target_pairs={{4,8},{8,4},{12,16},{16,12},{20,24},{24,20},{28,0},{0,28},{5,9},{9... | collective-permute-start | bytes 196616 | tf_op jit(solution)/shard_map/ppermute | solution.py:30
  17.7 6.0 %collective-permute-start.6 = (bf16[256,128]{1,0:T(8,128)(2,1)S(1)}, bf16[256,128]{1,0:T(8,128)(2,1)S(1)}, u32[]{:S(2)}, u32[]{:S(2)}) collective-permute-start(bf16[256,128]{1,0:T(8,128)(2,1)S(1)} %get-tuple-element.75.send_2), channel_id=1, source_target_pairs={{0,1},{1,0},{2,3},{3,2},{4,5},{5,4},{6,7},{7,6},{8,9},{9,8},{10,11... | collective-permute-start | bytes 196616 | tf_op jit(solution)/shard_map/ppermute | solution.py:30
  19.2 3.1 %collective-permute-start.4 = (bf16[256,128]{1,0:T(8,128)(2,1)S(1)}, bf16[256,128]{1,0:T(8,128)(2,1)S(1)}, u32[]{:S(2)}, u32[]{:S(2)}) collective-permute-start(bf16[256,128]{1,0:T(8,128)(2,1)S(1)} %get-tuple-element.76.send_3), channel_id=1, source_target_pairs={{0,4},{4,0},{8,12},{12,8},{16,20},{20,16},{24,28},{28,24},{1,5},{5... | collective-permute-start | bytes 196616 | tf_op jit(solution)/shard_map/ppermute | solution.py:30
  25.7 8.9 %collective-permute-start.11 = (bf16[256,128]{1,0:T(8,128)(2,1)S(1)}, bf16[256,128]{1,0:T(8,128)(2,1)S(1)}, u32[]{:S(2)}, u32[]{:S(2)}) collective-permute-start(bf16[256,128]{1,0:T(8,128)(2,1)S(1)} %get-tuple-element.86.send_0), channel_id=1, source_target_pairs={{1,2},{2,1},{3,0},{0,3},{5,6},{6,5},{7,4},{4,7},{9,10},{10,9},{11,... | collective-permute-start | bytes 196616 | tf_op jit(solution)/shard_map/ppermute | solution.py:30
  28.5 4.6 %collective-permute-start.9 = (bf16[256,128]{1,0:T(8,128)(2,1)S(1)}, bf16[256,128]{1,0:T(8,128)(2,1)S(1)}, u32[]{:S(2)}, u32[]{:S(2)}) collective-permute-start(bf16[256,128]{1,0:T(8,128)(2,1)S(1)} %get-tuple-element.87.send_1), channel_id=1, source_target_pairs={{4,8},{8,4},{12,16},{16,12},{20,24},{24,20},{28,0},{0,28},{5,9},{9... | collective-permute-start | bytes 196616 | tf_op jit(solution)/shard_map/ppermute | solution.py:30
  29.2 5.4 %collective-permute-start.10 = (bf16[256,128]{1,0:T(8,128)(2,1)S(1)}, bf16[256,128]{1,0:T(8,128)(2,1)S(1)}, u32[]{:S(2)}, u32[]{:S(2)}) collective-permute-start(bf16[256,128]{1,0:T(8,128)(2,1)S(1)} %get-tuple-element.88.send_2), channel_id=1, source_target_pairs={{0,1},{1,0},{2,3},{3,2},{4,5},{5,4},{6,7},{7,6},{8,9},{9,8},{10,11... | collective-permute-start | bytes 196616 | tf_op jit(solution)/shard_map/ppermute | solution.py:30
  29.2 3.9 %collective-permute-start.8 = (bf16[256,128]{1,0:T(8,128)(2,1)S(1)}, bf16[256,128]{1,0:T(8,128)(2,1)S(1)}, u32[]{:S(2)}, u32[]{:S(2)}) collective-permute-start(bf16[256,128]{1,0:T(8,128)(2,1)S(1)} %get-tuple-element.89.send_3), channel_id=1, source_target_pairs={{0,4},{4,0},{8,12},{12,8},{16,20},{20,16},{24,28},{28,24},{1,5},{5... | collective-permute-start | bytes 196616 | tf_op jit(solution)/shard_map/ppermute | solution.py:30
  36.6 7.4 %collective-permute-start.15 = (bf16[256,128]{1,0:T(8,128)(2,1)S(1)}, bf16[256,128]{1,0:T(8,128)(2,1)S(1)}, u32[]{:S(2)}, u32[]{:S(2)}) collective-permute-start(bf16[256,128]{1,0:T(8,128)(2,1)S(1)} %get-tuple-element.93.send_0), channel_id=1, source_target_pairs={{1,2},{2,1},{3,0},{0,3},{5,6},{6,5},{7,4},{4,7},{9,10},{10,9},{11,... | collective-permute-start | bytes 196616 | tf_op jit(solution)/shard_map/ppermute | solution.py:30
  38.1 4.6 %collective-permute-start.13 = (bf16[256,128]{1,0:T(8,128)(2,1)S(1)}, bf16[256,128]{1,0:T(8,128)(2,1)S(1)}, u32[]{:S(2)}, u32[]{:S(2)}) collective-permute-start(bf16[256,128]{1,0:T(8,128)(2,1)S(1)} %get-tuple-element.94.send_1), channel_id=1, source_target_pairs={{4,8},{8,4},{12,16},{16,12},{20,24},{24,20},{28,0},{0,28},{5,9},{9... | collective-permute-start | bytes 196616 | tf_op jit(solution)/shard_map/ppermute | solution.py:30
  38.7 5.3 %collective-permute-start.14 = (bf16[256,128]{1,0:T(8,128)(2,1)S(1)}, bf16[256,128]{1,0:T(8,128)(2,1)S(1)}, u32[]{:S(2)}, u32[]{:S(2)}) collective-permute-start(bf16[256,128]{1,0:T(8,128)(2,1)S(1)} %get-tuple-element.95.send_2), channel_id=1, source_target_pairs={{0,1},{1,0},{2,3},{3,2},{4,5},{5,4},{6,7},{7,6},{8,9},{9,8},{10,11... | collective-permute-start | bytes 196616 | tf_op jit(solution)/shard_map/ppermute | solution.py:30
  38.7 4.0 %collective-permute-start.12 = (bf16[256,128]{1,0:T(8,128)(2,1)S(1)}, bf16[256,128]{1,0:T(8,128)(2,1)S(1)}, u32[]{:S(2)}, u32[]{:S(2)}) collective-permute-start(bf16[256,128]{1,0:T(8,128)(2,1)S(1)} %get-tuple-element.96.send_3), channel_id=1, source_target_pairs={{0,4},{4,0},{8,12},{12,8},{16,20},{20,16},{24,28},{28,24},{1,5},{5... | collective-permute-start | bytes 196616 | tf_op jit(solution)/shard_map/ppermute | solution.py:30

commit v5 on v4

--- a/solution.py
+++ b/solution.py
@@ -15,6 +15,7 @@
 HBM = pl.BlockSpec(memory_space=pltpu.HBM)
 
 CUT = 128
+AHEAD = F32
 
 NEAR_X, FAR_X, NEAR_Y, FAR_Y = range(4)
 ORDER = (FAR_Y, FAR_X, NEAR_Y, NEAR_X)
@@ -204,8 +205,12 @@
 
 def inner_kernel(
     step, latent_ref, send_0, send_1, send_2, send_3, ends_w_ref, hidden_ref, biases_ref,
-    pick_ref, spread_ref, mask_ref, total_ref, table_ref,
+    pick_ref, spread_ref, mask_ref, *refs,
 ):
+    if step > 0:
+        own_gather_ref, lower_x_ref, lower_y_ref, total_ref, table_ref, ahead_ref = refs
+    else:
+        total_ref, table_ref = refs
     rows, width = latent_ref.shape
     half = rows // 2
     faces = table_ref.shape[1]
@@ -248,9 +253,15 @@
         ended = part if ended is None else ended + part
     total_ref[0:half, :] = total[0:half] + ended[:, :width]
     total_ref[half:, :] = total[half:] + ended[:, width:]
-
-
-def cross(step, d, upper, lower, ends_w_ref, hidden_ref, biases_ref, table_ref, groups):
+    if step > 0:
+        c0 = biases_ref[0, step : step + 1, :]
+        for d, lower_ref in enumerate((lower_x_ref, lower_y_ref)):
+            for i, gather in enumerate((own_gather_ref[d], lower_ref[...])):
+                link = 2 * d + i
+                ahead_ref[link] = (dot(gather[:, :faces], table_ref[link]) + c0).astype(ahead_ref.dtype)
+
+
+def cross(step, d, upper, lower, ends_w_ref, hidden_ref, biases_ref, table_ref, ahead_ref, groups):
     width = upper.shape[1]
     c0 = biases_ref[0, step : step + 1, :]
     c1 = biases_ref[1, step : step + 1, :]
@@ -261,8 +272,13 @@
     )
     first = []
     for i, (gather, _, _) in enumerate(groups):
-        table = jnp.concatenate([table_ref[2 * d + i], far[i]], axis=0)
-        first.append(half_silu(dot(gather, table) + c0).astype(BF))
+        if step > 0:
+            faces = far[i].shape[0]
+            y = dot(gather[:, faces:], far[i]) + ahead_ref[2 * d + i]
+        else:
+            table = jnp.concatenate([table_ref[2 * d + i], far[i]], axis=0)
+            y = dot(gather, table) + c0
+        first.append(half_silu(y).astype(BF))
     first = jnp.concatenate(first, axis=1)
     second = jnp.concatenate(
         [half_silu(dot(first[a : a + CUT], hidden_ref[step]) + c1).astype(BF)
@@ -288,6 +304,9 @@
 
 def along(step, d, refs, rows):
     near_ref, far_ref, ends_w_ref, hidden_ref, biases_ref, table_ref = refs[:6]
+    ahead_ref = None
+    if step > 0:
+        ahead_ref, refs = refs[6], refs[:6] + refs[7:]
     own = tuple(ref[d] for ref in refs[6:9])
     half = rows // 2
     faces = table_ref.shape[1]
@@ -302,9 +321,9 @@
         used = 12
     both = cross(
         step, d, upper[:faces], lower[:faces], ends_w_ref, hidden_ref, biases_ref, table_ref,
-        (own, tuple(ref[...] for ref in keep)),
-    )
-    return both, used
+        ahead_ref, (own, tuple(ref[...] for ref in keep)),
+    )
+    return both, used + (step > 0)
 
 
 def x_kernel(step, total_ref, *refs):
@@ -405,16 +424,18 @@
             inner, own = made[:3], made[3:6]
             ends_w, hidden, join, out_w, half_biases = made[6:]
             edge_net = (ends_w, hidden, half_biases)
-        total, table = call(
+        gathers = () if first else (own[0], kept_x[0], kept_y[0])
+        total, *tables = call(
             functools.partial(inner_kernel, step),
-            [like((rows, width), F32), like((4, faces, width), BF)],
-            (latent_now, *sends, *edge_net, *inner),
+            [like((rows, width), F32), like((4, faces, width), BF)]
+            + ([] if first else [like((4, slots, width), AHEAD)]),
+            (latent_now, *sends, *edge_net, *inner, *gathers),
             name="inner",
         )
         total, *made = call(
             functools.partial(x_kernel, step),
             [like((rows, width), F32)] + (group_like if first else []),
-            (total, got_near_x, got_far_x, *edge_net, table, *own,
+            (total, got_near_x, got_far_x, *edge_net, *tables, *own,
              *([bottoms] if first else kept_x)),
             name="along_x",
         )
@@ -423,7 +444,7 @@
             functools.partial(y_kernel, step, last),
             [like((rows, width), BF)] + ([] if last else [face] * 4)
             + (group_like if first else []),
-            (total, got_near_y, got_far_y, *edge_net, table, *own,
+            (total, got_near_y, got_far_y, *edge_net, *tables, *own,
              *([bottoms] if first else kept_y), latent_now, join, out_w,
              *([] if last else [pick, pick_mask])),
             name="along_y",

time: 46.4 us -> 45.4 us (0.978)
  waiting for transfers between devices: 6.79 us -> 4.9 us
  Pallas kernels: 23.7 us -> 24.5 us
    ppermute x16, waiting for transfers between devices: 6.79 us -> 4.9 us  [swapped(): return lax.ppermute(block, axis, route)]
    pallas_call x14, Pallas kernels: 23.7 us -> 24.5 us  [call(): pl.pallas_call(kernel, out_shape=outs, in_specs=in_specs or [VMEM] * len(...]
  transfers between devices with their start and end apart: 16 -> 16, of which waited for: 5 -> 5; matrix products, arithmetic and copies ran while one was open for 0% -> 0% of each run, Pallas kernels for 29% -> 32%
where the time goes in v5:
time: 45.4 us; the launch traced here: 45.2 us
  Pallas kernels  24.5 us (54%)
  starting transfers between devices  15.4 us (34%)
  waiting for transfers between devices  4.9 us (11%)
    pallas_call x14, Pallas kernels, call(): pl.pallas_call(kernel, out_shape=outs, in_specs=in_specs or [VMEM] * len(...  24.5 us
    ppermute x16, starting transfers between devices, swapped(): return lax.ppermute(block, axis, route)  15.4 us
    ppermute x16, waiting for transfers between devices, swapped(): return lax.ppermute(block, axis, route)  4.9 us
  transfers between devices with their start and end apart: 16, of which 5 were waited for; matrix products, arithmetic and copies ran while one was open for 0% of the time, Pallas kernels for 32%

profile of v5, /device:TPU:0, one launch (start us, length us, event | category | flops | bytes accessed | tf_op | source)
XLA Modules:
  0.0 45.2 jit_solution(1293555465952858572)
XLA Ops:
  0.0 2.2 %first.1 = (bf16[272,128]{1,0:T(8,128)(2,1)}, bf16[272,128]{1,0:T(8,128)(2,1)}, bf16[272,128]{1,0:T(8,128)(2,1)}, bf16[272,128]{1,0:T(8,128)(2,1)}, bf16[4,256,2...) custom-call(bf16[512,128]{1,0:T(8,128)(2,1)} %bitcast.9, s32[2,256]{1,0:T(2,128)} %bitcast.21, s32[2,256]{1,0:T(2,128)} %bitcast.12, ...), custom_call_target="tpu_custom_call" | custom-call | flops 1073741824 | bytes 151560 | tf_op jit(solution)/shard_map/first/pallas_call | solution.py:36
  2.3 0.0 copy-start.2
  2.4 5.1 %collective-permute-start.3 = (bf16[272,128]{1,0:T(8,128)(2,1)}, bf16[272,128]{1,0:T(8,128)(2,1)S(1)}, u32[]{:S(2)}, u32[]{:S(2)}) collective-permute-start(bf16[272,128]{1,0:T(8,128)(2,1)} %get-tuple-element.55.send_0), channel_id=1, source_target_pairs={{1,2},{2,1},{3,0},{0,3},{5,6},{6,5},{7,4},{4,7},{9,10},{10,9},{11,... | collective-permute-start | bytes 208904 | tf_op jit(solution)/shard_map/ppermute | solution.py:31
  7.5 1.6 %collective-permute-start.1 = (bf16[272,128]{1,0:T(8,128)(2,1)}, bf16[272,128]{1,0:T(8,128)(2,1)S(1)}, u32[]{:S(2)}, u32[]{:S(2)}) collective-permute-start(bf16[272,128]{1,0:T(8,128)(2,1)} %get-tuple-element.56.send_1), channel_id=1, source_target_pairs={{4,8},{8,4},{12,16},{16,12},{20,24},{24,20},{28,0},{0,28},{5,9},{9... | collective-permute-start | bytes 208904 | tf_op jit(solution)/shard_map/ppermute | solution.py:31
  9.2 1.9 %setup.1 = (bf16[2048,256]{1,0:T(8,128)(2,1)S(1)}, bf16[256,2048]{1,0:T(8,128)(2,1)S(1)}, bf16[2048,128]{1,0:T(8,128)(2,1)S(1)}, bf16[2,1024,512]{2,1,0:T(8,128)...) custom-call(s32[2,256]{1,0:T(2,128)S(1)} %bitcast.22, ...), custom_call_target="tpu_custom_call" | custom-call | flops 1073741824 | bytes 950280 | tf_op jit(solution)/shard_map/setup/pallas_call | solution.py:36
  11.0 0.0 copy-start.3
  11.1 1.6 %inner.4 = (f32[512,128]{1,0:T(8,128)S(1)}, bf16[4,256,128]{2,1,0:T(8,128)(2,1)S(1)}) custom-call(bf16[512,128]{1,0:T(8,128)(2,1)S(1)} %bitcast.10, bf16[272,128]{1,0:T(8,128)(2,1)S(1)} %copy-done.7, bf16[272,128]{1,0:T(8,128)(2,1)S(1)} %copy-done.9, bf16[272,128]{1,0:T(8,128)(2,1)S(1)} %copy-done.6, bf16[272,128]{1,0:T(8,128)(2,1)S(1)} %copy-done.8, ...), custom_call_target="tpu_custom_call" | custom-call | flops 1073741824 | bytes 3823616 | tf_op jit(solution)/shard_map/inner/pallas_call | solution.py:36
  12.7 0.3 collective-permute-done.1.refs_1_
  13.0 1.4 %along_x.4 = (f32[512,128]{1,0:T(8,128)S(1)}, bf16[1024,512]{1,0:T(8,128)(2,1)S(1)}, bf16[256,1024]{1,0:T(8,128)(2,1)S(1)}, bf16[1024,128]{1,0:T(8,128)(2,1)S(1)}) custom-call(f32[512,128]{1,0:T(8,128)S(1)} %get-tuple-element.65.total_ref, bf16[272,128]{1,0:T(8,128)(2,1)S(1)} %collective-permute-done.refs_0_, ...), custom_call_target="tpu_custom_call" | custom-call | flops 1073741824 | bytes 5128192 | tf_op jit(solution)/shard_map/along_x/pallas_call | solution.py:36
  14.4 2.0 %along_y.4 = (bf16[512,128]{1,0:T(8,128)(2,1)S(1)}, bf16[256,128]{1,0:T(8,128)(2,1)S(1)}, bf16[256,128]{1,0:T(8,128)(2,1)S(1)}, bf16[256,128]{1,0:T(8,128)(2,1)S...) custom-call(f32[512,128]{1,0:T(8,128)S(1)} %get-tuple-element.70.tot, ...), custom_call_target="tpu_custom_call" | custom-call | flops 1073741824 | bytes 6438912 | tf_op jit(solution)/shard_map/along_y/pallas_call | solution.py:36
  16.4 0.7 %collective-permute-start.7 = (bf16[256,128]{1,0:T(8,128)(2,1)S(1)}, bf16[256,128]{1,0:T(8,128)(2,1)S(1)}, u32[]{:S(2)}, u32[]{:S(2)}) collective-permute-start(bf16[256,128]{1,0:T(8,128)(2,1)S(1)} %get-tuple-element.76.send_0), channel_id=1, source_target_pairs={{1,2},{2,1},{3,0},{0,3},{5,6},{6,5},{7,4},{4,7},{9,10},{10,9},{11,... | collective-permute-start | bytes 196616 | tf_op jit(solution)/shard_map/ppermute | solution.py:31
  17.1 0.7 %collective-permute-start.5 = (bf16[256,128]{1,0:T(8,128)(2,1)S(1)}, bf16[256,128]{1,0:T(8,128)(2,1)S(1)}, u32[]{:S(2)}, u32[]{:S(2)}) collective-permute-start(bf16[256,128]{1,0:T(8,128)(2,1)S(1)} %get-tuple-element.77.send_1), channel_id=1, source_target_pairs={{4,8},{8,4},{12,16},{16,12},{20,24},{24,20},{28,0},{0,28},{5,9},{9... | collective-permute-start | bytes 196616 | tf_op jit(solution)/shard_map/ppermute | solution.py:31
  17.7 1.5 %collective-permute-start.6 = (bf16[256,128]{1,0:T(8,128)(2,1)S(1)}, bf16[256,128]{1,0:T(8,128)(2,1)S(1)}, u32[]{:S(2)}, u32[]{:S(2)}) collective-permute-start(bf16[256,128]{1,0:T(8,128)(2,1)S(1)} %get-tuple-element.78.send_2), channel_id=1, source_target_pairs={{0,1},{1,0},{2,3},{3,2},{4,5},{5,4},{6,7},{7,6},{8,9},{9,8},{10,11... | collective-permute-start | bytes 196616 | tf_op jit(solution)/shard_map/ppermute | solution.py:31
  19.2 0.1 collective-permute-start.4
  19.3 2.1 %inner.5 = (f32[512,128]{1,0:T(8,128)S(1)}, bf16[4,256,128]{2,1,0:T(8,128)(2,1)S(1)}, f32[4,1024,128]{2,1,0:T(8,128)S(1)}) custom-call(bf16[512,128]{1,0:T(8,128)(2,1)S(1)} %get-tuple-element.75.latent_ref.refs_13_, bf16[256,128]{1,0:T(8,128)(2,1)S(1)} %get-tuple-element.76.send_0, bf16[256,128]{1,0:T(8,128)(2,1)S(1)} %get-tuple-element.77.send_1, ...), custom_call_target="tpu_custom_call" | custom-call | flops 1073741824 | bytes 8001536 | tf_op jit(solution)/shard_map/inner/pallas_call | solution.py:36
  21.4 0.9 %collective-permute-done.5.refs_1_ = bf16[256,128]{1,0:T(8,128)(2,1)S(1)} collective-permute-done((bf16[256,128]{1,0:T(8,128)(2,1)S(1)}, bf16[256,128]{1,0:T(8,128)(2,1)S(1)}, u32[]{:S(2)}, u32[]{:S(2)}) %collective-permute-start.5) | collective-permute-done | bytes 65568 | tf_op jit(solution)/shard_map/ppermute | solution.py:31
  22.3 1.1 %along_x.5.total_ref = f32[512,128]{1,0:T(8,128)S(1)} custom-call(f32[512,128]{1,0:T(8,128)S(1)} %get-tuple-element.82.total_ref, bf16[256,128]{1,0:T(8,128)(2,1)S(1)} %collective-permute-done.4.refs_0_, bf16[256,128]{1,0:T(8,128)(2,1)S(1)} %collective-permute-done.5.refs_1_, bf16[4,2,128,128]{3,2,1,0:T(8,128)(2,1)S(1)} %get-tuple-element.59.ends_w_ref.refs_2_, ...), custom_call_target="tpu_custom_call" | custom-call | flops 1073741824 | bytes 9050112 | tf_op jit(solution)/shard_map/along_x/pallas_call | solution.py:36
  23.4 0.4 collective-permute-done.6.refs_0_
  23.8 1.7 %along_y.5 = (bf16[512,128]{1,0:T(8,128)(2,1)S(1)}, bf16[256,128]{1,0:T(8,128)(2,1)S(1)}, bf16[256,128]{1,0:T(8,128)(2,1)S(1)}, bf16[256,128]{1,0:T(8,128)(2,1)S(1)}, bf16[256,128]{1,0:T(8,128)(2,1)S(1)}) custom-call(f32[512,128]{1,0:T(8,128)S(1)} %along_x.5.total_ref, bf16[256,128]{1,0:T(8,128)(2,1)S(1)} %collective-permute-done.6.refs_0_, ...), custom_call_target="tpu_custom_call" | custom-call | flops 1073741824 | bytes 10360832 | tf_op jit(solution)/shard_map/along_y/pallas_call | solution.py:36
  25.5 2.7 %collective-permute-start.11 = (bf16[256,128]{1,0:T(8,128)(2,1)S(1)}, bf16[256,128]{1,0:T(8,128)(2,1)S(1)}, u32[]{:S(2)}, u32[]{:S(2)}) collective-permute-start(bf16[256,128]{1,0:T(8,128)(2,1)S(1)} %get-tuple-element.90.send_0), channel_id=1, source_target_pairs={{1,2},{2,1},{3,0},{0,3},{5,6},{6,5},{7,4},{4,7},{9,10},{10,9},{11,... | collective-permute-start | bytes 196616 | tf_op jit(solution)/shard_map/ppermute | solution.py:31
  28.2 0.6 %collective-permute-start.9 = (bf16[256,128]{1,0:T(8,128)(2,1)S(1)}, bf16[256,128]{1,0:T(8,128)(2,1)S(1)}, u32[]{:S(2)}, u32[]{:S(2)}) collective-permute-start(bf16[256,128]{1,0:T(8,128)(2,1)S(1)} %get-tuple-element.91.send_1), channel_id=1, source_target_pairs={{4,8},{8,4},{12,16},{16,12},{20,24},{24,20},{28,0},{0,28},{5,9},{9... | collective-permute-start | bytes 196616 | tf_op jit(solution)/shard_map/ppermute | solution.py:31
  28.9 2.3 %inner.6 = (f32[512,128]{1,0:T(8,128)S(1)}, bf16[4,256,128]{2,1,0:T(8,128)(2,1)S(1)}, f32[4,1024,128]{2,1,0:T(8,128)S(1)}) custom-call(bf16[512,128]{1,0:T(8,128)(2,1)S(1)} %get-tuple-element.89.latent_ref.refs_13_, bf16[256,128]{1,0:T(8,128)(2,1)S(1)} %get-tuple-element.90.send_0, bf16[256,128]{1,0:T(8,128)(2,1)S(1)} %get-tuple-element.91.send_1, ...), custom_call_target="tpu_custom_call" | custom-call | flops 1073741824 | bytes 8001536 | tf_op jit(solution)/shard_map/inner/pallas_call | solution.py:36
  31.2 1.6 %collective-permute-done.9.refs_1_ = bf16[256,128]{1,0:T(8,128)(2,1)S(1)} collective-permute-done((bf16[256,128]{1,0:T(8,128)(2,1)S(1)}, bf16[256,128]{1,0:T(8,128)(2,1)S(1)}, u32[]{:S(2)}, u32[]{:S(2)}) %collective-permute-start.9) | collective-permute-done | bytes 65568 | tf_op jit(solution)/shard_map/ppermute | solution.py:31
  32.8 1.1 %along_x.6.total_ref = f32[512,128]{1,0:T(8,128)S(1)} custom-call(f32[512,128]{1,0:T(8,128)S(1)} %get-tuple-element.94.total_ref, bf16[256,128]{1,0:T(8,128)(2,1)S(1)} %collective-permute-done.8.refs_0_, bf16[256,128]{1,0:T(8,128)(2,1)S(1)} %collective-permute-done.9.refs_1_, bf16[4,2,128,128]{3,2,1,0:T(8,128)(2,1)S(1)} %get-tuple-element.59.ends_w_ref.refs_2_, ...), custom_call_target="tpu_custom_call" | custom-call | flops 1073741824 | bytes 9050112 | tf_op jit(solution)/shard_map/along_x/pallas_call | solution.py:36
  34.0 1.7 %along_y.6 = (bf16[512,128]{1,0:T(8,128)(2,1)S(1)}, bf16[256,128]{1,0:T(8,128)(2,1)S(1)}, bf16[256,128]{1,0:T(8,128)(2,1)S(1)}, bf16[256,128]{1,0:T(8,128)(2,1)S(1)}, bf16[256,128]{1,0:T(8,128)(2,1)S(1)}) custom-call(f32[512,128]{1,0:T(8,128)S(1)} %along_x.6.total_ref, bf16[256,128]{1,0:T(8,128)(2,1)S(1)} %collective-permute-done.10.refs_0_, ...), custom_call_target="tpu_custom_call" | custom-call | flops 1073741824 | bytes 10360832 | tf_op jit(solution)/shard_map/along_y/pallas_call | solution.py:36
  35.7 1.7 %collective-permute-start.15 = (bf16[256,128]{1,0:T(8,128)(2,1)S(1)}, bf16[256,128]{1,0:T(8,128)(2,1)S(1)}, u32[]{:S(2)}, u32[]{:S(2)}) collective-permute-start(bf16[256,128]{1,0:T(8,128)(2,1)S(1)} %get-tuple-element.98.send_0), channel_id=1, source_target_pairs={{1,2},{2,1},{3,0},{0,3},{5,6},{6,5},{7,4},{4,7},{9,10},{10,9},{11,... | collective-permute-start | bytes 196616 | tf_op jit(solution)/shard_map/ppermute | solution.py:31
  37.4 0.6 %collective-permute-start.13 = (bf16[256,128]{1,0:T(8,128)(2,1)S(1)}, bf16[256,128]{1,0:T(8,128)(2,1)S(1)}, u32[]{:S(2)}, u32[]{:S(2)}) collective-permute-start(bf16[256,128]{1,0:T(8,128)(2,1)S(1)} %get-tuple-element.99.send_1), channel_id=1, source_target_pairs={{4,8},{8,4},{12,16},{16,12},{20,24},{24,20},{28,0},{0,28},{5,9},{9... | collective-permute-start | bytes 196616 | tf_op jit(solution)/shard_map/ppermute | solution.py:31
  38.0 0.2 collective-permute-start.12
  38.2 2.1 %inner.7 = (f32[512,128]{1,0:T(8,128)S(1)}, bf16[4,256,128]{2,1,0:T(8,128)(2,1)S(1)}, f32[4,1024,128]{2,1,0:T(8,128)S(1)}) custom-call(bf16[512,128]{1,0:T(8,128)(2,1)S(1)} %get-tuple-element.97.latent_ref.refs_13_, bf16[256,128]{1,0:T(8,128)(2,1)S(1)} %get-tuple-element.98.send_0, bf16[256,128]{1,0:T(8,128)(2,1)S(1)} %get-tuple-element.99.send_1, ...), custom_call_target="tpu_custom_call" | custom-call | flops 1073741824 | bytes 8001536 | tf_op jit(solution)/shard_map/inner/pallas_call | solution.py:36
  40.3 1.7 %collective-permute-done.13.refs_1_ = bf16[256,128]{1,0:T(8,128)(2,1)S(1)} collective-permute-done((bf16[256,128]{1,0:T(8,128)(2,1)S(1)}, bf16[256,128]{1,0:T(8,128)(2,1)S(1)}, u32[]{:S(2)}, u32[]{:S(2)}) %collective-permute-start.13) | collective-permute-done | bytes 65568 | tf_op jit(solution)/shard_map/ppermute | solution.py:31
  42.0 1.1 %along_x.7.total_ref = f32[512,128]{1,0:T(8,128)S(1)} custom-call(f32[512,128]{1,0:T(8,128)S(1)} %get-tuple-element.102.total_ref, bf16[256,128]{1,0:T(8,128)(2,1)S(1)} %collective-permute-done.12.refs_0_, bf16[256,128]{1,0:T(8,128)(2,1)S(1)} %collective-permute-done.13.refs_1_, bf16[4,2,128,128]{3,2,1,0:T(8,128)(2,1)S(1)} %get-tuple-element.59.ends_w_ref.refs_2_, ...), custom_call_target="tpu_custom_call" | custom-call | flops 1073741824 | bytes 9050112 | tf_op jit(solution)/shard_map/along_x/pallas_call | solution.py:36
  43.1 2.1 %along_y.7 = bf16[512,128]{1,0:T(8,128)(2,1)} custom-call(f32[512,128]{1,0:T(8,128)S(1)} %along_x.7.total_ref, bf16[256,128]{1,0:T(8,128)(2,1)S(1)} %collective-permute-done.14.refs_0_, bf16[256,128]{1,0:T(8,128)(2,1)S(1)} %collective-permute-done.15.refs_1_, bf16[4,2,128,128]{3,2,1,0:T(8,128)(2,1)S(1)} %get-tuple-element.59.ends_w_ref.refs_2_, ...), custom_call_target="tpu_custom_call" | custom-call | flops 1073741824 | bytes 9574400 | tf_op jit(solution)/shard_map/along_y/pallas_call | solution.py:36
  (46 shorter events, 0.1 us)
Async XLA Ops:
  0.0 9.1 %copy-start.15 = (s32[2,1]{0,1:T(1,128)S(1)}, s32[2,1]{0,1:T(1,128)}, u32[]{:S(2)}) copy-start(s32[2,1]{0,1:T(1,128)} %param.16) | copy-start | bytes 28
  0.0 9.1 %copy-start.11 = (s32[1,1,2,1024]{3,2,1,0:T(2,128)S(1)}, s32[1,1,2,1024]{3,2,1,0:T(2,128)}, u32[]{:S(2)}) copy-start(s32[1,1,2,1024]{3,2,1,0:T(2,128)} %param.15) | copy-start | bytes 24580
  0.0 9.1 %copy-start.10 = (s32[1,1,2,1024]{3,2,1,0:T(2,128)S(1)}, s32[1,1,2,1024]{3,2,1,0:T(2,128)}, u32[]{:S(2)}) copy-start(s32[1,1,2,1024]{3,2,1,0:T(2,128)} %param.14) | copy-start | bytes 24580
  0.0 9.1 %copy-start.14 = (s32[1,1,2,256]{3,2,1,0:T(2,128)S(1)}, s32[1,1,2,256]{3,2,1,0:T(2,128)}, u32[]{:S(2)}) copy-start(s32[1,1,2,256]{3,2,1,0:T(2,128)} %param.12) | copy-start | bytes 6148
  0.0 9.1 %copy-start.13 = (f32[4,3,128]{2,0,1:T(4,128)S(1)}, f32[4,3,128]{2,0,1:T(4,128)}, u32[]{:S(2)}) copy-start(f32[4,3,128]{2,0,1:T(4,128)} %param.19) | copy-start | bytes 18436
  0.0 9.1 %copy-start.5 = (bf16[4,3,128,128]{3,2,1,0:T(8,128)(2,1)S(1)}, bf16[4,3,128,128]{3,2,1,0:T(8,128)(2,1)}, u32[]{:S(2)}) copy-start(bf16[4,3,128,128]{3,2,1,0:T(8,128)(2,1)} %nodes_ref.1) | copy-start | bytes 1179652
  0.0 9.1 %copy-start.4 = (bf16[4,4,128,128]{3,2,1,0:T(8,128)(2,1)S(1)}, bf16[4,4,128,128]{3,2,1,0:T(8,128)(2,1)}, u32[]{:S(2)}) copy-start(bf16[4,4,128,128]{3,2,1,0:T(8,128)(2,1)} %weights_ref.1) | copy-start | bytes 1572868
  0.0 9.1 %copy-start.12 = (s32[1,1,4,512]{3,2,1,0:T(4,128)S(1)}, s32[1,1,4,512]{3,2,1,0:T(4,128)}, u32[]{:S(2)}) copy-start(s32[1,1,4,512]{3,2,1,0:T(4,128)} %param.11) | copy-start | bytes 24580
  2.3 8.7 %copy-start.2 = (bf16[1,1,512,128]{3,2,1,0:T(8,128)(2,1)S(1)}, bf16[1,1,512,128]{3,2,1,0:T(8,128)(2,1)}, u32[]{:S(2)}) copy-start(bf16[1,1,512,128]{3,2,1,0:T(8,128)(2,1)} %param.10) | copy-start | bytes 393220
  2.3 8.7 %copy-start.6 = (bf16[272,128]{1,0:T(8,128)(2,1)S(1)}, bf16[272,128]{1,0:T(8,128)(2,1)}, u32[]{:S(2)}) copy-start(bf16[272,128]{1,0:T(8,128)(2,1)} %get-tuple-element.57.send_2) | copy-start | bytes 208900
  2.3 8.7 %copy-start.7 = (bf16[272,128]{1,0:T(8,128)(2,1)S(1)}, bf16[272,128]{1,0:T(8,128)(2,1)}, u32[]{:S(2)}) copy-start(bf16[272,128]{1,0:T(8,128)(2,1)} %get-tuple-element.55.send_0) | copy-start | bytes 208900
  2.3 8.7 %copy-start.8 = (bf16[272,128]{1,0:T(8,128)(2,1)S(1)}, bf16[272,128]{1,0:T(8,128)(2,1)}, u32[]{:S(2)}) copy-start(bf16[272,128]{1,0:T(8,128)(2,1)} %get-tuple-element.58.send_3) | copy-start | bytes 208900
  2.3 8.7 %copy-start.9 = (bf16[272,128]{1,0:T(8,128)(2,1)S(1)}, bf16[272,128]{1,0:T(8,128)(2,1)}, u32[]{:S(2)}) copy-start(bf16[272,128]{1,0:T(8,128)(2,1)} %get-tuple-element.56.send_1) | copy-start | bytes 208900
  2.4 12.1 %collective-permute-start.3 = (bf16[272,128]{1,0:T(8,128)(2,1)}, bf16[272,128]{1,0:T(8,128)(2,1)S(1)}, u32[]{:S(2)}, u32[]{:S(2)}) collective-permute-start(bf16[272,128]{1,0:T(8,128)(2,1)} %get-tuple-element.55.send_0), channel_id=1, source_target_pairs={{1,2},{2,1},{3,0},{0,3},{5,6},{6,5},{7,4},{4,7},{9,10},{10,9},{11,... | collective-permute-start | bytes 208904 | tf_op jit(solution)/shard_map/ppermute | solution.py:31
  7.5 5.5 %collective-permute-start.1 = (bf16[272,128]{1,0:T(8,128)(2,1)}, bf16[272,128]{1,0:T(8,128)(2,1)S(1)}, u32[]{:S(2)}, u32[]{:S(2)}) collective-permute-start(bf16[272,128]{1,0:T(8,128)(2,1)} %get-tuple-element.56.send_1), channel_id=1, source_target_pairs={{4,8},{8,4},{12,16},{16,12},{20,24},{24,20},{28,0},{0,28},{5,9},{9... | collective-permute-start | bytes 208904 | tf_op jit(solution)/shard_map/ppermute | solution.py:31
  9.1 5.3 %collective-permute-start.2 = (bf16[272,128]{1,0:T(8,128)(2,1)}, bf16[272,128]{1,0:T(8,128)(2,1)S(1)}, u32[]{:S(2)}, u32[]{:S(2)}) collective-permute-start(bf16[272,128]{1,0:T(8,128)(2,1)} %get-tuple-element.57.send_2), channel_id=1, source_target_pairs={{0,1},{1,0},{2,3},{3,2},{4,5},{5,4},{6,7},{7,6},{8,9},{9,8},{10,11... | collective-permute-start | bytes 208904 | tf_op jit(solution)/shard_map/ppermute | solution.py:31
  9.1 3.9 %collective-permute-start = (bf16[272,128]{1,0:T(8,128)(2,1)}, bf16[272,128]{1,0:T(8,128)(2,1)S(1)}, u32[]{:S(2)}, u32[]{:S(2)}) collective-permute-start(bf16[272,128]{1,0:T(8,128)(2,1)} %get-tuple-element.58.send_3), channel_id=1, source_target_pairs={{0,4},{4,0},{8,12},{12,8},{16,20},{20,16},{24,28},{28,24},{1,5},{5... | collective-permute-start | bytes 208904 | tf_op jit(solution)/shard_map/ppermute | solution.py:31
  11.0 1.9 %copy-start.3 = (s32[1,1,2,256]{3,2,1,0:T(2,128)S(1)}, s32[1,1,2,256]{3,2,1,0:T(2,128)}, u32[]{:S(2)}) copy-start(s32[1,1,2,256]{3,2,1,0:T(2,128)} %param.13) | copy-start | bytes 6148
  13.0 1.5 %copy-start = (bf16[4,256,256]{2,1,0:T(8,128)(2,1)S(1)}, bf16[4,256,256]{2,1,0:T(8,128)(2,1)}, u32[]{:S(2)}) copy-start(bf16[4,256,256]{2,1,0:T(8,128)(2,1)} %get-tuple-element.73.refs_13_.refs_16_) | copy-start | bytes 1572868
  13.0 1.5 %copy-start.1 = (bf16[4,256,128]{2,1,0:T(8,128)(2,1)S(1)}, bf16[4,256,128]{2,1,0:T(8,128)(2,1)}, u32[]{:S(2)}) copy-start(bf16[4,256,128]{2,1,0:T(8,128)(2,1)} %get-tuple-element.74.refs_14_.refs_17_) | copy-start | bytes 786436
  16.4 7.0 %collective-permute-start.7 = (bf16[256,128]{1,0:T(8,128)(2,1)S(1)}, bf16[256,128]{1,0:T(8,128)(2,1)S(1)}, u32[]{:S(2)}, u32[]{:S(2)}) collective-permute-start(bf16[256,128]{1,0:T(8,128)(2,1)S(1)} %get-tuple-element.76.send_0), channel_id=1, source_target_pairs={{1,2},{2,1},{3,0},{0,3},{5,6},{6,5},{7,4},{4,7},{9,10},{10,9},{11,... | collective-permute-start | bytes 196616 | tf_op jit(solution)/shard_map/ppermute | solution.py:31
  17.1 5.2 %collective-permute-start.5 = (bf16[256,128]{1,0:T(8,128)(2,1)S(1)}, bf16[256,128]{1,0:T(8,128)(2,1)S(1)}, u32[]{:S(2)}, u32[]{:S(2)}) collective-permute-start(bf16[256,128]{1,0:T(8,128)(2,1)S(1)} %get-tuple-element.77.send_1), channel_id=1, source_target_pairs={{4,8},{8,4},{12,16},{16,12},{20,24},{24,20},{28,0},{0,28},{5,9},{9... | collective-permute-start | bytes 196616 | tf_op jit(solution)/shard_map/ppermute | solution.py:31
  17.7 6.0 %collective-permute-start.6 = (bf16[256,128]{1,0:T(8,128)(2,1)S(1)}, bf16[256,128]{1,0:T(8,128)(2,1)S(1)}, u32[]{:S(2)}, u32[]{:S(2)}) collective-permute-start(bf16[256,128]{1,0:T(8,128)(2,1)S(1)} %get-tuple-element.78.send_2), channel_id=1, source_target_pairs={{0,1},{1,0},{2,3},{3,2},{4,5},{5,4},{6,7},{7,6},{8,9},{9,8},{10,11... | collective-permute-start | bytes 196616 | tf_op jit(solution)/shard_map/ppermute | solution.py:31
  19.2 3.1 %collective-permute-start.4 = (bf16[256,128]{1,0:T(8,128)(2,1)S(1)}, bf16[256,128]{1,0:T(8,128)(2,1)S(1)}, u32[]{:S(2)}, u32[]{:S(2)}) collective-permute-start(bf16[256,128]{1,0:T(8,128)(2,1)S(1)} %get-tuple-element.79.send_3), channel_id=1, source_target_pairs={{0,4},{4,0},{8,12},{12,8},{16,20},{20,16},{24,28},{28,24},{1,5},{5... | collective-permute-start | bytes 196616 | tf_op jit(solution)/shard_map/ppermute | solution.py:31
  25.5 8.4 %collective-permute-start.11 = (bf16[256,128]{1,0:T(8,128)(2,1)S(1)}, bf16[256,128]{1,0:T(8,128)(2,1)S(1)}, u32[]{:S(2)}, u32[]{:S(2)}) collective-permute-start(bf16[256,128]{1,0:T(8,128)(2,1)S(1)} %get-tuple-element.90.send_0), channel_id=1, source_target_pairs={{1,2},{2,1},{3,0},{0,3},{5,6},{6,5},{7,4},{4,7},{9,10},{10,9},{11,... | collective-permute-start | bytes 196616 | tf_op jit(solution)/shard_map/ppermute | solution.py:31
  28.2 4.6 %collective-permute-start.9 = (bf16[256,128]{1,0:T(8,128)(2,1)S(1)}, bf16[256,128]{1,0:T(8,128)(2,1)S(1)}, u32[]{:S(2)}, u32[]{:S(2)}) collective-permute-start(bf16[256,128]{1,0:T(8,128)(2,1)S(1)} %get-tuple-element.91.send_1), channel_id=1, source_target_pairs={{4,8},{8,4},{12,16},{16,12},{20,24},{24,20},{28,0},{0,28},{5,9},{9... | collective-permute-start | bytes 196616 | tf_op jit(solution)/shard_map/ppermute | solution.py:31
  28.9 5.1 %collective-permute-start.10 = (bf16[256,128]{1,0:T(8,128)(2,1)S(1)}, bf16[256,128]{1,0:T(8,128)(2,1)S(1)}, u32[]{:S(2)}, u32[]{:S(2)}) collective-permute-start(bf16[256,128]{1,0:T(8,128)(2,1)S(1)} %get-tuple-element.92.send_2), channel_id=1, source_target_pairs={{0,1},{1,0},{2,3},{3,2},{4,5},{5,4},{6,7},{7,6},{8,9},{9,8},{10,11... | collective-permute-start | bytes 196616 | tf_op jit(solution)/shard_map/ppermute | solution.py:31
  28.9 3.9 %collective-permute-start.8 = (bf16[256,128]{1,0:T(8,128)(2,1)S(1)}, bf16[256,128]{1,0:T(8,128)(2,1)S(1)}, u32[]{:S(2)}, u32[]{:S(2)}) collective-permute-start(bf16[256,128]{1,0:T(8,128)(2,1)S(1)} %get-tuple-element.93.send_3), channel_id=1, source_target_pairs={{0,4},{4,0},{8,12},{12,8},{16,20},{20,16},{24,28},{28,24},{1,5},{5... | collective-permute-start | bytes 196616 | tf_op jit(solution)/shard_map/ppermute | solution.py:31
  35.7 7.4 %collective-permute-start.15 = (bf16[256,128]{1,0:T(8,128)(2,1)S(1)}, bf16[256,128]{1,0:T(8,128)(2,1)S(1)}, u32[]{:S(2)}, u32[]{:S(2)}) collective-permute-start(bf16[256,128]{1,0:T(8,128)(2,1)S(1)} %get-tuple-element.98.send_0), channel_id=1, source_target_pairs={{1,2},{2,1},{3,0},{0,3},{5,6},{6,5},{7,4},{4,7},{9,10},{10,9},{11,... | collective-permute-start | bytes 196616 | tf_op jit(solution)/shard_map/ppermute | solution.py:31
  37.4 4.6 %collective-permute-start.13 = (bf16[256,128]{1,0:T(8,128)(2,1)S(1)}, bf16[256,128]{1,0:T(8,128)(2,1)S(1)}, u32[]{:S(2)}, u32[]{:S(2)}) collective-permute-start(bf16[256,128]{1,0:T(8,128)(2,1)S(1)} %get-tuple-element.99.send_1), channel_id=1, source_target_pairs={{4,8},{8,4},{12,16},{16,12},{20,24},{24,20},{28,0},{0,28},{5,9},{9... | collective-permute-start | bytes 196616 | tf_op jit(solution)/shard_map/ppermute | solution.py:31
  38.0 5.1 %collective-permute-start.14 = (bf16[256,128]{1,0:T(8,128)(2,1)S(1)}, bf16[256,128]{1,0:T(8,128)(2,1)S(1)}, u32[]{:S(2)}, u32[]{:S(2)}) collective-permute-start(bf16[256,128]{1,0:T(8,128)(2,1)S(1)} %get-tuple-element.100.send_2), channel_id=1, source_target_pairs={{0,1},{1,0},{2,3},{3,2},{4,5},{5,4},{6,7},{7,6},{8,9},{9,8},{10,11... | collective-permute-start | bytes 196616 | tf_op jit(solution)/shard_map/ppermute | solution.py:31
  38.0 4.0 %collective-permute-start.12 = (bf16[256,128]{1,0:T(8,128)(2,1)S(1)}, bf16[256,128]{1,0:T(8,128)(2,1)S(1)}, u32[]{:S(2)}, u32[]{:S(2)}) collective-permute-start(bf16[256,128]{1,0:T(8,128)(2,1)S(1)} %get-tuple-element.101.send_3), channel_id=1, source_target_pairs={{0,4},{4,0},{8,12},{12,8},{16,20},{20,16},{24,28},{28,24},{1,5},{5... | collective-permute-start | bytes 196616 | tf_op jit(solution)/shard_map/ppermute | solution.py:31

commit v6 on v4

--- a/solution.py
+++ b/solution.py
@@ -11,13 +11,13 @@
 F32 = jnp.float32
 I32 = jnp.int32
 VMEM = pl.BlockSpec(memory_space=pltpu.VMEM)
-SMEM = pl.BlockSpec(memory_space=pltpu.SMEM)
 HBM = pl.BlockSpec(memory_space=pltpu.HBM)
 
 CUT = 128
 
 NEAR_X, FAR_X, NEAR_Y, FAR_Y = range(4)
 ORDER = (FAR_Y, FAR_X, NEAR_Y, NEAR_X)
+VISITS = ((NEAR_X, FAR_Y), (FAR_X, NEAR_Y))
 PLACE = tuple(ORDER.index(link) for link in range(4))
 
 
@@ -85,6 +85,10 @@
     return lax.axis_index("gx") % 2, lax.axis_index("gy") % 2
 
 
+def role_of(link):
+    return (odd_place()[link // 2] + link % 2) % 2
+
+
 def in_order(odd, first, second):
     turned = odd == 1
     return jnp.where(turned, second, first), jnp.where(turned, first, second)
@@ -104,7 +108,7 @@
 
 def first_kernel(
     latent_hbm, tops_hbm, bottoms_hbm, etop_hbm, ebot_hbm, live_hbm,
-    send_0, send_1, send_2, send_3, pick_ref, pick_mask_ref,
+    send_0, send_1, send_2, send_3, pick_ref, pick_mask_ref, ends_ref,
     latent_ref, tops_ref, bottoms_ref, etop_ref, ebot_ref, live_ref, sems,
 ):
     moves = [
@@ -138,6 +142,7 @@
         ebot = jnp.where(live, ebot_ref[d : d + 1, :], -1).astype(F32)
         rows = [v[:, i * width : (i + 1) * width] for v in (etop, ebot) for i in range(lines)]
         ends = jnp.concatenate(rows, axis=0).astype(BF)
+        ends_ref[d] = ends
         sends[PLACE[2 * d]][faces:, :] = ends
         sends[PLACE[2 * d + 1]][faces:, :] = ends
 
@@ -153,32 +158,92 @@
     return row(0), row(lines)
 
 
-def group(mine, theirs, face, live, sign, half, width):
-    faces = face.shape[1]
-    here = column_one_hot(mine, faces)
-    gather = jnp.concatenate([here, column_one_hot(theirs, faces)], axis=0).T
+def link_group(link, got_ref, ends_ref, tops_ref, bottoms_ref, half):
+    d = link // 2
+    owned = role_of(link) == 0
+    faces = tops_ref.shape[1]
+    width = got_ref.shape[1]
+    etop, ebot = unpacked(jnp.where(owned, ends_ref[d], got_ref[faces:, :]))
+    face = jnp.where(owned, tops_ref[d : d + 1, :], bottoms_ref[d : d + 1, :])
+    here = column_one_hot(jnp.where(owned, etop, ebot), faces)
+    there = column_one_hot(jnp.where(owned, ebot, etop), faces)
     bit, low = cut(face, half)
     lines = jnp.concatenate([low, bit, jnp.zeros((6, faces), I32)], axis=0)
-    ends = dot(lines.astype(F32).astype(BF), here).astype(I32)
-    low, bit = ends[0:1, :], ends[1:2, :]
-    ones = column_one_hot(jnp.where(live, low, -1), half)
-    return gather, ones if sign > 0 else -ones, column_mask(bit, width)
+    rows = dot(lines.astype(F32).astype(BF), here).astype(I32)
+    low, bit = rows[0:1, :], rows[1:2, :]
+    ones = column_one_hot(jnp.where(ebot >= 0, low, -1), half)
+    gather = jnp.concatenate([here, there], axis=0).T
+    return gather, jnp.where(owned, ones, -ones), column_mask(bit, width)
+
+
+def link_first(step, link, got_ref, gather, ends_w_ref, biases_ref, table_ref, ahead_ref):
+    role = role_of(link)
+    faces = table_ref.shape[1]
+    far = dot(got_ref[0:faces, :], ends_w_ref[step, 1 - role]).astype(BF)
+    if step > 0:
+        y = dot(gather[:, faces:], far) + ahead_ref[link]
+    else:
+        table = jnp.concatenate([table_ref[link], far], axis=0)
+        y = dot(gather, table) + biases_ref[0, step : step + 1, :]
+    return half_silu(y).astype(BF)
+
+
+def second_layer(first, weight, bias):
+    parts = [
+        half_silu(dot(first[a : a + CUT], weight) + bias).astype(BF)
+        for a in range(0, first.shape[0], CUT)
+    ]
+    return jnp.concatenate(parts, axis=0)
+
+
+def placed(places, values):
+    parts = []
+    for a in range(0, places[0].shape[0], CUT):
+        part = None
+        for place, value in zip(places, values):
+            product = dot(place[a : a + CUT], value)
+            part = product if part is None else part + product
+        parts.append(part)
+    return jnp.concatenate(parts, axis=0)
+
+
+def link_sums(step, links, gots, groups, ends_w_ref, hidden_ref, biases_ref, table_ref, ahead_ref):
+    width = ends_w_ref.shape[2]
+    wide = width * len(links)
+    first = [
+        link_first(step, link, got, group[0], ends_w_ref, biases_ref, table_ref, ahead_ref)
+        for link, got, group in zip(links, gots, groups)
+    ]
+    bias = biases_ref[1, step : step + 1, :]
+    second = second_layer(
+        jnp.concatenate(first, axis=1),
+        hidden_ref[step, 0:wide, 0:wide],
+        jnp.concatenate([bias] * len(links), axis=1),
+    )
+    values = [
+        by_half(second[:, i * width : (i + 1) * width], group[2]) for i, group in enumerate(groups)
+    ]
+    return placed([group[1] for group in groups], values)
+
+
+def prepared(step, links, got_refs, refs, half):
+    count = 3 * len(links)
+    if step > 0:
+        kept, rest = refs[:count], refs[count:]
+    else:
+        kept, rest = refs[-count:], refs[3:-count]
+        for i, (link, got_ref) in enumerate(zip(links, got_refs)):
+            for ref, value in zip(kept[3 * i :], link_group(link, got_ref, *refs[:3], half)):
+                ref[...] = value
+    return [tuple(ref[...] for ref in kept[i : i + 3]) for i in range(0, count, 3)], rest
 
 
 def setup_kernel(
-    tops_ref, etop_ref, ebot_ref, live_ref, nbr_ref, weights_ref, nodes_ref, raw_biases_ref,
-    pick_ref, spread_ref, mask_ref, gather_ref, sum_ref, half_ref,
-    ends_w_ref, hidden_ref, join_ref, out_w_ref, biases_ref,
+    nbr_ref, weights_ref, nodes_ref, raw_biases_ref,
+    pick_ref, spread_ref, mask_ref, ends_w_ref, hidden_ref, join_ref, out_w_ref, biases_ref,
 ):
     half = spread_ref.shape[0]
     width = mask_ref.shape[1]
-    slots = etop_ref.shape[1]
-    for d in range(2):
-        live = lax.broadcasted_iota(I32, (1, slots), 1) < live_ref[0, d]
-        gather_ref[d], sum_ref[d], half_ref[d] = group(
-            etop_ref[d : d + 1, :], ebot_ref[d : d + 1, :], tops_ref[d : d + 1, :],
-            live, 1, half, width,
-        )
     rows = nbr_ref.shape[1]
     for k in range(nbr_ref.shape[0]):
         here = slice(k * rows, (k + 1) * rows)
@@ -204,17 +269,19 @@
 
 def inner_kernel(
     step, latent_ref, send_0, send_1, send_2, send_3, ends_w_ref, hidden_ref, biases_ref,
-    pick_ref, spread_ref, mask_ref, total_ref, table_ref,
+    pick_ref, spread_ref, mask_ref, *refs,
 ):
     rows, width = latent_ref.shape
     half = rows // 2
+    sends = (send_0, send_1, send_2, send_3)
+    if step > 0:
+        gather_refs, (total_ref, table_ref, ahead_ref) = refs[:4], refs[4:]
+    else:
+        total_ref, table_ref = refs
     faces = table_ref.shape[1]
-    sends = (send_0, send_1, send_2, send_3)
-    for d, odd in enumerate(odd_place()):
-        near, far = (sends[PLACE[2 * d + i]][0:faces, :] for i in range(2))
-        top, bottom = in_order(odd, near, far)
-        table_ref[2 * d] = dot(top, ends_w_ref[step, 0]).astype(BF)
-        table_ref[2 * d + 1] = dot(bottom, ends_w_ref[step, 1]).astype(BF)
+    for link in range(4):
+        face = sends[PLACE[link]][0:faces, :]
+        table_ref[link] = dot(face, ends_w_ref[step, role_of(link)]).astype(BF)
     latent = latent_ref[...]
     source = dot(latent, ends_w_ref[step, 0]) + biases_ref[0, step : step + 1, :]
     table = halves(dot(latent, ends_w_ref[step, 1]).astype(BF))
@@ -248,80 +315,34 @@
         ended = part if ended is None else ended + part
     total_ref[0:half, :] = total[0:half] + ended[:, :width]
     total_ref[half:, :] = total[half:] + ended[:, width:]
-
-
-def cross(step, d, upper, lower, ends_w_ref, hidden_ref, biases_ref, table_ref, groups):
-    width = upper.shape[1]
-    c0 = biases_ref[0, step : step + 1, :]
-    c1 = biases_ref[1, step : step + 1, :]
-    c1 = jnp.concatenate([c1, c1], axis=1)
-    far = (
-        dot(upper, ends_w_ref[step, 1]).astype(BF),
-        dot(lower, ends_w_ref[step, 0]).astype(BF),
-    )
-    first = []
-    for i, (gather, _, _) in enumerate(groups):
-        table = jnp.concatenate([table_ref[2 * d + i], far[i]], axis=0)
-        first.append(half_silu(dot(gather, table) + c0).astype(BF))
-    first = jnp.concatenate(first, axis=1)
-    second = jnp.concatenate(
-        [half_silu(dot(first[a : a + CUT], hidden_ref[step]) + c1).astype(BF)
-         for a in range(0, first.shape[0], CUT)],
-        axis=0,
-    )
-    values = [
-        by_half(second[:, i * width : (i + 1) * width], mask)
-        for i, (_, _, mask) in enumerate(groups)
-    ]
-    total = jnp.concatenate(
-        [dot(groups[0][1][a : a + CUT], values[0]) + dot(groups[1][1][a : a + CUT], values[1])
-         for a in range(0, groups[0][1].shape[0], CUT)],
-        axis=0,
-    )
-    return total
-
-
-def lower_group(ends, bottoms_ref, d, half):
-    etop, ebot = unpacked(ends)
-    return group(ebot, etop, bottoms_ref[d : d + 1, :], ebot >= 0, -1, half, ends.shape[1])
-
-
-def along(step, d, refs, rows):
-    near_ref, far_ref, ends_w_ref, hidden_ref, biases_ref, table_ref = refs[:6]
-    own = tuple(ref[d] for ref in refs[6:9])
-    half = rows // 2
-    faces = table_ref.shape[1]
-    upper, lower = in_order(odd_place()[d], near_ref[...], far_ref[...])
-    if step == 0:
-        bottoms_ref, keep = refs[9], refs[-3:]
-        for ref, value in zip(keep, lower_group(lower[faces:], bottoms_ref, d, half)):
-            ref[...] = value
-        used = 10
-    else:
-        keep = refs[9:12]
-        used = 12
-    both = cross(
-        step, d, upper[:faces], lower[:faces], ends_w_ref, hidden_ref, biases_ref, table_ref,
-        (own, tuple(ref[...] for ref in keep)),
-    )
-    return both, used
-
-
-def x_kernel(step, total_ref, *refs):
+    if step > 0:
+        c0 = biases_ref[0, step : step + 1, :]
+        for link, ref in enumerate(gather_refs):
+            ahead_ref[link] = dot(ref[:, 0:faces], table_ref[link]) + c0
+
+
+def cross_kernel(step, links, total_ref, *refs):
     rows, width = total_ref.shape
     half = rows // 2
-    both, used = along(step, 0, refs, rows)
-    out_ref = refs[used]
+    gots, refs = refs[: len(links)], refs[len(links) :]
+    nets, refs = refs[: 4 + (step > 0)], refs[4 + (step > 0) :]
+    groups, (out_ref,) = prepared(step, links, gots, refs, half)
+    ahead_ref = nets[4] if step > 0 else None
+    both = link_sums(step, links, gots, groups, *nets[:4], ahead_ref)
     out_ref[0:half, :] = total_ref[0:half, :] + both[:, :width]
     out_ref[half:, :] = total_ref[half:, :] + both[:, width:]
 
 
-def y_kernel(step, last, total_ref, *refs):
+def last_kernel(step, links, last, total_ref, *refs):
     rows, width = total_ref.shape
-    both, used = along(step, 1, refs, rows)
-    biases_ref = refs[4]
-    latent_ref, join_ref, out_w_ref = refs[used : used + 3]
-    rest = refs[used + 3 :]
+    half = rows // 2
+    gots, refs = refs[: len(links)], refs[len(links) :]
+    nets, refs = refs[: 4 + (step > 0)], refs[4 + (step > 0) :]
+    (latent_ref, join_ref, out_w_ref), refs = refs[:3], refs[3:]
+    groups, rest = prepared(step, links, gots, refs, half)
+    ahead_ref = nets[4] if step > 0 else None
+    biases_ref = nets[2]
+    both = link_sums(step, links, gots, groups, *nets[:4], ahead_ref)
     arrived = total_ref[...] + jnp.concatenate([both[:, :width], both[:, width:]], axis=0)
     latent = latent_ref[...]
     joined = jnp.concatenate([latent, arrived.astype(BF)], axis=1)
@@ -365,9 +386,10 @@
     face = like((faces, width), BF)
     lines = 2 * (slots // width)
     packed = like((faces + lines, width), BF)
-    *sends, pick, pick_mask = call(
+    *sends, pick, pick_mask, ends = call(
         first_kernel,
-        [packed] * 4 + [like((4, faces, half), BF), like((4, faces, width), BF)],
+        [packed] * 4
+        + [like((4, faces, half), BF), like((4, faces, width), BF), like((2, lines, width), BF)],
         (latent_now, tops, bottoms, etop, ebot, live),
         in_specs=[HBM] * 6,
         scratch=[
@@ -381,55 +403,60 @@
     group_like = [
         like((slots, 2 * faces), BF), like((half, slots), BF), like((slots, width), BF)
     ]
-    kept_x = kept_y = None
+    groups = {}
     for step in range(steps):
-        first, last = step == 0, step == steps - 1
+        starting, last = step == 0, step == steps - 1
         near_x, far_x, near_y, far_y = (sends[place] for place in PLACE)
-        got_far_y = swapped(far_y, "gy", 1)
-        got_near_y = swapped(near_y, "gy", 0)
-        got_far_x = swapped(far_x, "gx", 1)
-        got_near_x = swapped(near_x, "gx", 0)
-        if first:
+        got = {
+            FAR_Y: swapped(far_y, "gy", 1),
+            FAR_X: swapped(far_x, "gx", 1),
+            NEAR_Y: swapped(near_y, "gy", 0),
+            NEAR_X: swapped(near_x, "gx", 0),
+        }
+        if starting:
             made = call(
                 setup_kernel,
                 [like((fanout * rows, half), BF), like((half, fanout * rows), BF),
-                 like((fanout * rows, width), BF)]
-                + [like((2,) + g.shape, BF) for g in group_like]
-                + [like((steps, 2, width, width), BF), like((steps, 2 * width, 2 * width), BF),
-                   like((steps, 2 * width, width), BF), like((steps, width, width), BF),
-                   like(bias_rows.shape, F32)],
-                (tops, etop, ebot, live, nbr, edge_weights, node_weights, bias_rows),
-                in_specs=[VMEM] * 3 + [SMEM] + [VMEM] * 4,
+                 like((fanout * rows, width), BF),
+                 like((steps, 2, width, width), BF), like((steps, 2 * width, 2 * width), BF),
+                 like((steps, 2 * width, width), BF), like((steps, width, width), BF),
+                 like(bias_rows.shape, F32)],
+                (nbr, edge_weights, node_weights, bias_rows),
                 name="setup",
             )
-            inner, own = made[:3], made[3:6]
-            ends_w, hidden, join, out_w, half_biases = made[6:]
+            inner, (ends_w, hidden, join, out_w, half_biases) = made[:3], made[3:]
             edge_net = (ends_w, hidden, half_biases)
-        total, table = call(
+        gathers = () if starting else tuple(groups[link][0] for link in range(4))
+        total, *tables = call(
             functools.partial(inner_kernel, step),
-            [like((rows, width), F32), like((4, faces, width), BF)],
-            (latent_now, *sends, *edge_net, *inner),
+            [like((rows, width), F32), like((4, faces, width), BF)]
+            + ([] if starting else [like((4, slots, width), F32)]),
+            (latent_now, *sends, *edge_net, *inner, *gathers),
             name="inner",
         )
-        total, *made = call(
-            functools.partial(x_kernel, step),
-            [like((rows, width), F32)] + (group_like if first else []),
-            (total, got_near_x, got_far_x, *edge_net, table, *own,
-             *([bottoms] if first else kept_x)),
-            name="along_x",
-        )
-        kept_x = made if first else kept_x
-        latent_now, *made = call(
-            functools.partial(y_kernel, step, last),
-            [like((rows, width), BF)] + ([] if last else [face] * 4)
-            + (group_like if first else []),
-            (total, got_near_y, got_far_y, *edge_net, table, *own,
-             *([bottoms] if first else kept_y), latent_now, join, out_w,
-             *([] if last else [pick, pick_mask])),
-            name="along_y",
-        )
-        sends, made = made[:4], made[4:]
-        kept_y = made if first else kept_y
+        for links in VISITS:
+            final = links == VISITS[-1]
+            kernel = functools.partial(cross_kernel, step, links)
+            outs = [like((rows, width), F32)]
+            operands = [total, *(got[link] for link in links), *edge_net, *tables]
+            if final:
+                kernel = functools.partial(last_kernel, step, links, last)
+                outs = [like((rows, width), BF)] + ([] if last else [face] * 4)
+                operands += [latent_now, join, out_w]
+            plain = len(outs)
+            if starting:
+                outs += group_like * len(links)
+                operands += [ends, tops, bottoms]
+            else:
+                operands += [part for link in links for part in groups[link]]
+            if final and not last:
+                operands += [pick, pick_mask]
+            total, *made = call(kernel, outs, operands, name="update" if final else "cross")
+            if starting:
+                for k, link in enumerate(links):
+                    groups[link] = made[plain - 1 + 3 * k :][:3]
+            if final:
+                latent_now, sends = total, made[: plain - 1]
     return latent_now[None, None]
 
 

time: 46.4 us -> 44.4 us (0.957)
  waiting for transfers between devices: 6.79 us -> 3.09 us
  starting transfers between devices: 15.3 us -> 17.3 us
    ppermute x16, waiting for transfers between devices: 6.79 us -> 3.09 us  [swapped(): return lax.ppermute(block, axis, route)]
    ppermute x16, starting transfers between devices: 15.3 us -> 17.3 us  [swapped(): return lax.ppermute(block, axis, route)]
  transfers between devices with their start and end apart: 16 -> 16, of which waited for: 5 -> 6; matrix products, arithmetic and copies ran while one was open for 0% -> 0% of each run, Pallas kernels for 29% -> 31%
where the time goes in v6:
time: 44.4 us; the launch traced here: 44.2 us
  Pallas kernels  23.4 us (53%)
  starting transfers between devices  17.3 us (39%)
  waiting for transfers between devices  3.09 us (7%)
    pallas_call x14, Pallas kernels, call(): pl.pallas_call(kernel, out_shape=outs, in_specs=in_specs or [VMEM] * len(...  23.4 us
    ppermute x16, starting transfers between devices, swapped(): return lax.ppermute(block, axis, route)  17.3 us
    ppermute x16, waiting for transfers between devices, swapped(): return lax.ppermute(block, axis, route)  3.09 us
  transfers between devices with their start and end apart: 16, of which 6 were waited for; matrix products, arithmetic and copies ran while one was open for 0% of the time, Pallas kernels for 31%

profile of v6, /device:TPU:0, one launch (start us, length us, event | category | flops | bytes accessed | tf_op | source)
XLA Modules:
  0.0 44.2 jit_solution(18101582332255418611)
XLA Ops:
  0.0 2.2 %first.1 = (bf16[272,128]{1,0:T(8,128)(2,1)}, bf16[272,128]{1,0:T(8,128)(2,1)}, bf16[272,128]{1,0:T(8,128)(2,1)}, bf16[272,128]{1,0:T(8,128)(2,1)}, bf16[4,256,2...) custom-call(bf16[512,128]{1,0:T(8,128)(2,1)} %bitcast.9, s32[2,256]{1,0:T(2,128)} %bitcast.14, ...), custom_call_target="tpu_custom_call" | custom-call | flops 1073741824 | bytes 151560 | tf_op jit(solution)/shard_map/first/pallas_call | solution.py:35
  2.3 5.1 %collective-permute-start.1 = (bf16[272,128]{1,0:T(8,128)(2,1)}, bf16[272,128]{1,0:T(8,128)(2,1)S(1)}, u32[]{:S(2)}, u32[]{:S(2)}) collective-permute-start(bf16[272,128]{1,0:T(8,128)(2,1)} %get-tuple-element.59.send_0), channel_id=1, source_target_pairs={{1,2},{2,1},{3,0},{0,3},{5,6},{6,5},{7,4},{4,7},{9,10},{10,9},{11,... | collective-permute-start | bytes 208904 | tf_op jit(solution)/shard_map/ppermute | solution.py:30
  7.4 1.6 %collective-permute-start.2 = (bf16[272,128]{1,0:T(8,128)(2,1)}, bf16[272,128]{1,0:T(8,128)(2,1)S(1)}, u32[]{:S(2)}, u32[]{:S(2)}) collective-permute-start(bf16[272,128]{1,0:T(8,128)(2,1)} %get-tuple-element.60.send_1), channel_id=1, source_target_pairs={{4,8},{8,4},{12,16},{16,12},{20,24},{24,20},{28,0},{0,28},{5,9},{9... | collective-permute-start | bytes 208904 | tf_op jit(solution)/shard_map/ppermute | solution.py:30
  9.1 0.5 %setup.1 = (bf16[2048,256]{1,0:T(8,128)(2,1)S(1)}, bf16[256,2048]{1,0:T(8,128)(2,1)S(1)}, bf16[2048,128]{1,0:T(8,128)(2,1)S(1)}, bf16[4,2,128,128]{3,2,1,0:T(8,1...) custom-call(s32[4,512]{1,0:T(4,128)S(1)} %bitcast.12, ...), custom_call_target="tpu_custom_call" | custom-call | flops 1073741824 | bytes 931840 | tf_op jit(solution)/shard_map/setup/pallas_call | solution.py:35
  9.7 1.6 %inner.4 = (f32[512,128]{1,0:T(8,128)S(1)}, bf16[4,256,128]{2,1,0:T(8,128)(2,1)S(1)}) custom-call(bf16[512,128]{1,0:T(8,128)(2,1)S(1)} %bitcast.10, bf16[272,128]{1,0:T(8,128)(2,1)S(1)} %copy-done.8, bf16[272,128]{1,0:T(8,128)(2,1)S(1)} %copy-done.6, bf16[272,128]{1,0:T(8,128)(2,1)S(1)} %copy-done.5, bf16[272,128]{1,0:T(8,128)(2,1)S(1)} %copy-done.7, ...), custom_call_target="tpu_custom_call" | custom-call | flops 1073741824 | bytes 3823616 | tf_op jit(solution)/shard_map/inner/pallas_call | solution.py:35
  11.4 1.4 %cross.4 = (f32[512,128]{1,0:T(8,128)S(1)}, bf16[1024,512]{1,0:T(8,128)(2,1)S(1)}, bf16[256,1024]{1,0:T(8,128)(2,1)S(1)}, bf16[1024,128]{1,0:T(8,128)(2,1)S(1)},...) custom-call(f32[512,128]{1,0:T(8,128)S(1)} %get-tuple-element.69.total_ref, ...), custom_call_target="tpu_custom_call" | custom-call | flops 1073741824 | bytes 1468416 | tf_op jit(solution)/shard_map/cross/pallas_call | solution.py:35
  12.8 0.1 collective-permute-done.2.refs_0_
  12.9 0.6 %collective-permute-done.3.refs_1_ = bf16[272,128]{1,0:T(8,128)(2,1)S(1)} collective-permute-done((bf16[272,128]{1,0:T(8,128)(2,1)}, bf16[272,128]{1,0:T(8,128)(2,1)S(1)}, u32[]{:S(2)}, u32[]{:S(2)}) %collective-permute-start.3) | collective-permute-done | bytes 69664 | tf_op jit(solution)/shard_map/ppermute | solution.py:30
  13.6 2.1 %update.4 = (bf16[512,128]{1,0:T(8,128)(2,1)S(1)}, bf16[256,128]{1,0:T(8,128)(2,1)S(1)}, bf16[256,128]{1,0:T(8,128)(2,1)S(1)}, bf16[256,128]{1,0:T(8,128)(2,1)S(...) custom-call(f32[512,128]{1,0:T(8,128)S(1)} %get-tuple-element.72.tot, ...), custom_call_target="tpu_custom_call" | custom-call | flops 1073741824 | bytes 2779136 | tf_op jit(solution)/shard_map/update/pallas_call | solution.py:35
  15.7 1.8 %collective-permute-start.5 = (bf16[256,128]{1,0:T(8,128)(2,1)S(1)}, bf16[256,128]{1,0:T(8,128)(2,1)S(1)}, u32[]{:S(2)}, u32[]{:S(2)}) collective-permute-start(bf16[256,128]{1,0:T(8,128)(2,1)S(1)} %get-tuple-element.78.send_0), channel_id=1, source_target_pairs={{1,2},{2,1},{3,0},{0,3},{5,6},{6,5},{7,4},{4,7},{9,10},{10,9},{11,... | collective-permute-start | bytes 196616 | tf_op jit(solution)/shard_map/ppermute | solution.py:30
  17.5 0.5 %collective-permute-start.6 = (bf16[256,128]{1,0:T(8,128)(2,1)S(1)}, bf16[256,128]{1,0:T(8,128)(2,1)S(1)}, u32[]{:S(2)}, u32[]{:S(2)}) collective-permute-start(bf16[256,128]{1,0:T(8,128)(2,1)S(1)} %get-tuple-element.79.send_1), channel_id=1, source_target_pairs={{4,8},{8,4},{12,16},{16,12},{20,24},{24,20},{28,0},{0,28},{5,9},{9... | collective-permute-start | bytes 196616 | tf_op jit(solution)/shard_map/ppermute | solution.py:30
  18.0 0.1 collective-permute-start.7
  18.1 1.0 %collective-permute-start.4 = (bf16[256,128]{1,0:T(8,128)(2,1)S(1)}, bf16[256,128]{1,0:T(8,128)(2,1)S(1)}, u32[]{:S(2)}, u32[]{:S(2)}) collective-permute-start(bf16[256,128]{1,0:T(8,128)(2,1)S(1)} %get-tuple-element.81.send_3), channel_id=1, source_target_pairs={{0,4},{4,0},{8,12},{12,8},{16,20},{20,16},{24,28},{28,24},{1,5},{5... | collective-permute-start | bytes 196616 | tf_op jit(solution)/shard_map/ppermute | solution.py:30
  19.1 2.1 %inner.5 = (f32[512,128]{1,0:T(8,128)S(1)}, bf16[4,256,128]{2,1,0:T(8,128)(2,1)S(1)}, f32[4,1024,128]{2,1,0:T(8,128)S(1)}) custom-call(bf16[512,128]{1,0:T(8,128)(2,1)S(1)} %get-tuple-element.77.latent_ref.refs_7_, bf16[256,128]{1,0:T(8,128)(2,1)S(1)} %get-tuple-element.78.send_0, bf16[256,128]{1,0:T(8,128)(2,1)S(1)} %get-tuple-element.79.send_1, ...), custom_call_target="tpu_custom_call" | custom-call | flops 1073741824 | bytes 8001536 | tf_op jit(solution)/shard_map/inner/pallas_call | solution.py:35
  21.2 0.7 %collective-permute-done.5.refs_1_ = bf16[256,128]{1,0:T(8,128)(2,1)S(1)} collective-permute-done((bf16[256,128]{1,0:T(8,128)(2,1)S(1)}, bf16[256,128]{1,0:T(8,128)(2,1)S(1)}, u32[]{:S(2)}, u32[]{:S(2)}) %collective-permute-start.5) | collective-permute-done | bytes 65568 | tf_op jit(solution)/shard_map/ppermute | solution.py:30
  21.9 1.1 %cross.5.total_ref = f32[512,128]{1,0:T(8,128)S(1)} custom-call(f32[512,128]{1,0:T(8,128)S(1)} %get-tuple-element.86.total_ref, bf16[256,128]{1,0:T(8,128)(2,1)S(1)} %collective-permute-done.4.refs_0_, bf16[256,128]{1,0:T(8,128)(2,1)S(1)} %collective-permute-done.5.refs_1_, bf16[4,2,128,128]{3,2,1,0:T(8,128)(2,1)S(1)} %get-tuple-element.63.ends_w_ref.refs_2_, ...), custom_call_target="tpu_custom_call" | custom-call | flops 1073741824 | bytes 7215104 | tf_op jit(solution)/shard_map/cross/pallas_call | solution.py:35
  23.1 0.0 collective-permute-done.7.refs_1_
  23.1 1.7 %update.5 = (bf16[512,128]{1,0:T(8,128)(2,1)S(1)}, bf16[256,128]{1,0:T(8,128)(2,1)S(1)}, bf16[256,128]{1,0:T(8,128)(2,1)S(1)}, bf16[256,128]{1,0:T(8,128)(2,1)S(1)}, bf16[256,128]{1,0:T(8,128)(2,1)S(1)}) custom-call(f32[512,128]{1,0:T(8,128)S(1)} %cross.5.total_ref, bf16[256,128]{1,0:T(8,128)(2,1)S(1)} %collective-permute-done.6.refs_0_, ...), custom_call_target="tpu_custom_call" | custom-call | flops 1073741824 | bytes 8525824 | tf_op jit(solution)/shard_map/update/pallas_call | solution.py:35
  24.9 1.9 %collective-permute-start.9 = (bf16[256,128]{1,0:T(8,128)(2,1)S(1)}, bf16[256,128]{1,0:T(8,128)(2,1)S(1)}, u32[]{:S(2)}, u32[]{:S(2)}) collective-permute-start(bf16[256,128]{1,0:T(8,128)(2,1)S(1)} %get-tuple-element.98.send_0), channel_id=1, source_target_pairs={{1,2},{2,1},{3,0},{0,3},{5,6},{6,5},{7,4},{4,7},{9,10},{10,9},{11,... | collective-permute-start | bytes 196616 | tf_op jit(solution)/shard_map/ppermute | solution.py:30
  26.8 1.7 %collective-permute-start.10 = (bf16[256,128]{1,0:T(8,128)(2,1)S(1)}, bf16[256,128]{1,0:T(8,128)(2,1)S(1)}, u32[]{:S(2)}, u32[]{:S(2)}) collective-permute-start(bf16[256,128]{1,0:T(8,128)(2,1)S(1)} %get-tuple-element.99.send_1), channel_id=1, source_target_pairs={{4,8},{8,4},{12,16},{16,12},{20,24},{24,20},{28,0},{0,28},{5,9},{9... | collective-permute-start | bytes 196616 | tf_op jit(solution)/shard_map/ppermute | solution.py:30
  28.5 2.3 %inner.6 = (f32[512,128]{1,0:T(8,128)S(1)}, bf16[4,256,128]{2,1,0:T(8,128)(2,1)S(1)}, f32[4,1024,128]{2,1,0:T(8,128)S(1)}) custom-call(bf16[512,128]{1,0:T(8,128)(2,1)S(1)} %get-tuple-element.97.latent_ref.refs_7_, bf16[256,128]{1,0:T(8,128)(2,1)S(1)} %get-tuple-element.98.send_0, bf16[256,128]{1,0:T(8,128)(2,1)S(1)} %get-tuple-element.99.send_1, ...), custom_call_target="tpu_custom_call" | custom-call | flops 1073741824 | bytes 8001536 | tf_op jit(solution)/shard_map/inner/pallas_call | solution.py:35
  30.8 0.3 collective-permute-done.9.refs_1_
  31.1 1.1 %cross.6.total_ref = f32[512,128]{1,0:T(8,128)S(1)} custom-call(f32[512,128]{1,0:T(8,128)S(1)} %get-tuple-element.102.total_ref, bf16[256,128]{1,0:T(8,128)(2,1)S(1)} %collective-permute-done.8.refs_0_, bf16[256,128]{1,0:T(8,128)(2,1)S(1)} %collective-permute-done.9.refs_1_, bf16[4,2,128,128]{3,2,1,0:T(8,128)(2,1)S(1)} %get-tuple-element.63.ends_w_ref.refs_2_, ...), custom_call_target="tpu_custom_call" | custom-call | flops 1073741824 | bytes 7215104 | tf_op jit(solution)/shard_map/cross/pallas_call | solution.py:35
  32.2 0.5 %collective-permute-done.11.refs_1_ = bf16[256,128]{1,0:T(8,128)(2,1)S(1)} collective-permute-done((bf16[256,128]{1,0:T(8,128)(2,1)S(1)}, bf16[256,128]{1,0:T(8,128)(2,1)S(1)}, u32[]{:S(2)}, u32[]{:S(2)}) %collective-permute-start.11) | collective-permute-done | bytes 65568 | tf_op jit(solution)/shard_map/ppermute | solution.py:30
  32.8 1.7 %update.6 = (bf16[512,128]{1,0:T(8,128)(2,1)S(1)}, bf16[256,128]{1,0:T(8,128)(2,1)S(1)}, bf16[256,128]{1,0:T(8,128)(2,1)S(1)}, bf16[256,128]{1,0:T(8,128)(2,1)S(1)}, bf16[256,128]{1,0:T(8,128)(2,1)S(1)}) custom-call(f32[512,128]{1,0:T(8,128)S(1)} %cross.6.total_ref, bf16[256,128]{1,0:T(8,128)(2,1)S(1)} %collective-permute-done.10.refs_0_, ...), custom_call_target="tpu_custom_call" | custom-call | flops 1073741824 | bytes 8525824 | tf_op jit(solution)/shard_map/update/pallas_call | solution.py:35
  34.5 1.6 %collective-permute-start.13 = (bf16[256,128]{1,0:T(8,128)(2,1)S(1)}, bf16[256,128]{1,0:T(8,128)(2,1)S(1)}, u32[]{:S(2)}, u32[]{:S(2)}) collective-permute-start(bf16[256,128]{1,0:T(8,128)(2,1)S(1)} %get-tuple-element.106.send_0), channel_id=1, source_target_pairs={{1,2},{2,1},{3,0},{0,3},{5,6},{6,5},{7,4},{4,7},{9,10},{10,9},{11,... | collective-permute-start | bytes 196616 | tf_op jit(solution)/shard_map/ppermute | solution.py:30
  36.1 1.6 %collective-permute-start.14 = (bf16[256,128]{1,0:T(8,128)(2,1)S(1)}, bf16[256,128]{1,0:T(8,128)(2,1)S(1)}, u32[]{:S(2)}, u32[]{:S(2)}) collective-permute-start(bf16[256,128]{1,0:T(8,128)(2,1)S(1)} %get-tuple-element.107.send_1), channel_id=1, source_target_pairs={{4,8},{8,4},{12,16},{16,12},{20,24},{24,20},{28,0},{0,28},{5,9},{9... | collective-permute-start | bytes 196616 | tf_op jit(solution)/shard_map/ppermute | solution.py:30
  37.6 0.4 collective-permute-start.12
  38.0 2.1 %inner.7 = (f32[512,128]{1,0:T(8,128)S(1)}, bf16[4,256,128]{2,1,0:T(8,128)(2,1)S(1)}, f32[4,1024,128]{2,1,0:T(8,128)S(1)}) custom-call(bf16[512,128]{1,0:T(8,128)(2,1)S(1)} %get-tuple-element.105.latent_ref.refs_7_, bf16[256,128]{1,0:T(8,128)(2,1)S(1)} %get-tuple-element.106.send_0, bf16[256,128]{1,0:T(8,128)(2,1)S(1)} %get-tuple-element.107.send_1, ...), custom_call_target="tpu_custom_call" | custom-call | flops 1073741824 | bytes 8001536 | tf_op jit(solution)/shard_map/inner/pallas_call | solution.py:35
  40.1 0.8 %collective-permute-done.13.refs_1_ = bf16[256,128]{1,0:T(8,128)(2,1)S(1)} collective-permute-done((bf16[256,128]{1,0:T(8,128)(2,1)S(1)}, bf16[256,128]{1,0:T(8,128)(2,1)S(1)}, u32[]{:S(2)}, u32[]{:S(2)}) %collective-permute-start.13) | collective-permute-done | bytes 65568 | tf_op jit(solution)/shard_map/ppermute | solution.py:30
  40.9 1.1 %cross.7.total_ref = f32[512,128]{1,0:T(8,128)S(1)} custom-call(f32[512,128]{1,0:T(8,128)S(1)} %get-tuple-element.110.total_ref, bf16[256,128]{1,0:T(8,128)(2,1)S(1)} %collective-permute-done.12.refs_0_, bf16[256,128]{1,0:T(8,128)(2,1)S(1)} %collective-permute-done.13.refs_1_, bf16[4,2,128,128]{3,2,1,0:T(8,128)(2,1)S(1)} %get-tuple-element.63.ends_w_ref.refs_2_, ...), custom_call_target="tpu_custom_call" | custom-call | flops 1073741824 | bytes 7215104 | tf_op jit(solution)/shard_map/cross/pallas_call | solution.py:35
  42.1 2.2 %update.7 = bf16[512,128]{1,0:T(8,128)(2,1)} custom-call(f32[512,128]{1,0:T(8,128)S(1)} %cross.7.total_ref, bf16[256,128]{1,0:T(8,128)(2,1)S(1)} %collective-permute-done.14.refs_0_, bf16[256,128]{1,0:T(8,128)(2,1)S(1)} %collective-permute-done.15.refs_1_, bf16[4,2,128,128]{3,2,1,0:T(8,128)(2,1)S(1)} %get-tuple-element.63.ends_w_ref.refs_2_, ...), custom_call_target="tpu_custom_call" | custom-call | flops 1073741824 | bytes 7739392 | tf_op jit(solution)/shard_map/update/pallas_call | solution.py:35
  (42 shorter events, 0.1 us)
Async XLA Ops:
  0.0 9.1 %copy-start.10 = (f32[4,3,128]{2,0,1:T(4,128)S(1)}, f32[4,3,128]{2,0,1:T(4,128)}, u32[]{:S(2)}) copy-start(f32[4,3,128]{2,0,1:T(4,128)} %param.19) | copy-start | bytes 18436
  0.0 9.1 %copy-start.3 = (bf16[4,3,128,128]{3,2,1,0:T(8,128)(2,1)S(1)}, bf16[4,3,128,128]{3,2,1,0:T(8,128)(2,1)}, u32[]{:S(2)}) copy-start(bf16[4,3,128,128]{3,2,1,0:T(8,128)(2,1)} %nodes_ref.1) | copy-start | bytes 1179652
  0.0 9.1 %copy-start.2 = (bf16[4,4,128,128]{3,2,1,0:T(8,128)(2,1)S(1)}, bf16[4,4,128,128]{3,2,1,0:T(8,128)(2,1)}, u32[]{:S(2)}) copy-start(bf16[4,4,128,128]{3,2,1,0:T(8,128)(2,1)} %weights_ref.1) | copy-start | bytes 1572868
  0.0 9.1 %copy-start.9 = (s32[1,1,4,512]{3,2,1,0:T(4,128)S(1)}, s32[1,1,4,512]{3,2,1,0:T(4,128)}, u32[]{:S(2)}) copy-start(s32[1,1,4,512]{3,2,1,0:T(4,128)} %param.11) | copy-start | bytes 24580
  2.3 7.4 %copy-start.4 = (bf16[1,1,512,128]{3,2,1,0:T(8,128)(2,1)S(1)}, bf16[1,1,512,128]{3,2,1,0:T(8,128)(2,1)}, u32[]{:S(2)}) copy-start(bf16[1,1,512,128]{3,2,1,0:T(8,128)(2,1)} %param.10) | copy-start | bytes 393220
  2.3 7.4 %copy-start.5 = (bf16[272,128]{1,0:T(8,128)(2,1)S(1)}, bf16[272,128]{1,0:T(8,128)(2,1)}, u32[]{:S(2)}) copy-start(bf16[272,128]{1,0:T(8,128)(2,1)} %get-tuple-element.61.send_2) | copy-start | bytes 208900
  2.3 7.4 %copy-start.6 = (bf16[272,128]{1,0:T(8,128)(2,1)S(1)}, bf16[272,128]{1,0:T(8,128)(2,1)}, u32[]{:S(2)}) copy-start(bf16[272,128]{1,0:T(8,128)(2,1)} %get-tuple-element.60.send_1) | copy-start | bytes 208900
  2.3 7.4 %copy-start.7 = (bf16[272,128]{1,0:T(8,128)(2,1)S(1)}, bf16[272,128]{1,0:T(8,128)(2,1)}, u32[]{:S(2)}) copy-start(bf16[272,128]{1,0:T(8,128)(2,1)} %get-tuple-element.62.send_3) | copy-start | bytes 208900
  2.3 7.4 %copy-start.8 = (bf16[272,128]{1,0:T(8,128)(2,1)S(1)}, bf16[272,128]{1,0:T(8,128)(2,1)}, u32[]{:S(2)}) copy-start(bf16[272,128]{1,0:T(8,128)(2,1)} %get-tuple-element.59.send_0) | copy-start | bytes 208900
  2.3 9.0 %collective-permute-start.1 = (bf16[272,128]{1,0:T(8,128)(2,1)}, bf16[272,128]{1,0:T(8,128)(2,1)S(1)}, u32[]{:S(2)}, u32[]{:S(2)}) collective-permute-start(bf16[272,128]{1,0:T(8,128)(2,1)} %get-tuple-element.59.send_0), channel_id=1, source_target_pairs={{1,2},{2,1},{3,0},{0,3},{5,6},{6,5},{7,4},{4,7},{9,10},{10,9},{11,... | collective-permute-start | bytes 208904 | tf_op jit(solution)/shard_map/ppermute | solution.py:30
  7.4 5.5 %collective-permute-start.2 = (bf16[272,128]{1,0:T(8,128)(2,1)}, bf16[272,128]{1,0:T(8,128)(2,1)S(1)}, u32[]{:S(2)}, u32[]{:S(2)}) collective-permute-start(bf16[272,128]{1,0:T(8,128)(2,1)} %get-tuple-element.60.send_1), channel_id=1, source_target_pairs={{4,8},{8,4},{12,16},{16,12},{20,24},{24,20},{28,0},{0,28},{5,9},{9... | collective-permute-start | bytes 208904 | tf_op jit(solution)/shard_map/ppermute | solution.py:30
  9.1 4.5 %collective-permute-start.3 = (bf16[272,128]{1,0:T(8,128)(2,1)}, bf16[272,128]{1,0:T(8,128)(2,1)S(1)}, u32[]{:S(2)}, u32[]{:S(2)}) collective-permute-start(bf16[272,128]{1,0:T(8,128)(2,1)} %get-tuple-element.61.send_2), channel_id=1, source_target_pairs={{0,1},{1,0},{2,3},{3,2},{4,5},{5,4},{6,7},{7,6},{8,9},{9,8},{10,11... | collective-permute-start | bytes 208904 | tf_op jit(solution)/shard_map/ppermute | solution.py:30
  9.1 2.3 %collective-permute-start = (bf16[272,128]{1,0:T(8,128)(2,1)}, bf16[272,128]{1,0:T(8,128)(2,1)S(1)}, u32[]{:S(2)}, u32[]{:S(2)}) collective-permute-start(bf16[272,128]{1,0:T(8,128)(2,1)} %get-tuple-element.62.send_3), channel_id=1, source_target_pairs={{0,4},{4,0},{8,12},{12,8},{16,20},{20,16},{24,28},{28,24},{1,5},{5... | collective-permute-start | bytes 208904 | tf_op jit(solution)/shard_map/ppermute | solution.py:30
  9.7 1.7 %copy-start.11 = (s32[1,1,2,256]{3,2,1,0:T(2,128)S(1)}, s32[1,1,2,256]{3,2,1,0:T(2,128)}, u32[]{:S(2)}) copy-start(s32[1,1,2,256]{3,2,1,0:T(2,128)} %param.12) | copy-start | bytes 6148
  9.7 1.7 %copy-start.12 = (s32[1,1,2,256]{3,2,1,0:T(2,128)S(1)}, s32[1,1,2,256]{3,2,1,0:T(2,128)}, u32[]{:S(2)}) copy-start(s32[1,1,2,256]{3,2,1,0:T(2,128)} %param.13) | copy-start | bytes 6148
  9.7 1.7 %copy-start.13 = (bf16[2,16,128]{2,1,0:T(8,128)(2,1)S(1)}, bf16[2,16,128]{2,1,0:T(8,128)(2,1)}, u32[]{:S(2)}) copy-start(bf16[2,16,128]{2,1,0:T(8,128)(2,1)} %get-tuple-element.71.refs_6_.refs_9_) | copy-start | bytes 24580
  11.3 2.3 %copy-start = (bf16[4,256,256]{2,1,0:T(8,128)(2,1)S(1)}, bf16[4,256,256]{2,1,0:T(8,128)(2,1)}, u32[]{:S(2)}) copy-start(bf16[4,256,256]{2,1,0:T(8,128)(2,1)} %get-tuple-element.75.refs_12_.refs_16_) | copy-start | bytes 1572868
  11.3 2.2 %copy-start.1 = (bf16[4,256,128]{2,1,0:T(8,128)(2,1)S(1)}, bf16[4,256,128]{2,1,0:T(8,128)(2,1)}, u32[]{:S(2)}) copy-start(bf16[4,256,128]{2,1,0:T(8,128)(2,1)} %get-tuple-element.76.refs_13_.refs_17_) | copy-start | bytes 786436
  15.7 6.3 %collective-permute-start.5 = (bf16[256,128]{1,0:T(8,128)(2,1)S(1)}, bf16[256,128]{1,0:T(8,128)(2,1)S(1)}, u32[]{:S(2)}, u32[]{:S(2)}) collective-permute-start(bf16[256,128]{1,0:T(8,128)(2,1)S(1)} %get-tuple-element.78.send_0), channel_id=1, source_target_pairs={{1,2},{2,1},{3,0},{0,3},{5,6},{6,5},{7,4},{4,7},{9,10},{10,9},{11,... | collective-permute-start | bytes 196616 | tf_op jit(solution)/shard_map/ppermute | solution.py:30
  17.5 5.6 %collective-permute-start.6 = (bf16[256,128]{1,0:T(8,128)(2,1)S(1)}, bf16[256,128]{1,0:T(8,128)(2,1)S(1)}, u32[]{:S(2)}, u32[]{:S(2)}) collective-permute-start(bf16[256,128]{1,0:T(8,128)(2,1)S(1)} %get-tuple-element.79.send_1), channel_id=1, source_target_pairs={{4,8},{8,4},{12,16},{16,12},{20,24},{24,20},{28,0},{0,28},{5,9},{9... | collective-permute-start | bytes 196616 | tf_op jit(solution)/shard_map/ppermute | solution.py:30
  18.0 5.1 %collective-permute-start.7 = (bf16[256,128]{1,0:T(8,128)(2,1)S(1)}, bf16[256,128]{1,0:T(8,128)(2,1)S(1)}, u32[]{:S(2)}, u32[]{:S(2)}) collective-permute-start(bf16[256,128]{1,0:T(8,128)(2,1)S(1)} %get-tuple-element.80.send_2), channel_id=1, source_target_pairs={{0,1},{1,0},{2,3},{3,2},{4,5},{5,4},{6,7},{7,6},{8,9},{9,8},{10,11... | collective-permute-start | bytes 196616 | tf_op jit(solution)/shard_map/ppermute | solution.py:30
  18.1 3.9 %collective-permute-start.4 = (bf16[256,128]{1,0:T(8,128)(2,1)S(1)}, bf16[256,128]{1,0:T(8,128)(2,1)S(1)}, u32[]{:S(2)}, u32[]{:S(2)}) collective-permute-start(bf16[256,128]{1,0:T(8,128)(2,1)S(1)} %get-tuple-element.81.send_3), channel_id=1, source_target_pairs={{0,4},{4,0},{8,12},{12,8},{16,20},{20,16},{24,28},{28,24},{1,5},{5... | collective-permute-start | bytes 196616 | tf_op jit(solution)/shard_map/ppermute | solution.py:30
  24.9 6.2 %collective-permute-start.9 = (bf16[256,128]{1,0:T(8,128)(2,1)S(1)}, bf16[256,128]{1,0:T(8,128)(2,1)S(1)}, u32[]{:S(2)}, u32[]{:S(2)}) collective-permute-start(bf16[256,128]{1,0:T(8,128)(2,1)S(1)} %get-tuple-element.98.send_0), channel_id=1, source_target_pairs={{1,2},{2,1},{3,0},{0,3},{5,6},{6,5},{7,4},{4,7},{9,10},{10,9},{11,... | collective-permute-start | bytes 196616 | tf_op jit(solution)/shard_map/ppermute | solution.py:30
  26.8 5.4 %collective-permute-start.10 = (bf16[256,128]{1,0:T(8,128)(2,1)S(1)}, bf16[256,128]{1,0:T(8,128)(2,1)S(1)}, u32[]{:S(2)}, u32[]{:S(2)}) collective-permute-start(bf16[256,128]{1,0:T(8,128)(2,1)S(1)} %get-tuple-element.99.send_1), channel_id=1, source_target_pairs={{4,8},{8,4},{12,16},{16,12},{20,24},{24,20},{28,0},{0,28},{5,9},{9... | collective-permute-start | bytes 196616 | tf_op jit(solution)/shard_map/ppermute | solution.py:30
  28.5 4.3 %collective-permute-start.11 = (bf16[256,128]{1,0:T(8,128)(2,1)S(1)}, bf16[256,128]{1,0:T(8,128)(2,1)S(1)}, u32[]{:S(2)}, u32[]{:S(2)}) collective-permute-start(bf16[256,128]{1,0:T(8,128)(2,1)S(1)} %get-tuple-element.100.send_2), channel_id=1, source_target_pairs={{0,1},{1,0},{2,3},{3,2},{4,5},{5,4},{6,7},{7,6},{8,9},{9,8},{10,11... | collective-permute-start | bytes 196616 | tf_op jit(solution)/shard_map/ppermute | solution.py:30
  28.5 2.6 %collective-permute-start.8 = (bf16[256,128]{1,0:T(8,128)(2,1)S(1)}, bf16[256,128]{1,0:T(8,128)(2,1)S(1)}, u32[]{:S(2)}, u32[]{:S(2)}) collective-permute-start(bf16[256,128]{1,0:T(8,128)(2,1)S(1)} %get-tuple-element.101.send_3), channel_id=1, source_target_pairs={{0,4},{4,0},{8,12},{12,8},{16,20},{20,16},{24,28},{28,24},{1,5},{5... | collective-permute-start | bytes 196616 | tf_op jit(solution)/shard_map/ppermute | solution.py:30
  34.5 6.4 %collective-permute-start.13 = (bf16[256,128]{1,0:T(8,128)(2,1)S(1)}, bf16[256,128]{1,0:T(8,128)(2,1)S(1)}, u32[]{:S(2)}, u32[]{:S(2)}) collective-permute-start(bf16[256,128]{1,0:T(8,128)(2,1)S(1)} %get-tuple-element.106.send_0), channel_id=1, source_target_pairs={{1,2},{2,1},{3,0},{0,3},{5,6},{6,5},{7,4},{4,7},{9,10},{10,9},{11,... | collective-permute-start | bytes 196616 | tf_op jit(solution)/shard_map/ppermute | solution.py:30
  36.1 6.0 %collective-permute-start.14 = (bf16[256,128]{1,0:T(8,128)(2,1)S(1)}, bf16[256,128]{1,0:T(8,128)(2,1)S(1)}, u32[]{:S(2)}, u32[]{:S(2)}) collective-permute-start(bf16[256,128]{1,0:T(8,128)(2,1)S(1)} %get-tuple-element.107.send_1), channel_id=1, source_target_pairs={{4,8},{8,4},{12,16},{16,12},{20,24},{24,20},{28,0},{0,28},{5,9},{9... | collective-permute-start | bytes 196616 | tf_op jit(solution)/shard_map/ppermute | solution.py:30
  37.6 4.4 %collective-permute-start.15 = (bf16[256,128]{1,0:T(8,128)(2,1)S(1)}, bf16[256,128]{1,0:T(8,128)(2,1)S(1)}, u32[]{:S(2)}, u32[]{:S(2)}) collective-permute-start(bf16[256,128]{1,0:T(8,128)(2,1)S(1)} %get-tuple-element.108.send_2), channel_id=1, source_target_pairs={{0,1},{1,0},{2,3},{3,2},{4,5},{5,4},{6,7},{7,6},{8,9},{9,8},{10,11... | collective-permute-start | bytes 196616 | tf_op jit(solution)/shard_map/ppermute | solution.py:30
  37.6 3.3 %collective-permute-start.12 = (bf16[256,128]{1,0:T(8,128)(2,1)S(1)}, bf16[256,128]{1,0:T(8,128)(2,1)S(1)}, u32[]{:S(2)}, u32[]{:S(2)}) collective-permute-start(bf16[256,128]{1,0:T(8,128)(2,1)S(1)} %get-tuple-element.109.send_3), channel_id=1, source_target_pairs={{0,4},{4,0},{8,12},{12,8},{16,20},{20,16},{24,28},{28,24},{1,5},{5... | collective-permute-start | bytes 196616 | tf_op jit(solution)/shard_map/ppermute | solution.py:30

commit v7 on v6

--- a/solution.py
+++ b/solution.py
@@ -16,7 +16,7 @@
 CUT = 128
 
 NEAR_X, FAR_X, NEAR_Y, FAR_Y = range(4)
-ORDER = (FAR_Y, FAR_X, NEAR_Y, NEAR_X)
+ORDER = (FAR_Y, NEAR_Y, FAR_X, NEAR_X)
 VISITS = ((NEAR_X, FAR_Y), (FAR_X, NEAR_Y))
 PLACE = tuple(ORDER.index(link) for link in range(4))
 

time: 44.4 us -> 44 us (level)
  waiting for transfers between devices: 3.09 us -> 0.99 us
  starting transfers between devices: 17.3 us -> 19 us
    ppermute x16, waiting for transfers between devices: 3.09 us -> 0.99 us  [swapped(): return lax.ppermute(block, axis, route)]
    ppermute x16, starting transfers between devices: 17.3 us -> 19 us  [swapped(): return lax.ppermute(block, axis, route)]
  transfers between devices with their start and end apart: 16 -> 16, of which waited for: 6 -> 4; matrix products, arithmetic and copies ran while one was open for 0% -> 0% of each run, Pallas kernels for 31% -> 31%
where the time goes in v7:
time: 44 us; the launch traced here: 43.8 us
  Pallas kernels  23.5 us (53%)
  starting transfers between devices  19 us (43%)
  waiting for transfers between devices  0.99 us (2%)
    pallas_call x14, Pallas kernels, call(): pl.pallas_call(kernel, out_shape=outs, in_specs=in_specs or [VMEM] * len(...  23.5 us
    ppermute x16, starting transfers between devices, swapped(): return lax.ppermute(block, axis, route)  19 us
    ppermute x16, waiting for transfers between devices, swapped(): return lax.ppermute(block, axis, route)  0.99 us
  transfers between devices with their start and end apart: 16, of which 4 were waited for; matrix products, arithmetic and copies ran while one was open for 0% of the time, Pallas kernels for 31%

profile of v7, /device:TPU:0, one launch (start us, length us, event | category | flops | bytes accessed | tf_op | source)
XLA Modules:
  0.0 43.8 jit_solution(5196453500236582826)
XLA Ops:
  0.0 2.3 %first.1 = (bf16[272,128]{1,0:T(8,128)(2,1)}, bf16[272,128]{1,0:T(8,128)(2,1)}, bf16[272,128]{1,0:T(8,128)(2,1)}, bf16[272,128]{1,0:T(8,128)(2,1)}, bf16[4,256,2...) custom-call(bf16[512,128]{1,0:T(8,128)(2,1)} %bitcast.9, s32[2,256]{1,0:T(2,128)} %bitcast.14, ...), custom_call_target="tpu_custom_call" | custom-call | flops 1073741824 | bytes 151560 | tf_op jit(solution)/shard_map/first/pallas_call | solution.py:35
  2.3 5.1 %collective-permute-start.1 = (bf16[272,128]{1,0:T(8,128)(2,1)}, bf16[272,128]{1,0:T(8,128)(2,1)S(1)}, u32[]{:S(2)}, u32[]{:S(2)}) collective-permute-start(bf16[272,128]{1,0:T(8,128)(2,1)} %get-tuple-element.59.send_0), channel_id=1, source_target_pairs={{1,2},{2,1},{3,0},{0,3},{5,6},{6,5},{7,4},{4,7},{9,10},{10,9},{11,... | collective-permute-start | bytes 208904 | tf_op jit(solution)/shard_map/ppermute | solution.py:30
  7.5 1.6 %collective-permute-start.2 = (bf16[272,128]{1,0:T(8,128)(2,1)}, bf16[272,128]{1,0:T(8,128)(2,1)S(1)}, u32[]{:S(2)}, u32[]{:S(2)}) collective-permute-start(bf16[272,128]{1,0:T(8,128)(2,1)} %get-tuple-element.61.send_2), channel_id=1, source_target_pairs={{4,8},{8,4},{12,16},{16,12},{20,24},{24,20},{28,0},{0,28},{5,9},{9... | collective-permute-start | bytes 208904 | tf_op jit(solution)/shard_map/ppermute | solution.py:30
  9.1 0.6 %setup.1 = (bf16[2048,256]{1,0:T(8,128)(2,1)S(1)}, bf16[256,2048]{1,0:T(8,128)(2,1)S(1)}, bf16[2048,128]{1,0:T(8,128)(2,1)S(1)}, bf16[4,2,128,128]{3,2,1,0:T(8,1...) custom-call(s32[4,512]{1,0:T(4,128)S(1)} %bitcast.12, ...), custom_call_target="tpu_custom_call" | custom-call | flops 1073741824 | bytes 931840 | tf_op jit(solution)/shard_map/setup/pallas_call | solution.py:35
  9.7 1.6 %inner.4 = (f32[512,128]{1,0:T(8,128)S(1)}, bf16[4,256,128]{2,1,0:T(8,128)(2,1)S(1)}) custom-call(bf16[512,128]{1,0:T(8,128)(2,1)S(1)} %bitcast.10, bf16[272,128]{1,0:T(8,128)(2,1)S(1)} %copy-done.8, bf16[272,128]{1,0:T(8,128)(2,1)S(1)} %copy-done.6, bf16[272,128]{1,0:T(8,128)(2,1)S(1)} %copy-done.5, bf16[272,128]{1,0:T(8,128)(2,1)S(1)} %copy-done.7, ...), custom_call_target="tpu_custom_call" | custom-call | flops 1073741824 | bytes 3823616 | tf_op jit(solution)/shard_map/inner/pallas_call | solution.py:35
  11.4 1.5 %cross.4 = (f32[512,128]{1,0:T(8,128)S(1)}, bf16[1024,512]{1,0:T(8,128)(2,1)S(1)}, bf16[256,1024]{1,0:T(8,128)(2,1)S(1)}, bf16[1024,128]{1,0:T(8,128)(2,1)S(1)},...) custom-call(f32[512,128]{1,0:T(8,128)S(1)} %get-tuple-element.69.total_ref, ...), custom_call_target="tpu_custom_call" | custom-call | flops 1073741824 | bytes 1468416 | tf_op jit(solution)/shard_map/cross/pallas_call | solution.py:35
  12.9 0.1 collective-permute-done.2.refs_0_
  12.9 2.1 %update.4 = (bf16[512,128]{1,0:T(8,128)(2,1)S(1)}, bf16[256,128]{1,0:T(8,128)(2,1)S(1)}, bf16[256,128]{1,0:T(8,128)(2,1)S(1)}, bf16[256,128]{1,0:T(8,128)(2,1)S(...) custom-call(f32[512,128]{1,0:T(8,128)S(1)} %get-tuple-element.72.tot, ...), custom_call_target="tpu_custom_call" | custom-call | flops 1073741824 | bytes 2779136 | tf_op jit(solution)/shard_map/update/pallas_call | solution.py:35
  15.0 2.8 %collective-permute-start.5 = (bf16[256,128]{1,0:T(8,128)(2,1)S(1)}, bf16[256,128]{1,0:T(8,128)(2,1)S(1)}, u32[]{:S(2)}, u32[]{:S(2)}) collective-permute-start(bf16[256,128]{1,0:T(8,128)(2,1)S(1)} %get-tuple-element.78.send_0), channel_id=1, source_target_pairs={{1,2},{2,1},{3,0},{0,3},{5,6},{6,5},{7,4},{4,7},{9,10},{10,9},{11,... | collective-permute-start | bytes 196616 | tf_op jit(solution)/shard_map/ppermute | solution.py:30
  17.8 0.2 collective-permute-start.6
  18.0 1.4 %collective-permute-start.4 = (bf16[256,128]{1,0:T(8,128)(2,1)S(1)}, bf16[256,128]{1,0:T(8,128)(2,1)S(1)}, u32[]{:S(2)}, u32[]{:S(2)}) collective-permute-start(bf16[256,128]{1,0:T(8,128)(2,1)S(1)} %get-tuple-element.81.send_3), channel_id=1, source_target_pairs={{0,4},{4,0},{8,12},{12,8},{16,20},{20,16},{24,28},{28,24},{1,5},{5... | collective-permute-start | bytes 196616 | tf_op jit(solution)/shard_map/ppermute | solution.py:30
  19.4 2.1 %inner.5 = (f32[512,128]{1,0:T(8,128)S(1)}, bf16[4,256,128]{2,1,0:T(8,128)(2,1)S(1)}, f32[4,1024,128]{2,1,0:T(8,128)S(1)}) custom-call(bf16[512,128]{1,0:T(8,128)(2,1)S(1)} %get-tuple-element.77.latent_ref.refs_7_, bf16[256,128]{1,0:T(8,128)(2,1)S(1)} %get-tuple-element.78.send_0, bf16[256,128]{1,0:T(8,128)(2,1)S(1)} %get-tuple-element.79.send_1, ...), custom_call_target="tpu_custom_call" | custom-call | flops 1073741824 | bytes 8001536 | tf_op jit(solution)/shard_map/inner/pallas_call | solution.py:35
  21.5 0.3 collective-permute-done.5.refs_1_
  21.8 1.1 %cross.5.total_ref = f32[512,128]{1,0:T(8,128)S(1)} custom-call(f32[512,128]{1,0:T(8,128)S(1)} %get-tuple-element.86.total_ref, bf16[256,128]{1,0:T(8,128)(2,1)S(1)} %collective-permute-done.4.refs_0_, bf16[256,128]{1,0:T(8,128)(2,1)S(1)} %collective-permute-done.5.refs_1_, bf16[4,2,128,128]{3,2,1,0:T(8,128)(2,1)S(1)} %get-tuple-element.63.ends_w_ref.refs_2_, ...), custom_call_target="tpu_custom_call" | custom-call | flops 1073741824 | bytes 7215104 | tf_op jit(solution)/shard_map/cross/pallas_call | solution.py:35
  23.0 0.0 collective-permute-done.6.refs_0_
  23.0 1.7 %update.5 = (bf16[512,128]{1,0:T(8,128)(2,1)S(1)}, bf16[256,128]{1,0:T(8,128)(2,1)S(1)}, bf16[256,128]{1,0:T(8,128)(2,1)S(1)}, bf16[256,128]{1,0:T(8,128)(2,1)S(1)}, bf16[256,128]{1,0:T(8,128)(2,1)S(1)}) custom-call(f32[512,128]{1,0:T(8,128)S(1)} %cross.5.total_ref, bf16[256,128]{1,0:T(8,128)(2,1)S(1)} %collective-permute-done.6.refs_0_, ...), custom_call_target="tpu_custom_call" | custom-call | flops 1073741824 | bytes 8525824 | tf_op jit(solution)/shard_map/update/pallas_call | solution.py:35
  24.7 2.1 %collective-permute-start.9 = (bf16[256,128]{1,0:T(8,128)(2,1)S(1)}, bf16[256,128]{1,0:T(8,128)(2,1)S(1)}, u32[]{:S(2)}, u32[]{:S(2)}) collective-permute-start(bf16[256,128]{1,0:T(8,128)(2,1)S(1)} %get-tuple-element.98.send_0), channel_id=1, source_target_pairs={{1,2},{2,1},{3,0},{0,3},{5,6},{6,5},{7,4},{4,7},{9,10},{10,9},{11,... | collective-permute-start | bytes 196616 | tf_op jit(solution)/shard_map/ppermute | solution.py:30
  26.9 0.0 collective-permute-start.11
  26.9 0.6 %collective-permute-start.10 = (bf16[256,128]{1,0:T(8,128)(2,1)S(1)}, bf16[256,128]{1,0:T(8,128)(2,1)S(1)}, u32[]{:S(2)}, u32[]{:S(2)}) collective-permute-start(bf16[256,128]{1,0:T(8,128)(2,1)S(1)} %get-tuple-element.100.send_2), channel_id=1, source_target_pairs={{4,8},{8,4},{12,16},{16,12},{20,24},{24,20},{28,0},{0,28},{5,9},{9... | collective-permute-start | bytes 196616 | tf_op jit(solution)/shard_map/ppermute | solution.py:30
  27.5 0.9 %collective-permute-start.8 = (bf16[256,128]{1,0:T(8,128)(2,1)S(1)}, bf16[256,128]{1,0:T(8,128)(2,1)S(1)}, u32[]{:S(2)}, u32[]{:S(2)}) collective-permute-start(bf16[256,128]{1,0:T(8,128)(2,1)S(1)} %get-tuple-element.101.send_3), channel_id=1, source_target_pairs={{0,4},{4,0},{8,12},{12,8},{16,20},{20,16},{24,28},{28,24},{1,5},{5... | collective-permute-start | bytes 196616 | tf_op jit(solution)/shard_map/ppermute | solution.py:30
  28.5 2.3 %inner.6 = (f32[512,128]{1,0:T(8,128)S(1)}, bf16[4,256,128]{2,1,0:T(8,128)(2,1)S(1)}, f32[4,1024,128]{2,1,0:T(8,128)S(1)}) custom-call(bf16[512,128]{1,0:T(8,128)(2,1)S(1)} %get-tuple-element.97.latent_ref.refs_7_, bf16[256,128]{1,0:T(8,128)(2,1)S(1)} %get-tuple-element.98.send_0, bf16[256,128]{1,0:T(8,128)(2,1)S(1)} %get-tuple-element.99.send_1, ...), custom_call_target="tpu_custom_call" | custom-call | flops 1073741824 | bytes 8001536 | tf_op jit(solution)/shard_map/inner/pallas_call | solution.py:35
  30.8 0.4 %collective-permute-done.9.refs_1_ = bf16[256,128]{1,0:T(8,128)(2,1)S(1)} collective-permute-done((bf16[256,128]{1,0:T(8,128)(2,1)S(1)}, bf16[256,128]{1,0:T(8,128)(2,1)S(1)}, u32[]{:S(2)}, u32[]{:S(2)}) %collective-permute-start.9) | collective-permute-done | bytes 65568 | tf_op jit(solution)/shard_map/ppermute | solution.py:30
  31.2 1.1 %cross.6.total_ref = f32[512,128]{1,0:T(8,128)S(1)} custom-call(f32[512,128]{1,0:T(8,128)S(1)} %get-tuple-element.102.total_ref, bf16[256,128]{1,0:T(8,128)(2,1)S(1)} %collective-permute-done.8.refs_0_, bf16[256,128]{1,0:T(8,128)(2,1)S(1)} %collective-permute-done.9.refs_1_, bf16[4,2,128,128]{3,2,1,0:T(8,128)(2,1)S(1)} %get-tuple-element.63.ends_w_ref.refs_2_, ...), custom_call_target="tpu_custom_call" | custom-call | flops 1073741824 | bytes 7215104 | tf_op jit(solution)/shard_map/cross/pallas_call | solution.py:35
  32.4 1.8 %update.6 = (bf16[512,128]{1,0:T(8,128)(2,1)S(1)}, bf16[256,128]{1,0:T(8,128)(2,1)S(1)}, bf16[256,128]{1,0:T(8,128)(2,1)S(1)}, bf16[256,128]{1,0:T(8,128)(2,1)S(1)}, bf16[256,128]{1,0:T(8,128)(2,1)S(1)}) custom-call(f32[512,128]{1,0:T(8,128)S(1)} %cross.6.total_ref, bf16[256,128]{1,0:T(8,128)(2,1)S(1)} %collective-permute-done.10.refs_0_, ...), custom_call_target="tpu_custom_call" | custom-call | flops 1073741824 | bytes 8525824 | tf_op jit(solution)/shard_map/update/pallas_call | solution.py:35
  34.1 2.3 %collective-permute-start.13 = (bf16[256,128]{1,0:T(8,128)(2,1)S(1)}, bf16[256,128]{1,0:T(8,128)(2,1)S(1)}, u32[]{:S(2)}, u32[]{:S(2)}) collective-permute-start(bf16[256,128]{1,0:T(8,128)(2,1)S(1)} %get-tuple-element.106.send_0), channel_id=1, source_target_pairs={{1,2},{2,1},{3,0},{0,3},{5,6},{6,5},{7,4},{4,7},{9,10},{10,9},{11,... | collective-permute-start | bytes 196616 | tf_op jit(solution)/shard_map/ppermute | solution.py:30
  36.4 0.2 collective-permute-start.15
  36.7 0.8 %collective-permute-start.14 = (bf16[256,128]{1,0:T(8,128)(2,1)S(1)}, bf16[256,128]{1,0:T(8,128)(2,1)S(1)}, u32[]{:S(2)}, u32[]{:S(2)}) collective-permute-start(bf16[256,128]{1,0:T(8,128)(2,1)S(1)} %get-tuple-element.108.send_2), channel_id=1, source_target_pairs={{4,8},{8,4},{12,16},{16,12},{20,24},{24,20},{28,0},{0,28},{5,9},{9... | collective-permute-start | bytes 196616 | tf_op jit(solution)/shard_map/ppermute | solution.py:30
  37.5 0.8 %collective-permute-start.12 = (bf16[256,128]{1,0:T(8,128)(2,1)S(1)}, bf16[256,128]{1,0:T(8,128)(2,1)S(1)}, u32[]{:S(2)}, u32[]{:S(2)}) collective-permute-start(bf16[256,128]{1,0:T(8,128)(2,1)S(1)} %get-tuple-element.109.send_3), channel_id=1, source_target_pairs={{0,4},{4,0},{8,12},{12,8},{16,20},{20,16},{24,28},{28,24},{1,5},{5... | collective-permute-start | bytes 196616 | tf_op jit(solution)/shard_map/ppermute | solution.py:30
  38.3 2.1 %inner.7 = (f32[512,128]{1,0:T(8,128)S(1)}, bf16[4,256,128]{2,1,0:T(8,128)(2,1)S(1)}, f32[4,1024,128]{2,1,0:T(8,128)S(1)}) custom-call(bf16[512,128]{1,0:T(8,128)(2,1)S(1)} %get-tuple-element.105.latent_ref.refs_7_, bf16[256,128]{1,0:T(8,128)(2,1)S(1)} %get-tuple-element.106.send_0, bf16[256,128]{1,0:T(8,128)(2,1)S(1)} %get-tuple-element.107.send_1, ...), custom_call_target="tpu_custom_call" | custom-call | flops 1073741824 | bytes 8001536 | tf_op jit(solution)/shard_map/inner/pallas_call | solution.py:35
  40.4 0.1 collective-permute-done.13.refs_1_
  40.5 1.1 %cross.7.total_ref = f32[512,128]{1,0:T(8,128)S(1)} custom-call(f32[512,128]{1,0:T(8,128)S(1)} %get-tuple-element.110.total_ref, bf16[256,128]{1,0:T(8,128)(2,1)S(1)} %collective-permute-done.12.refs_0_, bf16[256,128]{1,0:T(8,128)(2,1)S(1)} %collective-permute-done.13.refs_1_, bf16[4,2,128,128]{3,2,1,0:T(8,128)(2,1)S(1)} %get-tuple-element.63.ends_w_ref.refs_2_, ...), custom_call_target="tpu_custom_call" | custom-call | flops 1073741824 | bytes 7215104 | tf_op jit(solution)/shard_map/cross/pallas_call | solution.py:35
  41.7 2.2 %update.7 = bf16[512,128]{1,0:T(8,128)(2,1)} custom-call(f32[512,128]{1,0:T(8,128)S(1)} %cross.7.total_ref, bf16[256,128]{1,0:T(8,128)(2,1)S(1)} %collective-permute-done.14.refs_0_, bf16[256,128]{1,0:T(8,128)(2,1)S(1)} %collective-permute-done.15.refs_1_, bf16[4,2,128,128]{3,2,1,0:T(8,128)(2,1)S(1)} %get-tuple-element.63.ends_w_ref.refs_2_, ...), custom_call_target="tpu_custom_call" | custom-call | flops 1073741824 | bytes 7739392 | tf_op jit(solution)/shard_map/update/pallas_call | solution.py:35
  (42 shorter events, 0.1 us)
Async XLA Ops:
  0.0 9.1 %copy-start.10 = (f32[4,3,128]{2,0,1:T(4,128)S(1)}, f32[4,3,128]{2,0,1:T(4,128)}, u32[]{:S(2)}) copy-start(f32[4,3,128]{2,0,1:T(4,128)} %param.19) | copy-start | bytes 18436
  0.0 9.1 %copy-start.3 = (bf16[4,3,128,128]{3,2,1,0:T(8,128)(2,1)S(1)}, bf16[4,3,128,128]{3,2,1,0:T(8,128)(2,1)}, u32[]{:S(2)}) copy-start(bf16[4,3,128,128]{3,2,1,0:T(8,128)(2,1)} %nodes_ref.1) | copy-start | bytes 1179652
  0.0 9.1 %copy-start.2 = (bf16[4,4,128,128]{3,2,1,0:T(8,128)(2,1)S(1)}, bf16[4,4,128,128]{3,2,1,0:T(8,128)(2,1)}, u32[]{:S(2)}) copy-start(bf16[4,4,128,128]{3,2,1,0:T(8,128)(2,1)} %weights_ref.1) | copy-start | bytes 1572868
  0.0 9.1 %copy-start.9 = (s32[1,1,4,512]{3,2,1,0:T(4,128)S(1)}, s32[1,1,4,512]{3,2,1,0:T(4,128)}, u32[]{:S(2)}) copy-start(s32[1,1,4,512]{3,2,1,0:T(4,128)} %param.11) | copy-start | bytes 24580
  2.3 7.4 %copy-start.4 = (bf16[1,1,512,128]{3,2,1,0:T(8,128)(2,1)S(1)}, bf16[1,1,512,128]{3,2,1,0:T(8,128)(2,1)}, u32[]{:S(2)}) copy-start(bf16[1,1,512,128]{3,2,1,0:T(8,128)(2,1)} %param.10) | copy-start | bytes 393220
  2.3 7.4 %copy-start.5 = (bf16[272,128]{1,0:T(8,128)(2,1)S(1)}, bf16[272,128]{1,0:T(8,128)(2,1)}, u32[]{:S(2)}) copy-start(bf16[272,128]{1,0:T(8,128)(2,1)} %get-tuple-element.61.send_2) | copy-start | bytes 208900
  2.3 7.4 %copy-start.6 = (bf16[272,128]{1,0:T(8,128)(2,1)S(1)}, bf16[272,128]{1,0:T(8,128)(2,1)}, u32[]{:S(2)}) copy-start(bf16[272,128]{1,0:T(8,128)(2,1)} %get-tuple-element.60.send_1) | copy-start | bytes 208900
  2.3 7.4 %copy-start.7 = (bf16[272,128]{1,0:T(8,128)(2,1)S(1)}, bf16[272,128]{1,0:T(8,128)(2,1)}, u32[]{:S(2)}) copy-start(bf16[272,128]{1,0:T(8,128)(2,1)} %get-tuple-element.62.send_3) | copy-start | bytes 208900
  2.3 7.4 %copy-start.8 = (bf16[272,128]{1,0:T(8,128)(2,1)S(1)}, bf16[272,128]{1,0:T(8,128)(2,1)}, u32[]{:S(2)}) copy-start(bf16[272,128]{1,0:T(8,128)(2,1)} %get-tuple-element.59.send_0) | copy-start | bytes 208900
  2.3 9.0 %collective-permute-start.1 = (bf16[272,128]{1,0:T(8,128)(2,1)}, bf16[272,128]{1,0:T(8,128)(2,1)S(1)}, u32[]{:S(2)}, u32[]{:S(2)}) collective-permute-start(bf16[272,128]{1,0:T(8,128)(2,1)} %get-tuple-element.59.send_0), channel_id=1, source_target_pairs={{1,2},{2,1},{3,0},{0,3},{5,6},{6,5},{7,4},{4,7},{9,10},{10,9},{11,... | collective-permute-start | bytes 208904 | tf_op jit(solution)/shard_map/ppermute | solution.py:30
  7.5 5.4 %collective-permute-start.3 = (bf16[272,128]{1,0:T(8,128)(2,1)}, bf16[272,128]{1,0:T(8,128)(2,1)S(1)}, u32[]{:S(2)}, u32[]{:S(2)}) collective-permute-start(bf16[272,128]{1,0:T(8,128)(2,1)} %get-tuple-element.60.send_1), channel_id=1, source_target_pairs={{0,1},{1,0},{2,3},{3,2},{4,5},{5,4},{6,7},{7,6},{8,9},{9,8},{10,11... | collective-permute-start | bytes 208904 | tf_op jit(solution)/shard_map/ppermute | solution.py:30
  7.5 5.5 %collective-permute-start.2 = (bf16[272,128]{1,0:T(8,128)(2,1)}, bf16[272,128]{1,0:T(8,128)(2,1)S(1)}, u32[]{:S(2)}, u32[]{:S(2)}) collective-permute-start(bf16[272,128]{1,0:T(8,128)(2,1)} %get-tuple-element.61.send_2), channel_id=1, source_target_pairs={{4,8},{8,4},{12,16},{16,12},{20,24},{24,20},{28,0},{0,28},{5,9},{9... | collective-permute-start | bytes 208904 | tf_op jit(solution)/shard_map/ppermute | solution.py:30
  9.1 2.3 %collective-permute-start = (bf16[272,128]{1,0:T(8,128)(2,1)}, bf16[272,128]{1,0:T(8,128)(2,1)S(1)}, u32[]{:S(2)}, u32[]{:S(2)}) collective-permute-start(bf16[272,128]{1,0:T(8,128)(2,1)} %get-tuple-element.62.send_3), channel_id=1, source_target_pairs={{0,4},{4,0},{8,12},{12,8},{16,20},{20,16},{24,28},{28,24},{1,5},{5... | collective-permute-start | bytes 208904 | tf_op jit(solution)/shard_map/ppermute | solution.py:30
  9.7 1.7 %copy-start.11 = (s32[1,1,2,256]{3,2,1,0:T(2,128)S(1)}, s32[1,1,2,256]{3,2,1,0:T(2,128)}, u32[]{:S(2)}) copy-start(s32[1,1,2,256]{3,2,1,0:T(2,128)} %param.12) | copy-start | bytes 6148
  9.7 1.7 %copy-start.12 = (s32[1,1,2,256]{3,2,1,0:T(2,128)S(1)}, s32[1,1,2,256]{3,2,1,0:T(2,128)}, u32[]{:S(2)}) copy-start(s32[1,1,2,256]{3,2,1,0:T(2,128)} %param.13) | copy-start | bytes 6148
  9.7 1.7 %copy-start.13 = (bf16[2,16,128]{2,1,0:T(8,128)(2,1)S(1)}, bf16[2,16,128]{2,1,0:T(8,128)(2,1)}, u32[]{:S(2)}) copy-start(bf16[2,16,128]{2,1,0:T(8,128)(2,1)} %get-tuple-element.71.refs_6_.refs_9_) | copy-start | bytes 24580
  11.3 1.6 %copy-start = (bf16[4,256,256]{2,1,0:T(8,128)(2,1)S(1)}, bf16[4,256,256]{2,1,0:T(8,128)(2,1)}, u32[]{:S(2)}) copy-start(bf16[4,256,256]{2,1,0:T(8,128)(2,1)} %get-tuple-element.75.refs_12_.refs_16_) | copy-start | bytes 1572868
  11.3 1.6 %copy-start.1 = (bf16[4,256,128]{2,1,0:T(8,128)(2,1)S(1)}, bf16[4,256,128]{2,1,0:T(8,128)(2,1)}, u32[]{:S(2)}) copy-start(bf16[4,256,128]{2,1,0:T(8,128)(2,1)} %get-tuple-element.76.refs_13_.refs_17_) | copy-start | bytes 786436
  15.0 6.8 %collective-permute-start.5 = (bf16[256,128]{1,0:T(8,128)(2,1)S(1)}, bf16[256,128]{1,0:T(8,128)(2,1)S(1)}, u32[]{:S(2)}, u32[]{:S(2)}) collective-permute-start(bf16[256,128]{1,0:T(8,128)(2,1)S(1)} %get-tuple-element.78.send_0), channel_id=1, source_target_pairs={{1,2},{2,1},{3,0},{0,3},{5,6},{6,5},{7,4},{4,7},{9,10},{10,9},{11,... | collective-permute-start | bytes 196616 | tf_op jit(solution)/shard_map/ppermute | solution.py:30
  17.8 5.1 %collective-permute-start.7 = (bf16[256,128]{1,0:T(8,128)(2,1)S(1)}, bf16[256,128]{1,0:T(8,128)(2,1)S(1)}, u32[]{:S(2)}, u32[]{:S(2)}) collective-permute-start(bf16[256,128]{1,0:T(8,128)(2,1)S(1)} %get-tuple-element.79.send_1), channel_id=1, source_target_pairs={{0,1},{1,0},{2,3},{3,2},{4,5},{5,4},{6,7},{7,6},{8,9},{9,8},{10,11... | collective-permute-start | bytes 196616 | tf_op jit(solution)/shard_map/ppermute | solution.py:30
  17.8 5.2 %collective-permute-start.6 = (bf16[256,128]{1,0:T(8,128)(2,1)S(1)}, bf16[256,128]{1,0:T(8,128)(2,1)S(1)}, u32[]{:S(2)}, u32[]{:S(2)}) collective-permute-start(bf16[256,128]{1,0:T(8,128)(2,1)S(1)} %get-tuple-element.80.send_2), channel_id=1, source_target_pairs={{4,8},{8,4},{12,16},{16,12},{20,24},{24,20},{28,0},{0,28},{5,9},{9... | collective-permute-start | bytes 196616 | tf_op jit(solution)/shard_map/ppermute | solution.py:30
  18.0 3.8 %collective-permute-start.4 = (bf16[256,128]{1,0:T(8,128)(2,1)S(1)}, bf16[256,128]{1,0:T(8,128)(2,1)S(1)}, u32[]{:S(2)}, u32[]{:S(2)}) collective-permute-start(bf16[256,128]{1,0:T(8,128)(2,1)S(1)} %get-tuple-element.81.send_3), channel_id=1, source_target_pairs={{0,4},{4,0},{8,12},{12,8},{16,20},{20,16},{24,28},{28,24},{1,5},{5... | collective-permute-start | bytes 196616 | tf_op jit(solution)/shard_map/ppermute | solution.py:30
  24.7 6.5 %collective-permute-start.9 = (bf16[256,128]{1,0:T(8,128)(2,1)S(1)}, bf16[256,128]{1,0:T(8,128)(2,1)S(1)}, u32[]{:S(2)}, u32[]{:S(2)}) collective-permute-start(bf16[256,128]{1,0:T(8,128)(2,1)S(1)} %get-tuple-element.98.send_0), channel_id=1, source_target_pairs={{1,2},{2,1},{3,0},{0,3},{5,6},{6,5},{7,4},{4,7},{9,10},{10,9},{11,... | collective-permute-start | bytes 196616 | tf_op jit(solution)/shard_map/ppermute | solution.py:30
  26.9 5.5 %collective-permute-start.11 = (bf16[256,128]{1,0:T(8,128)(2,1)S(1)}, bf16[256,128]{1,0:T(8,128)(2,1)S(1)}, u32[]{:S(2)}, u32[]{:S(2)}) collective-permute-start(bf16[256,128]{1,0:T(8,128)(2,1)S(1)} %get-tuple-element.99.send_1), channel_id=1, source_target_pairs={{0,1},{1,0},{2,3},{3,2},{4,5},{5,4},{6,7},{7,6},{8,9},{9,8},{10,11... | collective-permute-start | bytes 196616 | tf_op jit(solution)/shard_map/ppermute | solution.py:30
  26.9 5.5 %collective-permute-start.10 = (bf16[256,128]{1,0:T(8,128)(2,1)S(1)}, bf16[256,128]{1,0:T(8,128)(2,1)S(1)}, u32[]{:S(2)}, u32[]{:S(2)}) collective-permute-start(bf16[256,128]{1,0:T(8,128)(2,1)S(1)} %get-tuple-element.100.send_2), channel_id=1, source_target_pairs={{4,8},{8,4},{12,16},{16,12},{20,24},{24,20},{28,0},{0,28},{5,9},{9... | collective-permute-start | bytes 196616 | tf_op jit(solution)/shard_map/ppermute | solution.py:30
  27.5 3.7 %collective-permute-start.8 = (bf16[256,128]{1,0:T(8,128)(2,1)S(1)}, bf16[256,128]{1,0:T(8,128)(2,1)S(1)}, u32[]{:S(2)}, u32[]{:S(2)}) collective-permute-start(bf16[256,128]{1,0:T(8,128)(2,1)S(1)} %get-tuple-element.101.send_3), channel_id=1, source_target_pairs={{0,4},{4,0},{8,12},{12,8},{16,20},{20,16},{24,28},{28,24},{1,5},{5... | collective-permute-start | bytes 196616 | tf_op jit(solution)/shard_map/ppermute | solution.py:30
  34.1 6.3 %collective-permute-start.13 = (bf16[256,128]{1,0:T(8,128)(2,1)S(1)}, bf16[256,128]{1,0:T(8,128)(2,1)S(1)}, u32[]{:S(2)}, u32[]{:S(2)}) collective-permute-start(bf16[256,128]{1,0:T(8,128)(2,1)S(1)} %get-tuple-element.106.send_0), channel_id=1, source_target_pairs={{1,2},{2,1},{3,0},{0,3},{5,6},{6,5},{7,4},{4,7},{9,10},{10,9},{11,... | collective-permute-start | bytes 196616 | tf_op jit(solution)/shard_map/ppermute | solution.py:30
  36.4 5.2 %collective-permute-start.15 = (bf16[256,128]{1,0:T(8,128)(2,1)S(1)}, bf16[256,128]{1,0:T(8,128)(2,1)S(1)}, u32[]{:S(2)}, u32[]{:S(2)}) collective-permute-start(bf16[256,128]{1,0:T(8,128)(2,1)S(1)} %get-tuple-element.107.send_1), channel_id=1, source_target_pairs={{0,1},{1,0},{2,3},{3,2},{4,5},{5,4},{6,7},{7,6},{8,9},{9,8},{10,11... | collective-permute-start | bytes 196616 | tf_op jit(solution)/shard_map/ppermute | solution.py:30
  36.7 5.0 %collective-permute-start.14 = (bf16[256,128]{1,0:T(8,128)(2,1)S(1)}, bf16[256,128]{1,0:T(8,128)(2,1)S(1)}, u32[]{:S(2)}, u32[]{:S(2)}) collective-permute-start(bf16[256,128]{1,0:T(8,128)(2,1)S(1)} %get-tuple-element.108.send_2), channel_id=1, source_target_pairs={{4,8},{8,4},{12,16},{16,12},{20,24},{24,20},{28,0},{0,28},{5,9},{9... | collective-permute-start | bytes 196616 | tf_op jit(solution)/shard_map/ppermute | solution.py:30
  37.5 3.0 %collective-permute-start.12 = (bf16[256,128]{1,0:T(8,128)(2,1)S(1)}, bf16[256,128]{1,0:T(8,128)(2,1)S(1)}, u32[]{:S(2)}, u32[]{:S(2)}) collective-permute-start(bf16[256,128]{1,0:T(8,128)(2,1)S(1)} %get-tuple-element.109.send_3), channel_id=1, source_target_pairs={{0,4},{4,0},{8,12},{12,8},{16,20},{20,16},{24,28},{28,24},{1,5},{5... | collective-permute-start | bytes 196616 | tf_op jit(solution)/shard_map/ppermute | solution.py:30

commit v8 on v7

--- a/solution.py
+++ b/solution.py
@@ -16,8 +16,8 @@
 CUT = 128
 
 NEAR_X, FAR_X, NEAR_Y, FAR_Y = range(4)
-ORDER = (FAR_Y, NEAR_Y, FAR_X, NEAR_X)
-VISITS = ((NEAR_X, FAR_Y), (FAR_X, NEAR_Y))
+ORDER = (NEAR_Y, FAR_Y, FAR_X, NEAR_X)
+VISITS = ((NEAR_X, NEAR_Y), (FAR_X, FAR_Y))
 PLACE = tuple(ORDER.index(link) for link in range(4))
 
 
@@ -30,13 +30,15 @@
     return lax.ppermute(block, axis, route)
 
 
-def call(kernel, outs, operands, in_specs=None, scratch=(), name=None, grant=40 << 20):
+def call(
+    kernel, outs, operands, in_specs=None, out_specs=None, scratch=(), name=None, grant=40 << 20
+):
     moved = sum(o.size * o.dtype.itemsize for o in operands)
     return pl.pallas_call(
         kernel,
         out_shape=outs,
         in_specs=in_specs or [VMEM] * len(operands),
-        out_specs=[VMEM] * len(outs),
+        out_specs=out_specs or [VMEM] * len(outs),
         scratch_shapes=list(scratch),
         compiler_params=pltpu.CompilerParams(vmem_limit_bytes=grant),
         cost_estimate=pl.CostEstimate(flops=1 << 30, bytes_accessed=moved, transcendentals=0),
@@ -108,6 +110,7 @@
 
 def first_kernel(
     latent_hbm, tops_hbm, bottoms_hbm, etop_hbm, ebot_hbm, live_hbm,
+    out_0, out_1, out_2, out_3, out_pick, out_pick_mask, out_ends,
     send_0, send_1, send_2, send_3, pick_ref, pick_mask_ref, ends_ref,
     latent_ref, tops_ref, bottoms_ref, etop_ref, ebot_ref, live_ref, sems,
 ):
@@ -116,12 +119,16 @@
         for i, (src, dst) in enumerate((
             (tops_hbm, tops_ref), (bottoms_hbm, bottoms_ref), (latent_hbm, latent_ref),
             (etop_hbm, etop_ref), (ebot_hbm, ebot_ref), (live_hbm, live_ref),
+            (pick_ref, out_pick), (pick_mask_ref, out_pick_mask),
+            (send_0, out_0), (send_1, out_1), (send_2, out_2), (send_3, out_3),
+            (ends_ref, out_ends),
         ))
     ]
-    for move in moves:
+    for move in moves[:6]:
         move.start()
     half = latent_ref.shape[0] // 2
     width = latent_ref.shape[1]
+    sends = (send_0, send_1, send_2, send_3)
     moves[0].wait()
     moves[1].wait()
     for face in range(4):
@@ -129,9 +136,10 @@
         bit, low = cut(ref[d : d + 1, :], half)
         pick_ref[face] = column_one_hot(low, half).T
         pick_mask_ref[face] = column_mask(bit, width)
-    for move in moves[2:]:
+    for move in moves[2:6]:
         move.wait()
-    sends = (send_0, send_1, send_2, send_3)
+    for move in moves[6:8]:
+        move.start()
     pick_faces(latent_ref[...], pick_ref, pick_mask_ref, sends)
     faces = tops_ref.shape[1]
     slots = etop_ref.shape[1]
@@ -145,6 +153,10 @@
         ends_ref[d] = ends
         sends[PLACE[2 * d]][faces:, :] = ends
         sends[PLACE[2 * d + 1]][faces:, :] = ends
+    for move in moves[8:]:
+        move.start()
+    for move in moves[6:]:
+        move.wait()
 
 
 def unpacked(ends):
@@ -392,10 +404,13 @@
         + [like((4, faces, half), BF), like((4, faces, width), BF), like((2, lines, width), BF)],
         (latent_now, tops, bottoms, etop, ebot, live),
         in_specs=[HBM] * 6,
-        scratch=[
+        out_specs=[HBM] * 7,
+        scratch=[pltpu.VMEM(packed.shape, BF)] * 4 + [
+            pltpu.VMEM((4, faces, half), BF), pltpu.VMEM((4, faces, width), BF),
+            pltpu.VMEM((2, lines, width), BF),
             pltpu.VMEM((rows, width), BF), pltpu.VMEM(tops.shape, I32),
             pltpu.VMEM(tops.shape, I32), pltpu.VMEM(etop.shape, I32), pltpu.VMEM(etop.shape, I32),
-            pltpu.SMEM(live.shape, I32), pltpu.SemaphoreType.DMA((6,)),
+            pltpu.SMEM(live.shape, I32), pltpu.SemaphoreType.DMA((13,)),
         ],
         name="first",
         grant=54 << 20,

time: 44 us -> 43.2 us (0.982)
  transfers between devices with their start and end apart: 16 -> 16, of which waited for: 4 -> 2; matrix products, arithmetic and copies ran while one was open for 0% -> 0% of each run, Pallas kernels for 31% -> 31%
where the time goes in v8:
time: 43.2 us; the launch traced here: 43 us
  Pallas kernels  23.4 us (54%)
  starting transfers between devices  18.7 us (43%)
  waiting for transfers between devices  0.55 us (1%)
    pallas_call x14, Pallas kernels, call(): pl.pallas_call(kernel, out_shape=outs, in_specs=in_specs or [VMEM] * len(...  23.4 us
    ppermute x16, starting transfers between devices, swapped(): return lax.ppermute(block, axis, route)  18.7 us
  transfers between devices with their start and end apart: 16, of which 2 were waited for; matrix products, arithmetic and copies ran while one was open for 0% of the time, Pallas kernels for 31%

profile of v8, /device:TPU:0, one launch (start us, length us, event | category | flops | bytes accessed | tf_op | source)
XLA Modules:
  0.0 43.0 jit_solution(17827112003142999123)
XLA Ops:
  0.0 2.2 %first.1 = (bf16[272,128]{1,0:T(8,128)(2,1)}, bf16[272,128]{1,0:T(8,128)(2,1)}, bf16[272,128]{1,0:T(8,128)(2,1)}, bf16[272,128]{1,0:T(8,128)(2,1)}, bf16[4,256,2...) custom-call(bf16[512,128]{1,0:T(8,128)(2,1)} %bitcast.9, s32[2,256]{1,0:T(2,128)} %bitcast.14, ...), custom_call_target="tpu_custom_call" | custom-call | flops 1073741824 | bytes 151560 | tf_op jit(solution)/shard_map/first/pallas_call | solution.py:37
  2.2 3.1 %collective-permute-start.1 = (bf16[272,128]{1,0:T(8,128)(2,1)}, bf16[272,128]{1,0:T(8,128)(2,1)S(1)}, u32[]{:S(2)}, u32[]{:S(2)}) collective-permute-start(bf16[272,128]{1,0:T(8,128)(2,1)} %get-tuple-element.59.send_0), channel_id=1, source_target_pairs={{0,1},{1,0},{2,3},{3,2},{4,5},{5,4},{6,7},{7,6},{8,9},{9,8},{10,11... | collective-permute-start | bytes 208904 | tf_op jit(solution)/shard_map/ppermute | solution.py:30
  5.3 2.5 %collective-permute-start.3 = (bf16[272,128]{1,0:T(8,128)(2,1)}, bf16[272,128]{1,0:T(8,128)(2,1)S(1)}, u32[]{:S(2)}, u32[]{:S(2)}) collective-permute-start(bf16[272,128]{1,0:T(8,128)(2,1)} %get-tuple-element.60.send_1), channel_id=1, source_target_pairs={{1,2},{2,1},{3,0},{0,3},{5,6},{6,5},{7,4},{4,7},{9,10},{10,9},{11,... | collective-permute-start | bytes 208904 | tf_op jit(solution)/shard_map/ppermute | solution.py:30
  7.8 1.3 %collective-permute-start.2 = (bf16[272,128]{1,0:T(8,128)(2,1)}, bf16[272,128]{1,0:T(8,128)(2,1)S(1)}, u32[]{:S(2)}, u32[]{:S(2)}) collective-permute-start(bf16[272,128]{1,0:T(8,128)(2,1)} %get-tuple-element.61.send_2), channel_id=1, source_target_pairs={{4,8},{8,4},{12,16},{16,12},{20,24},{24,20},{28,0},{0,28},{5,9},{9... | collective-permute-start | bytes 208904 | tf_op jit(solution)/shard_map/ppermute | solution.py:30
  9.1 0.3 collective-permute-start
  9.4 0.6 %setup.1 = (bf16[2048,256]{1,0:T(8,128)(2,1)S(1)}, bf16[256,2048]{1,0:T(8,128)(2,1)S(1)}, bf16[2048,128]{1,0:T(8,128)(2,1)S(1)}, bf16[4,2,128,128]{3,2,1,0:T(8,1...) custom-call(s32[4,512]{1,0:T(4,128)S(1)} %bitcast.12, ...), custom_call_target="tpu_custom_call" | custom-call | flops 1073741824 | bytes 931840 | tf_op jit(solution)/shard_map/setup/pallas_call | solution.py:37
  10.1 1.6 %inner.4 = (f32[512,128]{1,0:T(8,128)S(1)}, bf16[4,256,128]{2,1,0:T(8,128)(2,1)S(1)}) custom-call(bf16[512,128]{1,0:T(8,128)(2,1)S(1)} %bitcast.10, bf16[272,128]{1,0:T(8,128)(2,1)S(1)} %copy-done.8, bf16[272,128]{1,0:T(8,128)(2,1)S(1)} %copy-done.6, bf16[272,128]{1,0:T(8,128)(2,1)S(1)} %copy-done.5, bf16[272,128]{1,0:T(8,128)(2,1)S(1)} %copy-done.7, ...), custom_call_target="tpu_custom_call" | custom-call | flops 1073741824 | bytes 3823616 | tf_op jit(solution)/shard_map/inner/pallas_call | solution.py:37
  11.7 1.5 %cross.4 = (f32[512,128]{1,0:T(8,128)S(1)}, bf16[1024,512]{1,0:T(8,128)(2,1)S(1)}, bf16[256,1024]{1,0:T(8,128)(2,1)S(1)}, bf16[1024,128]{1,0:T(8,128)(2,1)S(1)},...) custom-call(f32[512,128]{1,0:T(8,128)S(1)} %get-tuple-element.69.total_ref, ...), custom_call_target="tpu_custom_call" | custom-call | flops 1073741824 | bytes 1468416 | tf_op jit(solution)/shard_map/cross/pallas_call | solution.py:37
  13.2 0.1 collective-permute-done.2.refs_0_
  13.3 2.1 %update.4 = (bf16[512,128]{1,0:T(8,128)(2,1)S(1)}, bf16[256,128]{1,0:T(8,128)(2,1)S(1)}, bf16[256,128]{1,0:T(8,128)(2,1)S(1)}, bf16[256,128]{1,0:T(8,128)(2,1)S(...) custom-call(f32[512,128]{1,0:T(8,128)S(1)} %get-tuple-element.72.tot, ...), custom_call_target="tpu_custom_call" | custom-call | flops 1073741824 | bytes 2779136 | tf_op jit(solution)/shard_map/update/pallas_call | solution.py:37
  15.4 0.7 %collective-permute-start.5 = (bf16[256,128]{1,0:T(8,128)(2,1)S(1)}, bf16[256,128]{1,0:T(8,128)(2,1)S(1)}, u32[]{:S(2)}, u32[]{:S(2)}) collective-permute-start(bf16[256,128]{1,0:T(8,128)(2,1)S(1)} %get-tuple-element.78.send_0), channel_id=1, source_target_pairs={{0,1},{1,0},{2,3},{3,2},{4,5},{5,4},{6,7},{7,6},{8,9},{9,8},{10,11... | collective-permute-start | bytes 196616 | tf_op jit(solution)/shard_map/ppermute | solution.py:30
  16.1 0.9 %collective-permute-start.7 = (bf16[256,128]{1,0:T(8,128)(2,1)S(1)}, bf16[256,128]{1,0:T(8,128)(2,1)S(1)}, u32[]{:S(2)}, u32[]{:S(2)}) collective-permute-start(bf16[256,128]{1,0:T(8,128)(2,1)S(1)} %get-tuple-element.79.send_1), channel_id=1, source_target_pairs={{1,2},{2,1},{3,0},{0,3},{5,6},{6,5},{7,4},{4,7},{9,10},{10,9},{11,... | collective-permute-start | bytes 196616 | tf_op jit(solution)/shard_map/ppermute | solution.py:30
  17.0 0.9 %collective-permute-start.6 = (bf16[256,128]{1,0:T(8,128)(2,1)S(1)}, bf16[256,128]{1,0:T(8,128)(2,1)S(1)}, u32[]{:S(2)}, u32[]{:S(2)}) collective-permute-start(bf16[256,128]{1,0:T(8,128)(2,1)S(1)} %get-tuple-element.80.send_2), channel_id=1, source_target_pairs={{4,8},{8,4},{12,16},{16,12},{20,24},{24,20},{28,0},{0,28},{5,9},{9... | collective-permute-start | bytes 196616 | tf_op jit(solution)/shard_map/ppermute | solution.py:30
  17.9 0.7 %collective-permute-start.4 = (bf16[256,128]{1,0:T(8,128)(2,1)S(1)}, bf16[256,128]{1,0:T(8,128)(2,1)S(1)}, u32[]{:S(2)}, u32[]{:S(2)}) collective-permute-start(bf16[256,128]{1,0:T(8,128)(2,1)S(1)} %get-tuple-element.81.send_3), channel_id=1, source_target_pairs={{0,4},{4,0},{8,12},{12,8},{16,20},{20,16},{24,28},{28,24},{1,5},{5... | collective-permute-start | bytes 196616 | tf_op jit(solution)/shard_map/ppermute | solution.py:30
  18.6 2.1 %inner.5 = (f32[512,128]{1,0:T(8,128)S(1)}, bf16[4,256,128]{2,1,0:T(8,128)(2,1)S(1)}, f32[4,1024,128]{2,1,0:T(8,128)S(1)}) custom-call(bf16[512,128]{1,0:T(8,128)(2,1)S(1)} %get-tuple-element.77.latent_ref.refs_7_, bf16[256,128]{1,0:T(8,128)(2,1)S(1)} %get-tuple-element.78.send_0, bf16[256,128]{1,0:T(8,128)(2,1)S(1)} %get-tuple-element.79.send_1, ...), custom_call_target="tpu_custom_call" | custom-call | flops 1073741824 | bytes 8001536 | tf_op jit(solution)/shard_map/inner/pallas_call | solution.py:37
  20.7 1.1 %cross.5.total_ref = f32[512,128]{1,0:T(8,128)S(1)} custom-call(f32[512,128]{1,0:T(8,128)S(1)} %get-tuple-element.86.total_ref, bf16[256,128]{1,0:T(8,128)(2,1)S(1)} %collective-permute-done.4.refs_0_, bf16[256,128]{1,0:T(8,128)(2,1)S(1)} %collective-permute-done.5.refs_1_, bf16[4,2,128,128]{3,2,1,0:T(8,128)(2,1)S(1)} %get-tuple-element.63.ends_w_ref.refs_2_, ...), custom_call_target="tpu_custom_call" | custom-call | flops 1073741824 | bytes 7215104 | tf_op jit(solution)/shard_map/cross/pallas_call | solution.py:37
  21.8 0.4 collective-permute-done.7.refs_1_
  22.2 1.8 %update.5 = (bf16[512,128]{1,0:T(8,128)(2,1)S(1)}, bf16[256,128]{1,0:T(8,128)(2,1)S(1)}, bf16[256,128]{1,0:T(8,128)(2,1)S(1)}, bf16[256,128]{1,0:T(8,128)(2,1)S(1)}, bf16[256,128]{1,0:T(8,128)(2,1)S(1)}) custom-call(f32[512,128]{1,0:T(8,128)S(1)} %cross.5.total_ref, bf16[256,128]{1,0:T(8,128)(2,1)S(1)} %collective-permute-done.6.refs_0_, ...), custom_call_target="tpu_custom_call" | custom-call | flops 1073741824 | bytes 8525824 | tf_op jit(solution)/shard_map/update/pallas_call | solution.py:37
  24.0 0.9 %collective-permute-start.9 = (bf16[256,128]{1,0:T(8,128)(2,1)S(1)}, bf16[256,128]{1,0:T(8,128)(2,1)S(1)}, u32[]{:S(2)}, u32[]{:S(2)}) collective-permute-start(bf16[256,128]{1,0:T(8,128)(2,1)S(1)} %get-tuple-element.98.send_0), channel_id=1, source_target_pairs={{0,1},{1,0},{2,3},{3,2},{4,5},{5,4},{6,7},{7,6},{8,9},{9,8},{10,11... | collective-permute-start | bytes 196616 | tf_op jit(solution)/shard_map/ppermute | solution.py:30
  24.9 2.2 %collective-permute-start.11 = (bf16[256,128]{1,0:T(8,128)(2,1)S(1)}, bf16[256,128]{1,0:T(8,128)(2,1)S(1)}, u32[]{:S(2)}, u32[]{:S(2)}) collective-permute-start(bf16[256,128]{1,0:T(8,128)(2,1)S(1)} %get-tuple-element.99.send_1), channel_id=1, source_target_pairs={{1,2},{2,1},{3,0},{0,3},{5,6},{6,5},{7,4},{4,7},{9,10},{10,9},{11,... | collective-permute-start | bytes 196616 | tf_op jit(solution)/shard_map/ppermute | solution.py:30
  27.1 0.5 %collective-permute-start.10 = (bf16[256,128]{1,0:T(8,128)(2,1)S(1)}, bf16[256,128]{1,0:T(8,128)(2,1)S(1)}, u32[]{:S(2)}, u32[]{:S(2)}) collective-permute-start(bf16[256,128]{1,0:T(8,128)(2,1)S(1)} %get-tuple-element.100.send_2), channel_id=1, source_target_pairs={{4,8},{8,4},{12,16},{16,12},{20,24},{24,20},{28,0},{0,28},{5,9},{9... | collective-permute-start | bytes 196616 | tf_op jit(solution)/shard_map/ppermute | solution.py:30
  27.6 1.1 %collective-permute-start.8 = (bf16[256,128]{1,0:T(8,128)(2,1)S(1)}, bf16[256,128]{1,0:T(8,128)(2,1)S(1)}, u32[]{:S(2)}, u32[]{:S(2)}) collective-permute-start(bf16[256,128]{1,0:T(8,128)(2,1)S(1)} %get-tuple-element.101.send_3), channel_id=1, source_target_pairs={{0,4},{4,0},{8,12},{12,8},{16,20},{20,16},{24,28},{28,24},{1,5},{5... | collective-permute-start | bytes 196616 | tf_op jit(solution)/shard_map/ppermute | solution.py:30
  28.7 2.3 %inner.6 = (f32[512,128]{1,0:T(8,128)S(1)}, bf16[4,256,128]{2,1,0:T(8,128)(2,1)S(1)}, f32[4,1024,128]{2,1,0:T(8,128)S(1)}) custom-call(bf16[512,128]{1,0:T(8,128)(2,1)S(1)} %get-tuple-element.97.latent_ref.refs_7_, bf16[256,128]{1,0:T(8,128)(2,1)S(1)} %get-tuple-element.98.send_0, bf16[256,128]{1,0:T(8,128)(2,1)S(1)} %get-tuple-element.99.send_1, ...), custom_call_target="tpu_custom_call" | custom-call | flops 1073741824 | bytes 8001536 | tf_op jit(solution)/shard_map/inner/pallas_call | solution.py:37
  31.0 1.1 %cross.6.total_ref = f32[512,128]{1,0:T(8,128)S(1)} custom-call(f32[512,128]{1,0:T(8,128)S(1)} %get-tuple-element.102.total_ref, bf16[256,128]{1,0:T(8,128)(2,1)S(1)} %collective-permute-done.8.refs_0_, bf16[256,128]{1,0:T(8,128)(2,1)S(1)} %collective-permute-done.9.refs_1_, bf16[4,2,128,128]{3,2,1,0:T(8,128)(2,1)S(1)} %get-tuple-element.63.ends_w_ref.refs_2_, ...), custom_call_target="tpu_custom_call" | custom-call | flops 1073741824 | bytes 7215104 | tf_op jit(solution)/shard_map/cross/pallas_call | solution.py:37
  32.2 1.8 %update.6 = (bf16[512,128]{1,0:T(8,128)(2,1)S(1)}, bf16[256,128]{1,0:T(8,128)(2,1)S(1)}, bf16[256,128]{1,0:T(8,128)(2,1)S(1)}, bf16[256,128]{1,0:T(8,128)(2,1)S(1)}, bf16[256,128]{1,0:T(8,128)(2,1)S(1)}) custom-call(f32[512,128]{1,0:T(8,128)S(1)} %cross.6.total_ref, bf16[256,128]{1,0:T(8,128)(2,1)S(1)} %collective-permute-done.10.refs_0_, ...), custom_call_target="tpu_custom_call" | custom-call | flops 1073741824 | bytes 8525824 | tf_op jit(solution)/shard_map/update/pallas_call | solution.py:37
  34.0 0.7 %collective-permute-start.13 = (bf16[256,128]{1,0:T(8,128)(2,1)S(1)}, bf16[256,128]{1,0:T(8,128)(2,1)S(1)}, u32[]{:S(2)}, u32[]{:S(2)}) collective-permute-start(bf16[256,128]{1,0:T(8,128)(2,1)S(1)} %get-tuple-element.106.send_0), channel_id=1, source_target_pairs={{0,1},{1,0},{2,3},{3,2},{4,5},{5,4},{6,7},{7,6},{8,9},{9,8},{10,11... | collective-permute-start | bytes 196616 | tf_op jit(solution)/shard_map/ppermute | solution.py:30
  34.7 1.3 %collective-permute-start.15 = (bf16[256,128]{1,0:T(8,128)(2,1)S(1)}, bf16[256,128]{1,0:T(8,128)(2,1)S(1)}, u32[]{:S(2)}, u32[]{:S(2)}) collective-permute-start(bf16[256,128]{1,0:T(8,128)(2,1)S(1)} %get-tuple-element.107.send_1), channel_id=1, source_target_pairs={{1,2},{2,1},{3,0},{0,3},{5,6},{6,5},{7,4},{4,7},{9,10},{10,9},{11,... | collective-permute-start | bytes 196616 | tf_op jit(solution)/shard_map/ppermute | solution.py:30
  36.0 0.5 %collective-permute-start.14 = (bf16[256,128]{1,0:T(8,128)(2,1)S(1)}, bf16[256,128]{1,0:T(8,128)(2,1)S(1)}, u32[]{:S(2)}, u32[]{:S(2)}) collective-permute-start(bf16[256,128]{1,0:T(8,128)(2,1)S(1)} %get-tuple-element.108.send_2), channel_id=1, source_target_pairs={{4,8},{8,4},{12,16},{16,12},{20,24},{24,20},{28,0},{0,28},{5,9},{9... | collective-permute-start | bytes 196616 | tf_op jit(solution)/shard_map/ppermute | solution.py:30
  36.5 1.1 %collective-permute-start.12 = (bf16[256,128]{1,0:T(8,128)(2,1)S(1)}, bf16[256,128]{1,0:T(8,128)(2,1)S(1)}, u32[]{:S(2)}, u32[]{:S(2)}) collective-permute-start(bf16[256,128]{1,0:T(8,128)(2,1)S(1)} %get-tuple-element.109.send_3), channel_id=1, source_target_pairs={{0,4},{4,0},{8,12},{12,8},{16,20},{20,16},{24,28},{28,24},{1,5},{5... | collective-permute-start | bytes 196616 | tf_op jit(solution)/shard_map/ppermute | solution.py:30
  37.6 2.1 %inner.7 = (f32[512,128]{1,0:T(8,128)S(1)}, bf16[4,256,128]{2,1,0:T(8,128)(2,1)S(1)}, f32[4,1024,128]{2,1,0:T(8,128)S(1)}) custom-call(bf16[512,128]{1,0:T(8,128)(2,1)S(1)} %get-tuple-element.105.latent_ref.refs_7_, bf16[256,128]{1,0:T(8,128)(2,1)S(1)} %get-tuple-element.106.send_0, bf16[256,128]{1,0:T(8,128)(2,1)S(1)} %get-tuple-element.107.send_1, ...), custom_call_target="tpu_custom_call" | custom-call | flops 1073741824 | bytes 8001536 | tf_op jit(solution)/shard_map/inner/pallas_call | solution.py:37
  39.7 1.1 %cross.7.total_ref = f32[512,128]{1,0:T(8,128)S(1)} custom-call(f32[512,128]{1,0:T(8,128)S(1)} %get-tuple-element.110.total_ref, bf16[256,128]{1,0:T(8,128)(2,1)S(1)} %collective-permute-done.12.refs_0_, bf16[256,128]{1,0:T(8,128)(2,1)S(1)} %collective-permute-done.13.refs_1_, bf16[4,2,128,128]{3,2,1,0:T(8,128)(2,1)S(1)} %get-tuple-element.63.ends_w_ref.refs_2_, ...), custom_call_target="tpu_custom_call" | custom-call | flops 1073741824 | bytes 7215104 | tf_op jit(solution)/shard_map/cross/pallas_call | solution.py:37
  40.9 2.1 %update.7 = bf16[512,128]{1,0:T(8,128)(2,1)} custom-call(f32[512,128]{1,0:T(8,128)S(1)} %cross.7.total_ref, bf16[256,128]{1,0:T(8,128)(2,1)S(1)} %collective-permute-done.14.refs_0_, bf16[256,128]{1,0:T(8,128)(2,1)S(1)} %collective-permute-done.15.refs_1_, bf16[4,2,128,128]{3,2,1,0:T(8,128)(2,1)S(1)} %get-tuple-element.63.ends_w_ref.refs_2_, ...), custom_call_target="tpu_custom_call" | custom-call | flops 1073741824 | bytes 7739392 | tf_op jit(solution)/shard_map/update/pallas_call | solution.py:37
  (42 shorter events, 0.1 us)
Async XLA Ops:
  0.0 9.4 %copy-start.10 = (f32[4,3,128]{2,0,1:T(4,128)S(1)}, f32[4,3,128]{2,0,1:T(4,128)}, u32[]{:S(2)}) copy-start(f32[4,3,128]{2,0,1:T(4,128)} %param.19) | copy-start | bytes 18436
  0.0 9.4 %copy-start.3 = (bf16[4,3,128,128]{3,2,1,0:T(8,128)(2,1)S(1)}, bf16[4,3,128,128]{3,2,1,0:T(8,128)(2,1)}, u32[]{:S(2)}) copy-start(bf16[4,3,128,128]{3,2,1,0:T(8,128)(2,1)} %nodes_ref.1) | copy-start | bytes 1179652
  0.0 9.4 %copy-start.2 = (bf16[4,4,128,128]{3,2,1,0:T(8,128)(2,1)S(1)}, bf16[4,4,128,128]{3,2,1,0:T(8,128)(2,1)}, u32[]{:S(2)}) copy-start(bf16[4,4,128,128]{3,2,1,0:T(8,128)(2,1)} %weights_ref.1) | copy-start | bytes 1572868
  0.0 9.4 %copy-start.9 = (s32[1,1,4,512]{3,2,1,0:T(4,128)S(1)}, s32[1,1,4,512]{3,2,1,0:T(4,128)}, u32[]{:S(2)}) copy-start(s32[1,1,4,512]{3,2,1,0:T(4,128)} %param.11) | copy-start | bytes 24580
  2.2 7.8 %copy-start.4 = (bf16[1,1,512,128]{3,2,1,0:T(8,128)(2,1)S(1)}, bf16[1,1,512,128]{3,2,1,0:T(8,128)(2,1)}, u32[]{:S(2)}) copy-start(bf16[1,1,512,128]{3,2,1,0:T(8,128)(2,1)} %param.10) | copy-start | bytes 393220
  2.2 7.8 %copy-start.5 = (bf16[272,128]{1,0:T(8,128)(2,1)S(1)}, bf16[272,128]{1,0:T(8,128)(2,1)}, u32[]{:S(2)}) copy-start(bf16[272,128]{1,0:T(8,128)(2,1)} %get-tuple-element.61.send_2) | copy-start | bytes 208900
  2.2 7.8 %copy-start.6 = (bf16[272,128]{1,0:T(8,128)(2,1)S(1)}, bf16[272,128]{1,0:T(8,128)(2,1)}, u32[]{:S(2)}) copy-start(bf16[272,128]{1,0:T(8,128)(2,1)} %get-tuple-element.60.send_1) | copy-start | bytes 208900
  2.2 7.8 %copy-start.7 = (bf16[272,128]{1,0:T(8,128)(2,1)S(1)}, bf16[272,128]{1,0:T(8,128)(2,1)}, u32[]{:S(2)}) copy-start(bf16[272,128]{1,0:T(8,128)(2,1)} %get-tuple-element.62.send_3) | copy-start | bytes 208900
  2.2 7.8 %copy-start.8 = (bf16[272,128]{1,0:T(8,128)(2,1)S(1)}, bf16[272,128]{1,0:T(8,128)(2,1)}, u32[]{:S(2)}) copy-start(bf16[272,128]{1,0:T(8,128)(2,1)} %get-tuple-element.59.send_0) | copy-start | bytes 208900
  2.2 9.5 %collective-permute-start.1 = (bf16[272,128]{1,0:T(8,128)(2,1)}, bf16[272,128]{1,0:T(8,128)(2,1)S(1)}, u32[]{:S(2)}, u32[]{:S(2)}) collective-permute-start(bf16[272,128]{1,0:T(8,128)(2,1)} %get-tuple-element.59.send_0), channel_id=1, source_target_pairs={{0,1},{1,0},{2,3},{3,2},{4,5},{5,4},{6,7},{7,6},{8,9},{9,8},{10,11... | collective-permute-start | bytes 208904 | tf_op jit(solution)/shard_map/ppermute | solution.py:30
  5.3 7.9 %collective-permute-start.3 = (bf16[272,128]{1,0:T(8,128)(2,1)}, bf16[272,128]{1,0:T(8,128)(2,1)S(1)}, u32[]{:S(2)}, u32[]{:S(2)}) collective-permute-start(bf16[272,128]{1,0:T(8,128)(2,1)} %get-tuple-element.60.send_1), channel_id=1, source_target_pairs={{1,2},{2,1},{3,0},{0,3},{5,6},{6,5},{7,4},{4,7},{9,10},{10,9},{11,... | collective-permute-start | bytes 208904 | tf_op jit(solution)/shard_map/ppermute | solution.py:30
  7.8 5.5 %collective-permute-start.2 = (bf16[272,128]{1,0:T(8,128)(2,1)}, bf16[272,128]{1,0:T(8,128)(2,1)S(1)}, u32[]{:S(2)}, u32[]{:S(2)}) collective-permute-start(bf16[272,128]{1,0:T(8,128)(2,1)} %get-tuple-element.61.send_2), channel_id=1, source_target_pairs={{4,8},{8,4},{12,16},{16,12},{20,24},{24,20},{28,0},{0,28},{5,9},{9... | collective-permute-start | bytes 208904 | tf_op jit(solution)/shard_map/ppermute | solution.py:30
  9.1 2.6 %collective-permute-start = (bf16[272,128]{1,0:T(8,128)(2,1)}, bf16[272,128]{1,0:T(8,128)(2,1)S(1)}, u32[]{:S(2)}, u32[]{:S(2)}) collective-permute-start(bf16[272,128]{1,0:T(8,128)(2,1)} %get-tuple-element.62.send_3), channel_id=1, source_target_pairs={{0,4},{4,0},{8,12},{12,8},{16,20},{20,16},{24,28},{28,24},{1,5},{5... | collective-permute-start | bytes 208904 | tf_op jit(solution)/shard_map/ppermute | solution.py:30
  10.0 1.7 %copy-start.11 = (s32[1,1,2,256]{3,2,1,0:T(2,128)S(1)}, s32[1,1,2,256]{3,2,1,0:T(2,128)}, u32[]{:S(2)}) copy-start(s32[1,1,2,256]{3,2,1,0:T(2,128)} %param.12) | copy-start | bytes 6148
  10.0 1.7 %copy-start.12 = (s32[1,1,2,256]{3,2,1,0:T(2,128)S(1)}, s32[1,1,2,256]{3,2,1,0:T(2,128)}, u32[]{:S(2)}) copy-start(s32[1,1,2,256]{3,2,1,0:T(2,128)} %param.13) | copy-start | bytes 6148
  10.0 1.7 %copy-start.13 = (bf16[2,16,128]{2,1,0:T(8,128)(2,1)S(1)}, bf16[2,16,128]{2,1,0:T(8,128)(2,1)}, u32[]{:S(2)}) copy-start(bf16[2,16,128]{2,1,0:T(8,128)(2,1)} %get-tuple-element.71.refs_6_.refs_9_) | copy-start | bytes 24580
  11.7 1.6 %copy-start = (bf16[4,256,256]{2,1,0:T(8,128)(2,1)S(1)}, bf16[4,256,256]{2,1,0:T(8,128)(2,1)}, u32[]{:S(2)}) copy-start(bf16[4,256,256]{2,1,0:T(8,128)(2,1)} %get-tuple-element.75.refs_12_.refs_16_) | copy-start | bytes 1572868
  11.7 1.6 %copy-start.1 = (bf16[4,256,128]{2,1,0:T(8,128)(2,1)S(1)}, bf16[4,256,128]{2,1,0:T(8,128)(2,1)}, u32[]{:S(2)}) copy-start(bf16[4,256,128]{2,1,0:T(8,128)(2,1)} %get-tuple-element.76.refs_13_.refs_17_) | copy-start | bytes 786436
  15.4 5.3 %collective-permute-start.5 = (bf16[256,128]{1,0:T(8,128)(2,1)S(1)}, bf16[256,128]{1,0:T(8,128)(2,1)S(1)}, u32[]{:S(2)}, u32[]{:S(2)}) collective-permute-start(bf16[256,128]{1,0:T(8,128)(2,1)S(1)} %get-tuple-element.78.send_0), channel_id=1, source_target_pairs={{0,1},{1,0},{2,3},{3,2},{4,5},{5,4},{6,7},{7,6},{8,9},{9,8},{10,11... | collective-permute-start | bytes 196616 | tf_op jit(solution)/shard_map/ppermute | solution.py:30
  16.1 6.1 %collective-permute-start.7 = (bf16[256,128]{1,0:T(8,128)(2,1)S(1)}, bf16[256,128]{1,0:T(8,128)(2,1)S(1)}, u32[]{:S(2)}, u32[]{:S(2)}) collective-permute-start(bf16[256,128]{1,0:T(8,128)(2,1)S(1)} %get-tuple-element.79.send_1), channel_id=1, source_target_pairs={{1,2},{2,1},{3,0},{0,3},{5,6},{6,5},{7,4},{4,7},{9,10},{10,9},{11,... | collective-permute-start | bytes 196616 | tf_op jit(solution)/shard_map/ppermute | solution.py:30
  17.0 5.2 %collective-permute-start.6 = (bf16[256,128]{1,0:T(8,128)(2,1)S(1)}, bf16[256,128]{1,0:T(8,128)(2,1)S(1)}, u32[]{:S(2)}, u32[]{:S(2)}) collective-permute-start(bf16[256,128]{1,0:T(8,128)(2,1)S(1)} %get-tuple-element.80.send_2), channel_id=1, source_target_pairs={{4,8},{8,4},{12,16},{16,12},{20,24},{24,20},{28,0},{0,28},{5,9},{9... | collective-permute-start | bytes 196616 | tf_op jit(solution)/shard_map/ppermute | solution.py:30
  17.9 2.8 %collective-permute-start.4 = (bf16[256,128]{1,0:T(8,128)(2,1)S(1)}, bf16[256,128]{1,0:T(8,128)(2,1)S(1)}, u32[]{:S(2)}, u32[]{:S(2)}) collective-permute-start(bf16[256,128]{1,0:T(8,128)(2,1)S(1)} %get-tuple-element.81.send_3), channel_id=1, source_target_pairs={{0,4},{4,0},{8,12},{12,8},{16,20},{20,16},{24,28},{28,24},{1,5},{5... | collective-permute-start | bytes 196616 | tf_op jit(solution)/shard_map/ppermute | solution.py:30
  24.0 7.0 %collective-permute-start.9 = (bf16[256,128]{1,0:T(8,128)(2,1)S(1)}, bf16[256,128]{1,0:T(8,128)(2,1)S(1)}, u32[]{:S(2)}, u32[]{:S(2)}) collective-permute-start(bf16[256,128]{1,0:T(8,128)(2,1)S(1)} %get-tuple-element.98.send_0), channel_id=1, source_target_pairs={{0,1},{1,0},{2,3},{3,2},{4,5},{5,4},{6,7},{7,6},{8,9},{9,8},{10,11... | collective-permute-start | bytes 196616 | tf_op jit(solution)/shard_map/ppermute | solution.py:30
  24.9 7.3 %collective-permute-start.11 = (bf16[256,128]{1,0:T(8,128)(2,1)S(1)}, bf16[256,128]{1,0:T(8,128)(2,1)S(1)}, u32[]{:S(2)}, u32[]{:S(2)}) collective-permute-start(bf16[256,128]{1,0:T(8,128)(2,1)S(1)} %get-tuple-element.99.send_1), channel_id=1, source_target_pairs={{1,2},{2,1},{3,0},{0,3},{5,6},{6,5},{7,4},{4,7},{9,10},{10,9},{11,... | collective-permute-start | bytes 196616 | tf_op jit(solution)/shard_map/ppermute | solution.py:30
  27.1 5.0 %collective-permute-start.10 = (bf16[256,128]{1,0:T(8,128)(2,1)S(1)}, bf16[256,128]{1,0:T(8,128)(2,1)S(1)}, u32[]{:S(2)}, u32[]{:S(2)}) collective-permute-start(bf16[256,128]{1,0:T(8,128)(2,1)S(1)} %get-tuple-element.100.send_2), channel_id=1, source_target_pairs={{4,8},{8,4},{12,16},{16,12},{20,24},{24,20},{28,0},{0,28},{5,9},{9... | collective-permute-start | bytes 196616 | tf_op jit(solution)/shard_map/ppermute | solution.py:30
  27.6 3.4 %collective-permute-start.8 = (bf16[256,128]{1,0:T(8,128)(2,1)S(1)}, bf16[256,128]{1,0:T(8,128)(2,1)S(1)}, u32[]{:S(2)}, u32[]{:S(2)}) collective-permute-start(bf16[256,128]{1,0:T(8,128)(2,1)S(1)} %get-tuple-element.101.send_3), channel_id=1, source_target_pairs={{0,4},{4,0},{8,12},{12,8},{16,20},{20,16},{24,28},{28,24},{1,5},{5... | collective-permute-start | bytes 196616 | tf_op jit(solution)/shard_map/ppermute | solution.py:30
  34.0 5.7 %collective-permute-start.13 = (bf16[256,128]{1,0:T(8,128)(2,1)S(1)}, bf16[256,128]{1,0:T(8,128)(2,1)S(1)}, u32[]{:S(2)}, u32[]{:S(2)}) collective-permute-start(bf16[256,128]{1,0:T(8,128)(2,1)S(1)} %get-tuple-element.106.send_0), channel_id=1, source_target_pairs={{0,1},{1,0},{2,3},{3,2},{4,5},{5,4},{6,7},{7,6},{8,9},{9,8},{10,11... | collective-permute-start | bytes 196616 | tf_op jit(solution)/shard_map/ppermute | solution.py:30
  34.7 6.2 %collective-permute-start.15 = (bf16[256,128]{1,0:T(8,128)(2,1)S(1)}, bf16[256,128]{1,0:T(8,128)(2,1)S(1)}, u32[]{:S(2)}, u32[]{:S(2)}) collective-permute-start(bf16[256,128]{1,0:T(8,128)(2,1)S(1)} %get-tuple-element.107.send_1), channel_id=1, source_target_pairs={{1,2},{2,1},{3,0},{0,3},{5,6},{6,5},{7,4},{4,7},{9,10},{10,9},{11,... | collective-permute-start | bytes 196616 | tf_op jit(solution)/shard_map/ppermute | solution.py:30
  36.0 4.9 %collective-permute-start.14 = (bf16[256,128]{1,0:T(8,128)(2,1)S(1)}, bf16[256,128]{1,0:T(8,128)(2,1)S(1)}, u32[]{:S(2)}, u32[]{:S(2)}) collective-permute-start(bf16[256,128]{1,0:T(8,128)(2,1)S(1)} %get-tuple-element.108.send_2), channel_id=1, source_target_pairs={{4,8},{8,4},{12,16},{16,12},{20,24},{24,20},{28,0},{0,28},{5,9},{9... | collective-permute-start | bytes 196616 | tf_op jit(solution)/shard_map/ppermute | solution.py:30
  36.5 3.2 %collective-permute-start.12 = (bf16[256,128]{1,0:T(8,128)(2,1)S(1)}, bf16[256,128]{1,0:T(8,128)(2,1)S(1)}, u32[]{:S(2)}, u32[]{:S(2)}) collective-permute-start(bf16[256,128]{1,0:T(8,128)(2,1)S(1)} %get-tuple-element.109.send_3), channel_id=1, source_target_pairs={{0,4},{4,0},{8,12},{12,8},{16,20},{20,16},{24,28},{28,24},{1,5},{5... | collective-permute-start | bytes 196616 | tf_op jit(solution)/shard_map/ppermute | solution.py:30

commit v9 on v8

--- a/solution.py
+++ b/solution.py
@@ -356,13 +356,26 @@
     biases_ref = nets[2]
     both = link_sums(step, links, gots, groups, *nets[:4], ahead_ref)
     arrived = total_ref[...] + jnp.concatenate([both[:, :width], both[:, width:]], axis=0)
-    latent = latent_ref[...]
-    joined = jnp.concatenate([latent, arrived.astype(BF)], axis=1)
-    update = half_silu(dot(joined, join_ref[step]) + biases_ref[2, step : step + 1, :]).astype(BF)
-    latent = (latent.astype(F32) + dot(update, out_w_ref[step])).astype(BF)
     if last:
-        rest[0][...] = latent
+        out_hbm, held_ref, sems = rest
+        moves = []
+        for i, a in enumerate((0, half)):
+            here = pl.ds(a, half)
+            old = latent_ref[a : a + half, :]
+            joined = jnp.concatenate([old, arrived[a : a + half].astype(BF)], axis=1)
+            update = half_silu(dot(joined, join_ref[step]) + biases_ref[2, step : step + 1, :])
+            held_ref[a : a + half, :] = (
+                old.astype(F32) + dot(update.astype(BF), out_w_ref[step])
+            ).astype(BF)
+            moves.append(pltpu.make_async_copy(held_ref.at[here], out_hbm.at[here], sems.at[i]))
+            moves[i].start()
+        for move in moves:
+            move.wait()
     else:
+        latent = latent_ref[...]
+        joined = jnp.concatenate([latent, arrived.astype(BF)], axis=1)
+        update = half_silu(dot(joined, join_ref[step]) + biases_ref[2, step : step + 1, :]).astype(BF)
+        latent = (latent.astype(F32) + dot(update, out_w_ref[step])).astype(BF)
         pick_ref, pick_mask_ref, out_ref = rest[:3]
         out_ref[...] = latent
         pick_faces(latent, pick_ref, pick_mask_ref, rest[3:7])
@@ -466,7 +479,13 @@
                 operands += [part for link in links for part in groups[link]]
             if final and not last:
                 operands += [pick, pick_mask]
-            total, *made = call(kernel, outs, operands, name="update" if final else "cross")
+            total, *made = call(
+                kernel, outs, operands,
+                out_specs=[HBM] if final and last else None,
+                scratch=[pltpu.VMEM((rows, width), BF), pltpu.SemaphoreType.DMA((2,))]
+                if final and last else (),
+                name="update" if final else "cross",
+            )
             if starting:
                 for k, link in enumerate(links):
                     groups[link] = made[plain - 1 + 3 * k :][:3]

time: 43.2 us -> 43.4 us (level)
  no operation moved by 1% of the time
where the time goes in v9:
time: 43.4 us; the launch traced here: 43.3 us
  Pallas kernels  23.5 us (54%)
  starting transfers between devices  18.7 us (43%)
  waiting for transfers between devices  0.55 us (1%)
  between operations  0.49 us (1%)
    pallas_call x14, Pallas kernels, call(): pl.pallas_call(kernel, out_shape=outs, in_specs=in_specs or [VMEM] * len(...  23.5 us
    ppermute x16, starting transfers between devices, swapped(): return lax.ppermute(block, axis, route)  18.7 us
  transfers between devices with their start and end apart: 16, of which 2 were waited for; matrix products, arithmetic and copies ran while one was open for 0% of the time, Pallas kernels for 31%

profile of v9, /device:TPU:0, one launch (start us, length us, event | category | flops | bytes accessed | tf_op | source)
XLA Modules:
  0.0 43.3 jit_solution(9805030963975778135)
XLA Ops:
  0.0 2.2 %first.1 = (bf16[272,128]{1,0:T(8,128)(2,1)}, bf16[272,128]{1,0:T(8,128)(2,1)}, bf16[272,128]{1,0:T(8,128)(2,1)}, bf16[272,128]{1,0:T(8,128)(2,1)}, bf16[4,256,2...) custom-call(bf16[512,128]{1,0:T(8,128)(2,1)} %bitcast.9, s32[2,256]{1,0:T(2,128)} %bitcast.14, ...), custom_call_target="tpu_custom_call" | custom-call | flops 1073741824 | bytes 151560 | tf_op jit(solution)/shard_map/first/pallas_call | solution.py:37
  2.2 3.1 %collective-permute-start.1 = (bf16[272,128]{1,0:T(8,128)(2,1)}, bf16[272,128]{1,0:T(8,128)(2,1)S(1)}, u32[]{:S(2)}, u32[]{:S(2)}) collective-permute-start(bf16[272,128]{1,0:T(8,128)(2,1)} %get-tuple-element.59.send_0), channel_id=1, source_target_pairs={{0,1},{1,0},{2,3},{3,2},{4,5},{5,4},{6,7},{7,6},{8,9},{9,8},{10,11... | collective-permute-start | bytes 208904 | tf_op jit(solution)/shard_map/ppermute | solution.py:30
  5.3 2.5 %collective-permute-start.3 = (bf16[272,128]{1,0:T(8,128)(2,1)}, bf16[272,128]{1,0:T(8,128)(2,1)S(1)}, u32[]{:S(2)}, u32[]{:S(2)}) collective-permute-start(bf16[272,128]{1,0:T(8,128)(2,1)} %get-tuple-element.60.send_1), channel_id=1, source_target_pairs={{1,2},{2,1},{3,0},{0,3},{5,6},{6,5},{7,4},{4,7},{9,10},{10,9},{11,... | collective-permute-start | bytes 208904 | tf_op jit(solution)/shard_map/ppermute | solution.py:30
  7.8 1.3 %collective-permute-start.2 = (bf16[272,128]{1,0:T(8,128)(2,1)}, bf16[272,128]{1,0:T(8,128)(2,1)S(1)}, u32[]{:S(2)}, u32[]{:S(2)}) collective-permute-start(bf16[272,128]{1,0:T(8,128)(2,1)} %get-tuple-element.61.send_2), channel_id=1, source_target_pairs={{4,8},{8,4},{12,16},{16,12},{20,24},{24,20},{28,0},{0,28},{5,9},{9... | collective-permute-start | bytes 208904 | tf_op jit(solution)/shard_map/ppermute | solution.py:30
  9.1 0.3 collective-permute-start
  9.4 0.6 %setup.1 = (bf16[2048,256]{1,0:T(8,128)(2,1)S(1)}, bf16[256,2048]{1,0:T(8,128)(2,1)S(1)}, bf16[2048,128]{1,0:T(8,128)(2,1)S(1)}, bf16[4,2,128,128]{3,2,1,0:T(8,1...) custom-call(s32[4,512]{1,0:T(4,128)S(1)} %bitcast.12, ...), custom_call_target="tpu_custom_call" | custom-call | flops 1073741824 | bytes 931840 | tf_op jit(solution)/shard_map/setup/pallas_call | solution.py:37
  10.1 1.6 %inner.4 = (f32[512,128]{1,0:T(8,128)S(1)}, bf16[4,256,128]{2,1,0:T(8,128)(2,1)S(1)}) custom-call(bf16[512,128]{1,0:T(8,128)(2,1)S(1)} %bitcast.10, bf16[272,128]{1,0:T(8,128)(2,1)S(1)} %copy-done.8, bf16[272,128]{1,0:T(8,128)(2,1)S(1)} %copy-done.6, bf16[272,128]{1,0:T(8,128)(2,1)S(1)} %copy-done.5, bf16[272,128]{1,0:T(8,128)(2,1)S(1)} %copy-done.7, ...), custom_call_target="tpu_custom_call" | custom-call | flops 1073741824 | bytes 3823616 | tf_op jit(solution)/shard_map/inner/pallas_call | solution.py:37
  11.7 1.5 %cross.4 = (f32[512,128]{1,0:T(8,128)S(1)}, bf16[1024,512]{1,0:T(8,128)(2,1)S(1)}, bf16[256,1024]{1,0:T(8,128)(2,1)S(1)}, bf16[1024,128]{1,0:T(8,128)(2,1)S(1)},...) custom-call(f32[512,128]{1,0:T(8,128)S(1)} %get-tuple-element.69.total_ref, ...), custom_call_target="tpu_custom_call" | custom-call | flops 1073741824 | bytes 1468416 | tf_op jit(solution)/shard_map/cross/pallas_call | solution.py:37
  13.2 0.1 collective-permute-done.2.refs_0_
  13.3 2.1 %update.4 = (bf16[512,128]{1,0:T(8,128)(2,1)S(1)}, bf16[256,128]{1,0:T(8,128)(2,1)S(1)}, bf16[256,128]{1,0:T(8,128)(2,1)S(1)}, bf16[256,128]{1,0:T(8,128)(2,1)S(...) custom-call(f32[512,128]{1,0:T(8,128)S(1)} %get-tuple-element.72.tot, ...), custom_call_target="tpu_custom_call" | custom-call | flops 1073741824 | bytes 2779136 | tf_op jit(solution)/shard_map/update/pallas_call | solution.py:37
  15.4 0.7 %collective-permute-start.5 = (bf16[256,128]{1,0:T(8,128)(2,1)S(1)}, bf16[256,128]{1,0:T(8,128)(2,1)S(1)}, u32[]{:S(2)}, u32[]{:S(2)}) collective-permute-start(bf16[256,128]{1,0:T(8,128)(2,1)S(1)} %get-tuple-element.78.send_0), channel_id=1, source_target_pairs={{0,1},{1,0},{2,3},{3,2},{4,5},{5,4},{6,7},{7,6},{8,9},{9,8},{10,11... | collective-permute-start | bytes 196616 | tf_op jit(solution)/shard_map/ppermute | solution.py:30
  16.1 0.9 %collective-permute-start.7 = (bf16[256,128]{1,0:T(8,128)(2,1)S(1)}, bf16[256,128]{1,0:T(8,128)(2,1)S(1)}, u32[]{:S(2)}, u32[]{:S(2)}) collective-permute-start(bf16[256,128]{1,0:T(8,128)(2,1)S(1)} %get-tuple-element.79.send_1), channel_id=1, source_target_pairs={{1,2},{2,1},{3,0},{0,3},{5,6},{6,5},{7,4},{4,7},{9,10},{10,9},{11,... | collective-permute-start | bytes 196616 | tf_op jit(solution)/shard_map/ppermute | solution.py:30
  17.0 0.9 %collective-permute-start.6 = (bf16[256,128]{1,0:T(8,128)(2,1)S(1)}, bf16[256,128]{1,0:T(8,128)(2,1)S(1)}, u32[]{:S(2)}, u32[]{:S(2)}) collective-permute-start(bf16[256,128]{1,0:T(8,128)(2,1)S(1)} %get-tuple-element.80.send_2), channel_id=1, source_target_pairs={{4,8},{8,4},{12,16},{16,12},{20,24},{24,20},{28,0},{0,28},{5,9},{9... | collective-permute-start | bytes 196616 | tf_op jit(solution)/shard_map/ppermute | solution.py:30
  17.9 0.7 %collective-permute-start.4 = (bf16[256,128]{1,0:T(8,128)(2,1)S(1)}, bf16[256,128]{1,0:T(8,128)(2,1)S(1)}, u32[]{:S(2)}, u32[]{:S(2)}) collective-permute-start(bf16[256,128]{1,0:T(8,128)(2,1)S(1)} %get-tuple-element.81.send_3), channel_id=1, source_target_pairs={{0,4},{4,0},{8,12},{12,8},{16,20},{20,16},{24,28},{28,24},{1,5},{5... | collective-permute-start | bytes 196616 | tf_op jit(solution)/shard_map/ppermute | solution.py:30
  18.6 2.1 %inner.5 = (f32[512,128]{1,0:T(8,128)S(1)}, bf16[4,256,128]{2,1,0:T(8,128)(2,1)S(1)}, f32[4,1024,128]{2,1,0:T(8,128)S(1)}) custom-call(bf16[512,128]{1,0:T(8,128)(2,1)S(1)} %get-tuple-element.77.latent_ref.refs_7_, bf16[256,128]{1,0:T(8,128)(2,1)S(1)} %get-tuple-element.78.send_0, bf16[256,128]{1,0:T(8,128)(2,1)S(1)} %get-tuple-element.79.send_1, ...), custom_call_target="tpu_custom_call" | custom-call | flops 1073741824 | bytes 8001536 | tf_op jit(solution)/shard_map/inner/pallas_call | solution.py:37
  20.7 1.1 %cross.5.total_ref = f32[512,128]{1,0:T(8,128)S(1)} custom-call(f32[512,128]{1,0:T(8,128)S(1)} %get-tuple-element.86.total_ref, bf16[256,128]{1,0:T(8,128)(2,1)S(1)} %collective-permute-done.4.refs_0_, bf16[256,128]{1,0:T(8,128)(2,1)S(1)} %collective-permute-done.5.refs_1_, bf16[4,2,128,128]{3,2,1,0:T(8,128)(2,1)S(1)} %get-tuple-element.63.ends_w_ref.refs_2_, ...), custom_call_target="tpu_custom_call" | custom-call | flops 1073741824 | bytes 7215104 | tf_op jit(solution)/shard_map/cross/pallas_call | solution.py:37
  21.8 0.4 collective-permute-done.7.refs_1_
  22.2 1.8 %update.5 = (bf16[512,128]{1,0:T(8,128)(2,1)S(1)}, bf16[256,128]{1,0:T(8,128)(2,1)S(1)}, bf16[256,128]{1,0:T(8,128)(2,1)S(1)}, bf16[256,128]{1,0:T(8,128)(2,1)S(1)}, bf16[256,128]{1,0:T(8,128)(2,1)S(1)}) custom-call(f32[512,128]{1,0:T(8,128)S(1)} %cross.5.total_ref, bf16[256,128]{1,0:T(8,128)(2,1)S(1)} %collective-permute-done.6.refs_0_, ...), custom_call_target="tpu_custom_call" | custom-call | flops 1073741824 | bytes 8525824 | tf_op jit(solution)/shard_map/update/pallas_call | solution.py:37
  24.0 0.9 %collective-permute-start.9 = (bf16[256,128]{1,0:T(8,128)(2,1)S(1)}, bf16[256,128]{1,0:T(8,128)(2,1)S(1)}, u32[]{:S(2)}, u32[]{:S(2)}) collective-permute-start(bf16[256,128]{1,0:T(8,128)(2,1)S(1)} %get-tuple-element.98.send_0), channel_id=1, source_target_pairs={{0,1},{1,0},{2,3},{3,2},{4,5},{5,4},{6,7},{7,6},{8,9},{9,8},{10,11... | collective-permute-start | bytes 196616 | tf_op jit(solution)/shard_map/ppermute | solution.py:30
  24.9 2.2 %collective-permute-start.11 = (bf16[256,128]{1,0:T(8,128)(2,1)S(1)}, bf16[256,128]{1,0:T(8,128)(2,1)S(1)}, u32[]{:S(2)}, u32[]{:S(2)}) collective-permute-start(bf16[256,128]{1,0:T(8,128)(2,1)S(1)} %get-tuple-element.99.send_1), channel_id=1, source_target_pairs={{1,2},{2,1},{3,0},{0,3},{5,6},{6,5},{7,4},{4,7},{9,10},{10,9},{11,... | collective-permute-start | bytes 196616 | tf_op jit(solution)/shard_map/ppermute | solution.py:30
  27.1 0.5 %collective-permute-start.10 = (bf16[256,128]{1,0:T(8,128)(2,1)S(1)}, bf16[256,128]{1,0:T(8,128)(2,1)S(1)}, u32[]{:S(2)}, u32[]{:S(2)}) collective-permute-start(bf16[256,128]{1,0:T(8,128)(2,1)S(1)} %get-tuple-element.100.send_2), channel_id=1, source_target_pairs={{4,8},{8,4},{12,16},{16,12},{20,24},{24,20},{28,0},{0,28},{5,9},{9... | collective-permute-start | bytes 196616 | tf_op jit(solution)/shard_map/ppermute | solution.py:30
  27.6 1.1 %collective-permute-start.8 = (bf16[256,128]{1,0:T(8,128)(2,1)S(1)}, bf16[256,128]{1,0:T(8,128)(2,1)S(1)}, u32[]{:S(2)}, u32[]{:S(2)}) collective-permute-start(bf16[256,128]{1,0:T(8,128)(2,1)S(1)} %get-tuple-element.101.send_3), channel_id=1, source_target_pairs={{0,4},{4,0},{8,12},{12,8},{16,20},{20,16},{24,28},{28,24},{1,5},{5... | collective-permute-start | bytes 196616 | tf_op jit(solution)/shard_map/ppermute | solution.py:30
  28.7 2.3 %inner.6 = (f32[512,128]{1,0:T(8,128)S(1)}, bf16[4,256,128]{2,1,0:T(8,128)(2,1)S(1)}, f32[4,1024,128]{2,1,0:T(8,128)S(1)}) custom-call(bf16[512,128]{1,0:T(8,128)(2,1)S(1)} %get-tuple-element.97.latent_ref.refs_7_, bf16[256,128]{1,0:T(8,128)(2,1)S(1)} %get-tuple-element.98.send_0, bf16[256,128]{1,0:T(8,128)(2,1)S(1)} %get-tuple-element.99.send_1, ...), custom_call_target="tpu_custom_call" | custom-call | flops 1073741824 | bytes 8001536 | tf_op jit(solution)/shard_map/inner/pallas_call | solution.py:37
  31.0 1.1 %cross.6.total_ref = f32[512,128]{1,0:T(8,128)S(1)} custom-call(f32[512,128]{1,0:T(8,128)S(1)} %get-tuple-element.102.total_ref, bf16[256,128]{1,0:T(8,128)(2,1)S(1)} %collective-permute-done.8.refs_0_, bf16[256,128]{1,0:T(8,128)(2,1)S(1)} %collective-permute-done.9.refs_1_, bf16[4,2,128,128]{3,2,1,0:T(8,128)(2,1)S(1)} %get-tuple-element.63.ends_w_ref.refs_2_, ...), custom_call_target="tpu_custom_call" | custom-call | flops 1073741824 | bytes 7215104 | tf_op jit(solution)/shard_map/cross/pallas_call | solution.py:37
  32.2 1.8 %update.6 = (bf16[512,128]{1,0:T(8,128)(2,1)S(1)}, bf16[256,128]{1,0:T(8,128)(2,1)S(1)}, bf16[256,128]{1,0:T(8,128)(2,1)S(1)}, bf16[256,128]{1,0:T(8,128)(2,1)S(1)}, bf16[256,128]{1,0:T(8,128)(2,1)S(1)}) custom-call(f32[512,128]{1,0:T(8,128)S(1)} %cross.6.total_ref, bf16[256,128]{1,0:T(8,128)(2,1)S(1)} %collective-permute-done.10.refs_0_, ...), custom_call_target="tpu_custom_call" | custom-call | flops 1073741824 | bytes 8525824 | tf_op jit(solution)/shard_map/update/pallas_call | solution.py:37
  34.0 0.7 %collective-permute-start.13 = (bf16[256,128]{1,0:T(8,128)(2,1)S(1)}, bf16[256,128]{1,0:T(8,128)(2,1)S(1)}, u32[]{:S(2)}, u32[]{:S(2)}) collective-permute-start(bf16[256,128]{1,0:T(8,128)(2,1)S(1)} %get-tuple-element.106.send_0), channel_id=1, source_target_pairs={{0,1},{1,0},{2,3},{3,2},{4,5},{5,4},{6,7},{7,6},{8,9},{9,8},{10,11... | collective-permute-start | bytes 196616 | tf_op jit(solution)/shard_map/ppermute | solution.py:30
  34.7 1.3 %collective-permute-start.15 = (bf16[256,128]{1,0:T(8,128)(2,1)S(1)}, bf16[256,128]{1,0:T(8,128)(2,1)S(1)}, u32[]{:S(2)}, u32[]{:S(2)}) collective-permute-start(bf16[256,128]{1,0:T(8,128)(2,1)S(1)} %get-tuple-element.107.send_1), channel_id=1, source_target_pairs={{1,2},{2,1},{3,0},{0,3},{5,6},{6,5},{7,4},{4,7},{9,10},{10,9},{11,... | collective-permute-start | bytes 196616 | tf_op jit(solution)/shard_map/ppermute | solution.py:30
  36.0 0.5 %collective-permute-start.14 = (bf16[256,128]{1,0:T(8,128)(2,1)S(1)}, bf16[256,128]{1,0:T(8,128)(2,1)S(1)}, u32[]{:S(2)}, u32[]{:S(2)}) collective-permute-start(bf16[256,128]{1,0:T(8,128)(2,1)S(1)} %get-tuple-element.108.send_2), channel_id=1, source_target_pairs={{4,8},{8,4},{12,16},{16,12},{20,24},{24,20},{28,0},{0,28},{5,9},{9... | collective-permute-start | bytes 196616 | tf_op jit(solution)/shard_map/ppermute | solution.py:30
  36.5 1.1 %collective-permute-start.12 = (bf16[256,128]{1,0:T(8,128)(2,1)S(1)}, bf16[256,128]{1,0:T(8,128)(2,1)S(1)}, u32[]{:S(2)}, u32[]{:S(2)}) collective-permute-start(bf16[256,128]{1,0:T(8,128)(2,1)S(1)} %get-tuple-element.109.send_3), channel_id=1, source_target_pairs={{0,4},{4,0},{8,12},{12,8},{16,20},{20,16},{24,28},{28,24},{1,5},{5... | collective-permute-start | bytes 196616 | tf_op jit(solution)/shard_map/ppermute | solution.py:30
  37.6 2.1 %inner.7 = (f32[512,128]{1,0:T(8,128)S(1)}, bf16[4,256,128]{2,1,0:T(8,128)(2,1)S(1)}, f32[4,1024,128]{2,1,0:T(8,128)S(1)}) custom-call(bf16[512,128]{1,0:T(8,128)(2,1)S(1)} %get-tuple-element.105.latent_ref.refs_7_, bf16[256,128]{1,0:T(8,128)(2,1)S(1)} %get-tuple-element.106.send_0, bf16[256,128]{1,0:T(8,128)(2,1)S(1)} %get-tuple-element.107.send_1, ...), custom_call_target="tpu_custom_call" | custom-call | flops 1073741824 | bytes 8001536 | tf_op jit(solution)/shard_map/inner/pallas_call | solution.py:37
  39.7 1.1 %cross.7.total_ref = f32[512,128]{1,0:T(8,128)S(1)} custom-call(f32[512,128]{1,0:T(8,128)S(1)} %get-tuple-element.110.total_ref, bf16[256,128]{1,0:T(8,128)(2,1)S(1)} %collective-permute-done.12.refs_0_, bf16[256,128]{1,0:T(8,128)(2,1)S(1)} %collective-permute-done.13.refs_1_, bf16[4,2,128,128]{3,2,1,0:T(8,128)(2,1)S(1)} %get-tuple-element.63.ends_w_ref.refs_2_, ...), custom_call_target="tpu_custom_call" | custom-call | flops 1073741824 | bytes 7215104 | tf_op jit(solution)/shard_map/cross/pallas_call | solution.py:37
  40.9 2.3 %update.7 = bf16[512,128]{1,0:T(8,128)(2,1)} custom-call(f32[512,128]{1,0:T(8,128)S(1)} %cross.7.total_ref, bf16[256,128]{1,0:T(8,128)(2,1)S(1)} %collective-permute-done.14.refs_0_, bf16[256,128]{1,0:T(8,128)(2,1)S(1)} %collective-permute-done.15.refs_1_, bf16[4,2,128,128]{3,2,1,0:T(8,128)(2,1)S(1)} %get-tuple-element.63.ends_w_ref.refs_2_, ...), custom_call_target="tpu_custom_call" | custom-call | flops 1073741824 | bytes 7739392 | tf_op jit(solution)/shard_map/update/pallas_call | solution.py:37
  (42 shorter events, 0.1 us)
Async XLA Ops:
  0.0 9.4 %copy-start.10 = (f32[4,3,128]{2,0,1:T(4,128)S(1)}, f32[4,3,128]{2,0,1:T(4,128)}, u32[]{:S(2)}) copy-start(f32[4,3,128]{2,0,1:T(4,128)} %param.19) | copy-start | bytes 18436
  0.0 9.4 %copy-start.3 = (bf16[4,3,128,128]{3,2,1,0:T(8,128)(2,1)S(1)}, bf16[4,3,128,128]{3,2,1,0:T(8,128)(2,1)}, u32[]{:S(2)}) copy-start(bf16[4,3,128,128]{3,2,1,0:T(8,128)(2,1)} %nodes_ref.1) | copy-start | bytes 1179652
  0.0 9.4 %copy-start.2 = (bf16[4,4,128,128]{3,2,1,0:T(8,128)(2,1)S(1)}, bf16[4,4,128,128]{3,2,1,0:T(8,128)(2,1)}, u32[]{:S(2)}) copy-start(bf16[4,4,128,128]{3,2,1,0:T(8,128)(2,1)} %weights_ref.1) | copy-start | bytes 1572868
  0.0 9.4 %copy-start.9 = (s32[1,1,4,512]{3,2,1,0:T(4,128)S(1)}, s32[1,1,4,512]{3,2,1,0:T(4,128)}, u32[]{:S(2)}) copy-start(s32[1,1,4,512]{3,2,1,0:T(4,128)} %param.11) | copy-start | bytes 24580
  2.2 7.8 %copy-start.4 = (bf16[1,1,512,128]{3,2,1,0:T(8,128)(2,1)S(1)}, bf16[1,1,512,128]{3,2,1,0:T(8,128)(2,1)}, u32[]{:S(2)}) copy-start(bf16[1,1,512,128]{3,2,1,0:T(8,128)(2,1)} %param.10) | copy-start | bytes 393220
  2.2 7.8 %copy-start.5 = (bf16[272,128]{1,0:T(8,128)(2,1)S(1)}, bf16[272,128]{1,0:T(8,128)(2,1)}, u32[]{:S(2)}) copy-start(bf16[272,128]{1,0:T(8,128)(2,1)} %get-tuple-element.61.send_2) | copy-start | bytes 208900
  2.2 7.8 %copy-start.6 = (bf16[272,128]{1,0:T(8,128)(2,1)S(1)}, bf16[272,128]{1,0:T(8,128)(2,1)}, u32[]{:S(2)}) copy-start(bf16[272,128]{1,0:T(8,128)(2,1)} %get-tuple-element.60.send_1) | copy-start | bytes 208900
  2.2 7.8 %copy-start.7 = (bf16[272,128]{1,0:T(8,128)(2,1)S(1)}, bf16[272,128]{1,0:T(8,128)(2,1)}, u32[]{:S(2)}) copy-start(bf16[272,128]{1,0:T(8,128)(2,1)} %get-tuple-element.62.send_3) | copy-start | bytes 208900
  2.2 7.8 %copy-start.8 = (bf16[272,128]{1,0:T(8,128)(2,1)S(1)}, bf16[272,128]{1,0:T(8,128)(2,1)}, u32[]{:S(2)}) copy-start(bf16[272,128]{1,0:T(8,128)(2,1)} %get-tuple-element.59.send_0) | copy-start | bytes 208900
  2.2 9.5 %collective-permute-start.1 = (bf16[272,128]{1,0:T(8,128)(2,1)}, bf16[272,128]{1,0:T(8,128)(2,1)S(1)}, u32[]{:S(2)}, u32[]{:S(2)}) collective-permute-start(bf16[272,128]{1,0:T(8,128)(2,1)} %get-tuple-element.59.send_0), channel_id=1, source_target_pairs={{0,1},{1,0},{2,3},{3,2},{4,5},{5,4},{6,7},{7,6},{8,9},{9,8},{10,11... | collective-permute-start | bytes 208904 | tf_op jit(solution)/shard_map/ppermute | solution.py:30
  5.3 7.9 %collective-permute-start.3 = (bf16[272,128]{1,0:T(8,128)(2,1)}, bf16[272,128]{1,0:T(8,128)(2,1)S(1)}, u32[]{:S(2)}, u32[]{:S(2)}) collective-permute-start(bf16[272,128]{1,0:T(8,128)(2,1)} %get-tuple-element.60.send_1), channel_id=1, source_target_pairs={{1,2},{2,1},{3,0},{0,3},{5,6},{6,5},{7,4},{4,7},{9,10},{10,9},{11,... | collective-permute-start | bytes 208904 | tf_op jit(solution)/shard_map/ppermute | solution.py:30
  7.8 5.5 %collective-permute-start.2 = (bf16[272,128]{1,0:T(8,128)(2,1)}, bf16[272,128]{1,0:T(8,128)(2,1)S(1)}, u32[]{:S(2)}, u32[]{:S(2)}) collective-permute-start(bf16[272,128]{1,0:T(8,128)(2,1)} %get-tuple-element.61.send_2), channel_id=1, source_target_pairs={{4,8},{8,4},{12,16},{16,12},{20,24},{24,20},{28,0},{0,28},{5,9},{9... | collective-permute-start | bytes 208904 | tf_op jit(solution)/shard_map/ppermute | solution.py:30
  9.1 2.6 %collective-permute-start = (bf16[272,128]{1,0:T(8,128)(2,1)}, bf16[272,128]{1,0:T(8,128)(2,1)S(1)}, u32[]{:S(2)}, u32[]{:S(2)}) collective-permute-start(bf16[272,128]{1,0:T(8,128)(2,1)} %get-tuple-element.62.send_3), channel_id=1, source_target_pairs={{0,4},{4,0},{8,12},{12,8},{16,20},{20,16},{24,28},{28,24},{1,5},{5... | collective-permute-start | bytes 208904 | tf_op jit(solution)/shard_map/ppermute | solution.py:30
  10.0 1.7 %copy-start.11 = (s32[1,1,2,256]{3,2,1,0:T(2,128)S(1)}, s32[1,1,2,256]{3,2,1,0:T(2,128)}, u32[]{:S(2)}) copy-start(s32[1,1,2,256]{3,2,1,0:T(2,128)} %param.12) | copy-start | bytes 6148
  10.0 1.7 %copy-start.12 = (s32[1,1,2,256]{3,2,1,0:T(2,128)S(1)}, s32[1,1,2,256]{3,2,1,0:T(2,128)}, u32[]{:S(2)}) copy-start(s32[1,1,2,256]{3,2,1,0:T(2,128)} %param.13) | copy-start | bytes 6148
  10.0 1.7 %copy-start.13 = (bf16[2,16,128]{2,1,0:T(8,128)(2,1)S(1)}, bf16[2,16,128]{2,1,0:T(8,128)(2,1)}, u32[]{:S(2)}) copy-start(bf16[2,16,128]{2,1,0:T(8,128)(2,1)} %get-tuple-element.71.refs_6_.refs_9_) | copy-start | bytes 24580
  11.7 1.6 %copy-start = (bf16[4,256,256]{2,1,0:T(8,128)(2,1)S(1)}, bf16[4,256,256]{2,1,0:T(8,128)(2,1)}, u32[]{:S(2)}) copy-start(bf16[4,256,256]{2,1,0:T(8,128)(2,1)} %get-tuple-element.75.refs_12_.refs_16_) | copy-start | bytes 1572868
  11.7 1.6 %copy-start.1 = (bf16[4,256,128]{2,1,0:T(8,128)(2,1)S(1)}, bf16[4,256,128]{2,1,0:T(8,128)(2,1)}, u32[]{:S(2)}) copy-start(bf16[4,256,128]{2,1,0:T(8,128)(2,1)} %get-tuple-element.76.refs_13_.refs_17_) | copy-start | bytes 786436
  15.4 5.3 %collective-permute-start.5 = (bf16[256,128]{1,0:T(8,128)(2,1)S(1)}, bf16[256,128]{1,0:T(8,128)(2,1)S(1)}, u32[]{:S(2)}, u32[]{:S(2)}) collective-permute-start(bf16[256,128]{1,0:T(8,128)(2,1)S(1)} %get-tuple-element.78.send_0), channel_id=1, source_target_pairs={{0,1},{1,0},{2,3},{3,2},{4,5},{5,4},{6,7},{7,6},{8,9},{9,8},{10,11... | collective-permute-start | bytes 196616 | tf_op jit(solution)/shard_map/ppermute | solution.py:30
  16.1 6.1 %collective-permute-start.7 = (bf16[256,128]{1,0:T(8,128)(2,1)S(1)}, bf16[256,128]{1,0:T(8,128)(2,1)S(1)}, u32[]{:S(2)}, u32[]{:S(2)}) collective-permute-start(bf16[256,128]{1,0:T(8,128)(2,1)S(1)} %get-tuple-element.79.send_1), channel_id=1, source_target_pairs={{1,2},{2,1},{3,0},{0,3},{5,6},{6,5},{7,4},{4,7},{9,10},{10,9},{11,... | collective-permute-start | bytes 196616 | tf_op jit(solution)/shard_map/ppermute | solution.py:30
  17.0 5.2 %collective-permute-start.6 = (bf16[256,128]{1,0:T(8,128)(2,1)S(1)}, bf16[256,128]{1,0:T(8,128)(2,1)S(1)}, u32[]{:S(2)}, u32[]{:S(2)}) collective-permute-start(bf16[256,128]{1,0:T(8,128)(2,1)S(1)} %get-tuple-element.80.send_2), channel_id=1, source_target_pairs={{4,8},{8,4},{12,16},{16,12},{20,24},{24,20},{28,0},{0,28},{5,9},{9... | collective-permute-start | bytes 196616 | tf_op jit(solution)/shard_map/ppermute | solution.py:30
  17.9 2.8 %collective-permute-start.4 = (bf16[256,128]{1,0:T(8,128)(2,1)S(1)}, bf16[256,128]{1,0:T(8,128)(2,1)S(1)}, u32[]{:S(2)}, u32[]{:S(2)}) collective-permute-start(bf16[256,128]{1,0:T(8,128)(2,1)S(1)} %get-tuple-element.81.send_3), channel_id=1, source_target_pairs={{0,4},{4,0},{8,12},{12,8},{16,20},{20,16},{24,28},{28,24},{1,5},{5... | collective-permute-start | bytes 196616 | tf_op jit(solution)/shard_map/ppermute | solution.py:30
  24.0 7.0 %collective-permute-start.9 = (bf16[256,128]{1,0:T(8,128)(2,1)S(1)}, bf16[256,128]{1,0:T(8,128)(2,1)S(1)}, u32[]{:S(2)}, u32[]{:S(2)}) collective-permute-start(bf16[256,128]{1,0:T(8,128)(2,1)S(1)} %get-tuple-element.98.send_0), channel_id=1, source_target_pairs={{0,1},{1,0},{2,3},{3,2},{4,5},{5,4},{6,7},{7,6},{8,9},{9,8},{10,11... | collective-permute-start | bytes 196616 | tf_op jit(solution)/shard_map/ppermute | solution.py:30
  24.9 7.3 %collective-permute-start.11 = (bf16[256,128]{1,0:T(8,128)(2,1)S(1)}, bf16[256,128]{1,0:T(8,128)(2,1)S(1)}, u32[]{:S(2)}, u32[]{:S(2)}) collective-permute-start(bf16[256,128]{1,0:T(8,128)(2,1)S(1)} %get-tuple-element.99.send_1), channel_id=1, source_target_pairs={{1,2},{2,1},{3,0},{0,3},{5,6},{6,5},{7,4},{4,7},{9,10},{10,9},{11,... | collective-permute-start | bytes 196616 | tf_op jit(solution)/shard_map/ppermute | solution.py:30
  27.1 5.0 %collective-permute-start.10 = (bf16[256,128]{1,0:T(8,128)(2,1)S(1)}, bf16[256,128]{1,0:T(8,128)(2,1)S(1)}, u32[]{:S(2)}, u32[]{:S(2)}) collective-permute-start(bf16[256,128]{1,0:T(8,128)(2,1)S(1)} %get-tuple-element.100.send_2), channel_id=1, source_target_pairs={{4,8},{8,4},{12,16},{16,12},{20,24},{24,20},{28,0},{0,28},{5,9},{9... | collective-permute-start | bytes 196616 | tf_op jit(solution)/shard_map/ppermute | solution.py:30
  27.6 3.4 %collective-permute-start.8 = (bf16[256,128]{1,0:T(8,128)(2,1)S(1)}, bf16[256,128]{1,0:T(8,128)(2,1)S(1)}, u32[]{:S(2)}, u32[]{:S(2)}) collective-permute-start(bf16[256,128]{1,0:T(8,128)(2,1)S(1)} %get-tuple-element.101.send_3), channel_id=1, source_target_pairs={{0,4},{4,0},{8,12},{12,8},{16,20},{20,16},{24,28},{28,24},{1,5},{5... | collective-permute-start | bytes 196616 | tf_op jit(solution)/shard_map/ppermute | solution.py:30
  34.0 5.7 %collective-permute-start.13 = (bf16[256,128]{1,0:T(8,128)(2,1)S(1)}, bf16[256,128]{1,0:T(8,128)(2,1)S(1)}, u32[]{:S(2)}, u32[]{:S(2)}) collective-permute-start(bf16[256,128]{1,0:T(8,128)(2,1)S(1)} %get-tuple-element.106.send_0), channel_id=1, source_target_pairs={{0,1},{1,0},{2,3},{3,2},{4,5},{5,4},{6,7},{7,6},{8,9},{9,8},{10,11... | collective-permute-start | bytes 196616 | tf_op jit(solution)/shard_map/ppermute | solution.py:30
  34.7 6.2 %collective-permute-start.15 = (bf16[256,128]{1,0:T(8,128)(2,1)S(1)}, bf16[256,128]{1,0:T(8,128)(2,1)S(1)}, u32[]{:S(2)}, u32[]{:S(2)}) collective-permute-start(bf16[256,128]{1,0:T(8,128)(2,1)S(1)} %get-tuple-element.107.send_1), channel_id=1, source_target_pairs={{1,2},{2,1},{3,0},{0,3},{5,6},{6,5},{7,4},{4,7},{9,10},{10,9},{11,... | collective-permute-start | bytes 196616 | tf_op jit(solution)/shard_map/ppermute | solution.py:30
  36.0 4.9 %collective-permute-start.14 = (bf16[256,128]{1,0:T(8,128)(2,1)S(1)}, bf16[256,128]{1,0:T(8,128)(2,1)S(1)}, u32[]{:S(2)}, u32[]{:S(2)}) collective-permute-start(bf16[256,128]{1,0:T(8,128)(2,1)S(1)} %get-tuple-element.108.send_2), channel_id=1, source_target_pairs={{4,8},{8,4},{12,16},{16,12},{20,24},{24,20},{28,0},{0,28},{5,9},{9... | collective-permute-start | bytes 196616 | tf_op jit(solution)/shard_map/ppermute | solution.py:30
  36.5 3.2 %collective-permute-start.12 = (bf16[256,128]{1,0:T(8,128)(2,1)S(1)}, bf16[256,128]{1,0:T(8,128)(2,1)S(1)}, u32[]{:S(2)}, u32[]{:S(2)}) collective-permute-start(bf16[256,128]{1,0:T(8,128)(2,1)S(1)} %get-tuple-element.109.send_3), channel_id=1, source_target_pairs={{0,4},{4,0},{8,12},{12,8},{16,20},{20,16},{24,28},{28,24},{1,5},{5... | collective-permute-start | bytes 196616 | tf_op jit(solution)/shard_map/ppermute | solution.py:30
